TPU v7x, 32 devices: a whole 2x2x4 slice. The times are simulated.
32 devices in a mesh: row: 8 (over z, x), col: 4 (over y, core).
Axes of the slice: x: 2, y: 2, z: 4, core: 2. Of those that a mesh axis runs over, the one named last changes fastest.
Arguments:
- data: float32 [32768, 4096], P('row', 'col'), may hold values from -17 to 17
- omega: float32 [4096, 128], P('col'), may hold values from -0.09375 to 0.09375
Outputs:
- basis: float32 [32768, 128], P(('row', 'col'))
- projected: float32 [128, 4096], P(None, 'col')
- small_gram: float32 [128, 128], replicated
All inputs are finite; a program needn't handle non-finite values.
Results may differ from a plain program's by a relative error of at most 0.0003.
Values sent between devices are 32-bit elements; how exact they have to be, the bound alone decides.
No kernel may reach another device: no remote copies, remote signals or barrier semaphores. Data moves between devices by JAX's collectives and lax.ppermute only.
A program may use at most 64 MiB of HBM per device.

v0:
```python
import jax
import jax.numpy as jnp
from jax import lax
from jax.sharding import PartitionSpec as P

high = lax.Precision.HIGHEST


def lower_factor(local_rows):
    gram = jnp.dot(local_rows.T, local_rows, precision=high, preferred_element_type=jnp.float32)
    summed = lax.psum(gram, ("row", "col"))
    return jnp.linalg.cholesky(summed)


def per_device(data, omega):
    ncol = lax.axis_size("col")
    part_rows = data.shape[0] // ncol
    total_rows = data.shape[0] * lax.axis_size("row")
    partial_value = jnp.dot(data, omega, precision=high, preferred_element_type=jnp.float32)
    sketch = lax.psum(partial_value, "col")
    own = lax.dynamic_slice_in_dim(sketch, lax.axis_index("col") * part_rows, part_rows, 0)
    lower = lower_factor(own)
    full_basis = jax.scipy.linalg.solve_triangular(lower, sketch.T, lower=True).T
    basis = lax.dynamic_slice_in_dim(full_basis, lax.axis_index("col") * part_rows, part_rows, 0)
    proj_part = lax.dot_general(
        full_basis,
        data,
        (((0,), (0,)), ((), ())),
        precision=high,
        preferred_element_type=jnp.float32,
    )
    projected = lax.psum(proj_part, "row")
    gram_part = jnp.dot(projected, projected.T, precision=high, preferred_element_type=jnp.float32)
    small_gram = lax.psum(gram_part, "col") / total_rows
    return (basis, projected, small_gram)


def solution(mesh):
    placed = (P("row", "col"), P("col", None))
    return jax.shard_map(
        per_device,
        mesh=mesh,
        in_specs=placed,
        out_specs=(P(("row", "col"), None), P(None, "col"), P()),
        check_vma=False,
    )
```

profile of v0, /device:TPU:0, one launch (start us, length us, event | category | flops | bytes accessed | tf_op | source)
XLA Modules:
  0.0 360.3 jit_solution(3946188736815196395)
XLA Ops:
  7.2 0.0 copy-start
  7.2 0.0 all-reduce.5.cloned.1.call-start
  7.2 1.0 copy-done
  8.2 17.2 %fusion.7 = f32[4096,128]{1,0:T(8,128)} fusion(f32[4096,1024]{1,0:T(8,128)} %param.2, f32[1024,128]{1,0:T(8,128)S(1)} %copy-done), kind=kOutput, calls=%fused_computation.15 | convolution fusion | flops 6442450944 | bytes 19398656 | tf_op jit(solution)/shard_map/dot_general | solution.py:19
  25.4 0.0 all-reduce.5.cloned.1.call-update
  25.4 0.0 all-reduce.7.cloned.1.call-start
  25.5 54.2 %all-reduce.5.cloned.1.call-done = f32[4096,128]{1,0:T(8,128)} async-done(((f32[4096,128]{1,0:T(8,128)}), f32[4096,128]{1,0:T(8,128)}) %all-reduce.5.cloned.1.call-update) | async-done | bytes 2097168 | tf_op jit(solution)/shard_map/psum | solution.py:20
  79.6 2.8 fusion
  82.5 0.0 all-reduce.7.cloned.1.call-update
  82.5 0.2 all-reduce.9.cloned.1.call-start
  82.7 121.6 %all-reduce.7.cloned.1.call-done = f32[128,128]{0,1:T(8,128)} async-done(((f32[128,128]{0,1:T(8,128)}), f32[128,128]{0,1:T(8,128)}) %all-reduce.7.cloned.1.call-update) | async-done | bytes 65552 | tf_op jit(solution)/shard_map/psum | solution.py:11
  204.4 0.9 copy.6
  205.3 0.9 fusion.5
  206.1 11.7 %cholesky.16 = f32[128,128]{1,0:T(8,128)S(1)} custom-call(f32[128,128]{1,0:T(8,128)S(1)} %fusion.5), custom_call_target="Cholesky" | custom-call | tf_op jit(solution)/shard_map/jit(cholesky)/cholesky | solution.py:12
  217.9 0.6 compare_reduce_fusion
  218.5 0.7 fusion.2
  219.2 9.8 %custom-call.7 = f32[1,128,128]{1,2,0:T(8,128)S(1)} custom-call(f32[1,128,128]{2,1,0:T(8,128)S(1)} %fusion.2), custom_call_target="InvertDiagBlocksLowerTriangular" | custom-call | tf_op jit(solution)/shard_map/jit(_solve_triangular)/triangular_solve | solution.py:23
  229.0 3.5 fusion.3
  232.5 12.6 %fusion.8 = f32[128,1024]{1,0:T(8,128)} fusion(f32[128,4096]{1,0:T(8,128)S(1)} %fusion.3, f32[4096,1024]{1,0:T(8,128)} %param.2), kind=kOutput, calls=%fused_computation.16 | convolution fusion | flops 6442450944 | bytes 19398656 | tf_op jit(solution)/shard_map/dot_general | solution.py:25
  245.1 0.0 all-reduce.9.cloned.1.call-update
  245.1 0.0 all-reduce.11.cloned.1.call-start
  245.2 73.2 %all-reduce.9.cloned.1.call-done = f32[128,1024]{1,0:T(8,128)} async-done(((f32[128,1024]{1,0:T(8,128)}), f32[128,1024]{1,0:T(8,128)}) %all-reduce.9.cloned.1.call-update) | async-done | bytes 524304 | tf_op jit(solution)/shard_map/psum | solution.py:32
  318.4 0.0 copy-start.1
  318.4 2.5 fusion.9
  320.9 0.0 all-reduce.11.cloned.1.call-update
  320.9 0.8 dynamic-slice_bitcast_fusion
  321.7 2.0 copy.7
  323.8 27.8 %all-reduce.11.cloned.1.call-done = f32[128,128]{1,0:T(8,128)} async-done(((f32[128,128]{1,0:T(8,128)}), f32[128,128]{1,0:T(8,128)}) %all-reduce.11.cloned.1.call-update) | async-done | bytes 65552 | tf_op jit(solution)/shard_map/psum | solution.py:34
  351.5 1.5 broadcast_multiply_fusion
  353.0 0.0 copy-done.1
  353.0 0.8 copy.13
  (1 shorter events, 0.0 us)
Async XLA Ops:
  7.2 1.0 copy-start
  7.2 72.5 %all-reduce.5.cloned.1.call-start = ((), (), s32[]{:S(2)}) async-start(), calls=%async_computation | async-start | bytes 4194304 | tf_op jit(solution)/shard_map/psum | solution.py:20
  25.4 178.9 %all-reduce.7.cloned.1.call-start = ((), (), s32[]{:S(2)}) async-start(), calls=%async_computation.1 | async-start | bytes 131072 | tf_op jit(solution)/shard_map/psum | solution.py:11
  82.5 235.9 %all-reduce.9.cloned.1.call-start = ((), (), s32[]{:S(2)}) async-start(), calls=%async_computation.2 | async-start | bytes 1048576 | tf_op jit(solution)/shard_map/psum | solution.py:32
  245.1 106.4 %all-reduce.11.cloned.1.call-start = ((), (), s32[]{:S(2)}) async-start(), calls=%async_computation.3 | async-start | bytes 131072 | tf_op jit(solution)/shard_map/psum | solution.py:34
  318.4 34.6 %copy-start.1 = (f32[128,1024]{1,0:T(8,128)S(1)}, f32[128,1024]{1,0:T(8,128)}, u32[]{:S(2)}) copy-start(f32[128,1024]{1,0:T(8,128)} %all-reduce.9.cloned.1.call-done) | copy-start | bytes 1572868
Sparse Core Ops, SparseCore 0:
  25.5 54.0 all-reduce.4
  86.7 117.5 all-reduce.6
  245.3 73.0 all-reduce.8
  321.1 30.3 all-reduce.10
where the time goes:
time: 361 us; the launch traced here: 360 us
  waiting for transfers between devices  277 us (77%)
  matrix products  38.6 us (11%)
  other arithmetic  25.2 us (7%)
  between operations  13.8 us (4%)
  local copies, waits for them, and re-layouts  5.59 us (2%)
    psum x1, waiting for transfers between devices, lower_factor(): summed = lax.psum(gram, ('row', 'col'))  122 us
    psum x1, waiting for transfers between devices, per_device(): projected = lax.psum(proj_part, 'row')  73.2 us
    psum x1, waiting for transfers between devices, per_device(): sketch = lax.psum(partial_value, 'col')  54.2 us
    psum x1, waiting for transfers between devices, per_device(): small_gram = lax.psum(gram_part, 'col') / total_rows  27.8 us
    dot_general x1, matrix products, per_device(): jnp.dot(data, omega, precision=high, preferred_element_type=jnp.float32)  17.2 us
    dot_general x1, matrix products, per_device(): lax.dot_general(full_basis, data, (((0,), (0,)), ((), ())), precision=hig...  12.6 us
    another operation x3, other arithmetic, lower_factor(): return jnp.linalg.cholesky(summed)  12.4 us
    another operation x2, other arithmetic, per_device(): jax.scipy.linalg.solve_triangular(lower, sketch.T, lower=True)  10.5 us
  transfers between devices with their start and end apart: 4, of which 4 were waited for; matrix products, arithmetic and copies ran while one was open for 1% of the time, Pallas kernels for 0%

commit v1 on v0

v1 whole, which is shorter than its diff:
```python
import functools

import jax
import jax.numpy as jnp
from jax import lax
from jax.experimental import pallas as pl
from jax.experimental.pallas import tpu as pltpu
from jax.sharding import PartitionSpec as P

high = lax.Precision.HIGHEST
f32 = jnp.float32
bf16 = jnp.bfloat16

BLOCK = 256
SLICE = 128
VMEM = 48 * 1024 * 1024


def split(value):
    upper = value.astype(bf16)
    return upper, (value - upper.astype(f32)).astype(bf16)


def swap(value, axis, bit):
    return lax.ppermute(value, axis, [(i, i ^ bit) for i in range(lax.axis_size(axis))])


def sketch_kernel(own_ref, data_ref, omega_ref, out_ref, wide_ref):
    @pl.when(pl.program_id(0) + pl.program_id(1) == 0)
    def _():
        upper, rest = split(omega_ref[...])
        width = omega_ref.shape[1]
        wide_ref[:, :width] = upper
        wide_ref[:, width:] = rest

    width = omega_ref.shape[1]
    upper, rest = split(data_ref[...])
    both = jnp.dot(upper, wide_ref[...], preferred_element_type=f32)
    more = jnp.dot(rest, wide_ref[:, :width], preferred_element_type=f32)
    out_ref[0] = both[:, :width] + both[:, width:] + more


def partial_sketch(own, data, omega, places, first, rows):
    quarter = data.shape[0] // lax.axis_size("col")
    per_quarter = quarter // BLOCK
    start = first // BLOCK
    steps = rows // BLOCK
    width = omega.shape[1]
    base = places[0]
    gap = places[1] - places[0]
    return pl.pallas_call(
        sketch_kernel,
        grid_spec=pltpu.PrefetchScalarGridSpec(
            num_scalar_prefetch=1,
            grid=(2, steps),
            in_specs=[
                pl.BlockSpec(
                    (BLOCK, data.shape[1]),
                    lambda p, i, own: (((base + gap * p) ^ own[0]) * per_quarter + start + i, 0),
                ),
                pl.BlockSpec(omega.shape, lambda p, i, own: (0, 0)),
            ],
            out_specs=pl.BlockSpec((1, BLOCK, width), lambda p, i, own: (p, i, 0)),
            scratch_shapes=[pltpu.VMEM((omega.shape[0], 2 * width), bf16)],
        ),
        out_shape=jax.ShapeDtypeStruct((2, rows, width), f32),
        compiler_params=pltpu.CompilerParams(vmem_limit_bytes=VMEM),
        cost_estimate=pl.CostEstimate(
            flops=2 * rows * data.shape[1] * width * 2 * 4,
            bytes_accessed=2 * rows * data.shape[1] * 4,
            transcendentals=0,
        ),
        name="partial_sketch",
    )(own, data, omega)


def project_kernel(count, split_out, own_ref, *refs):
    has_before = len(refs) > count + 1 + (3 if split_out else 1)
    data_ref = refs[0]
    parts = refs[1 : 1 + count]
    before = refs[1 + count] if has_before else None
    outs = refs[1 + count + (1 if has_before else 0) :]
    total = outs[-1] if split_out else outs[0]
    part, step = pl.program_id(0), pl.program_id(1)

    @pl.when(part + step == 0)
    def _():
        total[...] = before[...] if has_before else jnp.zeros_like(total)

    d_upper, d_rest = split(data_ref[...])
    for k in range(count):

        @pl.when(part == k)
        def _():
            turned = parts[k][...].T
            upper, rest = split(turned)
            both = jnp.dot(jnp.concatenate([upper, rest], 0), d_upper, preferred_element_type=f32)
            more = jnp.dot(upper, d_rest, preferred_element_type=f32)
            width = turned.shape[0]
            total[...] += both[:width] + both[width:] + more

    if split_out:
        send_ref, keep_ref = outs[0], outs[1]
        half = send_ref.shape[0]

        @pl.when((part == count - 1) & (step == pl.num_programs(1) - 1))
        def _():
            me = own_ref[1]
            for i in range(half):
                for ref, place in ((keep_ref, 2 * i), (send_ref, 2 * i + 1)):
                    at = pl.multiple_of((place ^ me) * SLICE, SLICE)
                    ref[i] = total[:, pl.ds(at, SLICE)]


def project(own, data, parts, places, first, before=None, split_out=False):
    count = len(parts)
    rows, width = parts[0].shape
    quarter = data.shape[0] // lax.axis_size("col")
    per_quarter = quarter // BLOCK
    start = first // BLOCK
    cols = data.shape[1]
    base = places[0]
    gap = places[1] - places[0] if count > 1 else 0
    whole = pl.BlockSpec((width, cols), lambda p, i, own: (0, 0))
    slices = cols // SLICE

    def part_spec(k):
        return pl.BlockSpec((BLOCK, width), lambda p, i, own: (jnp.where(p == k, i, 0 if k else rows // BLOCK - 1), 0))

    if split_out:
        half = pl.BlockSpec((slices // 2, width, SLICE), lambda p, i, own: (0, 0, 0))
        out_specs = [half, half]
        out_shape = [jax.ShapeDtypeStruct((slices // 2, width, SLICE), f32)] * 2
        scratch = [pltpu.VMEM((width, cols), f32)]
    else:
        out_specs = whole
        out_shape = jax.ShapeDtypeStruct((width, cols), f32)
        scratch = []
    args = [own, data, *parts]
    specs = [
        pl.BlockSpec(
            (BLOCK, cols),
            lambda p, i, own: (((base + gap * p) ^ own[0]) * per_quarter + start + i, 0),
        ),
        *[part_spec(k) for k in range(count)],
    ]
    if before is not None:
        args.append(before)
        specs.append(whole)
    return pl.pallas_call(
        functools.partial(project_kernel, count, split_out),
        grid_spec=pltpu.PrefetchScalarGridSpec(
            num_scalar_prefetch=1,
            grid=(count, rows // BLOCK),
            in_specs=specs,
            out_specs=out_specs,
            scratch_shapes=scratch,
        ),
        out_shape=out_shape,
        compiler_params=pltpu.CompilerParams(vmem_limit_bytes=VMEM),
        cost_estimate=pl.CostEstimate(
            flops=2 * count * rows * cols * width * 4,
            bytes_accessed=count * rows * cols * 4,
            transcendentals=0,
        ),
        name="project",
    )(*args)


def finish_kernel(own_ref, inverse_ref, first_ref, second_ref, out_ref, gram_ref):
    me = own_ref[1]
    gram = jnp.zeros_like(gram_ref)
    half = first_ref.shape[0]
    for i in range(half):
        for ref, place in ((first_ref, 2 * i), (second_ref, 2 * i + 1)):
            at = pl.multiple_of((place ^ me) * SLICE, SLICE)
            piece = jnp.dot(inverse_ref[...], ref[i], precision=high, preferred_element_type=f32)
            out_ref[:, pl.ds(at, SLICE)] = piece
            gram += lax.dot_general(
                piece, piece, (((1,), (1,)), ((), ())), precision=high, preferred_element_type=f32
            )
    gram_ref[...] = gram


def finish(own, inverse, evens, odds):
    half, width, _ = evens.shape
    return pl.pallas_call(
        finish_kernel,
        in_specs=[pl.BlockSpec(memory_space=pltpu.SMEM)] + [pl.BlockSpec(memory_space=pltpu.VMEM)] * 3,
        out_specs=[pl.BlockSpec(memory_space=pltpu.VMEM)] * 2,
        out_shape=[
            jax.ShapeDtypeStruct((width, 2 * half * SLICE), f32),
            jax.ShapeDtypeStruct((width, width), f32),
        ],
        compiler_params=pltpu.CompilerParams(vmem_limit_bytes=VMEM),
        name="finish",
    )(own, inverse, evens, odds)


CHUNKS = 2


def per_device(data, omega):
    nrow, ncol = lax.axis_size("row"), lax.axis_size("col")
    assert ncol == 4
    total_rows = data.shape[0] * nrow
    quarter = data.shape[0] // ncol
    slices = data.shape[1] // SLICE
    me_row = lax.axis_index("row")
    own = jnp.stack([lax.axis_index("col"), me_row % slices]).astype(jnp.int32)
    rows = quarter // CHUNKS

    owned = []
    for j in range(CHUNKS):
        send = partial_sketch(own, data, omega, (1, 3), j * rows, rows)
        keep = partial_sketch(own, data, omega, (0, 2), j * rows, rows)
        keep = keep + swap(send, "col", 1)
        owned.append(keep[0] + swap(keep[1], "col", 2))

    gram = sum(jnp.dot(v.T, v, precision=high, preferred_element_type=f32) for v in owned)
    bits = [1 << k for k in range(nrow.bit_length() - 1)]
    gram = gram + swap(gram, "col", 1)
    for bit in bits:
        gram = gram + swap(gram, "row", bit)
    gram = gram + swap(gram, "col", 2)

    second = [swap(v, "col", 1) for v in owned]
    third = [swap(v, "col", 2) for v in owned]
    fourth = [swap(v, "col", 1) for v in third]
    acc = None
    for j in range(CHUNKS):
        acc = project(own, data, [owned[j], second[j]], (0, 1), j * rows, acc)
    for j in range(CHUNKS):
        acc = project(own, data, [third[j], fourth[j]], (2, 3), j * rows, acc, j == CHUNKS - 1)
    send, keep = acc

    halving = [b for b in bits if b < slices]
    keep = keep + swap(send, "row", 1)
    for bit in reversed(halving[1:]):
        half = keep.shape[0] // 2
        keep = keep[:half] + swap(keep[half:], "row", bit)
    for bit in bits[len(halving) :]:
        keep = keep + swap(keep, "row", bit)
    for bit in halving[1:]:
        keep = jnp.concatenate([keep, swap(keep, "row", bit)], 0)
    other = swap(keep, "row", 1)

    lower = jnp.linalg.cholesky(gram)
    inverse = jax.scipy.linalg.solve_triangular(lower, jnp.eye(gram.shape[0], dtype=f32), lower=True)
    sketch = jnp.concatenate(owned, 0)
    basis = lax.dot_general(
        sketch, inverse, (((1,), (1,)), ((), ())), precision=high, preferred_element_type=f32
    )
    projected, small = finish(own, inverse, keep, other)
    small = small + swap(small, "col", 1)
    small = small + swap(small, "col", 2)
    return (basis, projected, small / total_rows)


def solution(mesh):
    placed = (P("row", "col"), P("col", None))
    return jax.shard_map(
        per_device,
        mesh=mesh,
        in_specs=placed,
        out_specs=(P(("row", "col"), None), P(None, "col"), P()),
        check_vma=False,
    )
```

time: 361 us -> 133 us (0.37)
  waiting for transfers between devices: 277 us -> 36.9 us
  Pallas kernels: 0 us -> 42.1 us
  matrix products: 38.6 us -> 2.8 us
  starting transfers between devices: 0.35 us -> 24.6 us
  between operations: 13.8 us -> 0.92 us
  local copies, waits for them, and re-layouts: 5.59 us -> 1.18 us
    psum x4 -> x0, waiting for transfers between devices: 277 us -> none  [the longest x1 122 us: lower_factor(): summed = lax.psum(gram, ('row', 'col'))]
    pallas_call x0 -> x9, Pallas kernels: none -> 42.1 us  [the longest x4 20.6 us: project(): pl.pallas_call(functools.partial(project_kernel, count, split_out), grid_...]
    ppermute x0 -> x23, waiting for transfers between devices: none -> 36.9 us  [swap(): lax.ppermute(value, axis, [(i, i ^ bit) for i in range(lax.axis_size(axis...]
    dot_general x4 -> x3, matrix products: 35.1 us -> 2.55 us  [the longest x1 1.38 us: per_device(): lax.dot_general(sketch, inverse, (((1,), (1,)), ((), ())), precision=high...]
    ppermute x0 -> x23, starting transfers between devices: none -> 24.6 us  [swap(): lax.ppermute(value, axis, [(i, i ^ bit) for i in range(lax.axis_size(axis...]
    another operation x5 -> x6, other arithmetic: 22.9 us -> 22.9 us  [the longest x3 12.4 us: per_device(): lower = jnp.linalg.cholesky(gram)]
  transfers between devices with their start and end apart: 4 -> 23, of which waited for: 4 -> 12; matrix products, arithmetic and copies ran while one was open for 1% -> 20% of each run, Pallas kernels for 0% -> 22%
where the time goes in v1:
time: 133 us; the launch traced here: 132 us
  Pallas kernels  42.1 us (32%)
  waiting for transfers between devices  36.9 us (28%)
  starting transfers between devices  24.6 us (18%)
  other arithmetic  23.9 us (18%)
  matrix products  2.8 us (2%)
    ppermute x23, waiting for transfers between devices, swap(): lax.ppermute(value, axis, [(i, i ^ bit) for i in range(lax.axis_size(axis...  36.9 us
    ppermute x23, starting transfers between devices, swap(): lax.ppermute(value, axis, [(i, i ^ bit) for i in range(lax.axis_size(axis...  24.6 us
    pallas_call x4, Pallas kernels, project(): pl.pallas_call(functools.partial(project_kernel, count, split_out), grid_...  20.6 us
    pallas_call x4, Pallas kernels, partial_sketch(): pl.pallas_call(sketch_kernel, grid_spec=pltpu.PrefetchScalarGridSpec(num_...  18.2 us
    another operation x3, other arithmetic, per_device(): lower = jnp.linalg.cholesky(gram)  12.4 us
    another operation x2, other arithmetic, per_device(): jax.scipy.linalg.solve_triangular(lower, jnp.eye(gram.shape[0], dtype=f32...  10.5 us
    pallas_call x1, Pallas kernels, finish(): pl.pallas_call(finish_kernel, in_specs=[pl.BlockSpec(memory_space=pltpu.S...  3.32 us
  transfers between devices with their start and end apart: 23, of which 12 were waited for; matrix products, arithmetic and copies ran while one was open for 20% of the time, Pallas kernels for 22%

profile of v1, /device:TPU:0, one launch (start us, length us, event | category | flops | bytes accessed | tf_op | source)
XLA Modules:
  0.0 132.5 jit_solution(967891999835283970)
XLA Ops:
  1.8 4.5 %partial_sketch.5 = f32[2,512,128]{2,1,0:T(8,128)S(1)} custom-call(s32[2]{0:T(128)S(1)} %pad_add_fusion.own_ref, f32[4096,1024]{1,0:T(8,128)} %refs_0_.7, f32[1024,128]{1,0:T(8,128)S(1)} %copy-done), custom_call_target="tpu_custom_call" | custom-call | flops 1073741824 | bytes 4194304 | tf_op jit(solution)/shard_map/partial_sketch/pallas_call | solution.py:51
  6.8 4.6 %partial_sketch.7 = f32[2,512,128]{2,1,0:T(8,128)S(1)} custom-call(s32[2]{0:T(128)S(1)} %pad_add_fusion.own_ref, f32[4096,1024]{1,0:T(8,128)} %refs_0_.7, f32[1024,128]{1,0:T(8,128)S(1)} %copy-done), custom_call_target="tpu_custom_call" | custom-call | flops 1073741824 | bytes 4194304 | tf_op jit(solution)/shard_map/partial_sketch/pallas_call | solution.py:51
  11.5 4.5 %partial_sketch.4 = f32[2,512,128]{2,1,0:T(8,128)S(1)} custom-call(s32[2]{0:T(128)S(1)} %pad_add_fusion.own_ref, f32[4096,1024]{1,0:T(8,128)} %refs_0_.7, f32[1024,128]{1,0:T(8,128)S(1)} %copy-done), custom_call_target="tpu_custom_call" | custom-call | flops 1073741824 | bytes 4194304 | tf_op jit(solution)/shard_map/partial_sketch/pallas_call | solution.py:51
  16.2 3.0 %collective-permute-start.1 = (f32[512,128]{1,0:T(8,128)S(1)}, f32[512,128]{1,0:T(8,128)S(1)}, u32[]{:S(2)}, u32[]{:S(2)}) collective-permute-start(f32[512,128]{1,0:T(8,128)S(1)} %slice_bitcast_fusion.2), channel_id=1, source_target_pairs={{0,2},{1,3},{2,0},{3,1},{4,6},{5,7},{6,4},{7,5},{8,10},{9,11},{10,... | collective-permute-start | bytes 786440 | tf_op jit(solution)/shard_map/ppermute | solution.py:25
  19.2 4.6 %partial_sketch.6 = f32[2,512,128]{2,1,0:T(8,128)S(1)} custom-call(s32[2]{0:T(128)S(1)} %pad_add_fusion.own_ref, f32[4096,1024]{1,0:T(8,128)} %refs_0_.7, f32[1024,128]{1,0:T(8,128)S(1)} %copy-done), custom_call_target="tpu_custom_call" | custom-call | flops 1073741824 | bytes 4194304 | tf_op jit(solution)/shard_map/partial_sketch/pallas_call | solution.py:51
  23.9 1.8 %collective-permute-done.1 = f32[512,128]{1,0:T(8,128)S(1)} collective-permute-done((f32[512,128]{1,0:T(8,128)S(1)}, f32[512,128]{1,0:T(8,128)S(1)}, u32[]{:S(2)}, u32[]{:S(2)}) %collective-permute-start.1) | collective-permute-done | bytes 262176 | tf_op jit(solution)/shard_map/ppermute | solution.py:25
  25.8 2.5 %collective-permute-start.11 = (f32[512,128]{1,0:T(8,128)S(1)}, f32[512,128]{1,0:T(8,128)S(1)}, u32[]{:S(2)}, u32[]{:S(2)}) collective-permute-start(f32[512,128]{1,0:T(8,128)S(1)} %fusion.5.refs_1_), channel_id=1, source_target_pairs={{0,2},{1,3},{2,0},{3,1},{4,6},{5,7},{6,4},{7,5},{8,10},{9,11},{10,... | collective-permute-start | bytes 786440 | tf_op jit(solution)/shard_map/ppermute | solution.py:25
  28.3 4.8 %collective-permute-done.3 = f32[512,128]{1,0:T(8,128)S(1)} collective-permute-done((f32[512,128]{1,0:T(8,128)S(1)}, f32[512,128]{1,0:T(8,128)S(1)}, u32[]{:S(2)}, u32[]{:S(2)}) %collective-permute-start.3) | collective-permute-done | bytes 262176 | tf_op jit(solution)/shard_map/ppermute | solution.py:25
  34.5 4.3 %collective-permute-done.11.refs_1_ = f32[512,128]{1,0:T(8,128)S(1)} collective-permute-done((f32[512,128]{1,0:T(8,128)S(1)}, f32[512,128]{1,0:T(8,128)S(1)}, u32[]{:S(2)}, u32[]{:S(2)}) %collective-permute-start.11) | collective-permute-done | bytes 262176 | tf_op jit(solution)/shard_map/ppermute | solution.py:25
  39.4 3.8 %collective-permute-done.9.refs_1_ = f32[512,128]{1,0:T(8,128)S(1)} collective-permute-done((f32[512,128]{1,0:T(8,128)S(1)}, f32[512,128]{1,0:T(8,128)S(1)}, u32[]{:S(2)}, u32[]{:S(2)}) %collective-permute-start.9) | collective-permute-done | bytes 262176 | tf_op jit(solution)/shard_map/ppermute | solution.py:25
  43.1 5.1 %project.4.refs_3_ = f32[128,1024]{1,0:T(8,128)S(1)} custom-call(s32[2]{0:T(128)S(1)} %pad_add_fusion.own_ref, f32[4096,1024]{1,0:T(8,128)} %refs_0_.7, f32[512,128]{1,0:T(8,128)S(1)} %fusion.5.refs_1_, f32[512,128]{1,0:T(8,128)S(1)} %collective-permute-done.14.refs_2_), custom_call_target="tpu_custom_call" | custom-call | flops 1073741824 | bytes 4194304 | tf_op jit(solution)/shard_map/project/pallas_call | solution.py:150
  48.2 5.1 %project.5.refs_3_ = f32[128,1024]{1,0:T(8,128)S(1)} custom-call(s32[2]{0:T(128)S(1)} %pad_add_fusion.own_ref, f32[4096,1024]{1,0:T(8,128)} %refs_0_.7, f32[512,128]{1,0:T(8,128)S(1)} %fusion.4.refs_1_, f32[512,128]{1,0:T(8,128)S(1)} %collective-permute-done.13.refs_2_, f32[128,1024]{1,0:T(8,128)S(1)} %project.4.refs_3_), custom_call_target="tpu_custom_call" | custom-call | flops 1073741824 | bytes 4194304 | tf_op jit(solution)/shard_map/project/pallas_call | solution.py:150
  53.3 5.1 %project.6.refs_3_ = f32[128,1024]{1,0:T(8,128)S(1)} custom-call(s32[2]{0:T(128)S(1)} %pad_add_fusion.own_ref, f32[4096,1024]{1,0:T(8,128)} %refs_0_.7, f32[512,128]{1,0:T(8,128)S(1)} %collective-permute-done.11.refs_1_, f32[512,128]{1,0:T(8,128)S(1)} %collective-permute-done.12.refs_2_, f32[128,1024]{1,0:T(8,128)S(1)} %project.5.refs_3_), custom_call_target="tpu_custom_call" | custom-call | flops 1073741824 | bytes 4194304 | tf_op jit(solution)/shard_map/project/pallas_call | solution.py:150
  58.4 5.4 %project.7 = (f32[4,128,128]{2,1,0:T(8,128)S(1)}, f32[4,128,128]{2,1,0:T(8,128)S(1)}) custom-call(s32[2]{0:T(128)S(1)} %pad_add_fusion.own_ref, f32[4096,1024]{1,0:T(8,128)} %refs_0_.7, f32[512,128]{1,0:T(8,128)S(1)} %collective-permute-done.9.refs_1_, f32[512,128]{1,0:T(8,128)S(1)} %collective-permute-done.10.refs_2_, f32[128,1024]{1,0:T(8,128)S(1)} %project.6.refs_3_), custom_call_target="tpu_custom_call" | custom-call | flops 1073741824 | bytes 4194304 | tf_op jit(solution)/shard_map/project/pallas_call | solution.py:150
  63.8 1.6 %collective-permute-start.15 = (f32[4,128,128]{2,1,0:T(8,128)S(1)}, f32[4,128,128]{2,1,0:T(8,128)S(1)}, u32[]{:S(2)}, u32[]{:S(2)}) collective-permute-start(f32[4,128,128]{2,1,0:T(8,128)S(1)} %get-tuple-element.8), channel_id=1, source_target_pairs={{0,4},{4,0},{8,12},{12,8},{16,20},{20,16},{24,28},{28,24},{1,5},{5... | collective-permute-start | bytes 786440 | tf_op jit(solution)/shard_map/ppermute | solution.py:25
  67.8 6.1 %collective-permute-done.5 = f32[128,128]{0,1:T(8,128)S(1)} collective-permute-done((f32[128,128]{0,1:T(8,128)S(1)}, f32[128,128]{0,1:T(8,128)S(1)}, u32[]{:S(2)}, u32[]{:S(2)}) %collective-permute-start.5) | collective-permute-done | bytes 65568 | tf_op jit(solution)/shard_map/ppermute | solution.py:25
  74.0 1.6 %collective-permute-start.6 = (f32[128,128]{0,1:T(8,128)S(1)}, f32[128,128]{0,1:T(8,128)S(1)}, u32[]{:S(2)}, u32[]{:S(2)}) collective-permute-start(f32[128,128]{0,1:T(8,128)S(1)} %add.68), channel_id=1, source_target_pairs={{0,8},{4,12},{8,0},{12,4},{16,24},{20,28},{24,16},{28,20},{1,9},{5... | collective-permute-start | bytes 196616 | tf_op jit(solution)/shard_map/ppermute | solution.py:25
  75.7 2.7 %collective-permute-start.16 = (f32[2,128,128]{2,1,0:T(8,128)S(1)}, f32[2,128,128]{2,1,0:T(8,128)S(1)}, u32[]{:S(2)}, u32[]{:S(2)}) collective-permute-start(f32[2,128,128]{2,1,0:T(8,128)S(1)} %slice.49), channel_id=1, source_target_pairs={{0,16},{4,20},{8,24},{12,28},{16,0},{20,4},{24,8},{28,12},{1,17},{... | collective-permute-start | bytes 393224 | tf_op jit(solution)/shard_map/ppermute | solution.py:25
  78.3 3.4 %collective-permute-start.7 = (f32[128,128]{0,1:T(8,128)S(1)}, f32[128,128]{0,1:T(8,128)S(1)}, u32[]{:S(2)}, u32[]{:S(2)}) collective-permute-start(f32[128,128]{0,1:T(8,128)S(1)} %add.69), channel_id=1, source_target_pairs={{0,16},{4,20},{8,24},{12,28},{16,0},{20,4},{24,8},{28,12},{1,17},{... | collective-permute-start | bytes 196616 | tf_op jit(solution)/shard_map/ppermute | solution.py:25
  81.7 5.4 %collective-permute-done.7 = f32[128,128]{0,1:T(8,128)S(1)} collective-permute-done((f32[128,128]{0,1:T(8,128)S(1)}, f32[128,128]{0,1:T(8,128)S(1)}, u32[]{:S(2)}, u32[]{:S(2)}) %collective-permute-start.7) | collective-permute-done | bytes 65568 | tf_op jit(solution)/shard_map/ppermute | solution.py:25
  87.1 1.2 collective-permute-start.8
  88.5 3.0 %collective-permute-done.8 = f32[128,128]{0,1:T(8,128)S(1)} collective-permute-done((f32[128,128]{0,1:T(8,128)S(1)}, f32[128,128]{0,1:T(8,128)S(1)}, u32[]{:S(2)}, u32[]{:S(2)}) %collective-permute-start.8) | collective-permute-done | bytes 65568 | tf_op jit(solution)/shard_map/ppermute | solution.py:25
  91.5 1.2 collective-permute-done.17
  92.8 11.7 %cholesky.17 = f32[128,128]{1,0:T(8,128)S(1)} custom-call(f32[128,128]{1,0:T(8,128)S(1)} %fusion.9), custom_call_target="Cholesky" | custom-call | tf_op jit(solution)/shard_map/jit(cholesky)/cholesky | solution.py:248
  104.6 3.1 %collective-permute-start.19 = (f32[2,128,128]{2,1,0:T(8,128)S(1)}, f32[2,128,128]{2,1,0:T(8,128)S(1)}, u32[]{:S(2)}, u32[]{:S(2)}) collective-permute-start(f32[2,128,128]{2,1,0:T(8,128)S(1)} %pad_maximum_fusion.1), channel_id=1, source_target_pairs={{0,16},{4,20},{8,24},{12,28},{16,0},{20,4},{24,8},{28,12},{1,17},{... | collective-permute-start | bytes 393224 | tf_op jit(solution)/shard_map/ppermute | solution.py:25
  108.3 2.3 %collective-permute-done.19 = f32[2,128,128]{2,1,0:T(8,128)S(1)} collective-permute-done((f32[2,128,128]{2,1,0:T(8,128)S(1)}, f32[2,128,128]{2,1,0:T(8,128)S(1)}, u32[]{:S(2)}, u32[]{:S(2)}) %collective-permute-start.19) | collective-permute-done | bytes 131104 | tf_op jit(solution)/shard_map/ppermute | solution.py:25
  110.6 1.6 %collective-permute-start.20 = (f32[4,128,128]{2,1,0:T(8,128)S(1)}, f32[4,128,128]{2,1,0:T(8,128)S(1)}, u32[]{:S(2)}, u32[]{:S(2)}) collective-permute-start(f32[4,128,128]{2,1,0:T(8,128)S(1)} %pad_maximum_fusion.first_ref), channel_id=1, source_target_pairs={{0,4},{4,0},{8,12},{12,8},{16,20},{20,16},{24,28},{28,24},{1,5},{5... | collective-permute-start | bytes 786440 | tf_op jit(solution)/shard_map/ppermute | solution.py:25
  112.9 9.8 %custom-call.7 = f32[1,128,128]{1,2,0:T(8,128)S(1)} custom-call(f32[1,128,128]{2,1,0:T(8,128)S(1)} %fusion.6), custom_call_target="InvertDiagBlocksLowerTriangular" | custom-call | tf_op jit(solution)/shard_map/jit(_solve_triangular)/triangular_solve | solution.py:249
  122.9 3.3 %finish.1 = (f32[128,1024]{1,0:T(8,128)}, f32[128,128]{1,0:T(8,128)S(1)}) custom-call(s32[2]{0:T(128)S(1)} %pad_add_fusion.own_ref, f32[128,128]{1,0:T(8,128)S(1)} %fusion.7.inverse_ref, f32[4,128,128]{2,1,0:T(8,128)S(1)} %pad_maximum_fusion.first_ref, f32[4,128,128]{2,1,0:T(8,128)S(1)} %collective-permute-done.20.second_ref), custom_call_target="tpu_custom_call" | custom-call | tf_op jit(solution)/shard_map/finish/pallas_call | solution.py:187
  126.2 1.3 collective-permute-done.21
  128.4 1.4 %fusion = f32[1024,128]{1,0:T(8,128)} fusion(f32[128,128]{1,0:T(8,128)S(1)} %fusion.7.inverse_ref, f32[512,128]{1,0:T(8,128)S(1)} %fusion.4.refs_1_, f32[512,128]{1,0:T(8,128)S(1)} %fusion.5.refs_1_), kind=kOutput, calls=%fused_computation.1 | convolution fusion | flops 201457664 | bytes 1114112 | tf_op jit(solution)/shard_map/dot_general | solution.py:251
  129.8 2.0 %collective-permute-done.22 = f32[128,128]{1,0:T(8,128)S(1)} collective-permute-done((f32[128,128]{1,0:T(8,128)S(1)}, f32[128,128]{1,0:T(8,128)S(1)}, u32[]{:S(2)}, u32[]{:S(2)}) %collective-permute-start.22) | collective-permute-done | bytes 65568 | tf_op jit(solution)/shard_map/ppermute | solution.py:25
  (57 shorter events, 10.0 us)
Async XLA Ops:
  0.7 1.0 copy-start
  6.3 9.8 %collective-permute-start = (f32[2,512,128]{2,1,0:T(8,128)S(1)}, f32[2,512,128]{2,1,0:T(8,128)S(1)}, u32[]{:S(2)}, u32[]{:S(2)}) collective-permute-start(f32[2,512,128]{2,1,0:T(8,128)S(1)} %partial_sketch.5), channel_id=1, source_target_pairs={{0,1},{1,0},{2,3},{3,2},{4,5},{5,4},{6,7},{7,6},{8,9},{9,8},{10,11... | collective-permute-start | bytes 1572872 | tf_op jit(solution)/shard_map/ppermute | solution.py:25
  11.4 12.4 %collective-permute-start.2 = (f32[2,512,128]{2,1,0:T(8,128)S(1)}, f32[2,512,128]{2,1,0:T(8,128)S(1)}, u32[]{:S(2)}, u32[]{:S(2)}) collective-permute-start(f32[2,512,128]{2,1,0:T(8,128)S(1)} %partial_sketch.7), channel_id=1, source_target_pairs={{0,1},{1,0},{2,3},{3,2},{4,5},{5,4},{6,7},{7,6},{8,9},{9,8},{10,11... | collective-permute-start | bytes 1572872 | tf_op jit(solution)/shard_map/ppermute | solution.py:25
  16.2 9.6 %collective-permute-start.1 = (f32[512,128]{1,0:T(8,128)S(1)}, f32[512,128]{1,0:T(8,128)S(1)}, u32[]{:S(2)}, u32[]{:S(2)}) collective-permute-start(f32[512,128]{1,0:T(8,128)S(1)} %slice_bitcast_fusion.2), channel_id=1, source_target_pairs={{0,2},{1,3},{2,0},{3,1},{4,6},{5,7},{6,4},{7,5},{8,10},{9,11},{10,... | collective-permute-start | bytes 786440 | tf_op jit(solution)/shard_map/ppermute | solution.py:25
  23.9 9.3 %collective-permute-start.3 = (f32[512,128]{1,0:T(8,128)S(1)}, f32[512,128]{1,0:T(8,128)S(1)}, u32[]{:S(2)}, u32[]{:S(2)}) collective-permute-start(f32[512,128]{1,0:T(8,128)S(1)} %slice_bitcast_fusion), channel_id=1, source_target_pairs={{0,2},{1,3},{2,0},{3,1},{4,6},{5,7},{6,4},{7,5},{8,10},{9,11},{10,... | collective-permute-start | bytes 786440 | tf_op jit(solution)/shard_map/ppermute | solution.py:25
  25.8 13.0 %collective-permute-start.11 = (f32[512,128]{1,0:T(8,128)S(1)}, f32[512,128]{1,0:T(8,128)S(1)}, u32[]{:S(2)}, u32[]{:S(2)}) collective-permute-start(f32[512,128]{1,0:T(8,128)S(1)} %fusion.5.refs_1_), channel_id=1, source_target_pairs={{0,2},{1,3},{2,0},{3,1},{4,6},{5,7},{6,4},{7,5},{8,10},{9,11},{10,... | collective-permute-start | bytes 786440 | tf_op jit(solution)/shard_map/ppermute | solution.py:25
  33.2 9.9 %collective-permute-start.9 = (f32[512,128]{1,0:T(8,128)S(1)}, f32[512,128]{1,0:T(8,128)S(1)}, u32[]{:S(2)}, u32[]{:S(2)}) collective-permute-start(f32[512,128]{1,0:T(8,128)S(1)} %fusion.4.refs_1_), channel_id=1, source_target_pairs={{0,2},{1,3},{2,0},{3,1},{4,6},{5,7},{6,4},{7,5},{8,10},{9,11},{10,... | collective-permute-start | bytes 786440 | tf_op jit(solution)/shard_map/ppermute | solution.py:25
  34.0 9.2 %collective-permute-start.14 = (f32[512,128]{1,0:T(8,128)S(1)}, f32[512,128]{1,0:T(8,128)S(1)}, u32[]{:S(2)}, u32[]{:S(2)}) collective-permute-start(f32[512,128]{1,0:T(8,128)S(1)} %fusion.5.refs_1_), channel_id=1, source_target_pairs={{0,1},{1,0},{2,3},{3,2},{4,5},{5,4},{6,7},{7,6},{8,9},{9,8},{10,11... | collective-permute-start | bytes 786440 | tf_op jit(solution)/shard_map/ppermute | solution.py:25
  34.0 14.2 %collective-permute-start.13 = (f32[512,128]{1,0:T(8,128)S(1)}, f32[512,128]{1,0:T(8,128)S(1)}, u32[]{:S(2)}, u32[]{:S(2)}) collective-permute-start(f32[512,128]{1,0:T(8,128)S(1)} %fusion.4.refs_1_), channel_id=1, source_target_pairs={{0,1},{1,0},{2,3},{3,2},{4,5},{5,4},{6,7},{7,6},{8,9},{9,8},{10,11... | collective-permute-start | bytes 786440 | tf_op jit(solution)/shard_map/ppermute | solution.py:25
  38.8 14.5 %collective-permute-start.12 = (f32[512,128]{1,0:T(8,128)S(1)}, f32[512,128]{1,0:T(8,128)S(1)}, u32[]{:S(2)}, u32[]{:S(2)}) collective-permute-start(f32[512,128]{1,0:T(8,128)S(1)} %collective-permute-done.11.refs_1_), channel_id=1, source_target_pairs={{0,1},{1,0},{2,3},{3,2},{4,5},{5,4},{6,7},{7,6},{8,9},{9,8},{10,11... | collective-permute-start | bytes 786440 | tf_op jit(solution)/shard_map/ppermute | solution.py:25
  43.1 15.3 %collective-permute-start.10 = (f32[512,128]{1,0:T(8,128)S(1)}, f32[512,128]{1,0:T(8,128)S(1)}, u32[]{:S(2)}, u32[]{:S(2)}) collective-permute-start(f32[512,128]{1,0:T(8,128)S(1)} %collective-permute-done.9.refs_1_), channel_id=1, source_target_pairs={{0,1},{1,0},{2,3},{3,2},{4,5},{5,4},{6,7},{7,6},{8,9},{9,8},{10,11... | collective-permute-start | bytes 786440 | tf_op jit(solution)/shard_map/ppermute | solution.py:25
  63.8 11.8 %collective-permute-start.15 = (f32[4,128,128]{2,1,0:T(8,128)S(1)}, f32[4,128,128]{2,1,0:T(8,128)S(1)}, u32[]{:S(2)}, u32[]{:S(2)}) collective-permute-start(f32[4,128,128]{2,1,0:T(8,128)S(1)} %get-tuple-element.8), channel_id=1, source_target_pairs={{0,4},{4,0},{8,12},{12,8},{16,20},{20,16},{24,28},{28,24},{1,5},{5... | collective-permute-start | bytes 786440 | tf_op jit(solution)/shard_map/ppermute | solution.py:25
  65.9 1.3 collective-permute-start.4
  67.2 6.7 %collective-permute-start.5 = (f32[128,128]{0,1:T(8,128)S(1)}, f32[128,128]{0,1:T(8,128)S(1)}, u32[]{:S(2)}, u32[]{:S(2)}) collective-permute-start(f32[128,128]{0,1:T(8,128)S(1)} %add.67), channel_id=1, source_target_pairs={{0,4},{4,0},{8,12},{12,8},{16,20},{20,16},{24,28},{28,24},{1,5},{5... | collective-permute-start | bytes 196616 | tf_op jit(solution)/shard_map/ppermute | solution.py:25
  74.0 4.4 %collective-permute-start.6 = (f32[128,128]{0,1:T(8,128)S(1)}, f32[128,128]{0,1:T(8,128)S(1)}, u32[]{:S(2)}, u32[]{:S(2)}) collective-permute-start(f32[128,128]{0,1:T(8,128)S(1)} %add.68), channel_id=1, source_target_pairs={{0,8},{4,12},{8,0},{12,4},{16,24},{20,28},{24,16},{28,20},{1,9},{5... | collective-permute-start | bytes 196616 | tf_op jit(solution)/shard_map/ppermute | solution.py:25
  75.7 12.7 %collective-permute-start.16 = (f32[2,128,128]{2,1,0:T(8,128)S(1)}, f32[2,128,128]{2,1,0:T(8,128)S(1)}, u32[]{:S(2)}, u32[]{:S(2)}) collective-permute-start(f32[2,128,128]{2,1,0:T(8,128)S(1)} %slice.49), channel_id=1, source_target_pairs={{0,16},{4,20},{8,24},{12,28},{16,0},{20,4},{24,8},{28,12},{1,17},{... | collective-permute-start | bytes 393224 | tf_op jit(solution)/shard_map/ppermute | solution.py:25
  78.3 8.8 %collective-permute-start.7 = (f32[128,128]{0,1:T(8,128)S(1)}, f32[128,128]{0,1:T(8,128)S(1)}, u32[]{:S(2)}, u32[]{:S(2)}) collective-permute-start(f32[128,128]{0,1:T(8,128)S(1)} %add.69), channel_id=1, source_target_pairs={{0,16},{4,20},{8,24},{12,28},{16,0},{20,4},{24,8},{28,12},{1,17},{... | collective-permute-start | bytes 196616 | tf_op jit(solution)/shard_map/ppermute | solution.py:25
  87.1 4.3 %collective-permute-start.8 = (f32[128,128]{0,1:T(8,128)S(1)}, f32[128,128]{0,1:T(8,128)S(1)}, u32[]{:S(2)}, u32[]{:S(2)}) collective-permute-start(f32[128,128]{0,1:T(8,128)S(1)} %add.70), channel_id=1, source_target_pairs={{0,2},{1,3},{2,0},{3,1},{4,6},{5,7},{6,4},{7,5},{8,10},{9,11},{10,... | collective-permute-start | bytes 196616 | tf_op jit(solution)/shard_map/ppermute | solution.py:25
  88.4 4.3 %collective-permute-start.17 = (f32[1,128,128]{2,1,0:T(8,128)S(1)}, f32[1,128,128]{2,1,0:T(8,128)S(1)}, u32[]{:S(2)}, u32[]{:S(2)}) collective-permute-start(f32[1,128,128]{2,1,0:T(8,128)S(1)} %slice.51), channel_id=1, source_target_pairs={{0,8},{4,12},{8,0},{12,4},{16,24},{20,28},{24,16},{28,20},{1,9},{5... | collective-permute-start | bytes 196616 | tf_op jit(solution)/shard_map/ppermute | solution.py:25
  92.7 11.8 %collective-permute-start.18 = (f32[1,128,128]{2,1,0:T(8,128)S(1)}, f32[1,128,128]{2,1,0:T(8,128)S(1)}, u32[]{:S(2)}, u32[]{:S(2)}) collective-permute-start(f32[1,128,128]{2,1,0:T(8,128)S(1)} %slice_add_fusion.1), channel_id=1, source_target_pairs={{0,8},{4,12},{8,0},{12,4},{16,24},{20,28},{24,16},{28,20},{1,9},{5... | collective-permute-start | bytes 196616 | tf_op jit(solution)/shard_map/ppermute | solution.py:25
  104.6 6.0 %collective-permute-start.19 = (f32[2,128,128]{2,1,0:T(8,128)S(1)}, f32[2,128,128]{2,1,0:T(8,128)S(1)}, u32[]{:S(2)}, u32[]{:S(2)}) collective-permute-start(f32[2,128,128]{2,1,0:T(8,128)S(1)} %pad_maximum_fusion.1), channel_id=1, source_target_pairs={{0,16},{4,20},{8,24},{12,28},{16,0},{20,4},{24,8},{28,12},{1,17},{... | collective-permute-start | bytes 393224 | tf_op jit(solution)/shard_map/ppermute | solution.py:25
  110.6 12.3 %collective-permute-start.20 = (f32[4,128,128]{2,1,0:T(8,128)S(1)}, f32[4,128,128]{2,1,0:T(8,128)S(1)}, u32[]{:S(2)}, u32[]{:S(2)}) collective-permute-start(f32[4,128,128]{2,1,0:T(8,128)S(1)} %pad_maximum_fusion.first_ref), channel_id=1, source_target_pairs={{0,4},{4,0},{8,12},{12,8},{16,20},{20,16},{24,28},{28,24},{1,5},{5... | collective-permute-start | bytes 786440 | tf_op jit(solution)/shard_map/ppermute | solution.py:25
  126.2 1.3 collective-permute-start.21
  127.5 4.3 %collective-permute-start.22 = (f32[128,128]{1,0:T(8,128)S(1)}, f32[128,128]{1,0:T(8,128)S(1)}, u32[]{:S(2)}, u32[]{:S(2)}) collective-permute-start(f32[128,128]{1,0:T(8,128)S(1)} %add.76), channel_id=1, source_target_pairs={{0,2},{1,3},{2,0},{3,1},{4,6},{5,7},{6,4},{7,5},{8,10},{9,11},{10,... | collective-permute-start | bytes 196616 | tf_op jit(solution)/shard_map/ppermute | solution.py:25

commit v2 on v0

v2 whole, which is shorter than its diff:
```python
import jax
import jax.numpy as jnp
from jax import lax
from jax.sharding import PartitionSpec as P

full = lax.Precision.HIGHEST
three = lax.Precision.HIGH
f32 = jnp.float32

HALVES = 2


def swap(value, axis, bit):
    return lax.ppermute(value, axis, [(i, i ^ bit) for i in range(lax.axis_size(axis))])


def dot(a, b, a_dim, b_dim, precision=full):
    return lax.dot_general(
        a, b, (((a_dim,), (b_dim,)), ((), ())), precision=precision, preferred_element_type=f32
    )


def halves(value):
    rows = value.shape[0] // HALVES
    return [value[h * rows : (h + 1) * rows] for h in range(HALVES)]


def row_sum(value, me, bits, least=8):
    taken = []
    for bit in bits:
        rows = value.shape[0] // 2
        if rows < least:
            value = value + swap(value, "row", bit)
            continue
        mine = (me // bit) % 2
        send = lax.dynamic_slice_in_dim(value, (1 - mine) * rows, rows, 0)
        keep = lax.dynamic_slice_in_dim(value, mine * rows, rows, 0)
        value = keep + swap(send, "row", bit)
        taken.append(bit)
    for bit in reversed(taken):
        other = swap(value, "row", bit)
        mine = (me // bit) % 2
        value = jnp.where(
            mine == 0, jnp.concatenate([value, other], 0), jnp.concatenate([other, value], 0)
        )
    return value


def per_device(data, omega):
    nrow, ncol = lax.axis_size("row"), lax.axis_size("col")
    assert ncol == 4
    total_rows = data.shape[0] * nrow
    quarter = data.shape[0] // ncol
    me_row, me_col = lax.axis_index("row"), lax.axis_index("col")
    bits = [1 << k for k in range(nrow.bit_length() - 1)]

    places = [
        lax.dynamic_slice_in_dim(data, (me_col ^ q) * quarter, quarter, 0) for q in range(4)
    ]

    def part(q):
        return dot(omega, places[q], 0, 1, three)

    away = halves(part(2) + swap(part(3), "col", 1))
    away = [swap(v, "col", 2) for v in away]
    here = halves(part(0) + swap(part(1), "col", 1))
    owned = [a + b for a, b in zip(here, away)]
    turned = jnp.concatenate(owned, 0)

    gram = dot(turned, turned, 1, 1)
    gram = gram + swap(gram, "col", 1)
    for bit in bits:
        gram = gram + swap(gram, "row", bit)
    gram = gram + swap(gram, "col", 2)

    third = [swap(v, "col", 2) for v in owned]
    second = swap(turned, "col", 1)
    fourth = [swap(v, "col", 1) for v in third]
    near = halves(dot(turned, places[0], 1, 0, three) + dot(second, places[1], 1, 0, three))
    sums = []
    for h in range(HALVES):
        acc = near[h] + dot(third[h], places[2], 1, 0, three) + dot(fourth[h], places[3], 1, 0, three)
        sums.append(row_sum(acc, me_row, bits))
    raw = jnp.concatenate(sums, 0)

    lower = jnp.linalg.cholesky(gram)
    inverse = jax.scipy.linalg.solve_triangular(lower, jnp.eye(gram.shape[0], dtype=f32), lower=True)
    basis = dot(turned, inverse, 0, 1)
    projected = dot(inverse, raw, 1, 0)
    small = dot(projected, projected, 1, 1)
    small = small + swap(small, "col", 1)
    small = small + swap(small, "col", 2)
    return (basis, projected, small / total_rows)


def solution(mesh):
    placed = (P("row", "col"), P("col", None))
    return jax.shard_map(
        per_device,
        mesh=mesh,
        in_specs=placed,
        out_specs=(P(("row", "col"), None), P(None, "col"), P()),
        check_vma=False,
    )
```

time: 361 us -> 132 us (0.37)
  waiting for transfers between devices: 277 us -> 31.1 us
  starting transfers between devices: 0.35 us -> 30 us
  between operations: 13.8 us -> 0.99 us
  local copies, waits for them, and re-layouts: 5.59 us -> 1.25 us
  matrix products: 38.6 us -> 42.9 us
    psum x4 -> x0, waiting for transfers between devices: 277 us -> none  [the longest x1 122 us: lower_factor(): summed = lax.psum(gram, ('row', 'col'))]
    ppermute x0 -> x28, waiting for transfers between devices: none -> 31.1 us  [swap(): lax.ppermute(value, axis, [(i, i ^ bit) for i in range(lax.axis_size(axis...]
    ppermute x0 -> x28, starting transfers between devices: none -> 30 us  [swap(): lax.ppermute(value, axis, [(i, i ^ bit) for i in range(lax.axis_size(axis...]
    dot_general x4 -> x14, matrix products: 35.1 us -> 42.7 us  [dot(): lax.dot_general(a, b, (((a_dim,), (b_dim,)), ((), ())), precision=precisi...]
  transfers between devices with their start and end apart: 4 -> 28, of which waited for: 4 -> 18; matrix products, arithmetic and copies ran while one was open for 1% -> 47% of each run, Pallas kernels for 0% -> 0%
where the time goes in v2:
time: 132 us
  matrix products  42.9 us (32%)
  waiting for transfers between devices  31.1 us (24%)
  starting transfers between devices  30 us (23%)
  other arithmetic  25.4 us (19%)
    dot_general x14, matrix products, dot(): lax.dot_general(a, b, (((a_dim,), (b_dim,)), ((), ())), precision=precisi...  42.7 us
    ppermute x28, waiting for transfers between devices, swap(): lax.ppermute(value, axis, [(i, i ^ bit) for i in range(lax.axis_size(axis...  31.1 us
    ppermute x28, starting transfers between devices, swap(): lax.ppermute(value, axis, [(i, i ^ bit) for i in range(lax.axis_size(axis...  30 us
    another operation x3, other arithmetic, per_device(): lower = jnp.linalg.cholesky(gram)  13.4 us
    another operation x2, other arithmetic, per_device(): jax.scipy.linalg.solve_triangular(lower, jnp.eye(gram.shape[0], dtype=f32...  10.5 us
  transfers between devices with their start and end apart: 28, of which 18 were waited for; matrix products, arithmetic and copies ran while one was open for 47% of the time, Pallas kernels for 0%

profile of v2, /device:TPU:0, one launch (start us, length us, event | category | flops | bytes accessed | tf_op | source)
XLA Modules:
  0.0 131.7 jit_solution(15371094569983510544)
XLA Ops:
  1.7 4.4 %fusion.23 = f32[128,1024]{1,0:T(8,128)S(1)} fusion(f32[1024,128]{1,0:T(8,128)S(1)} %copy-done, f32[4096,1024]{1,0:T(8,128)} %param.2, s32[]{:T(128)S(6)} %select_n.129), kind=kOutput, calls=%fused_computation.21 | convolution fusion | flops 805306368 | bytes 5242884 | tf_op jit(solution)/shard_map/dot_general | solution.py:18
  6.6 4.4 %fusion.29 = f32[128,1024]{1,0:T(8,128)S(1)} fusion(f32[1024,128]{1,0:T(8,128)S(1)} %copy-done, f32[4096,1024]{1,0:T(8,128)} %param.2, s32[]{:T(128)S(6)} %select_n.127), kind=kOutput, calls=%fused_computation.23 | convolution fusion | flops 805306368 | bytes 5242884 | tf_op jit(solution)/shard_map/dot_general | solution.py:18
  11.1 4.4 %fusion.35 = f32[128,1024]{1,0:T(8,128)S(1)} fusion(f32[128,1024]{1,0:T(8,128)S(1)} %collective-permute-done.1, f32[1024,128]{1,0:T(8,128)S(1)} %copy-done, f32[4096,1024]{1,0:T(8,128)} %param.2, s32[]{:T(128)S(6)} %select_n.128), kind=kOutput, calls=%fused_computation.25 | convolution fusion | flops 805437440 | bytes 5767172 | tf_op jit(solution)/shard_map/dot_general | solution.py:18
  15.5 3.0 %collective-permute-start.2 = (f32[64,1024]{1,0:T(8,128)S(1)}, f32[64,1024]{1,0:T(8,128)S(1)}, u32[]{:S(2)}, u32[]{:S(2)}) collective-permute-start(f32[64,1024]{1,0:T(8,128)S(1)} %get-tuple-element.5), channel_id=1, source_target_pairs={{0,2},{1,3},{2,0},{3,1},{4,6},{5,7},{6,4},{7,5},{8,10},{9,11},{10,... | collective-permute-start | bytes 786440 | tf_op jit(solution)/shard_map/ppermute | solution.py:14
  18.6 4.4 %fusion.32 = f32[128,1024]{1,0:T(8,128)S(1)} fusion(f32[128,1024]{1,0:T(8,128)S(1)} %collective-permute-done, f32[1024,128]{1,0:T(8,128)S(1)} %copy-done, f32[4096,1024]{1,0:T(8,128)} %param.2, s32[]{:T(128)S(6)} %select_n.126), kind=kOutput, calls=%fused_computation.24 | convolution fusion | flops 805437440 | bytes 5767172 | tf_op jit(solution)/shard_map/dot_general | solution.py:18
  23.0 2.6 %collective-permute-done.2 = f32[64,1024]{1,0:T(8,128)S(1)} collective-permute-done((f32[64,1024]{1,0:T(8,128)S(1)}, f32[64,1024]{1,0:T(8,128)S(1)}, u32[]{:S(2)}, u32[]{:S(2)}) %collective-permute-start.2) | collective-permute-done | bytes 262176 | tf_op jit(solution)/shard_map/ppermute | solution.py:14
  25.7 5.0 %collective-permute-done.3 = f32[64,1024]{1,0:T(8,128)S(1)} collective-permute-done((f32[64,1024]{1,0:T(8,128)S(1)}, f32[64,1024]{1,0:T(8,128)S(1)}, u32[]{:S(2)}, u32[]{:S(2)}) %collective-permute-start.3) | collective-permute-done | bytes 262176 | tf_op jit(solution)/shard_map/ppermute | solution.py:14
  30.7 1.8 %collective-permute-start.10 = (f32[64,1024]{1,0:T(8,128)S(1)}, f32[64,1024]{1,0:T(8,128)S(1)}, u32[]{:S(2)}, u32[]{:S(2)}) collective-permute-start(f32[64,1024]{1,0:T(8,128)S(1)} %get-tuple-element.3), channel_id=1, source_target_pairs={{0,2},{1,3},{2,0},{3,1},{4,6},{5,7},{6,4},{7,5},{8,10},{9,11},{10,... | collective-permute-start | bytes 786440 | tf_op jit(solution)/shard_map/ppermute | solution.py:14
  34.5 1.6 %collective-permute-start.5 = (f32[128,128]{0,1:T(8,128)S(1)}, f32[128,128]{0,1:T(8,128)S(1)}, u32[]{:S(2)}, u32[]{:S(2)}) collective-permute-start(f32[128,128]{0,1:T(8,128)S(1)} %add.144), channel_id=1, source_target_pairs={{0,4},{4,0},{8,12},{12,8},{16,20},{20,16},{24,28},{28,24},{1,5},{5... | collective-permute-start | bytes 196616 | tf_op jit(solution)/shard_map/ppermute | solution.py:14
  36.5 2.3 %collective-permute-done.5 = f32[128,128]{0,1:T(8,128)S(1)} collective-permute-done((f32[128,128]{0,1:T(8,128)S(1)}, f32[128,128]{0,1:T(8,128)S(1)}, u32[]{:S(2)}, u32[]{:S(2)}) %collective-permute-start.5) | collective-permute-done | bytes 65568 | tf_op jit(solution)/shard_map/ppermute | solution.py:14
  38.8 1.6 %collective-permute-start.6 = (f32[128,128]{0,1:T(8,128)S(1)}, f32[128,128]{0,1:T(8,128)S(1)}, u32[]{:S(2)}, u32[]{:S(2)}) collective-permute-start(f32[128,128]{0,1:T(8,128)S(1)} %add.145), channel_id=1, source_target_pairs={{0,8},{4,12},{8,0},{12,4},{16,24},{20,28},{24,16},{28,20},{1,9},{5... | collective-permute-start | bytes 196616 | tf_op jit(solution)/shard_map/ppermute | solution.py:14
  40.6 2.6 %collective-permute-done.6 = f32[128,128]{0,1:T(8,128)S(1)} collective-permute-done((f32[128,128]{0,1:T(8,128)S(1)}, f32[128,128]{0,1:T(8,128)S(1)}, u32[]{:S(2)}, u32[]{:S(2)}) %collective-permute-start.6) | collective-permute-done | bytes 65568 | tf_op jit(solution)/shard_map/ppermute | solution.py:14
  43.2 2.7 %collective-permute-start.7 = (f32[128,128]{0,1:T(8,128)S(1)}, f32[128,128]{0,1:T(8,128)S(1)}, u32[]{:S(2)}, u32[]{:S(2)}) collective-permute-start(f32[128,128]{0,1:T(8,128)S(1)} %add.146), channel_id=1, source_target_pairs={{0,16},{4,20},{8,24},{12,28},{16,0},{20,4},{24,8},{28,12},{1,17},{... | collective-permute-start | bytes 196616 | tf_op jit(solution)/shard_map/ppermute | solution.py:14
  45.8 3.6 %fusion.16 = f32[64,1024]{1,0:T(8,128)S(1)} fusion(f32[64,1024]{1,0:T(8,128)S(1)} %collective-permute-done.10, f32[4096,1024]{1,0:T(8,128)} %param.2, s32[]{:T(128)S(6)} %select_n.128), kind=kOutput, calls=%fused_computation.16 | convolution fusion | flops 402653184 | bytes 4718596 | tf_op jit(solution)/shard_map/dot_general | solution.py:18
  50.1 3.6 %fusion.14 = f32[64,1024]{1,0:T(8,128)S(1)} fusion(f32[64,1024]{1,0:T(8,128)S(1)} %collective-permute-done.18, f32[4096,1024]{1,0:T(8,128)} %param.2, s32[]{:T(128)S(6)} %select_n.128), kind=kOutput, calls=%fused_computation.14 | convolution fusion | flops 402653184 | bytes 4718596 | tf_op jit(solution)/shard_map/dot_general | solution.py:18
  54.8 12.7 %cholesky.17 = f32[128,128]{1,0:T(8,128)S(1)} custom-call(f32[128,128]{1,0:T(8,128)} %fusion.54), custom_call_target="Cholesky" | custom-call | tf_op jit(solution)/shard_map/jit(cholesky)/cholesky | solution.py:86
  68.9 9.8 %custom-call.7 = f32[1,128,128]{1,2,0:T(8,128)S(1)} custom-call(f32[1,128,128]{2,1,0:T(8,128)S(1)} %fusion.51), custom_call_target="InvertDiagBlocksLowerTriangular" | custom-call | tf_op jit(solution)/shard_map/jit(_solve_triangular)/triangular_solve | solution.py:87
  78.7 3.6 %fusion = f32[128,1024]{1,0:T(8,128)S(1)} fusion(f32[128,1024]{1,0:T(8,128)S(1)} %collective-permute-done.9, f32[4096,1024]{1,0:T(8,128)} %param.2, s32[]{:T(128)S(6)} %select_n.127), kind=kOutput, calls=%fused_computation | convolution fusion | flops 805306368 | bytes 5242884 | tf_op jit(solution)/shard_map/dot_general | solution.py:18
  82.3 3.6 %fusion.38 = f32[128,1024]{1,0:T(8,128)S(1)} fusion(f32[128,1024]{1,0:T(8,128)S(1)} %fusion, f32[4096,1024]{1,0:T(8,128)} %param.2, s32[]{:T(128)S(6)} %select_n.126, f32[64,1024]{1,0:T(8,128)S(1)} %get-tuple-element.4, f32[64,1024]{1,0:T(8,128)S(1)} %get-tuple-element.3), kind=kOutput, calls=%fused_computation.26 | convolution fusion | flops 805568512 | bytes 5767172 | tf_op jit(solution)/shard_map/dot_general | solution.py:18
  85.9 3.6 %fusion.41 = f32[64,1024]{1,0:T(8,128)S(1)} fusion(f32[64,1024]{1,0:T(8,128)S(1)} %collective-permute-done.11, f32[4096,1024]{1,0:T(8,128)} %param.2, s32[]{:T(128)S(6)} %select_n.129, f32[64,1024]{1,0:T(8,128)S(1)} %fusion.16, f32[128,1024]{1,0:T(8,128)S(1)} %fusion.38), kind=kOutput, calls=%fused_computation.27 | convolution fusion | flops 402784256 | bytes 5242884 | tf_op jit(solution)/shard_map/dot_general | solution.py:18
  91.1 3.7 %fusion.44 = f32[64,1024]{1,0:T(8,128)S(1)} fusion(f32[64,1024]{1,0:T(8,128)} %collective-permute-done.19, f32[4096,1024]{1,0:T(8,128)} %param.2, s32[]{:T(128)S(6)} %select_n.129, f32[64,1024]{1,0:T(8,128)S(1)} %fusion.14, f32[128,1024]{1,0:T(8,128)S(1)} %fusion.38), kind=kOutput, calls=%fused_computation.28 | convolution fusion | flops 402784256 | bytes 5242884 | tf_op jit(solution)/shard_map/dot_general | solution.py:18
  95.5 1.6 %collective-permute-start.13 = (f32[16,1024]{1,0:T(8,128)S(1)}, f32[16,1024]{1,0:T(8,128)S(1)}, u32[]{:S(2)}, u32[]{:S(2)}) collective-permute-start(f32[16,1024]{1,0:T(8,128)S(1)} %constant_dynamic-slice_fusion.4), channel_id=1, source_target_pairs={{0,8},{4,12},{8,0},{12,4},{16,24},{20,28},{24,16},{28,20},{1,9},{5... | collective-permute-start | bytes 196616 | tf_op jit(solution)/shard_map/ppermute | solution.py:14
  97.1 3.1 %collective-permute-done.20 = f32[32,1024]{1,0:T(8,128)S(1)} collective-permute-done((f32[32,1024]{1,0:T(8,128)S(1)}, f32[32,1024]{1,0:T(8,128)S(1)}, u32[]{:S(2)}, u32[]{:S(2)}) %collective-permute-start.20) | collective-permute-done | bytes 131104 | tf_op jit(solution)/shard_map/ppermute | solution.py:14
  100.3 1.6 %collective-permute-start.21 = (f32[16,1024]{1,0:T(8,128)S(1)}, f32[16,1024]{1,0:T(8,128)S(1)}, u32[]{:S(2)}, u32[]{:S(2)}) collective-permute-start(f32[16,1024]{1,0:T(8,128)S(1)} %constant_dynamic-slice_fusion.1), channel_id=1, source_target_pairs={{0,8},{4,12},{8,0},{12,4},{16,24},{20,28},{24,16},{28,20},{1,9},{5... | collective-permute-start | bytes 196616 | tf_op jit(solution)/shard_map/ppermute | solution.py:14
  102.0 2.1 %collective-permute-start.14 = (f32[8,1024]{1,0:T(8,128)S(1)}, f32[8,1024]{1,0:T(8,128)S(1)}, u32[]{:S(2)}, u32[]{:S(2)}) collective-permute-start(f32[8,1024]{1,0:T(8,128)S(1)} %constant_dynamic-slice_fusion.3), channel_id=1, source_target_pairs={{0,16},{4,20},{8,24},{12,28},{16,0},{20,4},{24,8},{28,12},{1,17},{... | collective-permute-start | bytes 98312 | tf_op jit(solution)/shard_map/ppermute | solution.py:14
  104.7 1.6 %collective-permute-start.22 = (f32[8,1024]{1,0:T(8,128)S(1)}, f32[8,1024]{1,0:T(8,128)S(1)}, u32[]{:S(2)}, u32[]{:S(2)}) collective-permute-start(f32[8,1024]{1,0:T(8,128)S(1)} %constant_dynamic-slice_fusion), channel_id=1, source_target_pairs={{0,16},{4,20},{8,24},{12,28},{16,0},{20,4},{24,8},{28,12},{1,17},{... | collective-permute-start | bytes 98312 | tf_op jit(solution)/shard_map/ppermute | solution.py:14
  111.3 1.6 %collective-permute-done.15 = f32[8,1024]{1,0:T(8,128)S(1)} collective-permute-done((f32[8,1024]{1,0:T(8,128)S(1)}, f32[8,1024]{1,0:T(8,128)S(1)}, u32[]{:S(2)}, u32[]{:S(2)}) %collective-permute-start.15) | collective-permute-done | bytes 32800 | tf_op jit(solution)/shard_map/ppermute | solution.py:14
  114.8 1.9 %collective-permute-start.24 = (f32[16,1024]{1,0:T(8,128)S(1)}, f32[16,1024]{1,0:T(8,128)S(1)}, u32[]{:S(2)}, u32[]{:S(2)}) collective-permute-start(f32[16,1024]{1,0:T(8,128)S(1)} %maximum_select_fusion.5), channel_id=1, source_target_pairs={{0,8},{4,12},{8,0},{12,4},{16,24},{20,28},{24,16},{28,20},{1,9},{5... | collective-permute-start | bytes 196616 | tf_op jit(solution)/shard_map/ppermute | solution.py:14
  120.0 2.3 %collective-permute-done.17 = f32[32,1024]{1,0:T(8,128)S(1)} collective-permute-done((f32[32,1024]{1,0:T(8,128)S(1)}, f32[32,1024]{1,0:T(8,128)S(1)}, u32[]{:S(2)}, u32[]{:S(2)}) %collective-permute-start.17) | collective-permute-done | bytes 131104 | tf_op jit(solution)/shard_map/ppermute | solution.py:14
  122.4 1.9 %collective-permute-done.25 = f32[32,1024]{1,0:T(8,128)S(1)} collective-permute-done((f32[32,1024]{1,0:T(8,128)S(1)}, f32[32,1024]{1,0:T(8,128)S(1)}, u32[]{:S(2)}, u32[]{:S(2)}) %collective-permute-start.25) | collective-permute-done | bytes 131104 | tf_op jit(solution)/shard_map/ppermute | solution.py:14
  126.8 1.6 %collective-permute-start.27 = (f32[128,128]{1,0:T(8,128)S(1)}, f32[128,128]{1,0:T(8,128)S(1)}, u32[]{:S(2)}, u32[]{:S(2)}) collective-permute-start(f32[128,128]{1,0:T(8,128)S(1)} %add.170), channel_id=1, source_target_pairs={{0,2},{1,3},{2,0},{3,1},{4,6},{5,7},{6,4},{7,5},{8,10},{9,11},{10,... | collective-permute-start | bytes 196616 | tf_op jit(solution)/shard_map/ppermute | solution.py:14
  128.3 1.8 %fusion.66 = f32[1024,128]{1,0:T(8,128)} fusion(f32[128,128]{1,0:T(8,128)S(1)} %fusion.52, f32[64,1024]{1,0:T(8,128)S(1)} %get-tuple-element.4, f32[64,1024]{1,0:T(8,128)S(1)} %get-tuple-element.3), kind=kOutput, calls=%fused_computation.78 | convolution fusion | flops 201457664 | bytes 1114112 | tf_op jit(solution)/shard_map/dot_general | solution.py:18
  (78 shorter events, 24.7 us)
Async XLA Ops:
  0.6 1.0 copy-start
  6.1 5.0 %collective-permute-start.1 = (f32[128,1024]{1,0:T(8,128)S(1)}, f32[128,1024]{1,0:T(8,128)S(1)}, u32[]{:S(2)}, u32[]{:S(2)}) collective-permute-start(f32[128,1024]{1,0:T(8,128)S(1)} %fusion.23), channel_id=1, source_target_pairs={{0,1},{1,0},{2,3},{3,2},{4,5},{5,4},{6,7},{7,6},{8,9},{9,8},{10,11... | collective-permute-start | bytes 1572872 | tf_op jit(solution)/shard_map/ppermute | solution.py:14
  11.0 7.7 %collective-permute-start = (f32[128,1024]{1,0:T(8,128)S(1)}, f32[128,1024]{1,0:T(8,128)S(1)}, u32[]{:S(2)}, u32[]{:S(2)}) collective-permute-start(f32[128,1024]{1,0:T(8,128)S(1)} %fusion.29), channel_id=1, source_target_pairs={{0,1},{1,0},{2,3},{3,2},{4,5},{5,4},{6,7},{7,6},{8,9},{9,8},{10,11... | collective-permute-start | bytes 1572872 | tf_op jit(solution)/shard_map/ppermute | solution.py:14
  15.5 10.1 %collective-permute-start.2 = (f32[64,1024]{1,0:T(8,128)S(1)}, f32[64,1024]{1,0:T(8,128)S(1)}, u32[]{:S(2)}, u32[]{:S(2)}) collective-permute-start(f32[64,1024]{1,0:T(8,128)S(1)} %get-tuple-element.5), channel_id=1, source_target_pairs={{0,2},{1,3},{2,0},{3,1},{4,6},{5,7},{6,4},{7,5},{8,10},{9,11},{10,... | collective-permute-start | bytes 786440 | tf_op jit(solution)/shard_map/ppermute | solution.py:14
  18.6 12.1 %collective-permute-start.3 = (f32[64,1024]{1,0:T(8,128)S(1)}, f32[64,1024]{1,0:T(8,128)S(1)}, u32[]{:S(2)}, u32[]{:S(2)}) collective-permute-start(f32[64,1024]{1,0:T(8,128)S(1)} %get-tuple-element.6), channel_id=1, source_target_pairs={{0,2},{1,3},{2,0},{3,1},{4,6},{5,7},{6,4},{7,5},{8,10},{9,11},{10,... | collective-permute-start | bytes 786440 | tf_op jit(solution)/shard_map/ppermute | solution.py:14
  30.7 15.1 %collective-permute-start.10 = (f32[64,1024]{1,0:T(8,128)S(1)}, f32[64,1024]{1,0:T(8,128)S(1)}, u32[]{:S(2)}, u32[]{:S(2)}) collective-permute-start(f32[64,1024]{1,0:T(8,128)S(1)} %get-tuple-element.3), channel_id=1, source_target_pairs={{0,2},{1,3},{2,0},{3,1},{4,6},{5,7},{6,4},{7,5},{8,10},{9,11},{10,... | collective-permute-start | bytes 786440 | tf_op jit(solution)/shard_map/ppermute | solution.py:14
  33.1 1.3 %collective-permute-start.4 = (f32[128,128]{0,1:T(8,128)S(1)}, f32[128,128]{0,1:T(8,128)S(1)}, u32[]{:S(2)}, u32[]{:S(2)}) collective-permute-start(f32[128,128]{0,1:T(8,128)S(1)} %fusion.67), channel_id=1, source_target_pairs={{0,1},{1,0},{2,3},{3,2},{4,5},{5,4},{6,7},{7,6},{8,9},{9,8},{10,11... | collective-permute-start | bytes 196616 | tf_op jit(solution)/shard_map/ppermute | solution.py:14
  34.5 4.3 %collective-permute-start.5 = (f32[128,128]{0,1:T(8,128)S(1)}, f32[128,128]{0,1:T(8,128)S(1)}, u32[]{:S(2)}, u32[]{:S(2)}) collective-permute-start(f32[128,128]{0,1:T(8,128)S(1)} %add.144), channel_id=1, source_target_pairs={{0,4},{4,0},{8,12},{12,8},{16,20},{20,16},{24,28},{28,24},{1,5},{5... | collective-permute-start | bytes 196616 | tf_op jit(solution)/shard_map/ppermute | solution.py:14
  36.0 14.1 %collective-permute-start.18 = (f32[64,1024]{1,0:T(8,128)S(1)}, f32[64,1024]{1,0:T(8,128)S(1)}, u32[]{:S(2)}, u32[]{:S(2)}) collective-permute-start(f32[64,1024]{1,0:T(8,128)S(1)} %get-tuple-element.4), channel_id=1, source_target_pairs={{0,2},{1,3},{2,0},{3,1},{4,6},{5,7},{6,4},{7,5},{8,10},{9,11},{10,... | collective-permute-start | bytes 786440 | tf_op jit(solution)/shard_map/ppermute | solution.py:14
  38.8 4.3 %collective-permute-start.6 = (f32[128,128]{0,1:T(8,128)S(1)}, f32[128,128]{0,1:T(8,128)S(1)}, u32[]{:S(2)}, u32[]{:S(2)}) collective-permute-start(f32[128,128]{0,1:T(8,128)S(1)} %add.145), channel_id=1, source_target_pairs={{0,8},{4,12},{8,0},{12,4},{16,24},{20,28},{24,16},{28,20},{1,9},{5... | collective-permute-start | bytes 196616 | tf_op jit(solution)/shard_map/ppermute | solution.py:14
  40.5 38.2 %collective-permute-start.9 = (f32[128,1024]{1,0:T(8,128)S(1)}, f32[128,1024]{1,0:T(8,128)S(1)}, u32[]{:S(2)}, u32[]{:S(2)}) collective-permute-start(f32[128,1024]{1,0:T(8,128)S(1)} %pad_maximum_fusion), channel_id=1, source_target_pairs={{0,1},{1,0},{2,3},{3,2},{4,5},{5,4},{6,7},{7,6},{8,9},{9,8},{10,11... | collective-permute-start | bytes 1572872 | tf_op jit(solution)/shard_map/ppermute | solution.py:14
  43.2 6.4 %collective-permute-start.7 = (f32[128,128]{0,1:T(8,128)S(1)}, f32[128,128]{0,1:T(8,128)S(1)}, u32[]{:S(2)}, u32[]{:S(2)}) collective-permute-start(f32[128,128]{0,1:T(8,128)S(1)} %add.146), channel_id=1, source_target_pairs={{0,16},{4,20},{8,24},{12,28},{16,0},{20,4},{24,8},{28,12},{1,17},{... | collective-permute-start | bytes 196616 | tf_op jit(solution)/shard_map/ppermute | solution.py:14
  49.4 36.4 %collective-permute-start.11 = (f32[64,1024]{1,0:T(8,128)S(1)}, f32[64,1024]{1,0:T(8,128)S(1)}, u32[]{:S(2)}, u32[]{:S(2)}) collective-permute-start(f32[64,1024]{1,0:T(8,128)S(1)} %collective-permute-done.10), channel_id=1, source_target_pairs={{0,1},{1,0},{2,3},{3,2},{4,5},{5,4},{6,7},{7,6},{8,9},{9,8},{10,11... | collective-permute-start | bytes 786440 | tf_op jit(solution)/shard_map/ppermute | solution.py:14
  49.5 4.5 %collective-permute-start.8 = (f32[128,128]{0,1:T(8,128)S(1)}, f32[128,128]{0,1:T(8,128)S(1)}, u32[]{:S(2)}, u32[]{:S(2)}) collective-permute-start(f32[128,128]{0,1:T(8,128)S(1)} %add.147), channel_id=1, source_target_pairs={{0,2},{1,3},{2,0},{3,1},{4,6},{5,7},{6,4},{7,5},{8,10},{9,11},{10,... | collective-permute-start | bytes 196616 | tf_op jit(solution)/shard_map/ppermute | solution.py:14
  53.7 37.4 %collective-permute-start.19 = (f32[64,1024]{1,0:T(8,128)S(1)}, f32[64,1024]{1,0:T(8,128)}, u32[]{:S(2)}, u32[]{:S(2)}) collective-permute-start(f32[64,1024]{1,0:T(8,128)S(1)} %collective-permute-done.18), channel_id=1, source_target_pairs={{0,1},{1,0},{2,3},{3,2},{4,5},{5,4},{6,7},{7,6},{8,9},{9,8},{10,11... | collective-permute-start | bytes 786440 | tf_op jit(solution)/shard_map/ppermute | solution.py:14
  89.5 5.9 %collective-permute-start.12 = (f32[32,1024]{1,0:T(8,128)S(1)}, f32[32,1024]{1,0:T(8,128)S(1)}, u32[]{:S(2)}, u32[]{:S(2)}) collective-permute-start(f32[32,1024]{1,0:T(8,128)S(1)} %constant_dynamic-slice_fusion.5), channel_id=1, source_target_pairs={{0,4},{4,0},{8,12},{12,8},{16,20},{20,16},{24,28},{28,24},{1,5},{5... | collective-permute-start | bytes 393224 | tf_op jit(solution)/shard_map/ppermute | solution.py:14
  94.8 5.4 %collective-permute-start.20 = (f32[32,1024]{1,0:T(8,128)S(1)}, f32[32,1024]{1,0:T(8,128)S(1)}, u32[]{:S(2)}, u32[]{:S(2)}) collective-permute-start(f32[32,1024]{1,0:T(8,128)S(1)} %constant_dynamic-slice_fusion.2), channel_id=1, source_target_pairs={{0,4},{4,0},{8,12},{12,8},{16,20},{20,16},{24,28},{28,24},{1,5},{5... | collective-permute-start | bytes 393224 | tf_op jit(solution)/shard_map/ppermute | solution.py:14
  95.5 6.4 %collective-permute-start.13 = (f32[16,1024]{1,0:T(8,128)S(1)}, f32[16,1024]{1,0:T(8,128)S(1)}, u32[]{:S(2)}, u32[]{:S(2)}) collective-permute-start(f32[16,1024]{1,0:T(8,128)S(1)} %constant_dynamic-slice_fusion.4), channel_id=1, source_target_pairs={{0,8},{4,12},{8,0},{12,4},{16,24},{20,28},{24,16},{28,20},{1,9},{5... | collective-permute-start | bytes 196616 | tf_op jit(solution)/shard_map/ppermute | solution.py:14
  100.3 4.4 %collective-permute-start.21 = (f32[16,1024]{1,0:T(8,128)S(1)}, f32[16,1024]{1,0:T(8,128)S(1)}, u32[]{:S(2)}, u32[]{:S(2)}) collective-permute-start(f32[16,1024]{1,0:T(8,128)S(1)} %constant_dynamic-slice_fusion.1), channel_id=1, source_target_pairs={{0,8},{4,12},{8,0},{12,4},{16,24},{20,28},{24,16},{28,20},{1,9},{5... | collective-permute-start | bytes 196616 | tf_op jit(solution)/shard_map/ppermute | solution.py:14
  102.0 5.8 %collective-permute-start.14 = (f32[8,1024]{1,0:T(8,128)S(1)}, f32[8,1024]{1,0:T(8,128)S(1)}, u32[]{:S(2)}, u32[]{:S(2)}) collective-permute-start(f32[8,1024]{1,0:T(8,128)S(1)} %constant_dynamic-slice_fusion.3), channel_id=1, source_target_pairs={{0,16},{4,20},{8,24},{12,28},{16,0},{20,4},{24,8},{28,12},{1,17},{... | collective-permute-start | bytes 98312 | tf_op jit(solution)/shard_map/ppermute | solution.py:14
  104.7 5.2 %collective-permute-start.22 = (f32[8,1024]{1,0:T(8,128)S(1)}, f32[8,1024]{1,0:T(8,128)S(1)}, u32[]{:S(2)}, u32[]{:S(2)}) collective-permute-start(f32[8,1024]{1,0:T(8,128)S(1)} %constant_dynamic-slice_fusion), channel_id=1, source_target_pairs={{0,16},{4,20},{8,24},{12,28},{16,0},{20,4},{24,8},{28,12},{1,17},{... | collective-permute-start | bytes 98312 | tf_op jit(solution)/shard_map/ppermute | solution.py:14
  107.8 5.2 %collective-permute-start.15 = (f32[8,1024]{1,0:T(8,128)S(1)}, f32[8,1024]{1,0:T(8,128)S(1)}, u32[]{:S(2)}, u32[]{:S(2)}) collective-permute-start(f32[8,1024]{1,0:T(8,128)S(1)} %dynamic-slice_add_fusion.5), channel_id=1, source_target_pairs={{0,16},{4,20},{8,24},{12,28},{16,0},{20,4},{24,8},{28,12},{1,17},{... | collective-permute-start | bytes 98312 | tf_op jit(solution)/shard_map/ppermute | solution.py:14
  109.9 4.9 %collective-permute-start.23 = (f32[8,1024]{1,0:T(8,128)S(1)}, f32[8,1024]{1,0:T(8,128)S(1)}, u32[]{:S(2)}, u32[]{:S(2)}) collective-permute-start(f32[8,1024]{1,0:T(8,128)S(1)} %dynamic-slice_add_fusion.4), channel_id=1, source_target_pairs={{0,16},{4,20},{8,24},{12,28},{16,0},{20,4},{24,8},{28,12},{1,17},{... | collective-permute-start | bytes 98312 | tf_op jit(solution)/shard_map/ppermute | solution.py:14
  113.0 4.3 %collective-permute-start.16 = (f32[16,1024]{1,0:T(8,128)S(1)}, f32[16,1024]{1,0:T(8,128)S(1)}, u32[]{:S(2)}, u32[]{:S(2)}) collective-permute-start(f32[16,1024]{1,0:T(8,128)S(1)} %maximum_select_fusion.4), channel_id=1, source_target_pairs={{0,8},{4,12},{8,0},{12,4},{16,24},{20,28},{24,16},{28,20},{1,9},{5... | collective-permute-start | bytes 196616 | tf_op jit(solution)/shard_map/ppermute | solution.py:14
  114.8 4.3 %collective-permute-start.24 = (f32[16,1024]{1,0:T(8,128)S(1)}, f32[16,1024]{1,0:T(8,128)S(1)}, u32[]{:S(2)}, u32[]{:S(2)}) collective-permute-start(f32[16,1024]{1,0:T(8,128)S(1)} %maximum_select_fusion.5), channel_id=1, source_target_pairs={{0,8},{4,12},{8,0},{12,4},{16,24},{20,28},{24,16},{28,20},{1,9},{5... | collective-permute-start | bytes 196616 | tf_op jit(solution)/shard_map/ppermute | solution.py:14
  117.3 5.0 %collective-permute-start.17 = (f32[32,1024]{1,0:T(8,128)S(1)}, f32[32,1024]{1,0:T(8,128)S(1)}, u32[]{:S(2)}, u32[]{:S(2)}) collective-permute-start(f32[32,1024]{1,0:T(8,128)S(1)} %maximum_select_fusion.2), channel_id=1, source_target_pairs={{0,4},{4,0},{8,12},{12,8},{16,20},{20,16},{24,28},{28,24},{1,5},{5... | collective-permute-start | bytes 393224 | tf_op jit(solution)/shard_map/ppermute | solution.py:14
  119.2 5.0 %collective-permute-start.25 = (f32[32,1024]{1,0:T(8,128)S(1)}, f32[32,1024]{1,0:T(8,128)S(1)}, u32[]{:S(2)}, u32[]{:S(2)}) collective-permute-start(f32[32,1024]{1,0:T(8,128)S(1)} %maximum_select_fusion.3), channel_id=1, source_target_pairs={{0,4},{4,0},{8,12},{12,8},{16,20},{20,16},{24,28},{28,24},{1,5},{5... | collective-permute-start | bytes 393224 | tf_op jit(solution)/shard_map/ppermute | solution.py:14
  124.8 6.9 %copy-start.1 = (f32[128,1024]{1,0:T(8,128)}, f32[128,1024]{1,0:T(8,128)S(1)}, u32[]{:S(2)}) copy-start(f32[128,1024]{1,0:T(8,128)S(1)} %fusion.47) | copy-start | bytes 1572868
  125.4 1.3 %collective-permute-start.26 = (f32[128,128]{1,0:T(8,128)S(1)}, f32[128,128]{1,0:T(8,128)S(1)}, u32[]{:S(2)}, u32[]{:S(2)}) collective-permute-start(f32[128,128]{1,0:T(8,128)S(1)} %fusion.69), channel_id=1, source_target_pairs={{0,1},{1,0},{2,3},{3,2},{4,5},{5,4},{6,7},{7,6},{8,9},{9,8},{10,11... | collective-permute-start | bytes 196616 | tf_op jit(solution)/shard_map/ppermute | solution.py:14
  126.8 4.3 %collective-permute-start.27 = (f32[128,128]{1,0:T(8,128)S(1)}, f32[128,128]{1,0:T(8,128)S(1)}, u32[]{:S(2)}, u32[]{:S(2)}) collective-permute-start(f32[128,128]{1,0:T(8,128)S(1)} %add.170), channel_id=1, source_target_pairs={{0,2},{1,3},{2,0},{3,1},{4,6},{5,7},{6,4},{7,5},{8,10},{9,11},{10,... | collective-permute-start | bytes 196616 | tf_op jit(solution)/shard_map/ppermute | solution.py:14

commit v3 on v2

v3 whole, which is shorter than its diff:
```python
import jax
import jax.numpy as jnp
from jax import lax
from jax.sharding import PartitionSpec as P

full = lax.Precision.HIGHEST
three = lax.Precision.HIGH
f32 = jnp.float32

HALVES = 2


def swap(value, axis, bit):
    return lax.ppermute(value, axis, [(i, i ^ bit) for i in range(lax.axis_size(axis))])


def dot(a, b, a_dim, b_dim, precision=full):
    return lax.dot_general(
        a, b, (((a_dim,), (b_dim,)), ((), ())), precision=precision, preferred_element_type=f32
    )


def halves(value):
    rows = value.shape[0] // HALVES
    return [value[h * rows : (h + 1) * rows] for h in range(HALVES)]


def scatter_sum(value, axes):
    return jnp.sum(lax.all_to_all(value, axes, 0, 0), 0)


def spread(value, axes, count):
    return lax.all_to_all(jnp.broadcast_to(value[None], (count, *value.shape)), axes, 0, 0)


def small_sum(value, axes, count):
    rows = value.shape[0] // count
    mine = scatter_sum(value.reshape(count, rows, value.shape[1]), axes)
    return spread(mine, axes, count).reshape(value.shape)


def per_device(data, omega):
    nrow, ncol = lax.axis_size("row"), lax.axis_size("col")
    assert ncol == 4
    total_rows = data.shape[0] * nrow
    quarter = data.shape[0] // ncol
    me_col = lax.axis_index("col")

    places = [
        lax.dynamic_slice_in_dim(data, (me_col ^ q) * quarter, quarter, 0) for q in range(4)
    ]

    def part(q):
        return dot(omega, places[q], 0, 1, three)

    away = halves(part(2) + swap(part(3), "col", 1))
    away = [swap(v, "col", 2) for v in away]
    here = halves(part(0) + swap(part(1), "col", 1))
    owned = [a + b for a, b in zip(here, away)]
    turned = jnp.concatenate(owned, 0)

    gram = dot(turned, turned, 1, 1)
    gram = small_sum(gram, ("row", "col"), nrow * ncol)

    third = [swap(v, "col", 2) for v in owned]
    second = swap(turned, "col", 1)
    fourth = [swap(v, "col", 1) for v in third]
    near = halves(dot(turned, places[0], 1, 0, three) + dot(second, places[1], 1, 0, three))
    sums = []
    for h in range(HALVES):
        acc = near[h] + dot(third[h], places[2], 1, 0, three) + dot(fourth[h], places[3], 1, 0, three)
        cut = acc.reshape(acc.shape[0], nrow, -1).transpose(1, 0, 2)
        sums.append(scatter_sum(cut, "row"))
    raw = jnp.concatenate(sums, 0)

    lower = jnp.linalg.cholesky(gram)
    inverse = jax.scipy.linalg.solve_triangular(lower, jnp.eye(gram.shape[0], dtype=f32), lower=True)
    basis = dot(turned, inverse, 0, 1)
    own_part = dot(inverse, raw, 1, 0)
    small = small_sum(dot(own_part, own_part, 1, 1), ("row", "col"), nrow * ncol)
    spreaded = spread(own_part, "row", nrow)
    projected = spreaded.transpose(1, 0, 2).reshape(raw.shape[0], data.shape[1])
    return (basis, projected, small / total_rows)


def solution(mesh):
    placed = (P("row", "col"), P("col", None))
    return jax.shard_map(
        per_device,
        mesh=mesh,
        in_specs=placed,
        out_specs=(P(("row", "col"), None), P(None, "col"), P()),
        check_vma=False,
    )
```

time: 132 us -> 155 us (1.17)
  blocking collectives: 0 us -> 34.7 us
  starting transfers between devices: 30 us -> 20.7 us
  waiting for transfers between devices: 31.1 us -> 26.7 us
  local copies, waits for them, and re-layouts: 1.25 us -> 5.28 us
  other arithmetic: 25.4 us -> 23.7 us
    all_to_all x0 -> x3, blocking collectives: none -> 34.7 us  [the longest x2 25.6 us: scatter_sum(): return jnp.sum(lax.all_to_all(value, axes, 0, 0), 0)]
    ppermute x28 -> x9, starting transfers between devices: 30 us -> 6.48 us  [swap(): lax.ppermute(value, axis, [(i, i ^ bit) for i in range(lax.axis_size(axis...]
    ppermute x28 -> x9, waiting for transfers between devices: 31.1 us -> 7.67 us  [swap(): lax.ppermute(value, axis, [(i, i ^ bit) for i in range(lax.axis_size(axis...]
    all_to_all x0 -> x4, waiting for transfers between devices: none -> 19 us  [the longest x2 17.6 us: spread(): lax.all_to_all(jnp.broadcast_to(value[None], (count, *value.shape)), axes...]
    all_to_all x0 -> x4, starting transfers between devices: none -> 14.2 us  [the longest x2 7.99 us: scatter_sum(): return jnp.sum(lax.all_to_all(value, axes, 0, 0), 0)]
  transfers between devices with their start and end apart: 28 -> 13, of which waited for: 18 -> 5; matrix products, arithmetic and copies ran while one was open for 47% -> 40% of each run, Pallas kernels for 0% -> 0%
where the time goes in v3:
time: 155 us; the launch traced here: 154 us
  matrix products  42.2 us (27%)
  blocking collectives  34.7 us (22%)
  waiting for transfers between devices  26.7 us (17%)
  other arithmetic  23.7 us (15%)
  starting transfers between devices  20.7 us (13%)
  local copies, waits for them, and re-layouts  5.28 us (3%)
    dot_general x14, matrix products, dot(): lax.dot_general(a, b, (((a_dim,), (b_dim,)), ((), ())), precision=precisi...  42 us
    all_to_all x2, blocking collectives, scatter_sum(): return jnp.sum(lax.all_to_all(value, axes, 0, 0), 0)  25.6 us
    all_to_all x2, waiting for transfers between devices, spread(): lax.all_to_all(jnp.broadcast_to(value[None], (count, *value.shape)), axes...  17.6 us
    another operation x3, other arithmetic, per_device(): lower = jnp.linalg.cholesky(gram)  12.4 us
    another operation x2, other arithmetic, per_device(): jax.scipy.linalg.solve_triangular(lower, jnp.eye(gram.shape[0], dtype=f32...  10.5 us
    all_to_all x1, blocking collectives, spread(): lax.all_to_all(jnp.broadcast_to(value[None], (count, *value.shape)), axes...  9.1 us
    all_to_all x2, starting transfers between devices, scatter_sum(): return jnp.sum(lax.all_to_all(value, axes, 0, 0), 0)  7.99 us
    ppermute x9, waiting for transfers between devices, swap(): lax.ppermute(value, axis, [(i, i ^ bit) for i in range(lax.axis_size(axis...  7.67 us
  transfers between devices with their start and end apart: 13, of which 5 were waited for; matrix products, arithmetic and copies ran while one was open for 40% of the time, Pallas kernels for 0%

profile of v3, /device:TPU:0, one launch (start us, length us, event | category | flops | bytes accessed | tf_op | source)
XLA Modules:
  0.0 154.2 jit_solution(1573925293353312157)
XLA Ops:
  0.7 1.0 copy-done
  1.7 4.4 %fusion.23 = f32[128,1024]{1,0:T(8,128)S(1)} fusion(f32[1024,128]{1,0:T(8,128)S(1)} %copy-done, f32[4096,1024]{1,0:T(8,128)} %param.2, s32[]{:T(128)S(6)} %select_n.19), kind=kOutput, calls=%fused_computation.21 | convolution fusion | flops 805306368 | bytes 5242884 | tf_op jit(solution)/shard_map/dot_general | solution.py:18
  6.6 4.4 %fusion.29 = f32[128,1024]{1,0:T(8,128)S(1)} fusion(f32[1024,128]{1,0:T(8,128)S(1)} %copy-done, f32[4096,1024]{1,0:T(8,128)} %param.2, s32[]{:T(128)S(6)} %select_n.17), kind=kOutput, calls=%fused_computation.23 | convolution fusion | flops 805306368 | bytes 5242884 | tf_op jit(solution)/shard_map/dot_general | solution.py:18
  11.1 4.4 %fusion.35 = f32[128,1024]{1,0:T(8,128)S(1)} fusion(f32[128,1024]{1,0:T(8,128)S(1)} %collective-permute-done.1, f32[1024,128]{1,0:T(8,128)S(1)} %copy-done, f32[4096,1024]{1,0:T(8,128)} %param.2, s32[]{:T(128)S(6)} %select_n.18), kind=kOutput, calls=%fused_computation.25 | convolution fusion | flops 805437440 | bytes 5767172 | tf_op jit(solution)/shard_map/dot_general | solution.py:18
  15.5 3.0 %collective-permute-start.2 = (f32[64,1024]{1,0:T(8,128)S(1)}, f32[64,1024]{1,0:T(8,128)S(1)}, u32[]{:S(2)}, u32[]{:S(2)}) collective-permute-start(f32[64,1024]{1,0:T(8,128)S(1)} %get-tuple-element.8), channel_id=1, source_target_pairs={{0,2},{1,3},{2,0},{3,1},{4,6},{5,7},{6,4},{7,5},{8,10},{9,11},{10,... | collective-permute-start | bytes 786440 | tf_op jit(solution)/shard_map/ppermute | solution.py:14
  18.6 4.4 %fusion.32 = f32[128,1024]{1,0:T(8,128)S(1)} fusion(f32[128,1024]{1,0:T(8,128)S(1)} %collective-permute-done, f32[1024,128]{1,0:T(8,128)S(1)} %copy-done, f32[4096,1024]{1,0:T(8,128)} %param.2, s32[]{:T(128)S(6)} %select_n.16), kind=kOutput, calls=%fused_computation.24 | convolution fusion | flops 805437440 | bytes 5767172 | tf_op jit(solution)/shard_map/dot_general | solution.py:18
  23.0 2.6 %collective-permute-done.2 = f32[64,1024]{1,0:T(8,128)S(1)} collective-permute-done((f32[64,1024]{1,0:T(8,128)S(1)}, f32[64,1024]{1,0:T(8,128)S(1)}, u32[]{:S(2)}, u32[]{:S(2)}) %collective-permute-start.2) | collective-permute-done | bytes 262176 | tf_op jit(solution)/shard_map/ppermute | solution.py:14
  25.7 5.0 %collective-permute-done.3 = f32[64,1024]{1,0:T(8,128)S(1)} collective-permute-done((f32[64,1024]{1,0:T(8,128)S(1)}, f32[64,1024]{1,0:T(8,128)S(1)}, u32[]{:S(2)}, u32[]{:S(2)}) %collective-permute-start.3) | collective-permute-done | bytes 262176 | tf_op jit(solution)/shard_map/ppermute | solution.py:14
  31.3 13.3 %all_to_all.35 = f32[32,4,128]{2,1,0:T(4,128)S(1)} all-to-all(f32[32,4,128]{2,1,0:T(4,128)S(1)} %bitcast.60), channel_id=1, replica_groups=mesh['row'=8,'col'=4] {'row','col'}, dimensions={0} | all-to-all | bytes 131072 | tf_op jit(solution)/shard_map/all_to_all | solution.py:29
  45.3 2.8 %all-to-all-start.1 = ((f32[32,4,128]{2,1,0:T(4,128)}), f32[32,4,128]{2,1,0:T(4,128)S(1)}, u32[]{:S(2)}, u32[]{:S(2)}) async-start(f32[32,4,128]{2,1,0:T(4,128)} %broadcast_in_dim.8), calls=%async_computation.1 | async-start | bytes 131072 | tf_op jit(solution)/shard_map/all_to_all | solution.py:33
  48.2 1.6 %collective-permute-start.5 = (f32[64,1024]{1,0:T(8,128)S(1)}, f32[64,1024]{1,0:T(8,128)S(1)}, u32[]{:S(2)}, u32[]{:S(2)}) collective-permute-start(f32[64,1024]{1,0:T(8,128)S(1)} %get-tuple-element.6), channel_id=1, source_target_pairs={{0,2},{1,3},{2,0},{3,1},{4,6},{5,7},{6,4},{7,5},{8,10},{9,11},{10,... | collective-permute-start | bytes 786440 | tf_op jit(solution)/shard_map/ppermute | solution.py:14
  50.3 5.1 %all-to-all-done.1 = f32[32,4,128]{2,1,0:T(4,128)S(1)} async-done(((f32[32,4,128]{2,1,0:T(4,128)}), f32[32,4,128]{2,1,0:T(4,128)S(1)}, u32[]{:S(2)}, u32[]{:S(2)}) %all-to-all-start.1) | async-done | bytes 65568 | tf_op jit(solution)/shard_map/all_to_all | solution.py:33
  55.5 11.7 %cholesky.17 = f32[128,128]{1,0:T(8,128)S(1)} custom-call(f32[128,128]{1,0:T(8,128)S(1)} %fusion.60), custom_call_target="Cholesky" | custom-call | tf_op jit(solution)/shard_map/jit(cholesky)/cholesky | solution.py:76
  67.8 3.6 %fusion.16 = f32[64,1024]{1,0:T(8,128)S(1)} fusion(f32[64,1024]{1,0:T(8,128)S(1)} %collective-permute-done.5, f32[4096,1024]{1,0:T(8,128)} %param.2, s32[]{:T(128)S(6)} %select_n.18), kind=kOutput, calls=%fused_computation.16 | convolution fusion | flops 402653184 | bytes 4718596 | tf_op jit(solution)/shard_map/dot_general | solution.py:18
  71.4 3.6 %fusion = f32[128,1024]{1,0:T(8,128)S(1)} fusion(f32[128,1024]{1,0:T(8,128)S(1)} %collective-permute-done.4, f32[4096,1024]{1,0:T(8,128)} %param.2, s32[]{:T(128)S(6)} %select_n.17), kind=kOutput, calls=%fused_computation | convolution fusion | flops 805306368 | bytes 5242884 | tf_op jit(solution)/shard_map/dot_general | solution.py:18
  75.0 3.6 %fusion.38 = f32[128,1024]{1,0:T(8,128)S(1)} fusion(f32[128,1024]{1,0:T(8,128)S(1)} %fusion, f32[4096,1024]{1,0:T(8,128)} %param.2, s32[]{:T(128)S(6)} %select_n.16, f32[64,1024]{1,0:T(8,128)S(1)} %get-tuple-element.7, f32[64,1024]{1,0:T(8,128)S(1)} %get-tuple-element.6), kind=kOutput, calls=%fused_computation.26 | convolution fusion | flops 805568512 | bytes 5767172 | tf_op jit(solution)/shard_map/dot_general | solution.py:18
  78.6 3.6 %fusion.44 = f32[8,8,8,128]{3,2,1,0:T(8,128)S(1)} fusion(f32[64,1024]{1,0:T(8,128)S(1)} %collective-permute-done.6, f32[4096,1024]{1,0:T(8,128)} %param.2, s32[]{:T(128)S(6)} %select_n.19, f32[64,1024]{1,0:T(8,128)S(1)} %fusion.16, f32[128,1024]{1,0:T(8,128)S(1)} %fusion.38), kind=kOutput, calls=%fused_computation.28 | convolution fusion | flops 402784256 | bytes 5242884 | tf_op jit(solution)/shard_map/dot_general | solution.py:18
  82.2 0.7 copy.30
  83.0 3.4 %all-to-all-start.2 = ((f32[8,64,128]{2,1,0:T(8,128)}), f32[8,64,128]{2,1,0:T(8,128)S(1)}, u32[]{:S(2)}, u32[]{:S(2)}) async-start(f32[8,64,128]{2,1,0:T(8,128)} %bitcast.56), calls=%async_computation.2 | async-start | bytes 524288 | tf_op jit(solution)/shard_map/all_to_all | solution.py:29
  86.4 3.6 %fusion.14 = f32[64,1024]{1,0:T(8,128)S(1)} fusion(f32[64,1024]{1,0:T(8,128)S(1)} %collective-permute-done.7, f32[4096,1024]{1,0:T(8,128)} %param.2, s32[]{:T(128)S(6)} %select_n.18), kind=kOutput, calls=%fused_computation.14 | convolution fusion | flops 402653184 | bytes 4718596 | tf_op jit(solution)/shard_map/dot_general | solution.py:18
  90.0 3.6 %fusion.50 = f32[8,8,8,128]{3,2,1,0:T(8,128)S(1)} fusion(f32[64,1024]{1,0:T(8,128)S(1)} %collective-permute-done.8, f32[4096,1024]{1,0:T(8,128)} %param.2, s32[]{:T(128)S(6)} %select_n.19, f32[64,1024]{1,0:T(8,128)S(1)} %fusion.14, f32[128,1024]{1,0:T(8,128)S(1)} %fusion.38), kind=kOutput, calls=%fused_computation.30 | convolution fusion | flops 402784256 | bytes 5242884 | tf_op jit(solution)/shard_map/dot_general | solution.py:18
  93.7 0.7 copy.29
  94.4 1.4 all-to-all-done.2
  95.8 4.6 %all-to-all-start.3 = ((f32[8,64,128]{2,1,0:T(8,128)}), f32[8,64,128]{2,1,0:T(8,128)S(1)}, u32[]{:S(2)}, u32[]{:S(2)}) async-start(f32[8,64,128]{2,1,0:T(8,128)} %bitcast.54), calls=%async_computation.3 | async-start | bytes 524288 | tf_op jit(solution)/shard_map/all_to_all | solution.py:29
  101.6 9.8 %custom-call.7 = f32[1,128,128]{1,2,0:T(8,128)S(1)} custom-call(f32[1,128,128]{2,1,0:T(8,128)S(1)} %fusion.53), custom_call_target="InvertDiagBlocksLowerTriangular" | custom-call | tf_op jit(solution)/shard_map/jit(_solve_triangular)/triangular_solve | solution.py:77
  112.2 12.3 %all_to_all.36 = f32[32,4,128]{2,1,0:T(4,128)S(1)} all-to-all(f32[32,4,128]{2,1,0:T(4,128)S(1)} %bitcast.61), channel_id=1, replica_groups=mesh['row'=8,'col'=4] {'row','col'}, dimensions={0} | all-to-all | bytes 131072 | tf_op jit(solution)/shard_map/all_to_all | solution.py:29
  124.6 9.1 %all_to_all.37 = f32[32,4,128]{2,1,0:T(4,128)S(1)} all-to-all(f32[32,4,128]{2,1,0:T(4,128)S(1)} %broadcast_in_dim.10), channel_id=1, replica_groups=mesh['row'=8,'col'=4] {'row','col'}, dimensions={0} | all-to-all | bytes 131072 | tf_op jit(solution)/shard_map/all_to_all | solution.py:33
  133.7 0.8 broadcast_in_dim.9
  134.5 3.5 %all-to-all-start.4 = ((f32[8,128,128]{2,1,0:T(8,128)}), f32[8,128,128]{2,1,0:T(8,128)S(1)}, u32[]{:S(2)}, u32[]{:S(2)}) async-start(f32[8,128,128]{2,1,0:T(8,128)} %broadcast_in_dim.9), calls=%async_computation.4 | async-start | bytes 1048576 | tf_op jit(solution)/shard_map/all_to_all | solution.py:33
  138.0 1.8 %fusion.72 = f32[1024,128]{1,0:T(8,128)} fusion(f32[128,128]{1,0:T(8,128)S(1)} %fusion.58, f32[64,1024]{1,0:T(8,128)S(1)} %get-tuple-element.7, f32[64,1024]{1,0:T(8,128)S(1)} %get-tuple-element.6), kind=kOutput, calls=%fused_computation.64 | convolution fusion | flops 201457664 | bytes 1114112 | tf_op jit(solution)/shard_map/dot_general | solution.py:18
  140.5 12.5 %all-to-all-done.4 = f32[8,128,128]{2,1,0:T(8,128)S(1)} async-done(((f32[8,128,128]{2,1,0:T(8,128)}), f32[8,128,128]{2,1,0:T(8,128)S(1)}, u32[]{:S(2)}, u32[]{:S(2)}) %all-to-all-start.4) | async-done | bytes 524320 | tf_op jit(solution)/shard_map/all_to_all | solution.py:33
  153.2 1.0 copy.22
  (36 shorter events, 6.3 us)
Async XLA Ops:
  0.6 1.0 copy-start
  6.1 5.0 %collective-permute-start.1 = (f32[128,1024]{1,0:T(8,128)S(1)}, f32[128,1024]{1,0:T(8,128)S(1)}, u32[]{:S(2)}, u32[]{:S(2)}) collective-permute-start(f32[128,1024]{1,0:T(8,128)S(1)} %fusion.23), channel_id=1, source_target_pairs={{0,1},{1,0},{2,3},{3,2},{4,5},{5,4},{6,7},{7,6},{8,9},{9,8},{10,11... | collective-permute-start | bytes 1572872 | tf_op jit(solution)/shard_map/ppermute | solution.py:14
  11.0 7.7 %collective-permute-start = (f32[128,1024]{1,0:T(8,128)S(1)}, f32[128,1024]{1,0:T(8,128)S(1)}, u32[]{:S(2)}, u32[]{:S(2)}) collective-permute-start(f32[128,1024]{1,0:T(8,128)S(1)} %fusion.29), channel_id=1, source_target_pairs={{0,1},{1,0},{2,3},{3,2},{4,5},{5,4},{6,7},{7,6},{8,9},{9,8},{10,11... | collective-permute-start | bytes 1572872 | tf_op jit(solution)/shard_map/ppermute | solution.py:14
  15.5 10.1 %collective-permute-start.2 = (f32[64,1024]{1,0:T(8,128)S(1)}, f32[64,1024]{1,0:T(8,128)S(1)}, u32[]{:S(2)}, u32[]{:S(2)}) collective-permute-start(f32[64,1024]{1,0:T(8,128)S(1)} %get-tuple-element.8), channel_id=1, source_target_pairs={{0,2},{1,3},{2,0},{3,1},{4,6},{5,7},{6,4},{7,5},{8,10},{9,11},{10,... | collective-permute-start | bytes 786440 | tf_op jit(solution)/shard_map/ppermute | solution.py:14
  18.6 12.1 %collective-permute-start.3 = (f32[64,1024]{1,0:T(8,128)S(1)}, f32[64,1024]{1,0:T(8,128)S(1)}, u32[]{:S(2)}, u32[]{:S(2)}) collective-permute-start(f32[64,1024]{1,0:T(8,128)S(1)} %get-tuple-element.9), channel_id=1, source_target_pairs={{0,2},{1,3},{2,0},{3,1},{4,6},{5,7},{6,4},{7,5},{8,10},{9,11},{10,... | collective-permute-start | bytes 786440 | tf_op jit(solution)/shard_map/ppermute | solution.py:14
  45.3 10.1 %all-to-all-start.1 = ((f32[32,4,128]{2,1,0:T(4,128)}), f32[32,4,128]{2,1,0:T(4,128)S(1)}, u32[]{:S(2)}, u32[]{:S(2)}) async-start(f32[32,4,128]{2,1,0:T(4,128)} %broadcast_in_dim.8), calls=%async_computation.1 | async-start | bytes 131072 | tf_op jit(solution)/shard_map/all_to_all | solution.py:33
  48.1 23.3 %collective-permute-start.4 = (f32[128,1024]{1,0:T(8,128)S(1)}, f32[128,1024]{1,0:T(8,128)S(1)}, u32[]{:S(2)}, u32[]{:S(2)}) collective-permute-start(f32[128,1024]{1,0:T(8,128)S(1)} %pad_maximum_fusion), channel_id=1, source_target_pairs={{0,1},{1,0},{2,3},{3,2},{4,5},{5,4},{6,7},{7,6},{8,9},{9,8},{10,11... | collective-permute-start | bytes 1572872 | tf_op jit(solution)/shard_map/ppermute | solution.py:14
  48.2 19.0 %collective-permute-start.5 = (f32[64,1024]{1,0:T(8,128)S(1)}, f32[64,1024]{1,0:T(8,128)S(1)}, u32[]{:S(2)}, u32[]{:S(2)}) collective-permute-start(f32[64,1024]{1,0:T(8,128)S(1)} %get-tuple-element.6), channel_id=1, source_target_pairs={{0,2},{1,3},{2,0},{3,1},{4,6},{5,7},{6,4},{7,5},{8,10},{9,11},{10,... | collective-permute-start | bytes 786440 | tf_op jit(solution)/shard_map/ppermute | solution.py:14
  49.8 17.5 %collective-permute-start.7 = (f32[64,1024]{1,0:T(8,128)S(1)}, f32[64,1024]{1,0:T(8,128)S(1)}, u32[]{:S(2)}, u32[]{:S(2)}) collective-permute-start(f32[64,1024]{1,0:T(8,128)S(1)} %get-tuple-element.7), channel_id=1, source_target_pairs={{0,2},{1,3},{2,0},{3,1},{4,6},{5,7},{6,4},{7,5},{8,10},{9,11},{10,... | collective-permute-start | bytes 786440 | tf_op jit(solution)/shard_map/ppermute | solution.py:14
  67.2 11.3 %collective-permute-start.6 = (f32[64,1024]{1,0:T(8,128)S(1)}, f32[64,1024]{1,0:T(8,128)S(1)}, u32[]{:S(2)}, u32[]{:S(2)}) collective-permute-start(f32[64,1024]{1,0:T(8,128)S(1)} %collective-permute-done.5), channel_id=1, source_target_pairs={{0,1},{1,0},{2,3},{3,2},{4,5},{5,4},{6,7},{7,6},{8,9},{9,8},{10,11... | collective-permute-start | bytes 786440 | tf_op jit(solution)/shard_map/ppermute | solution.py:14
  67.3 22.7 %collective-permute-start.8 = (f32[64,1024]{1,0:T(8,128)S(1)}, f32[64,1024]{1,0:T(8,128)S(1)}, u32[]{:S(2)}, u32[]{:S(2)}) collective-permute-start(f32[64,1024]{1,0:T(8,128)S(1)} %collective-permute-done.7), channel_id=1, source_target_pairs={{0,1},{1,0},{2,3},{3,2},{4,5},{5,4},{6,7},{7,6},{8,9},{9,8},{10,11... | collective-permute-start | bytes 786440 | tf_op jit(solution)/shard_map/ppermute | solution.py:14
  83.0 12.8 %all-to-all-start.2 = ((f32[8,64,128]{2,1,0:T(8,128)}), f32[8,64,128]{2,1,0:T(8,128)S(1)}, u32[]{:S(2)}, u32[]{:S(2)}) async-start(f32[8,64,128]{2,1,0:T(8,128)} %bitcast.56), calls=%async_computation.2 | async-start | bytes 524288 | tf_op jit(solution)/shard_map/all_to_all | solution.py:29
  95.8 16.0 %all-to-all-start.3 = ((f32[8,64,128]{2,1,0:T(8,128)}), f32[8,64,128]{2,1,0:T(8,128)S(1)}, u32[]{:S(2)}, u32[]{:S(2)}) async-start(f32[8,64,128]{2,1,0:T(8,128)} %bitcast.54), calls=%async_computation.3 | async-start | bytes 524288 | tf_op jit(solution)/shard_map/all_to_all | solution.py:29
  134.5 18.5 %all-to-all-start.4 = ((f32[8,128,128]{2,1,0:T(8,128)}), f32[8,128,128]{2,1,0:T(8,128)S(1)}, u32[]{:S(2)}, u32[]{:S(2)}) async-start(f32[8,128,128]{2,1,0:T(8,128)} %broadcast_in_dim.9), calls=%async_computation.4 | async-start | bytes 1048576 | tf_op jit(solution)/shard_map/all_to_all | solution.py:33

commit v4 on v0

v4 whole, which is shorter than its diff:
```python
import functools

import jax
import jax.numpy as jnp
from jax import lax
from jax.experimental import pallas as pl
from jax.experimental.pallas import tpu as pltpu
from jax.sharding import PartitionSpec as P

full = lax.Precision.HIGHEST
f32 = jnp.float32
bf16 = jnp.bfloat16

PIECE = 512
TILE = 256
SMEM = pl.BlockSpec(memory_space=pltpu.SMEM)
VMEM = pl.BlockSpec(memory_space=pltpu.VMEM)
ANY = pl.BlockSpec(memory_space=pl.ANY)
FREE = pl.CostEstimate(flops=1, bytes_accessed=1, transcendentals=0)


def params(mib):
    return pltpu.CompilerParams(vmem_limit_bytes=mib * 1024 * 1024)


def swap(value, axis, bit):
    return lax.ppermute(value, axis, [(i, i ^ bit) for i in range(lax.axis_size(axis))])


def dot(a, b, a_dim, b_dim, precision=full):
    return lax.dot_general(
        a, b, (((a_dim,), (b_dim,)), ((), ())), precision=precision, preferred_element_type=f32
    )


def split(value):
    upper = value.astype(bf16)
    return upper, (value - upper.astype(f32)).astype(bf16)


def start_copies(own_ref, data_ref, held, sems, pieces, quarter):
    copies = []
    for k, (place, first) in enumerate(pieces):
        at = pl.multiple_of((own_ref[0] ^ place) * quarter + first, PIECE)
        row = []
        for t in range(data_ref.shape[1] // TILE):
            cols = pl.ds(t * TILE, TILE)
            copy = pltpu.make_async_copy(
                data_ref.at[pl.ds(at, PIECE), cols], held.at[k, :, cols], sems.at[k, t]
            )
            copy.start()
            row.append(copy)
        copies.append(row)
    return copies


def sketch_kernel(pieces, quarter, first, own_ref, data_ref, omega_ref, *refs):
    outs, (held, sems) = refs[:-2], refs[-2:]
    copies = start_copies(own_ref, data_ref, held, sems, pieces, quarter)
    if first:
        width = omega_ref.shape[1]
        wide = outs[-1]
        upper, rest = split(omega_ref[...])
        wide[:, :width] = upper
        wide[:, width:] = rest
    else:
        wide = omega_ref
        width = omega_ref.shape[1] // 2
    for k in range(len(pieces)):
        both = more = None
        for t, copy in enumerate(copies[k]):
            copy.wait()
            upper, rest = split(held[k, :, t * TILE : (t + 1) * TILE])
            omega = wide[t * TILE : (t + 1) * TILE, :]
            one = jnp.dot(upper, omega, preferred_element_type=f32)
            two = jnp.dot(rest, omega[:, :width], preferred_element_type=f32)
            both = one if both is None else both + one
            more = two if more is None else more + two
        outs[k][...] = both[:, :width] + both[:, width:] + more


def sketch(own, data, omega, pieces, first=False):
    cols = data.shape[1]
    width = omega.shape[1] if first else omega.shape[1] // 2
    quarter = data.shape[0] // lax.axis_size("col")
    out = [jax.ShapeDtypeStruct((PIECE, width), f32)] * len(pieces)
    if first:
        out.append(jax.ShapeDtypeStruct((cols, 2 * width), bf16))
    return pl.pallas_call(
        functools.partial(sketch_kernel, pieces, quarter, first),
        in_specs=[SMEM, ANY, VMEM],
        out_specs=[VMEM] * len(out),
        out_shape=out,
        scratch_shapes=[
            pltpu.VMEM((len(pieces), PIECE, cols), f32),
            pltpu.SemaphoreType.DMA((len(pieces), cols // TILE)),
        ],
        compiler_params=params(20),
        cost_estimate=FREE,
        name="partial_sketch",
    )(own, data, omega)


def order(bits):
    places = [0]
    for bit in reversed(bits):
        places = places + [place ^ bit for place in places]
    return places


def project_kernel(pieces, quarter, before, orders, own_ref, data_ref, *refs):
    count = len(pieces)
    parts, refs = refs[:count], refs[count:]
    old, refs = (refs[0], refs[1:]) if before else (None, refs)
    outs, (total, held, sems) = refs[:-3], refs[-3:]
    if orders is None:
        total = outs[0]
    copies = start_copies(own_ref, data_ref, held, sems, pieces, quarter)
    for k in range(count):
        upper, rest = split(parts[k][...].T)
        stack = jnp.concatenate([upper, rest], 0)
        width = upper.shape[0]
        for t, copy in enumerate(copies[k]):
            copy.wait()
            cols = slice(t * TILE, (t + 1) * TILE)
            d_upper, d_rest = split(held[k, :, cols])
            both = jnp.dot(stack, d_upper, preferred_element_type=f32)
            value = both[:width] + both[width:] + jnp.dot(upper, d_rest, preferred_element_type=f32)
            if k > 0:
                value += total[:, cols]
            elif before:
                value += old[:, cols]
            total[:, cols] = value
    if orders is not None:
        for piece, places in enumerate(orders):
            send, keep = outs[2 * piece], outs[2 * piece + 1]
            half = len(places) // 2
            step = send.shape[0] // half
            for i in range(half):
                for ref, place in ((keep, places[i]), (send, places[half + i])):
                    at = piece * 2 * half * step + (place ^ own_ref[1]) * step
                    ref[i * step : (i + 1) * step] = total[pl.ds(pl.multiple_of(at, step), step)]


def project(own, data, pieces, parts, before=None, orders=None):
    cols = data.shape[1]
    width = parts[0].shape[1]
    quarter = data.shape[0] // lax.axis_size("col")
    args = [own, data, *parts] + ([] if before is None else [before])
    if orders is None:
        out = [jax.ShapeDtypeStruct((width, cols), f32)]
    else:
        out = [jax.ShapeDtypeStruct((width // len(orders) // 2, cols), f32)] * (2 * len(orders))
    return pl.pallas_call(
        functools.partial(project_kernel, pieces, quarter, before is not None, orders),
        in_specs=[SMEM, ANY] + [VMEM] * (len(args) - 2),
        out_specs=[VMEM] * len(out),
        out_shape=out,
        scratch_shapes=[
            pltpu.VMEM((width, cols) if orders is not None else (8, 128), f32),
            pltpu.VMEM((len(pieces), PIECE, cols), f32),
            pltpu.SemaphoreType.DMA((len(pieces), cols // TILE)),
        ],
        compiler_params=params(24),
        cost_estimate=FREE,
        name="project",
    )(*args)


def factor_kernel(gram_ref, out_ref, work):
    n = gram_ref.shape[0]
    row = lax.broadcasted_iota(jnp.int32, (n, n), 0)
    col = lax.broadcasted_iota(jnp.int32, (n, n), 1)
    work[:, :n] = gram_ref[...]
    work[:, n:] = jnp.where(row == col, 1.0, 0.0).astype(f32)
    sub = lax.broadcasted_iota(jnp.int32, (8, n), 0)
    for b in range(n // 8):
        top = slice(8 * b, 8 * b + 8)
        panel = work[top, :]
        spread = [jnp.broadcast_to(panel[:, 8 * b + j : 8 * b + j + 1], (8, n)) for j in range(8)]
        e = [
            [jnp.broadcast_to(spread[j][i : i + 1, :], (8, n)) for j in range(i + 1)]
            for i in range(8)
        ]
        left = [jnp.broadcast_to(panel[i : i + 1, :n], (8, n)) for i in range(8)]
        right = [jnp.broadcast_to(panel[i : i + 1, n:], (8, n)) for i in range(8)]
        for j in range(8):
            scale = lax.rsqrt(e[j][j])
            left[j] = left[j] * scale
            right[j] = right[j] * scale
            low = {i: e[i][j] * scale for i in range(j + 1, 8)}
            for i in range(j + 1, 8):
                for k in range(j + 1, i + 1):
                    e[i][k] = e[i][k] - low[i] * low[k]
                left[i] = left[i] - low[i] * left[j]
                right[i] = right[i] - low[i] * right[j]
        l_panel, r_panel = left[0], right[0]
        for i in range(1, 8):
            l_panel = jnp.where(sub == i, left[i], l_panel)
            r_panel = jnp.where(sub == i, right[i], r_panel)
        out_ref[top, :] = r_panel
        if b < n // 8 - 1:
            done = jnp.concatenate([l_panel, r_panel], 1)
            change = dot(l_panel, done, 0, 0)
            below = slice(8 * b + 8, n)
            work[below, :] = work[below, :] - change[8 * b + 8 :, :]


def factor(gram):
    n = gram.shape[0]
    return pl.pallas_call(
        factor_kernel,
        in_specs=[VMEM],
        out_specs=VMEM,
        out_shape=jax.ShapeDtypeStruct((n, n), f32),
        scratch_shapes=[pltpu.VMEM((n, 2 * n), f32)],
        compiler_params=params(8),
        cost_estimate=FREE,
        name="factor",
    )(gram)


def finish_kernel(orders, own_ref, inverse_ref, *refs):
    count = 2 * len(orders)
    parts, (out_ref, gram_ref, total) = refs[:count], refs[count:]
    for piece, places in enumerate(orders):
        keep, other = parts[2 * piece], parts[2 * piece + 1]
        half = len(places) // 2
        step = keep.shape[0] // half
        for i in range(half):
            for ref, place in ((keep, places[i]), (other, places[half + i])):
                at = piece * 2 * half * step + (place ^ own_ref[1]) * step
                total[pl.ds(pl.multiple_of(at, step), step)] = ref[i * step : (i + 1) * step]
    value = jnp.dot(inverse_ref[...], total[...], precision=full, preferred_element_type=f32)
    out_ref[...] = value
    gram_ref[...] = dot(value, value, 1, 1)


def finish(own, inverse, parts, orders):
    width = inverse.shape[0]
    cols = parts[0].shape[1]
    return pl.pallas_call(
        functools.partial(finish_kernel, orders),
        in_specs=[SMEM] + [VMEM] * (1 + len(parts)),
        out_specs=[VMEM] * 2,
        out_shape=[
            jax.ShapeDtypeStruct((width, cols), f32),
            jax.ShapeDtypeStruct((width, width), f32),
        ],
        scratch_shapes=[pltpu.VMEM((width, cols), f32)],
        compiler_params=params(16),
        cost_estimate=FREE,
        name="finish",
    )(own, inverse, *parts)


def per_device(data, omega):
    nrow, ncol = lax.axis_size("row"), lax.axis_size("col")
    quarter = data.shape[0] // ncol
    assert ncol == 4 and quarter == 2 * PIECE and nrow >= 8
    total_rows = data.shape[0] * nrow
    own = jnp.stack([lax.axis_index("col"), lax.axis_index("row") % 8]).astype(jnp.int32)
    bits = [1 << k for k in range(nrow.bit_length() - 1)]

    a3, wide = sketch(own, data, omega, [(3, 0)], True)
    (a2,) = sketch(own, data, wide, [(2, 0)])
    away_a = swap(a2 + swap(a3, "col", 1), "col", 2)
    (b3,) = sketch(own, data, wide, [(3, PIECE)])
    (b2,) = sketch(own, data, wide, [(2, PIECE)])
    away_b = swap(b2 + swap(b3, "col", 1), "col", 2)
    a1, b1 = sketch(own, data, wide, [(1, 0), (1, PIECE)])
    a0, b0 = sketch(own, data, wide, [(0, 0), (0, PIECE)])
    own_a = a0 + swap(a1, "col", 1) + away_a
    own_b = b0 + swap(b1, "col", 1) + away_b

    third_a = swap(own_a, "col", 2)
    third_b = swap(own_b, "col", 2)
    second_a = swap(own_a, "col", 1)
    second_b = swap(own_b, "col", 1)
    fourth_a = swap(third_a, "col", 1)
    fourth_b = swap(third_b, "col", 1)

    gram = dot(own_a, own_a, 0, 0) + dot(own_b, own_b, 0, 0)
    gram = gram + swap(gram, "col", 1)
    for bit in bits:
        gram = gram + swap(gram, "row", bit)
    gram = gram + swap(gram, "col", 2)
    inverse = factor(gram)
    basis = dot(jnp.concatenate([own_a, own_b], 0), inverse, 1, 1)

    cuts = [(1, 2, 4), (2, 4, 1)]
    orders = [order(cut) for cut in cuts]
    (acc,) = project(
        own, data, [(0, 0), (1, 0), (0, PIECE), (1, PIECE)], [own_a, second_a, own_b, second_b]
    )
    (acc,) = project(own, data, [(2, 0), (3, 0)], [third_a, fourth_a], acc)
    sums = project(own, data, [(2, PIECE), (3, PIECE)], [third_b, fourth_b], acc, orders)

    parts = []
    for piece, cut in enumerate(cuts):
        send, keep = sums[2 * piece], sums[2 * piece + 1]
        for k, bit in enumerate(cut):
            if k > 0:
                half = keep.shape[0] // 2
                keep, send = keep[:half], keep[half:]
            keep = keep + swap(send, "row", bit)
        for bit in bits[3:]:
            keep = keep + swap(keep, "row", bit)
        for bit in reversed(cut[1:]):
            keep = jnp.concatenate([keep, swap(keep, "row", bit)], 0)
        parts += [keep, swap(keep, "row", cut[0])]

    projected, small = finish(own, inverse, parts, orders)
    small = small + swap(small, "col", 1)
    small = small + swap(small, "col", 2)
    return (basis, projected, small / total_rows)


def solution(mesh):
    placed = (P("row", "col"), P("col", None))
    return jax.shard_map(
        per_device,
        mesh=mesh,
        in_specs=placed,
        out_specs=(P(("row", "col"), None), P(None, "col"), P()),
        check_vma=False,
    )
```

time: 361 us -> 119 us (0.33)
  waiting for transfers between devices: 277 us -> 33.9 us
  Pallas kernels: 0 us -> 40 us
  matrix products: 38.6 us -> 2.57 us
  starting transfers between devices: 0.35 us -> 33.1 us
  other arithmetic: 25.2 us -> 1.01 us
  between operations: 13.8 us -> 1 us
    psum x4 -> x0, waiting for transfers between devices: 277 us -> none  [the longest x1 122 us: lower_factor(): summed = lax.psum(gram, ('row', 'col'))]
    pallas_call x0 -> x11, Pallas kernels: none -> 40 us  [the longest x6 15 us: sketch(): pl.pallas_call(functools.partial(sketch_kernel, pieces, quarter, first),...]
    ppermute x0 -> x31, waiting for transfers between devices: none -> 33.9 us  [swap(): lax.ppermute(value, axis, [(i, i ^ bit) for i in range(lax.axis_size(axis...]
    ppermute x0 -> x31, starting transfers between devices: none -> 33.1 us  [swap(): lax.ppermute(value, axis, [(i, i ^ bit) for i in range(lax.axis_size(axis...]
    dot_general x4 -> x3, matrix products: 35.1 us -> 2.57 us  [dot(): lax.dot_general(a, b, (((a_dim,), (b_dim,)), ((), ())), precision=precisi...]
    another operation x5 -> x1, other arithmetic: 22.9 us -> 0.08 us  [per_device(): jnp.stack([lax.axis_index('col'), lax.axis_index('row') % 8])]
  transfers between devices with their start and end apart: 4 -> 31, of which waited for: 4 -> 14; matrix products, arithmetic and copies ran while one was open for 1% -> 2% of each run, Pallas kernels for 0% -> 30%
where the time goes in v4:
time: 119 us; the launch traced here: 118 us
  Pallas kernels  40 us (34%)
  waiting for transfers between devices  33.9 us (28%)
  starting transfers between devices  33.1 us (28%)
  local copies, waits for them, and re-layouts  6.85 us (6%)
  matrix products  2.57 us (2%)
    ppermute x31, waiting for transfers between devices, swap(): lax.ppermute(value, axis, [(i, i ^ bit) for i in range(lax.axis_size(axis...  33.9 us
    ppermute x31, starting transfers between devices, swap(): lax.ppermute(value, axis, [(i, i ^ bit) for i in range(lax.axis_size(axis...  33.1 us
    pallas_call x6, Pallas kernels, sketch(): pl.pallas_call(functools.partial(sketch_kernel, pieces, quarter, first),...  15 us
    pallas_call x3, Pallas kernels, project(): pl.pallas_call(functools.partial(project_kernel, pieces, quarter, before...  14 us
    pallas_call x1, Pallas kernels, factor(): pl.pallas_call(factor_kernel, in_specs=[VMEM], out_specs=VMEM, out_shape=...  8.72 us
    unnamed x12, local copies, waits for them, and re-layouts  6.83 us
    dot_general x3, matrix products, dot(): lax.dot_general(a, b, (((a_dim,), (b_dim,)), ((), ())), precision=precisi...  2.57 us
  transfers between devices with their start and end apart: 31, of which 14 were waited for; matrix products, arithmetic and copies ran while one was open for 2% of the time, Pallas kernels for 30%

profile of v4, /device:TPU:0, one launch (start us, length us, event | category | flops | bytes accessed | tf_op | source)
XLA Modules:
  0.0 118.4 jit_solution(9956702401924960418)
XLA Ops:
  0.7 5.8 %copy-done = f32[4096,1024]{1,0:T(8,128)S(1)} copy-done((f32[4096,1024]{1,0:T(8,128)S(1)}, f32[4096,1024]{1,0:T(8,128)}, u32[]{:S(2)}) %copy-start) | copy-done | bytes 16777240
  7.5 2.1 %partial_sketch.6 = (f32[512,128]{1,0:T(8,128)S(1)}, bf16[1024,256]{1,0:T(8,128)(2,1)S(1)}) custom-call(s32[2]{0:T(128)S(1)} %pad_add_fusion.own_ref, f32[4096,1024]{1,0:T(8,128)S(1)} %copy-done, f32[1024,128]{1,0:T(8,128)S(1)} %copy-done.1), custom_call_target="tpu_custom_call" | custom-call | flops 1 | bytes 1 | tf_op jit(solution)/shard_map/partial_sketch/pallas_call | solution.py:89
  10.2 2.0 %partial_sketch.11 = f32[512,128]{1,0:T(8,128)S(1)} custom-call(s32[2]{0:T(128)S(1)} %pad_add_fusion.own_ref, f32[4096,1024]{1,0:T(8,128)S(1)} %copy-done, bf16[1024,256]{1,0:T(8,128)(2,1)S(1)} %get-tuple-element.15.omega_ref), custom_call_target="tpu_custom_call" | custom-call | flops 1 | bytes 1 | tf_op jit(solution)/shard_map/partial_sketch/pallas_call | solution.py:89
  12.3 3.4 %partial_sketch.8 = (f32[512,128]{1,0:T(8,128)S(1)}, f32[512,128]{1,0:T(8,128)S(1)}) custom-call(s32[2]{0:T(128)S(1)} %pad_add_fusion.own_ref, f32[4096,1024]{1,0:T(8,128)S(1)} %copy-done, bf16[1024,256]{1,0:T(8,128)(2,1)S(1)} %get-tuple-element.15.omega_ref), custom_call_target="tpu_custom_call" | custom-call | flops 1 | bytes 1 | tf_op jit(solution)/shard_map/partial_sketch/pallas_call | solution.py:89
  16.2 2.0 %partial_sketch.9 = f32[512,128]{1,0:T(8,128)S(1)} custom-call(s32[2]{0:T(128)S(1)} %pad_add_fusion.own_ref, f32[4096,1024]{1,0:T(8,128)S(1)} %copy-done, bf16[1024,256]{1,0:T(8,128)(2,1)S(1)} %get-tuple-element.15.omega_ref), custom_call_target="tpu_custom_call" | custom-call | flops 1 | bytes 1 | tf_op jit(solution)/shard_map/partial_sketch/pallas_call | solution.py:89
  18.3 2.6 %collective-permute-start.2 = (f32[512,128]{1,0:T(8,128)S(1)}, f32[512,128]{1,0:T(8,128)S(1)}, u32[]{:S(2)}, u32[]{:S(2)}) collective-permute-start(f32[512,128]{1,0:T(8,128)S(1)} %add.66), channel_id=1, source_target_pairs={{0,2},{1,3},{2,0},{3,1},{4,6},{5,7},{6,4},{7,5},{8,10},{9,11},{10,... | collective-permute-start | bytes 786440 | tf_op jit(solution)/shard_map/ppermute | solution.py:27
  21.1 2.0 %partial_sketch.10 = f32[512,128]{1,0:T(8,128)S(1)} custom-call(s32[2]{0:T(128)S(1)} %pad_add_fusion.own_ref, f32[4096,1024]{1,0:T(8,128)S(1)} %copy-done, bf16[1024,256]{1,0:T(8,128)(2,1)S(1)} %get-tuple-element.15.omega_ref), custom_call_target="tpu_custom_call" | custom-call | flops 1 | bytes 1 | tf_op jit(solution)/shard_map/partial_sketch/pallas_call | solution.py:89
  23.6 3.4 %partial_sketch.7 = (f32[512,128]{1,0:T(8,128)S(1)}, f32[512,128]{1,0:T(8,128)S(1)}) custom-call(s32[2]{0:T(128)S(1)} %pad_add_fusion.own_ref, f32[4096,1024]{1,0:T(8,128)S(1)} %copy-done, bf16[1024,256]{1,0:T(8,128)(2,1)S(1)} %get-tuple-element.15.omega_ref), custom_call_target="tpu_custom_call" | custom-call | flops 1 | bytes 1 | tf_op jit(solution)/shard_map/partial_sketch/pallas_call | solution.py:89
  28.1 2.0 %collective-permute-start.13 = (f32[512,128]{1,0:T(8,128)S(1)}, f32[512,128]{1,0:T(8,128)S(1)}, u32[]{:S(2)}, u32[]{:S(2)}) collective-permute-start(f32[512,128]{1,0:T(8,128)S(1)} %add_add_fusion.1.refs_0_), channel_id=1, source_target_pairs={{0,2},{1,3},{2,0},{3,1},{4,6},{5,7},{6,4},{7,5},{8,10},{9,11},{10,... | collective-permute-start | bytes 786440 | tf_op jit(solution)/shard_map/ppermute | solution.py:27
  30.1 3.6 %collective-permute-done.5 = f32[512,128]{1,0:T(8,128)S(1)} collective-permute-done((f32[512,128]{1,0:T(8,128)S(1)}, f32[512,128]{1,0:T(8,128)S(1)}, u32[]{:S(2)}, u32[]{:S(2)}) %collective-permute-start.5) | collective-permute-done | bytes 262176 | tf_op jit(solution)/shard_map/ppermute | solution.py:27
  33.7 2.0 %collective-permute-start.11 = (f32[512,128]{1,0:T(8,128)S(1)}, f32[512,128]{1,0:T(8,128)S(1)}, u32[]{:S(2)}, u32[]{:S(2)}) collective-permute-start(f32[512,128]{1,0:T(8,128)S(1)} %add_add_fusion.refs_2_), channel_id=1, source_target_pairs={{0,2},{1,3},{2,0},{3,1},{4,6},{5,7},{6,4},{7,5},{8,10},{9,11},{10,... | collective-permute-start | bytes 786440 | tf_op jit(solution)/shard_map/ppermute | solution.py:27
  36.2 3.1 %collective-permute-done.13.refs_0_ = f32[512,128]{1,0:T(8,128)S(1)} collective-permute-done((f32[512,128]{1,0:T(8,128)S(1)}, f32[512,128]{1,0:T(8,128)S(1)}, u32[]{:S(2)}, u32[]{:S(2)}) %collective-permute-start.13) | collective-permute-done | bytes 262176 | tf_op jit(solution)/shard_map/ppermute | solution.py:27
  39.3 5.4 %collective-permute-done.11.refs_0_ = f32[512,128]{1,0:T(8,128)S(1)} collective-permute-done((f32[512,128]{1,0:T(8,128)S(1)}, f32[512,128]{1,0:T(8,128)S(1)}, u32[]{:S(2)}, u32[]{:S(2)}) %collective-permute-start.11) | collective-permute-done | bytes 262176 | tf_op jit(solution)/shard_map/ppermute | solution.py:27
  46.5 6.4 %project.3.refs_2_ = f32[128,1024]{1,0:T(8,128)S(1)} custom-call(s32[2]{0:T(128)S(1)} %pad_add_fusion.own_ref, f32[4096,1024]{1,0:T(8,128)S(1)} %bitcast.8, f32[512,128]{1,0:T(8,128)S(1)} %add_add_fusion.1.refs_0_, f32[512,128]{1,0:T(8,128)S(1)} %collective-permute-done.15.refs_1_, f32[512,128]{1,0:T(8,128)S(1)} %add_add_fusion.refs_2_, ...), custom_call_target="tpu_custom_call" | custom-call | flops 1 | bytes 1 | tf_op jit(solution)/shard_map/project/pallas_call | solution.py:154
  53.0 3.8 %project.4.refs_2_ = f32[128,1024]{1,0:T(8,128)S(1)} custom-call(s32[2]{0:T(128)S(1)} %pad_add_fusion.own_ref, f32[4096,1024]{1,0:T(8,128)S(1)} %bitcast.8, f32[512,128]{1,0:T(8,128)S(1)} %collective-permute-done.13.refs_0_, f32[512,128]{1,0:T(8,128)S(1)} %collective-permute-done.14.refs_1_, f32[128,1024]{1,0:T(8,128)S(1)} %project.3.refs_2_), custom_call_target="tpu_custom_call" | custom-call | flops 1 | bytes 1 | tf_op jit(solution)/shard_map/project/pallas_call | solution.py:154
  56.7 3.8 %project.5 = (f32[32,1024]{1,0:T(8,128)S(1)}, f32[32,1024]{1,0:T(8,128)S(1)}, f32[32,1024]{1,0:T(8,128)S(1)}, f32[32,1024]{1,0:T(8,128)S(1)}) custom-call(s32[2]{0:T(128)S(1)} %pad_add_fusion.own_ref, f32[4096,1024]{1,0:T(8,128)S(1)} %bitcast.8, f32[512,128]{1,0:T(8,128)S(1)} %collective-permute-done.11.refs_0_, ...), custom_call_target="tpu_custom_call" | custom-call | flops 1 | bytes 1 | tf_op jit(solution)/shard_map/project/pallas_call | solution.py:154
  60.5 1.9 %collective-permute-start.23 = (f32[32,1024]{1,0:T(8,128)S(1)}, f32[32,1024]{1,0:T(8,128)S(1)}, u32[]{:S(2)}, u32[]{:S(2)}) collective-permute-start(f32[32,1024]{1,0:T(8,128)S(1)} %get-tuple-element.24), channel_id=1, source_target_pairs={{0,8},{4,12},{8,0},{12,4},{16,24},{20,28},{24,16},{28,20},{1,9},{5... | collective-permute-start | bytes 393224 | tf_op jit(solution)/shard_map/ppermute | solution.py:27
  64.5 2.9 %collective-permute-done.7 = f32[128,128]{1,0:T(8,128)S(1)} collective-permute-done((f32[128,128]{1,0:T(8,128)S(1)}, f32[128,128]{1,0:T(8,128)S(1)}, u32[]{:S(2)}, u32[]{:S(2)}) %collective-permute-start.7) | collective-permute-done | bytes 65568 | tf_op jit(solution)/shard_map/ppermute | solution.py:27
  67.6 3.1 %collective-permute-start.24 = (f32[16,1024]{1,0:T(8,128)S(1)}, f32[16,1024]{1,0:T(8,128)S(1)}, u32[]{:S(2)}, u32[]{:S(2)}) collective-permute-start(f32[16,1024]{1,0:T(8,128)S(1)} %slice.37), channel_id=1, source_target_pairs={{0,16},{4,20},{8,24},{12,28},{16,0},{20,4},{24,8},{28,12},{1,17},{... | collective-permute-start | bytes 196616 | tf_op jit(solution)/shard_map/ppermute | solution.py:27
  71.8 3.4 %collective-permute-start.9 = (f32[128,128]{1,0:T(8,128)S(1)}, f32[128,128]{1,0:T(8,128)S(1)}, u32[]{:S(2)}, u32[]{:S(2)}) collective-permute-start(f32[128,128]{1,0:T(8,128)S(1)} %add.74), channel_id=1, source_target_pairs={{0,16},{4,20},{8,24},{12,28},{16,0},{20,4},{24,8},{28,12},{1,17},{... | collective-permute-start | bytes 196616 | tf_op jit(solution)/shard_map/ppermute | solution.py:27
  75.5 1.7 %collective-permute-start.25 = (f32[8,1024]{1,0:T(8,128)S(1)}, f32[8,1024]{1,0:T(8,128)S(1)}, u32[]{:S(2)}, u32[]{:S(2)}) collective-permute-start(f32[8,1024]{1,0:T(8,128)S(1)} %slice.39), channel_id=1, source_target_pairs={{0,4},{4,0},{8,12},{12,8},{16,20},{20,16},{24,28},{28,24},{1,5},{5... | collective-permute-start | bytes 98312 | tf_op jit(solution)/shard_map/ppermute | solution.py:27
  77.2 2.3 %collective-permute-done.18 = f32[16,1024]{1,0:T(8,128)S(1)} collective-permute-done((f32[16,1024]{1,0:T(8,128)S(1)}, f32[16,1024]{1,0:T(8,128)S(1)}, u32[]{:S(2)}, u32[]{:S(2)}) %collective-permute-start.18) | collective-permute-done | bytes 65568 | tf_op jit(solution)/shard_map/ppermute | solution.py:27
  79.7 1.8 %collective-permute-start.26 = (f32[8,1024]{1,0:T(8,128)S(1)}, f32[8,1024]{1,0:T(8,128)S(1)}, u32[]{:S(2)}, u32[]{:S(2)}) collective-permute-start(f32[8,1024]{1,0:T(8,128)S(1)} %slice_add_fusion.2), channel_id=1, source_target_pairs={{0,4},{4,0},{8,12},{12,8},{16,20},{20,16},{24,28},{28,24},{1,5},{5... | collective-permute-start | bytes 98312 | tf_op jit(solution)/shard_map/ppermute | solution.py:27
  81.5 4.1 %collective-permute-done.19 = f32[8,1024]{1,0:T(8,128)S(1)} collective-permute-done((f32[8,1024]{1,0:T(8,128)S(1)}, f32[8,1024]{1,0:T(8,128)S(1)}, u32[]{:S(2)}, u32[]{:S(2)}) %collective-permute-start.19) | collective-permute-done | bytes 32800 | tf_op jit(solution)/shard_map/ppermute | solution.py:27
  85.6 3.0 %collective-permute-start.27 = (f32[16,1024]{1,0:T(8,128)S(1)}, f32[16,1024]{1,0:T(8,128)S(1)}, u32[]{:S(2)}, u32[]{:S(2)}) collective-permute-start(f32[16,1024]{1,0:T(8,128)S(1)} %pad_maximum_fusion.3), channel_id=1, source_target_pairs={{0,16},{4,20},{8,24},{12,28},{16,0},{20,4},{24,8},{28,12},{1,17},{... | collective-permute-start | bytes 196616 | tf_op jit(solution)/shard_map/ppermute | solution.py:27
  88.6 2.1 %collective-permute-done.20 = f32[8,1024]{1,0:T(8,128)S(1)} collective-permute-done((f32[8,1024]{1,0:T(8,128)S(1)}, f32[8,1024]{1,0:T(8,128)S(1)}, u32[]{:S(2)}, u32[]{:S(2)}) %collective-permute-start.20) | collective-permute-done | bytes 32800 | tf_op jit(solution)/shard_map/ppermute | solution.py:27
  92.9 2.2 %collective-permute-done.21 = f32[16,1024]{1,0:T(8,128)S(1)} collective-permute-done((f32[16,1024]{1,0:T(8,128)S(1)}, f32[16,1024]{1,0:T(8,128)S(1)}, u32[]{:S(2)}, u32[]{:S(2)}) %collective-permute-start.21) | collective-permute-done | bytes 65568 | tf_op jit(solution)/shard_map/ppermute | solution.py:27
  95.0 1.7 %collective-permute-start.22 = (f32[32,1024]{1,0:T(8,128)S(1)}, f32[32,1024]{1,0:T(8,128)S(1)}, u32[]{:S(2)}, u32[]{:S(2)}) collective-permute-start(f32[32,1024]{1,0:T(8,128)S(1)} %pad_maximum_fusion.refs_0_), channel_id=1, source_target_pairs={{0,4},{4,0},{8,12},{12,8},{16,20},{20,16},{24,28},{28,24},{1,5},{5... | collective-permute-start | bytes 393224 | tf_op jit(solution)/shard_map/ppermute | solution.py:27
  96.7 1.6 %collective-permute-start.10 = (f32[128,128]{1,0:T(8,128)S(1)}, f32[128,128]{1,0:T(8,128)S(1)}, u32[]{:S(2)}, u32[]{:S(2)}) collective-permute-start(f32[128,128]{1,0:T(8,128)S(1)} %add.75), channel_id=1, source_target_pairs={{0,2},{1,3},{2,0},{3,1},{4,6},{5,7},{6,4},{7,5},{8,10},{9,11},{10,... | collective-permute-start | bytes 196616 | tf_op jit(solution)/shard_map/ppermute | solution.py:27
  98.3 2.7 %collective-permute-done.10 = f32[128,128]{1,0:T(8,128)S(1)} collective-permute-done((f32[128,128]{1,0:T(8,128)S(1)}, f32[128,128]{1,0:T(8,128)S(1)}, u32[]{:S(2)}, u32[]{:S(2)}) %collective-permute-start.10) | collective-permute-done | bytes 65568 | tf_op jit(solution)/shard_map/ppermute | solution.py:27
  101.1 8.7 %factor.1.inverse_ref = f32[128,128]{1,0:T(8,128)S(1)} custom-call(f32[128,128]{1,0:T(8,128)S(1)} %add.76.gram_ref), custom_call_target="tpu_custom_call" | custom-call | flops 1 | bytes 1 | tf_op jit(solution)/shard_map/factor/pallas_call | solution.py:211
  109.8 2.3 %finish.1 = (f32[128,1024]{1,0:T(8,128)}, f32[128,128]{1,0:T(8,128)S(1)}) custom-call(s32[2]{0:T(128)S(1)} %pad_add_fusion.own_ref, f32[128,128]{1,0:T(8,128)S(1)} %factor.1.inverse_ref, f32[32,1024]{1,0:T(8,128)S(1)} %pad_maximum_fusion.refs_0_, f32[32,1024]{1,0:T(8,128)S(1)} %collective-permute-done.22.refs_1_, f32[32,1024]{1,0:T(8,128)S(1)} %pad_maximum_fusion.1.refs_2_, ...), custom_call_target="tpu_custom_call" | custom-call | flops 1 | bytes 1 | tf_op jit(solution)/shard_map/finish/pallas_call | solution.py:242
  (83 shorter events, 18.5 us)
Async XLA Ops:
  9.6 8.6 %collective-permute-start.1 = (f32[512,128]{1,0:T(8,128)S(1)}, f32[512,128]{1,0:T(8,128)S(1)}, u32[]{:S(2)}, u32[]{:S(2)}) collective-permute-start(f32[512,128]{1,0:T(8,128)S(1)} %get-tuple-element.18), channel_id=1, source_target_pairs={{0,1},{1,0},{2,3},{3,2},{4,5},{5,4},{6,7},{7,6},{8,9},{9,8},{10,11... | collective-permute-start | bytes 786440 | tf_op jit(solution)/shard_map/ppermute | solution.py:27
  12.2 10.9 %collective-permute-start.4 = (f32[512,128]{1,0:T(8,128)S(1)}, f32[512,128]{1,0:T(8,128)S(1)}, u32[]{:S(2)}, u32[]{:S(2)}) collective-permute-start(f32[512,128]{1,0:T(8,128)S(1)} %partial_sketch.11), channel_id=1, source_target_pairs={{0,1},{1,0},{2,3},{3,2},{4,5},{5,4},{6,7},{7,6},{8,9},{9,8},{10,11... | collective-permute-start | bytes 786440 | tf_op jit(solution)/shard_map/ppermute | solution.py:27
  15.7 11.4 %collective-permute-start = (f32[512,128]{1,0:T(8,128)S(1)}, f32[512,128]{1,0:T(8,128)S(1)}, u32[]{:S(2)}, u32[]{:S(2)}) collective-permute-start(f32[512,128]{1,0:T(8,128)S(1)} %get-tuple-element.17), channel_id=1, source_target_pairs={{0,1},{1,0},{2,3},{3,2},{4,5},{5,4},{6,7},{7,6},{8,9},{9,8},{10,11... | collective-permute-start | bytes 786440 | tf_op jit(solution)/shard_map/ppermute | solution.py:27
  18.3 9.8 %collective-permute-start.2 = (f32[512,128]{1,0:T(8,128)S(1)}, f32[512,128]{1,0:T(8,128)S(1)}, u32[]{:S(2)}, u32[]{:S(2)}) collective-permute-start(f32[512,128]{1,0:T(8,128)S(1)} %add.66), channel_id=1, source_target_pairs={{0,2},{1,3},{2,0},{3,1},{4,6},{5,7},{6,4},{7,5},{8,10},{9,11},{10,... | collective-permute-start | bytes 786440 | tf_op jit(solution)/shard_map/ppermute | solution.py:27
  20.9 25.6 %slice-start.1 = ((s8[16777216]{0:T(1024)(128)(4,1)}), s8[4194304]{0:T(1024)(128)(4,1)S(1)}, s32[]{:S(2)}) async-start(s8[16777216]{0:T(1024)(128)(4,1)} %bitcast.7), calls=%async_computation.1 | async-start | bytes 8388608
  20.9 9.2 %collective-permute-start.3 = (f32[512,128]{1,0:T(8,128)S(1)}, f32[512,128]{1,0:T(8,128)S(1)}, u32[]{:S(2)}, u32[]{:S(2)}) collective-permute-start(f32[512,128]{1,0:T(8,128)S(1)} %get-tuple-element.20), channel_id=1, source_target_pairs={{0,1},{1,0},{2,3},{3,2},{4,5},{5,4},{6,7},{7,6},{8,9},{9,8},{10,11... | collective-permute-start | bytes 786440 | tf_op jit(solution)/shard_map/ppermute | solution.py:27
  23.2 10.5 %collective-permute-start.5 = (f32[512,128]{1,0:T(8,128)S(1)}, f32[512,128]{1,0:T(8,128)S(1)}, u32[]{:S(2)}, u32[]{:S(2)}) collective-permute-start(f32[512,128]{1,0:T(8,128)S(1)} %add.69), channel_id=1, source_target_pairs={{0,2},{1,3},{2,0},{3,1},{4,6},{5,7},{6,4},{7,5},{8,10},{9,11},{10,... | collective-permute-start | bytes 786440 | tf_op jit(solution)/shard_map/ppermute | solution.py:27
  28.1 11.2 %collective-permute-start.13 = (f32[512,128]{1,0:T(8,128)S(1)}, f32[512,128]{1,0:T(8,128)S(1)}, u32[]{:S(2)}, u32[]{:S(2)}) collective-permute-start(f32[512,128]{1,0:T(8,128)S(1)} %add_add_fusion.1.refs_0_), channel_id=1, source_target_pairs={{0,2},{1,3},{2,0},{3,1},{4,6},{5,7},{6,4},{7,5},{8,10},{9,11},{10,... | collective-permute-start | bytes 786440 | tf_op jit(solution)/shard_map/ppermute | solution.py:27
  33.7 11.0 %collective-permute-start.11 = (f32[512,128]{1,0:T(8,128)S(1)}, f32[512,128]{1,0:T(8,128)S(1)}, u32[]{:S(2)}, u32[]{:S(2)}) collective-permute-start(f32[512,128]{1,0:T(8,128)S(1)} %add_add_fusion.refs_2_), channel_id=1, source_target_pairs={{0,2},{1,3},{2,0},{3,1},{4,6},{5,7},{6,4},{7,5},{8,10},{9,11},{10,... | collective-permute-start | bytes 786440 | tf_op jit(solution)/shard_map/ppermute | solution.py:27
  35.7 10.8 %collective-permute-start.15 = (f32[512,128]{1,0:T(8,128)S(1)}, f32[512,128]{1,0:T(8,128)S(1)}, u32[]{:S(2)}, u32[]{:S(2)}) collective-permute-start(f32[512,128]{1,0:T(8,128)S(1)} %add_add_fusion.1.refs_0_), channel_id=1, source_target_pairs={{0,1},{1,0},{2,3},{3,2},{4,5},{5,4},{6,7},{7,6},{8,9},{9,8},{10,11... | collective-permute-start | bytes 786440 | tf_op jit(solution)/shard_map/ppermute | solution.py:27
  35.7 10.8 %collective-permute-start.16 = (f32[512,128]{1,0:T(8,128)S(1)}, f32[512,128]{1,0:T(8,128)S(1)}, u32[]{:S(2)}, u32[]{:S(2)}) collective-permute-start(f32[512,128]{1,0:T(8,128)S(1)} %add_add_fusion.refs_2_), channel_id=1, source_target_pairs={{0,1},{1,0},{2,3},{3,2},{4,5},{5,4},{6,7},{7,6},{8,9},{9,8},{10,11... | collective-permute-start | bytes 786440 | tf_op jit(solution)/shard_map/ppermute | solution.py:27
  39.3 13.7 %collective-permute-start.14 = (f32[512,128]{1,0:T(8,128)S(1)}, f32[512,128]{1,0:T(8,128)S(1)}, u32[]{:S(2)}, u32[]{:S(2)}) collective-permute-start(f32[512,128]{1,0:T(8,128)S(1)} %collective-permute-done.13.refs_0_), channel_id=1, source_target_pairs={{0,1},{1,0},{2,3},{3,2},{4,5},{5,4},{6,7},{7,6},{8,9},{9,8},{10,11... | collective-permute-start | bytes 786440 | tf_op jit(solution)/shard_map/ppermute | solution.py:27
  44.7 12.0 %collective-permute-start.12 = (f32[512,128]{1,0:T(8,128)S(1)}, f32[512,128]{1,0:T(8,128)S(1)}, u32[]{:S(2)}, u32[]{:S(2)}) collective-permute-start(f32[512,128]{1,0:T(8,128)S(1)} %collective-permute-done.11.refs_0_), channel_id=1, source_target_pairs={{0,1},{1,0},{2,3},{3,2},{4,5},{5,4},{6,7},{7,6},{8,9},{9,8},{10,11... | collective-permute-start | bytes 786440 | tf_op jit(solution)/shard_map/ppermute | solution.py:27
  45.9 16.5 %collective-permute-start.6 = (f32[128,128]{1,0:T(8,128)S(1)}, f32[128,128]{1,0:T(8,128)S(1)}, u32[]{:S(2)}, u32[]{:S(2)}) collective-permute-start(f32[128,128]{1,0:T(8,128)S(1)} %convolution_add_fusion), channel_id=1, source_target_pairs={{0,1},{1,0},{2,3},{3,2},{4,5},{5,4},{6,7},{7,6},{8,9},{9,8},{10,11... | collective-permute-start | bytes 196616 | tf_op jit(solution)/shard_map/ppermute | solution.py:27
  60.5 7.0 %collective-permute-start.23 = (f32[32,1024]{1,0:T(8,128)S(1)}, f32[32,1024]{1,0:T(8,128)S(1)}, u32[]{:S(2)}, u32[]{:S(2)}) collective-permute-start(f32[32,1024]{1,0:T(8,128)S(1)} %get-tuple-element.24), channel_id=1, source_target_pairs={{0,8},{4,12},{8,0},{12,4},{16,24},{20,28},{24,16},{28,20},{1,9},{5... | collective-permute-start | bytes 393224 | tf_op jit(solution)/shard_map/ppermute | solution.py:27
  62.4 5.0 %collective-permute-start.7 = (f32[128,128]{1,0:T(8,128)S(1)}, f32[128,128]{1,0:T(8,128)S(1)}, u32[]{:S(2)}, u32[]{:S(2)}) collective-permute-start(f32[128,128]{1,0:T(8,128)S(1)} %add.72), channel_id=1, source_target_pairs={{0,4},{4,0},{8,12},{12,8},{16,20},{20,16},{24,28},{28,24},{1,5},{5... | collective-permute-start | bytes 196616 | tf_op jit(solution)/shard_map/ppermute | solution.py:27
  64.0 11.2 %collective-permute-start.17 = (f32[32,1024]{1,0:T(8,128)S(1)}, f32[32,1024]{1,0:T(8,128)S(1)}, u32[]{:S(2)}, u32[]{:S(2)}) collective-permute-start(f32[32,1024]{1,0:T(8,128)S(1)} %get-tuple-element.22), channel_id=1, source_target_pairs={{0,4},{4,0},{8,12},{12,8},{16,20},{20,16},{24,28},{28,24},{1,5},{5... | collective-permute-start | bytes 393224 | tf_op jit(solution)/shard_map/ppermute | solution.py:27
  67.5 4.3 %collective-permute-start.8 = (f32[128,128]{1,0:T(8,128)S(1)}, f32[128,128]{1,0:T(8,128)S(1)}, u32[]{:S(2)}, u32[]{:S(2)}) collective-permute-start(f32[128,128]{1,0:T(8,128)S(1)} %add.73), channel_id=1, source_target_pairs={{0,8},{4,12},{8,0},{12,4},{16,24},{20,28},{24,16},{28,20},{1,9},{5... | collective-permute-start | bytes 196616 | tf_op jit(solution)/shard_map/ppermute | solution.py:27
  67.6 7.9 %collective-permute-start.24 = (f32[16,1024]{1,0:T(8,128)S(1)}, f32[16,1024]{1,0:T(8,128)S(1)}, u32[]{:S(2)}, u32[]{:S(2)}) collective-permute-start(f32[16,1024]{1,0:T(8,128)S(1)} %slice.37), channel_id=1, source_target_pairs={{0,16},{4,20},{8,24},{12,28},{16,0},{20,4},{24,8},{28,12},{1,17},{... | collective-permute-start | bytes 196616 | tf_op jit(solution)/shard_map/ppermute | solution.py:27
  71.8 24.9 %collective-permute-start.9 = (f32[128,128]{1,0:T(8,128)S(1)}, f32[128,128]{1,0:T(8,128)S(1)}, u32[]{:S(2)}, u32[]{:S(2)}) collective-permute-start(f32[128,128]{1,0:T(8,128)S(1)} %add.74), channel_id=1, source_target_pairs={{0,16},{4,20},{8,24},{12,28},{16,0},{20,4},{24,8},{28,12},{1,17},{... | collective-permute-start | bytes 196616 | tf_op jit(solution)/shard_map/ppermute | solution.py:27
  75.2 4.3 %collective-permute-start.18 = (f32[16,1024]{1,0:T(8,128)S(1)}, f32[16,1024]{1,0:T(8,128)S(1)}, u32[]{:S(2)}, u32[]{:S(2)}) collective-permute-start(f32[16,1024]{1,0:T(8,128)S(1)} %slice.33), channel_id=1, source_target_pairs={{0,8},{4,12},{8,0},{12,4},{16,24},{20,28},{24,16},{28,20},{1,9},{5... | collective-permute-start | bytes 196616 | tf_op jit(solution)/shard_map/ppermute | solution.py:27
  75.5 4.1 %collective-permute-start.25 = (f32[8,1024]{1,0:T(8,128)S(1)}, f32[8,1024]{1,0:T(8,128)S(1)}, u32[]{:S(2)}, u32[]{:S(2)}) collective-permute-start(f32[8,1024]{1,0:T(8,128)S(1)} %slice.39), channel_id=1, source_target_pairs={{0,4},{4,0},{8,12},{12,8},{16,20},{20,16},{24,28},{28,24},{1,5},{5... | collective-permute-start | bytes 98312 | tf_op jit(solution)/shard_map/ppermute | solution.py:27
  79.6 6.0 %collective-permute-start.19 = (f32[8,1024]{1,0:T(8,128)S(1)}, f32[8,1024]{1,0:T(8,128)S(1)}, u32[]{:S(2)}, u32[]{:S(2)}) collective-permute-start(f32[8,1024]{1,0:T(8,128)S(1)} %slice.35), channel_id=1, source_target_pairs={{0,16},{4,20},{8,24},{12,28},{16,0},{20,4},{24,8},{28,12},{1,17},{... | collective-permute-start | bytes 98312 | tf_op jit(solution)/shard_map/ppermute | solution.py:27
  79.7 5.9 %collective-permute-start.26 = (f32[8,1024]{1,0:T(8,128)S(1)}, f32[8,1024]{1,0:T(8,128)S(1)}, u32[]{:S(2)}, u32[]{:S(2)}) collective-permute-start(f32[8,1024]{1,0:T(8,128)S(1)} %slice_add_fusion.2), channel_id=1, source_target_pairs={{0,4},{4,0},{8,12},{12,8},{16,20},{20,16},{24,28},{28,24},{1,5},{5... | collective-permute-start | bytes 98312 | tf_op jit(solution)/shard_map/ppermute | solution.py:27
  85.6 5.2 %collective-permute-start.20 = (f32[8,1024]{1,0:T(8,128)S(1)}, f32[8,1024]{1,0:T(8,128)S(1)}, u32[]{:S(2)}, u32[]{:S(2)}) collective-permute-start(f32[8,1024]{1,0:T(8,128)S(1)} %slice_add_fusion.3), channel_id=1, source_target_pairs={{0,16},{4,20},{8,24},{12,28},{16,0},{20,4},{24,8},{28,12},{1,17},{... | collective-permute-start | bytes 98312 | tf_op jit(solution)/shard_map/ppermute | solution.py:27
  85.6 5.8 %collective-permute-start.27 = (f32[16,1024]{1,0:T(8,128)S(1)}, f32[16,1024]{1,0:T(8,128)S(1)}, u32[]{:S(2)}, u32[]{:S(2)}) collective-permute-start(f32[16,1024]{1,0:T(8,128)S(1)} %pad_maximum_fusion.3), channel_id=1, source_target_pairs={{0,16},{4,20},{8,24},{12,28},{16,0},{20,4},{24,8},{28,12},{1,17},{... | collective-permute-start | bytes 196616 | tf_op jit(solution)/shard_map/ppermute | solution.py:27
  90.8 4.3 %collective-permute-start.21 = (f32[16,1024]{1,0:T(8,128)S(1)}, f32[16,1024]{1,0:T(8,128)S(1)}, u32[]{:S(2)}, u32[]{:S(2)}) collective-permute-start(f32[16,1024]{1,0:T(8,128)S(1)} %pad_maximum_fusion.2), channel_id=1, source_target_pairs={{0,8},{4,12},{8,0},{12,4},{16,24},{20,28},{24,16},{28,20},{1,9},{5... | collective-permute-start | bytes 196616 | tf_op jit(solution)/shard_map/ppermute | solution.py:27
  91.5 18.3 %collective-permute-start.28 = (f32[32,1024]{1,0:T(8,128)S(1)}, f32[32,1024]{1,0:T(8,128)S(1)}, u32[]{:S(2)}, u32[]{:S(2)}) collective-permute-start(f32[32,1024]{1,0:T(8,128)S(1)} %pad_maximum_fusion.1.refs_2_), channel_id=1, source_target_pairs={{0,8},{4,12},{8,0},{12,4},{16,24},{20,28},{24,16},{28,20},{1,9},{5... | collective-permute-start | bytes 393224 | tf_op jit(solution)/shard_map/ppermute | solution.py:27
  95.0 14.8 %collective-permute-start.22 = (f32[32,1024]{1,0:T(8,128)S(1)}, f32[32,1024]{1,0:T(8,128)S(1)}, u32[]{:S(2)}, u32[]{:S(2)}) collective-permute-start(f32[32,1024]{1,0:T(8,128)S(1)} %pad_maximum_fusion.refs_0_), channel_id=1, source_target_pairs={{0,4},{4,0},{8,12},{12,8},{16,20},{20,16},{24,28},{28,24},{1,5},{5... | collective-permute-start | bytes 393224 | tf_op jit(solution)/shard_map/ppermute | solution.py:27
  96.7 4.3 %collective-permute-start.10 = (f32[128,128]{1,0:T(8,128)S(1)}, f32[128,128]{1,0:T(8,128)S(1)}, u32[]{:S(2)}, u32[]{:S(2)}) collective-permute-start(f32[128,128]{1,0:T(8,128)S(1)} %add.75), channel_id=1, source_target_pairs={{0,2},{1,3},{2,0},{3,1},{4,6},{5,7},{6,4},{7,5},{8,10},{9,11},{10,... | collective-permute-start | bytes 196616 | tf_op jit(solution)/shard_map/ppermute | solution.py:27
  112.1 1.3 %collective-permute-start.29 = (f32[128,128]{1,0:T(8,128)S(1)}, f32[128,128]{1,0:T(8,128)S(1)}, u32[]{:S(2)}, u32[]{:S(2)}) collective-permute-start(f32[128,128]{1,0:T(8,128)S(1)} %get-tuple-element.26), channel_id=1, source_target_pairs={{0,1},{1,0},{2,3},{3,2},{4,5},{5,4},{6,7},{7,6},{8,9},{9,8},{10,11... | collective-permute-start | bytes 196616 | tf_op jit(solution)/shard_map/ppermute | solution.py:27
  113.4 4.3 %collective-permute-start.30 = (f32[128,128]{1,0:T(8,128)S(1)}, f32[128,128]{1,0:T(8,128)S(1)}, u32[]{:S(2)}, u32[]{:S(2)}) collective-permute-start(f32[128,128]{1,0:T(8,128)S(1)} %add.83), channel_id=1, source_target_pairs={{0,2},{1,3},{2,0},{3,1},{4,6},{5,7},{6,4},{7,5},{8,10},{9,11},{10,... | collective-permute-start | bytes 196616 | tf_op jit(solution)/shard_map/ppermute | solution.py:27
  (5 other events, 79.1 us)

commit v5 on v4

--- a/solution.py
+++ b/solution.py
@@ -15,12 +15,16 @@
 TILE = 256
 SMEM = pl.BlockSpec(memory_space=pltpu.SMEM)
 VMEM = pl.BlockSpec(memory_space=pltpu.VMEM)
-ANY = pl.BlockSpec(memory_space=pl.ANY)
-FREE = pl.CostEstimate(flops=1, bytes_accessed=1, transcendentals=0)
-
-
-def params(mib):
-    return pltpu.CompilerParams(vmem_limit_bytes=mib * 1024 * 1024)
+HBM = pl.BlockSpec(memory_space=pltpu.HBM)
+fence = lax.optimization_barrier
+
+
+def cost(mib):
+    return pl.CostEstimate(flops=1, bytes_accessed=int(mib * 2**20), transcendentals=0)
+
+
+def params():
+    return pltpu.CompilerParams(vmem_limit_bytes=52 * 1024 * 1024)
 
 
 def swap(value, axis, bit):
@@ -55,12 +59,17 @@
 
 
 def sketch_kernel(pieces, quarter, first, own_ref, data_ref, omega_ref, *refs):
+    if first:
+        refs, (omega_held, omega_sem) = refs[:-2], refs[-2:]
+        omega_copy = pltpu.make_async_copy(omega_ref, omega_held, omega_sem)
+        omega_copy.start()
     outs, (held, sems) = refs[:-2], refs[-2:]
     copies = start_copies(own_ref, data_ref, held, sems, pieces, quarter)
     if first:
         width = omega_ref.shape[1]
         wide = outs[-1]
-        upper, rest = split(omega_ref[...])
+        omega_copy.wait()
+        upper, rest = split(omega_held[...])
         wide[:, :width] = upper
         wide[:, width:] = rest
     else:
@@ -76,27 +85,33 @@
             two = jnp.dot(rest, omega[:, :width], preferred_element_type=f32)
             both = one if both is None else both + one
             more = two if more is None else more + two
-        outs[k][...] = both[:, :width] + both[:, width:] + more
-
-
-def sketch(own, data, omega, pieces, first=False):
+        first_row = pieces[k][1]
+        out = outs[k // 2]
+        out[first_row : first_row + PIECE] = both[:, :width] + both[:, width:] + more
+
+
+def sketch(own, data, omega, places, first=False):
+    pieces = [(place, row) for place in places for row in (0, PIECE)]
     cols = data.shape[1]
     width = omega.shape[1] if first else omega.shape[1] // 2
     quarter = data.shape[0] // lax.axis_size("col")
-    out = [jax.ShapeDtypeStruct((PIECE, width), f32)] * len(pieces)
+    out = [jax.ShapeDtypeStruct((quarter, width), f32)] * len(places)
     if first:
         out.append(jax.ShapeDtypeStruct((cols, 2 * width), bf16))
+    scratch = [
+        pltpu.VMEM((len(pieces), PIECE, cols), f32),
+        pltpu.SemaphoreType.DMA((len(pieces), cols // TILE)),
+    ]
+    if first:
+        scratch += [pltpu.VMEM(omega.shape, f32), pltpu.SemaphoreType.DMA]
     return pl.pallas_call(
         functools.partial(sketch_kernel, pieces, quarter, first),
-        in_specs=[SMEM, ANY, VMEM],
+        in_specs=[SMEM, HBM, HBM if first else VMEM],
         out_specs=[VMEM] * len(out),
         out_shape=out,
-        scratch_shapes=[
-            pltpu.VMEM((len(pieces), PIECE, cols), f32),
-            pltpu.SemaphoreType.DMA((len(pieces), cols // TILE)),
-        ],
-        compiler_params=params(20),
-        cost_estimate=FREE,
+        scratch_shapes=scratch,
+        compiler_params=params(),
+        cost_estimate=cost(0.01 * len(pieces)),
         name="partial_sketch",
     )(own, data, omega)
 
@@ -110,14 +125,15 @@
 
 def project_kernel(pieces, quarter, before, orders, own_ref, data_ref, *refs):
     count = len(pieces)
-    parts, refs = refs[:count], refs[count:]
+    parts, refs = refs[: count // 2], refs[count // 2 :]
     old, refs = (refs[0], refs[1:]) if before else (None, refs)
     outs, (total, held, sems) = refs[:-3], refs[-3:]
     if orders is None:
         total = outs[0]
     copies = start_copies(own_ref, data_ref, held, sems, pieces, quarter)
     for k in range(count):
-        upper, rest = split(parts[k][...].T)
+        first = pieces[k][1]
+        upper, rest = split(parts[k // 2][first : first + PIECE].T)
         stack = jnp.concatenate([upper, rest], 0)
         width = upper.shape[0]
         for t, copy in enumerate(copies[k]):
@@ -142,7 +158,8 @@
                     ref[i * step : (i + 1) * step] = total[pl.ds(pl.multiple_of(at, step), step)]
 
 
-def project(own, data, pieces, parts, before=None, orders=None):
+def project(own, data, places, parts, before=None, orders=None):
+    pieces = [(place, first) for place in places for first in (0, PIECE)]
     cols = data.shape[1]
     width = parts[0].shape[1]
     quarter = data.shape[0] // lax.axis_size("col")
@@ -153,7 +170,7 @@
         out = [jax.ShapeDtypeStruct((width // len(orders) // 2, cols), f32)] * (2 * len(orders))
     return pl.pallas_call(
         functools.partial(project_kernel, pieces, quarter, before is not None, orders),
-        in_specs=[SMEM, ANY] + [VMEM] * (len(args) - 2),
+        in_specs=[SMEM, HBM] + [VMEM] * (len(args) - 2),
         out_specs=[VMEM] * len(out),
         out_shape=out,
         scratch_shapes=[
@@ -161,20 +178,26 @@
             pltpu.VMEM((len(pieces), PIECE, cols), f32),
             pltpu.SemaphoreType.DMA((len(pieces), cols // TILE)),
         ],
-        compiler_params=params(24),
-        cost_estimate=FREE,
+        compiler_params=params(),
+        cost_estimate=cost(6 * len(pieces)),
         name="project",
     )(*args)
 
 
-def factor_kernel(gram_ref, out_ref, work):
-    n = gram_ref.shape[0]
-    row = lax.broadcasted_iota(jnp.int32, (n, n), 0)
-    col = lax.broadcasted_iota(jnp.int32, (n, n), 1)
-    work[:, :n] = gram_ref[...]
-    work[:, n:] = jnp.where(row == col, 1.0, 0.0).astype(f32)
+def factor_kernel(index, count, in_ref, out_ref, *scratch):
+    n = in_ref.shape[0]
+    last = index == count - 1
+    work = scratch[0] if last else out_ref
+    if index == 0:
+        row = lax.broadcasted_iota(jnp.int32, (n, n), 0)
+        col = lax.broadcasted_iota(jnp.int32, (n, n), 1)
+        work[:, :n] = in_ref[...]
+        work[:, n:] = jnp.where(row == col, 1.0, 0.0).astype(f32)
+    else:
+        work[...] = in_ref[...]
     sub = lax.broadcasted_iota(jnp.int32, (8, n), 0)
-    for b in range(n // 8):
+    panels = n // 8
+    for b in range(panels * index // count, panels * (index + 1) // count):
         top = slice(8 * b, 8 * b + 8)
         panel = work[top, :]
         spread = [jnp.broadcast_to(panel[:, 8 * b + j : 8 * b + j + 1], (8, n)) for j in range(8)]
@@ -198,26 +221,29 @@
         for i in range(1, 8):
             l_panel = jnp.where(sub == i, left[i], l_panel)
             r_panel = jnp.where(sub == i, right[i], r_panel)
-        out_ref[top, :] = r_panel
-        if b < n // 8 - 1:
+        work[top, n:] = r_panel
+        if b < panels - 1:
             done = jnp.concatenate([l_panel, r_panel], 1)
             change = dot(l_panel, done, 0, 0)
             below = slice(8 * b + 8, n)
             work[below, :] = work[below, :] - change[8 * b + 8 :, :]
-
-
-def factor(gram):
-    n = gram.shape[0]
+    if last:
+        out_ref[...] = work[:, n:]
+
+
+def factor(index, count, value):
+    n = value.shape[0]
+    last = index == count - 1
     return pl.pallas_call(
-        factor_kernel,
+        functools.partial(factor_kernel, index, count),
         in_specs=[VMEM],
         out_specs=VMEM,
-        out_shape=jax.ShapeDtypeStruct((n, n), f32),
-        scratch_shapes=[pltpu.VMEM((n, 2 * n), f32)],
-        compiler_params=params(8),
-        cost_estimate=FREE,
+        out_shape=jax.ShapeDtypeStruct((n, n if last else 2 * n), f32),
+        scratch_shapes=[pltpu.VMEM((n, 2 * n), f32)] if last else [],
+        compiler_params=params(),
+        cost_estimate=cost(32 / count),
         name="factor",
-    )(gram)
+    )(value)
 
 
 def finish_kernel(orders, own_ref, inverse_ref, *refs):
@@ -248,8 +274,8 @@
             jax.ShapeDtypeStruct((width, width), f32),
         ],
         scratch_shapes=[pltpu.VMEM((width, cols), f32)],
-        compiler_params=params(16),
-        cost_estimate=FREE,
+        compiler_params=params(),
+        cost_estimate=cost(8),
         name="finish",
     )(own, inverse, *parts)
 
@@ -262,53 +288,55 @@
     own = jnp.stack([lax.axis_index("col"), lax.axis_index("row") % 8]).astype(jnp.int32)
     bits = [1 << k for k in range(nrow.bit_length() - 1)]
 
-    a3, wide = sketch(own, data, omega, [(3, 0)], True)
-    (a2,) = sketch(own, data, wide, [(2, 0)])
-    away_a = swap(a2 + swap(a3, "col", 1), "col", 2)
-    (b3,) = sketch(own, data, wide, [(3, PIECE)])
-    (b2,) = sketch(own, data, wide, [(2, PIECE)])
-    away_b = swap(b2 + swap(b3, "col", 1), "col", 2)
-    a1, b1 = sketch(own, data, wide, [(1, 0), (1, PIECE)])
-    a0, b0 = sketch(own, data, wide, [(0, 0), (0, PIECE)])
-    own_a = a0 + swap(a1, "col", 1) + away_a
-    own_b = b0 + swap(b1, "col", 1) + away_b
-
-    third_a = swap(own_a, "col", 2)
-    third_b = swap(own_b, "col", 2)
-    second_a = swap(own_a, "col", 1)
-    second_b = swap(own_b, "col", 1)
-    fourth_a = swap(third_a, "col", 1)
-    fourth_b = swap(third_b, "col", 1)
-
-    gram = dot(own_a, own_a, 0, 0) + dot(own_b, own_b, 0, 0)
+    part, wide = sketch(own, data, omega, [3], True)
+    (pair,) = sketch(own, data, wide, [2])
+    pair, wide = fence((pair + swap(part, "col", 1), wide))
+    away = swap(pair, "col", 2)
+    part, here = sketch(own, data, wide, [1, 0])
+    part, away = fence((swap(part, "col", 1), away))
+    sketched = here + part + away
+
+    third = swap(sketched, "col", 2)
+    second = swap(sketched, "col", 1)
+    gram = dot(sketched, sketched, 0, 0)
+    gram = gram + swap(gram, "row", bits[0])
+    (acc,) = project(own, data, [0], [sketched])
+    gram, acc, second = fence((gram, acc, second))
+    gram = gram + swap(gram, "row", bits[1])
+    (acc,) = project(own, data, [1], [second], acc)
+    gram, acc = fence((gram, acc))
+    for bit in bits[2:]:
+        gram = gram + swap(gram, "row", bit)
     gram = gram + swap(gram, "col", 1)
-    for bit in bits:
-        gram = gram + swap(gram, "row", bit)
+    third, gram, acc = fence((third, gram, acc))
+    fourth = swap(third, "col", 1)
     gram = gram + swap(gram, "col", 2)
-    inverse = factor(gram)
-    basis = dot(jnp.concatenate([own_a, own_b], 0), inverse, 1, 1)
-
+    (acc,) = project(own, data, [2], [third], acc)
+    gram, acc, fourth = fence((gram, acc, fourth))
     cuts = [(1, 2, 4), (2, 4, 1)]
     orders = [order(cut) for cut in cuts]
-    (acc,) = project(
-        own, data, [(0, 0), (1, 0), (0, PIECE), (1, PIECE)], [own_a, second_a, own_b, second_b]
-    )
-    (acc,) = project(own, data, [(2, 0), (3, 0)], [third_a, fourth_a], acc)
-    sums = project(own, data, [(2, PIECE), (3, PIECE)], [third_b, fourth_b], acc, orders)
-
+    sums = project(own, data, [3], [fourth], acc, orders)
+
+    *sums, state = fence((*sums, gram))
+    sends, keeps = sums[0::2], sums[1::2]
+    for k in range(3):
+        if k > 0:
+            half = keeps[0].shape[0] // 2
+            sends, keeps = [v[half:] for v in keeps], [v[:half] for v in keeps]
+        keeps = [v + swap(w, "row", cut[k]) for v, w, cut in zip(keeps, sends, cuts)]
+        state = factor(k, 4, state)
+        *keeps, state = fence((*keeps, state))
+    for bit in bits[3:]:
+        keeps = [v + swap(v, "row", bit) for v in keeps]
+    keeps = [jnp.concatenate([v, swap(v, "row", cut[2])], 0) for v, cut in zip(keeps, cuts)]
+    inverse = factor(3, 4, state)
+    *keeps, inverse = fence((*keeps, inverse))
+    keeps = [jnp.concatenate([v, swap(v, "row", cut[1])], 0) for v, cut in zip(keeps, cuts)]
+    basis = dot(sketched, inverse, 1, 1)
+    *keeps, basis = fence((*keeps, basis))
     parts = []
-    for piece, cut in enumerate(cuts):
-        send, keep = sums[2 * piece], sums[2 * piece + 1]
-        for k, bit in enumerate(cut):
-            if k > 0:
-                half = keep.shape[0] // 2
-                keep, send = keep[:half], keep[half:]
-            keep = keep + swap(send, "row", bit)
-        for bit in bits[3:]:
-            keep = keep + swap(keep, "row", bit)
-        for bit in reversed(cut[1:]):
-            keep = jnp.concatenate([keep, swap(keep, "row", bit)], 0)
-        parts += [keep, swap(keep, "row", cut[0])]
+    for v, cut in zip(keeps, cuts):
+        parts += [v, swap(v, "row", cut[0])]
 
     projected, small = finish(own, inverse, parts, orders)
     small = small + swap(small, "col", 1)

time: 119 us -> 114 us (0.958)
  starting transfers between devices: 33.1 us -> 26.5 us
  waiting for transfers between devices: 33.9 us -> 40.4 us
  local copies, waits for them, and re-layouts: 6.85 us -> 1.06 us
  Pallas kernels: 40 us -> 41.9 us
    ppermute x31 -> x25, starting transfers between devices: 33.1 us -> 26.5 us  [swap(): lax.ppermute(value, axis, [(i, i ^ bit) for i in range(lax.axis_size(axis...]
    ppermute x31 -> x25, waiting for transfers between devices: 33.9 us -> 40.4 us  [swap(): lax.ppermute(value, axis, [(i, i ^ bit) for i in range(lax.axis_size(axis...]
    unnamed x12 -> x2, local copies, waits for them, and re-layouts: 6.83 us -> 1.04 us
    pallas_call x3 -> x4, Pallas kernels: 14 us -> 16.5 us  [project(): pl.pallas_call(functools.partial(project_kernel, pieces, quarter, before...]
    pallas_call x6 -> x3, Pallas kernels: 15 us -> 14.4 us  [sketch(): pl.pallas_call(functools.partial(sketch_kernel, pieces, quarter, first),...]
    dot_general x3 -> x2, matrix products: 2.57 us -> 2.4 us  [dot(): lax.dot_general(a, b, (((a_dim,), (b_dim,)), ((), ())), precision=precisi...]
    pallas_call x1 -> x4, Pallas kernels: 8.72 us -> 8.69 us  [factor(): pl.pallas_call(functools.partial(factor_kernel, index, count), in_specs=[...]
  transfers between devices with their start and end apart: 31 -> 25, of which waited for: 14 -> 15; matrix products, arithmetic and copies ran while one was open for 2% -> 2% of each run, Pallas kernels for 30% -> 22%
where the time goes in v5:
time: 114 us
  Pallas kernels  41.9 us (37%)
  waiting for transfers between devices  40.4 us (35%)
  starting transfers between devices  26.5 us (23%)
  matrix products  2.4 us (2%)
    ppermute x25, waiting for transfers between devices, swap(): lax.ppermute(value, axis, [(i, i ^ bit) for i in range(lax.axis_size(axis...  40.4 us
    ppermute x25, starting transfers between devices, swap(): lax.ppermute(value, axis, [(i, i ^ bit) for i in range(lax.axis_size(axis...  26.5 us
    pallas_call x4, Pallas kernels, project(): pl.pallas_call(functools.partial(project_kernel, pieces, quarter, before...  16.5 us
    pallas_call x3, Pallas kernels, sketch(): pl.pallas_call(functools.partial(sketch_kernel, pieces, quarter, first),...  14.4 us
    pallas_call x4, Pallas kernels, factor(): pl.pallas_call(functools.partial(factor_kernel, index, count), in_specs=[...  8.69 us
    dot_general x2, matrix products, dot(): lax.dot_general(a, b, (((a_dim,), (b_dim,)), ((), ())), precision=precisi...  2.4 us
    pallas_call x1, Pallas kernels, finish(): pl.pallas_call(functools.partial(finish_kernel, orders), in_specs=[SMEM]...  2.3 us
  transfers between devices with their start and end apart: 25, of which 15 were waited for; matrix products, arithmetic and copies ran while one was open for 2% of the time, Pallas kernels for 22%

profile of v5, /device:TPU:0, one launch (start us, length us, event | category | flops | bytes accessed | tf_op | source)
XLA Modules:
  0.0 114.1 jit_solution(9349709690069777563)
XLA Ops:
  1.8 4.0 %partial_sketch.3 = (f32[1024,128]{1,0:T(8,128)S(1)}, bf16[1024,256]{1,0:T(8,128)(2,1)S(1)}) custom-call(s32[2]{0:T(128)S(1)} %pad_add_fusion.own_ref, f32[4096,1024]{1,0:T(8,128)} %data_ref.13, f32[1024,128]{1,0:T(8,128)S(1)} %copy-done), custom_call_target="tpu_custom_call" | custom-call | flops 1 | bytes 20971 | tf_op jit(solution)/shard_map/partial_sketch/pallas_call | solution.py:107
  6.3 4.0 %partial_sketch.4 = f32[1024,128]{1,0:T(8,128)S(1)} custom-call(s32[2]{0:T(128)S(1)} %pad_add_fusion.own_ref, f32[4096,1024]{1,0:T(8,128)} %data_ref.13, bf16[1024,256]{1,0:T(8,128)(2,1)S(1)} %get-tuple-element.50.omega_ref), custom_call_target="tpu_custom_call" | custom-call | flops 1 | bytes 20971 | tf_op jit(solution)/shard_map/partial_sketch/pallas_call | solution.py:107
  10.4 6.3 %partial_sketch.5 = (f32[1024,128]{1,0:T(8,128)S(1)}, f32[1024,128]{1,0:T(8,128)S(1)}) custom-call(s32[2]{0:T(128)S(1)} %pad_add_fusion.own_ref, f32[4096,1024]{1,0:T(8,128)} %data_ref.13, bf16[1024,256]{1,0:T(8,128)(2,1)S(1)} %get-tuple-element.50.omega_ref), custom_call_target="tpu_custom_call" | custom-call | flops 1 | bytes 41943 | tf_op jit(solution)/shard_map/partial_sketch/pallas_call | solution.py:107
  16.9 3.0 %collective-permute-start.2 = (f32[1024,128]{1,0:T(8,128)S(1)}, f32[1024,128]{1,0:T(8,128)S(1)}, u32[]{:S(2)}, u32[]{:S(2)}) collective-permute-start(f32[1024,128]{1,0:T(8,128)S(1)} %add.53), channel_id=1, source_target_pairs={{0,2},{1,3},{2,0},{3,1},{4,6},{5,7},{6,4},{7,5},{8,10},{9,11},{10,... | collective-permute-start | bytes 1572872 | tf_op jit(solution)/shard_map/ppermute | solution.py:31
  19.8 12.2 %collective-permute-done.2 = f32[1024,128]{1,0:T(8,128)S(1)} collective-permute-done((f32[1024,128]{1,0:T(8,128)S(1)}, f32[1024,128]{1,0:T(8,128)S(1)}, u32[]{:S(2)}, u32[]{:S(2)}) %collective-permute-start.2) | collective-permute-done | bytes 524320 | tf_op jit(solution)/shard_map/ppermute | solution.py:31
  32.2 1.8 %collective-permute-start.3 = (f32[1024,128]{1,0:T(8,128)S(1)}, f32[1024,128]{1,0:T(8,128)S(1)}, u32[]{:S(2)}, u32[]{:S(2)}) collective-permute-start(f32[1024,128]{1,0:T(8,128)S(1)} %add_add_fusion.refs_0_), channel_id=1, source_target_pairs={{0,2},{1,3},{2,0},{3,1},{4,6},{5,7},{6,4},{7,5},{8,10},{9,11},{10,... | collective-permute-start | bytes 1572872 | tf_op jit(solution)/shard_map/ppermute | solution.py:31
  35.0 1.6 %collective-permute-start.4 = (f32[128,128]{1,0:T(8,128)S(1)}, f32[128,128]{1,0:T(8,128)S(1)}, u32[]{:S(2)}, u32[]{:S(2)}) collective-permute-start(f32[128,128]{1,0:T(8,128)S(1)} %fusion), channel_id=1, source_target_pairs={{0,4},{4,0},{8,12},{12,8},{16,20},{20,16},{24,28},{28,24},{1,5},{5... | collective-permute-start | bytes 196616 | tf_op jit(solution)/shard_map/ppermute | solution.py:31
  36.6 4.0 %project.4.refs_1_ = f32[128,1024]{1,0:T(8,128)S(1)} custom-call(s32[2]{0:T(128)S(1)} %pad_add_fusion.own_ref, f32[4096,1024]{1,0:T(8,128)} %data_ref.13, f32[1024,128]{1,0:T(8,128)S(1)} %add_add_fusion.refs_0_), custom_call_target="tpu_custom_call" | custom-call | flops 1 | bytes 12582912 | tf_op jit(solution)/shard_map/project/pallas_call | solution.py:171
  40.6 1.6 %collective-permute-start.6 = (f32[128,128]{1,0:T(8,128)S(1)}, f32[128,128]{1,0:T(8,128)S(1)}, u32[]{:S(2)}, u32[]{:S(2)}) collective-permute-start(f32[128,128]{1,0:T(8,128)S(1)} %add.56), channel_id=1, source_target_pairs={{0,8},{4,12},{8,0},{12,4},{16,24},{20,28},{24,16},{28,20},{1,9},{5... | collective-permute-start | bytes 196616 | tf_op jit(solution)/shard_map/ppermute | solution.py:31
  42.3 4.3 %project.5.refs_1_ = f32[128,1024]{1,0:T(8,128)S(1)} custom-call(s32[2]{0:T(128)S(1)} %pad_add_fusion.own_ref, f32[4096,1024]{1,0:T(8,128)} %data_ref.13, f32[1024,128]{1,0:T(8,128)S(1)} %collective-permute-done.5.refs_0_, f32[128,1024]{1,0:T(8,128)S(1)} %project.4.refs_1_), custom_call_target="tpu_custom_call" | custom-call | flops 1 | bytes 12582912 | tf_op jit(solution)/shard_map/project/pallas_call | solution.py:171
  46.6 2.7 %collective-permute-start.7 = (f32[128,128]{1,0:T(8,128)S(1)}, f32[128,128]{1,0:T(8,128)S(1)}, u32[]{:S(2)}, u32[]{:S(2)}) collective-permute-start(f32[128,128]{1,0:T(8,128)S(1)} %add.57), channel_id=1, source_target_pairs={{0,16},{4,20},{8,24},{12,28},{16,0},{20,4},{24,8},{28,12},{1,17},{... | collective-permute-start | bytes 196616 | tf_op jit(solution)/shard_map/ppermute | solution.py:31
  49.2 3.2 %collective-permute-done.7 = f32[128,128]{1,0:T(8,128)S(1)} collective-permute-done((f32[128,128]{1,0:T(8,128)S(1)}, f32[128,128]{1,0:T(8,128)S(1)}, u32[]{:S(2)}, u32[]{:S(2)}) %collective-permute-start.7) | collective-permute-done | bytes 65568 | tf_op jit(solution)/shard_map/ppermute | solution.py:31
  54.5 4.1 %project.6.refs_1_ = f32[128,1024]{1,0:T(8,128)S(1)} custom-call(s32[2]{0:T(128)S(1)} %pad_add_fusion.own_ref, f32[4096,1024]{1,0:T(8,128)} %data_ref.13, f32[1024,128]{1,0:T(8,128)S(1)} %collective-permute-done.3.refs_0_, f32[128,1024]{1,0:T(8,128)S(1)} %project.5.refs_1_), custom_call_target="tpu_custom_call" | custom-call | flops 1 | bytes 12582912 | tf_op jit(solution)/shard_map/project/pallas_call | solution.py:171
  58.7 4.1 %project.7 = (f32[32,1024]{1,0:T(8,128)S(1)}, f32[32,1024]{1,0:T(8,128)S(1)}, f32[32,1024]{1,0:T(8,128)S(1)}, f32[32,1024]{1,0:T(8,128)S(1)}) custom-call(s32[2]{0:T(128)S(1)} %pad_add_fusion.own_ref, f32[4096,1024]{1,0:T(8,128)} %data_ref.13, f32[1024,128]{1,0:T(8,128)S(1)} %collective-permute-done.10.refs_0_, f32[128,1024]{1,0:T(8,128)S(1)} %project.6.refs_1_), custom_call_target="tpu_custom_call" | custom-call | flops 1 | bytes 12582912 | tf_op jit(solution)/shard_map/project/pallas_call | solution.py:171
  63.4 2.2 %factor.4.in_ref = f32[128,256]{1,0:T(8,128)S(1)} custom-call(f32[128,128]{1,0:T(8,128)S(1)} %add.60.in_ref), custom_call_target="tpu_custom_call" | custom-call | flops 1 | bytes 8388608 | tf_op jit(solution)/shard_map/factor/pallas_call | solution.py:237
  65.6 2.7 %collective-permute-done.11 = f32[32,1024]{1,0:T(8,128)S(1)} collective-permute-done((f32[32,1024]{1,0:T(8,128)S(1)}, f32[32,1024]{1,0:T(8,128)S(1)}, u32[]{:S(2)}, u32[]{:S(2)}) %collective-permute-start.11) | collective-permute-done | bytes 131104 | tf_op jit(solution)/shard_map/ppermute | solution.py:31
  68.6 2.1 %collective-permute-start.14 = (f32[16,1024]{1,0:T(8,128)S(1)}, f32[16,1024]{1,0:T(8,128)S(1)}, u32[]{:S(2)}, u32[]{:S(2)}) collective-permute-start(f32[16,1024]{1,0:T(8,128)S(1)} %slice.27), channel_id=1, source_target_pairs={{0,16},{4,20},{8,24},{12,28},{16,0},{20,4},{24,8},{28,12},{1,17},{... | collective-permute-start | bytes 196616 | tf_op jit(solution)/shard_map/ppermute | solution.py:31
  70.7 2.3 %factor.5.in_ref = f32[128,256]{1,0:T(8,128)S(1)} custom-call(f32[128,256]{1,0:T(8,128)S(1)} %factor.4.in_ref), custom_call_target="tpu_custom_call" | custom-call | flops 1 | bytes 8388608 | tf_op jit(solution)/shard_map/factor/pallas_call | solution.py:237
  74.2 3.1 %collective-permute-done.13 = f32[16,1024]{1,0:T(8,128)S(1)} collective-permute-done((f32[16,1024]{1,0:T(8,128)S(1)}, f32[16,1024]{1,0:T(8,128)S(1)}, u32[]{:S(2)}, u32[]{:S(2)}) %collective-permute-start.13) | collective-permute-done | bytes 65568 | tf_op jit(solution)/shard_map/ppermute | solution.py:31
  77.4 1.6 %collective-permute-start.16 = (f32[8,1024]{1,0:T(8,128)S(1)}, f32[8,1024]{1,0:T(8,128)S(1)}, u32[]{:S(2)}, u32[]{:S(2)}) collective-permute-start(f32[8,1024]{1,0:T(8,128)S(1)} %slice.31), channel_id=1, source_target_pairs={{0,4},{4,0},{8,12},{12,8},{16,20},{20,16},{24,28},{28,24},{1,5},{5... | collective-permute-start | bytes 98312 | tf_op jit(solution)/shard_map/ppermute | solution.py:31
  78.9 2.3 %factor.6.in_ref = f32[128,256]{1,0:T(8,128)S(1)} custom-call(f32[128,256]{1,0:T(8,128)S(1)} %factor.5.in_ref), custom_call_target="tpu_custom_call" | custom-call | flops 1 | bytes 8388608 | tf_op jit(solution)/shard_map/factor/pallas_call | solution.py:237
  82.2 4.7 %collective-permute-done.15 = f32[8,1024]{1,0:T(8,128)S(1)} collective-permute-done((f32[8,1024]{1,0:T(8,128)S(1)}, f32[8,1024]{1,0:T(8,128)S(1)}, u32[]{:S(2)}, u32[]{:S(2)}) %collective-permute-start.15) | collective-permute-done | bytes 32800 | tf_op jit(solution)/shard_map/ppermute | solution.py:31
  87.3 1.9 %factor.7.inverse_ref = f32[128,128]{1,0:T(8,128)S(1)} custom-call(f32[128,256]{1,0:T(8,128)S(1)} %factor.6.in_ref), custom_call_target="tpu_custom_call" | custom-call | flops 1 | bytes 8388608 | tf_op jit(solution)/shard_map/factor/pallas_call | solution.py:237
  89.7 2.2 %collective-permute-done.17 = f32[8,1024]{1,0:T(8,128)S(1)} collective-permute-done((f32[8,1024]{1,0:T(8,128)S(1)}, f32[8,1024]{1,0:T(8,128)S(1)}, u32[]{:S(2)}, u32[]{:S(2)}) %collective-permute-start.17) | collective-permute-done | bytes 32800 | tf_op jit(solution)/shard_map/ppermute | solution.py:31
  93.2 1.4 %fusion.1 = f32[1024,128]{1,0:T(8,128)} fusion(f32[1024,128]{1,0:T(8,128)S(1)} %add_add_fusion.refs_0_, f32[128,128]{1,0:T(8,128)S(1)} %factor.7.inverse_ref), kind=kOutput, calls=%fused_computation.12 | convolution fusion | flops 201326592 | bytes 1114112 | tf_op jit(solution)/shard_map/dot_general | solution.py:35
  94.6 2.9 %collective-permute-start.20 = (f32[16,1024]{1,0:T(8,128)S(1)}, f32[16,1024]{1,0:T(8,128)S(1)}, u32[]{:S(2)}, u32[]{:S(2)}) collective-permute-start(f32[16,1024]{1,0:T(8,128)S(1)} %pad_maximum_fusion.3), channel_id=1, source_target_pairs={{0,16},{4,20},{8,24},{12,28},{16,0},{20,4},{24,8},{28,12},{1,17},{... | collective-permute-start | bytes 196616 | tf_op jit(solution)/shard_map/ppermute | solution.py:31
  97.5 2.2 %collective-permute-done.20 = f32[16,1024]{1,0:T(8,128)S(1)} collective-permute-done((f32[16,1024]{1,0:T(8,128)S(1)}, f32[16,1024]{1,0:T(8,128)S(1)}, u32[]{:S(2)}, u32[]{:S(2)}) %collective-permute-start.20) | collective-permute-done | bytes 65568 | tf_op jit(solution)/shard_map/ppermute | solution.py:31
  100.4 2.2 %collective-permute-start.22 = (f32[32,1024]{1,0:T(8,128)S(1)}, f32[32,1024]{1,0:T(8,128)S(1)}, u32[]{:S(2)}, u32[]{:S(2)}) collective-permute-start(f32[32,1024]{1,0:T(8,128)S(1)} %pad_maximum_fusion.1.refs_2_), channel_id=1, source_target_pairs={{0,8},{4,12},{8,0},{12,4},{16,24},{20,28},{24,16},{28,20},{1,9},{5... | collective-permute-start | bytes 393224 | tf_op jit(solution)/shard_map/ppermute | solution.py:31
  102.6 2.2 %collective-permute-done.21.refs_1_ = f32[32,1024]{1,0:T(8,128)S(1)} collective-permute-done((f32[32,1024]{1,0:T(8,128)S(1)}, f32[32,1024]{1,0:T(8,128)S(1)}, u32[]{:S(2)}, u32[]{:S(2)}) %collective-permute-start.21) | collective-permute-done | bytes 131104 | tf_op jit(solution)/shard_map/ppermute | solution.py:31
  105.6 2.3 %finish.1 = (f32[128,1024]{1,0:T(8,128)}, f32[128,128]{1,0:T(8,128)S(1)}) custom-call(s32[2]{0:T(128)S(1)} %pad_add_fusion.own_ref, f32[128,128]{1,0:T(8,128)S(1)} %factor.7.inverse_ref, f32[32,1024]{1,0:T(8,128)S(1)} %pad_maximum_fusion.refs_0_, f32[32,1024]{1,0:T(8,128)S(1)} %collective-permute-done.21.refs_1_, f32[32,1024]{1,0:T(8,128)S(1)} %pad_maximum_fusion.1.refs_2_, ...), custom_call_target="tpu_custom_call" | custom-call | flops 1 | bytes 8388608 | tf_op jit(solution)/shard_map/finish/pallas_call | solution.py:268
  109.1 1.6 %collective-permute-start.24 = (f32[128,128]{1,0:T(8,128)S(1)}, f32[128,128]{1,0:T(8,128)S(1)}, u32[]{:S(2)}, u32[]{:S(2)}) collective-permute-start(f32[128,128]{1,0:T(8,128)S(1)} %add.67), channel_id=1, source_target_pairs={{0,2},{1,3},{2,0},{3,1},{4,6},{5,7},{6,4},{7,5},{8,10},{9,11},{10,... | collective-permute-start | bytes 196616 | tf_op jit(solution)/shard_map/ppermute | solution.py:31
  110.7 2.7 %collective-permute-done.24 = f32[128,128]{1,0:T(8,128)S(1)} collective-permute-done((f32[128,128]{1,0:T(8,128)S(1)}, f32[128,128]{1,0:T(8,128)S(1)}, u32[]{:S(2)}, u32[]{:S(2)}) %collective-permute-start.24) | collective-permute-done | bytes 65568 | tf_op jit(solution)/shard_map/ppermute | solution.py:31
  (58 shorter events, 13.7 us)
Async XLA Ops:
  0.7 1.0 copy-start
  5.8 4.5 %collective-permute-start = (f32[1024,128]{1,0:T(8,128)S(1)}, f32[1024,128]{1,0:T(8,128)S(1)}, u32[]{:S(2)}, u32[]{:S(2)}) collective-permute-start(f32[1024,128]{1,0:T(8,128)S(1)} %get-tuple-element.49), channel_id=1, source_target_pairs={{0,1},{1,0},{2,3},{3,2},{4,5},{5,4},{6,7},{7,6},{8,9},{9,8},{10,11... | collective-permute-start | bytes 1572872 | tf_op jit(solution)/shard_map/ppermute | solution.py:31
  16.7 3.1 %collective-permute-start.1 = (f32[1024,128]{1,0:T(8,128)S(1)}, f32[1024,128]{1,0:T(8,128)S(1)}, u32[]{:S(2)}, u32[]{:S(2)}) collective-permute-start(f32[1024,128]{1,0:T(8,128)S(1)} %get-tuple-element.52), channel_id=1, source_target_pairs={{0,1},{1,0},{2,3},{3,2},{4,5},{5,4},{6,7},{7,6},{8,9},{9,8},{10,11... | collective-permute-start | bytes 1572872 | tf_op jit(solution)/shard_map/ppermute | solution.py:31
  16.9 15.1 %collective-permute-start.2 = (f32[1024,128]{1,0:T(8,128)S(1)}, f32[1024,128]{1,0:T(8,128)S(1)}, u32[]{:S(2)}, u32[]{:S(2)}) collective-permute-start(f32[1024,128]{1,0:T(8,128)S(1)} %add.53), channel_id=1, source_target_pairs={{0,2},{1,3},{2,0},{3,1},{4,6},{5,7},{6,4},{7,5},{8,10},{9,11},{10,... | collective-permute-start | bytes 1572872 | tf_op jit(solution)/shard_map/ppermute | solution.py:31
  32.1 8.6 %collective-permute-start.5 = (f32[1024,128]{1,0:T(8,128)S(1)}, f32[1024,128]{1,0:T(8,128)S(1)}, u32[]{:S(2)}, u32[]{:S(2)}) collective-permute-start(f32[1024,128]{1,0:T(8,128)S(1)} %add_add_fusion.refs_0_), channel_id=1, source_target_pairs={{0,1},{1,0},{2,3},{3,2},{4,5},{5,4},{6,7},{7,6},{8,9},{9,8},{10,11... | collective-permute-start | bytes 1572872 | tf_op jit(solution)/shard_map/ppermute | solution.py:31
  32.2 21.6 %collective-permute-start.3 = (f32[1024,128]{1,0:T(8,128)S(1)}, f32[1024,128]{1,0:T(8,128)S(1)}, u32[]{:S(2)}, u32[]{:S(2)}) collective-permute-start(f32[1024,128]{1,0:T(8,128)S(1)} %add_add_fusion.refs_0_), channel_id=1, source_target_pairs={{0,2},{1,3},{2,0},{3,1},{4,6},{5,7},{6,4},{7,5},{8,10},{9,11},{10,... | collective-permute-start | bytes 1572872 | tf_op jit(solution)/shard_map/ppermute | solution.py:31
  35.0 5.6 %collective-permute-start.4 = (f32[128,128]{1,0:T(8,128)S(1)}, f32[128,128]{1,0:T(8,128)S(1)}, u32[]{:S(2)}, u32[]{:S(2)}) collective-permute-start(f32[128,128]{1,0:T(8,128)S(1)} %fusion), channel_id=1, source_target_pairs={{0,4},{4,0},{8,12},{12,8},{16,20},{20,16},{24,28},{28,24},{1,5},{5... | collective-permute-start | bytes 196616 | tf_op jit(solution)/shard_map/ppermute | solution.py:31
  40.6 5.9 %collective-permute-start.6 = (f32[128,128]{1,0:T(8,128)S(1)}, f32[128,128]{1,0:T(8,128)S(1)}, u32[]{:S(2)}, u32[]{:S(2)}) collective-permute-start(f32[128,128]{1,0:T(8,128)S(1)} %add.56), channel_id=1, source_target_pairs={{0,8},{4,12},{8,0},{12,4},{16,24},{20,28},{24,16},{28,20},{1,9},{5... | collective-permute-start | bytes 196616 | tf_op jit(solution)/shard_map/ppermute | solution.py:31
  46.6 5.9 %collective-permute-start.7 = (f32[128,128]{1,0:T(8,128)S(1)}, f32[128,128]{1,0:T(8,128)S(1)}, u32[]{:S(2)}, u32[]{:S(2)}) collective-permute-start(f32[128,128]{1,0:T(8,128)S(1)} %add.57), channel_id=1, source_target_pairs={{0,16},{4,20},{8,24},{12,28},{16,0},{20,4},{24,8},{28,12},{1,17},{... | collective-permute-start | bytes 196616 | tf_op jit(solution)/shard_map/ppermute | solution.py:31
  52.5 1.3 %collective-permute-start.8 = (f32[128,128]{1,0:T(8,128)S(1)}, f32[128,128]{1,0:T(8,128)S(1)}, u32[]{:S(2)}, u32[]{:S(2)}) collective-permute-start(f32[128,128]{1,0:T(8,128)S(1)} %add.58), channel_id=1, source_target_pairs={{0,1},{1,0},{2,3},{3,2},{4,5},{5,4},{6,7},{7,6},{8,9},{9,8},{10,11... | collective-permute-start | bytes 196616 | tf_op jit(solution)/shard_map/ppermute | solution.py:31
  53.8 4.9 %collective-permute-start.10 = (f32[1024,128]{1,0:T(8,128)S(1)}, f32[1024,128]{1,0:T(8,128)S(1)}, u32[]{:S(2)}, u32[]{:S(2)}) collective-permute-start(f32[1024,128]{1,0:T(8,128)S(1)} %collective-permute-done.3.refs_0_), channel_id=1, source_target_pairs={{0,1},{1,0},{2,3},{3,2},{4,5},{5,4},{6,7},{7,6},{8,9},{9,8},{10,11... | collective-permute-start | bytes 1572872 | tf_op jit(solution)/shard_map/ppermute | solution.py:31
  54.0 4.6 %collective-permute-start.9 = (f32[128,128]{1,0:T(8,128)S(1)}, f32[128,128]{1,0:T(8,128)S(1)}, u32[]{:S(2)}, u32[]{:S(2)}) collective-permute-start(f32[128,128]{1,0:T(8,128)S(1)} %add.59), channel_id=1, source_target_pairs={{0,2},{1,3},{2,0},{3,1},{4,6},{5,7},{6,4},{7,5},{8,10},{9,11},{10,... | collective-permute-start | bytes 196616 | tf_op jit(solution)/shard_map/ppermute | solution.py:31
  62.8 5.5 %collective-permute-start.11 = (f32[32,1024]{1,0:T(8,128)S(1)}, f32[32,1024]{1,0:T(8,128)S(1)}, u32[]{:S(2)}, u32[]{:S(2)}) collective-permute-start(f32[32,1024]{1,0:T(8,128)S(1)} %get-tuple-element.72), channel_id=1, source_target_pairs={{0,4},{4,0},{8,12},{12,8},{16,20},{20,16},{24,28},{28,24},{1,5},{5... | collective-permute-start | bytes 393224 | tf_op jit(solution)/shard_map/ppermute | solution.py:31
  63.4 5.2 %collective-permute-start.12 = (f32[32,1024]{1,0:T(8,128)S(1)}, f32[32,1024]{1,0:T(8,128)S(1)}, u32[]{:S(2)}, u32[]{:S(2)}) collective-permute-start(f32[32,1024]{1,0:T(8,128)S(1)} %get-tuple-element.74), channel_id=1, source_target_pairs={{0,8},{4,12},{8,0},{12,4},{16,24},{20,28},{24,16},{28,20},{1,9},{5... | collective-permute-start | bytes 393224 | tf_op jit(solution)/shard_map/ppermute | solution.py:31
  68.6 5.7 %collective-permute-start.14 = (f32[16,1024]{1,0:T(8,128)S(1)}, f32[16,1024]{1,0:T(8,128)S(1)}, u32[]{:S(2)}, u32[]{:S(2)}) collective-permute-start(f32[16,1024]{1,0:T(8,128)S(1)} %slice.27), channel_id=1, source_target_pairs={{0,16},{4,20},{8,24},{12,28},{16,0},{20,4},{24,8},{28,12},{1,17},{... | collective-permute-start | bytes 196616 | tf_op jit(solution)/shard_map/ppermute | solution.py:31
  73.0 4.3 %collective-permute-start.13 = (f32[16,1024]{1,0:T(8,128)S(1)}, f32[16,1024]{1,0:T(8,128)S(1)}, u32[]{:S(2)}, u32[]{:S(2)}) collective-permute-start(f32[16,1024]{1,0:T(8,128)S(1)} %slice.25), channel_id=1, source_target_pairs={{0,8},{4,12},{8,0},{12,4},{16,24},{20,28},{24,16},{28,20},{1,9},{5... | collective-permute-start | bytes 196616 | tf_op jit(solution)/shard_map/ppermute | solution.py:31
  77.4 4.9 %collective-permute-start.16 = (f32[8,1024]{1,0:T(8,128)S(1)}, f32[8,1024]{1,0:T(8,128)S(1)}, u32[]{:S(2)}, u32[]{:S(2)}) collective-permute-start(f32[8,1024]{1,0:T(8,128)S(1)} %slice.31), channel_id=1, source_target_pairs={{0,4},{4,0},{8,12},{12,8},{16,20},{20,16},{24,28},{28,24},{1,5},{5... | collective-permute-start | bytes 98312 | tf_op jit(solution)/shard_map/ppermute | solution.py:31
  81.2 5.7 %collective-permute-start.15 = (f32[8,1024]{1,0:T(8,128)S(1)}, f32[8,1024]{1,0:T(8,128)S(1)}, u32[]{:S(2)}, u32[]{:S(2)}) collective-permute-start(f32[8,1024]{1,0:T(8,128)S(1)} %slice.29), channel_id=1, source_target_pairs={{0,16},{4,20},{8,24},{12,28},{16,0},{20,4},{24,8},{28,12},{1,17},{... | collective-permute-start | bytes 98312 | tf_op jit(solution)/shard_map/ppermute | solution.py:31
  86.9 5.0 %collective-permute-start.17 = (f32[8,1024]{1,0:T(8,128)S(1)}, f32[8,1024]{1,0:T(8,128)S(1)}, u32[]{:S(2)}, u32[]{:S(2)}) collective-permute-start(f32[8,1024]{1,0:T(8,128)S(1)} %slice_add_fusion.3), channel_id=1, source_target_pairs={{0,16},{4,20},{8,24},{12,28},{16,0},{20,4},{24,8},{28,12},{1,17},{... | collective-permute-start | bytes 98312 | tf_op jit(solution)/shard_map/ppermute | solution.py:31
  89.2 4.0 %collective-permute-start.18 = (f32[8,1024]{1,0:T(8,128)S(1)}, f32[8,1024]{1,0:T(8,128)S(1)}, u32[]{:S(2)}, u32[]{:S(2)}) collective-permute-start(f32[8,1024]{1,0:T(8,128)S(1)} %slice_add_fusion.2), channel_id=1, source_target_pairs={{0,4},{4,0},{8,12},{12,8},{16,20},{20,16},{24,28},{28,24},{1,5},{5... | collective-permute-start | bytes 98312 | tf_op jit(solution)/shard_map/ppermute | solution.py:31
  93.2 4.3 %collective-permute-start.19 = (f32[16,1024]{1,0:T(8,128)S(1)}, f32[16,1024]{1,0:T(8,128)S(1)}, u32[]{:S(2)}, u32[]{:S(2)}) collective-permute-start(f32[16,1024]{1,0:T(8,128)S(1)} %pad_maximum_fusion.2), channel_id=1, source_target_pairs={{0,8},{4,12},{8,0},{12,4},{16,24},{20,28},{24,16},{28,20},{1,9},{5... | collective-permute-start | bytes 196616 | tf_op jit(solution)/shard_map/ppermute | solution.py:31
  94.6 5.2 %collective-permute-start.20 = (f32[16,1024]{1,0:T(8,128)S(1)}, f32[16,1024]{1,0:T(8,128)S(1)}, u32[]{:S(2)}, u32[]{:S(2)}) collective-permute-start(f32[16,1024]{1,0:T(8,128)S(1)} %pad_maximum_fusion.3), channel_id=1, source_target_pairs={{0,16},{4,20},{8,24},{12,28},{16,0},{20,4},{24,8},{28,12},{1,17},{... | collective-permute-start | bytes 196616 | tf_op jit(solution)/shard_map/ppermute | solution.py:31
  99.8 5.0 %collective-permute-start.21 = (f32[32,1024]{1,0:T(8,128)S(1)}, f32[32,1024]{1,0:T(8,128)S(1)}, u32[]{:S(2)}, u32[]{:S(2)}) collective-permute-start(f32[32,1024]{1,0:T(8,128)S(1)} %pad_maximum_fusion.refs_0_), channel_id=1, source_target_pairs={{0,4},{4,0},{8,12},{12,8},{16,20},{20,16},{24,28},{28,24},{1,5},{5... | collective-permute-start | bytes 393224 | tf_op jit(solution)/shard_map/ppermute | solution.py:31
  100.4 5.2 %collective-permute-start.22 = (f32[32,1024]{1,0:T(8,128)S(1)}, f32[32,1024]{1,0:T(8,128)S(1)}, u32[]{:S(2)}, u32[]{:S(2)}) collective-permute-start(f32[32,1024]{1,0:T(8,128)S(1)} %pad_maximum_fusion.1.refs_2_), channel_id=1, source_target_pairs={{0,8},{4,12},{8,0},{12,4},{16,24},{20,28},{24,16},{28,20},{1,9},{5... | collective-permute-start | bytes 393224 | tf_op jit(solution)/shard_map/ppermute | solution.py:31
  107.9 1.3 %collective-permute-start.23 = (f32[128,128]{1,0:T(8,128)S(1)}, f32[128,128]{1,0:T(8,128)S(1)}, u32[]{:S(2)}, u32[]{:S(2)}) collective-permute-start(f32[128,128]{1,0:T(8,128)S(1)} %get-tuple-element.92), channel_id=1, source_target_pairs={{0,1},{1,0},{2,3},{3,2},{4,5},{5,4},{6,7},{7,6},{8,9},{9,8},{10,11... | collective-permute-start | bytes 196616 | tf_op jit(solution)/shard_map/ppermute | solution.py:31
  109.1 4.3 %collective-permute-start.24 = (f32[128,128]{1,0:T(8,128)S(1)}, f32[128,128]{1,0:T(8,128)S(1)}, u32[]{:S(2)}, u32[]{:S(2)}) collective-permute-start(f32[128,128]{1,0:T(8,128)S(1)} %add.67), channel_id=1, source_target_pairs={{0,2},{1,3},{2,0},{3,1},{4,6},{5,7},{6,4},{7,5},{8,10},{9,11},{10,... | collective-permute-start | bytes 196616 | tf_op jit(solution)/shard_map/ppermute | solution.py:31

commit v6 on v5

--- a/solution.py
+++ b/solution.py
@@ -24,7 +24,7 @@
 
 
 def params():
-    return pltpu.CompilerParams(vmem_limit_bytes=52 * 1024 * 1024)
+    return pltpu.CompilerParams(vmem_limit_bytes=16 * 1024 * 1024)
 
 
 def swap(value, axis, bit):
@@ -42,15 +42,19 @@
     return upper, (value - upper.astype(f32)).astype(bf16)
 
 
+def rows_of(own_ref, piece, quarter):
+    place, first = piece
+    return pl.ds(pl.multiple_of((own_ref[0] ^ place) * quarter + first, PIECE), PIECE)
+
+
 def start_copies(own_ref, data_ref, held, sems, pieces, quarter):
     copies = []
-    for k, (place, first) in enumerate(pieces):
-        at = pl.multiple_of((own_ref[0] ^ place) * quarter + first, PIECE)
+    for k, piece in enumerate(pieces):
         row = []
         for t in range(data_ref.shape[1] // TILE):
             cols = pl.ds(t * TILE, TILE)
             copy = pltpu.make_async_copy(
-                data_ref.at[pl.ds(at, PIECE), cols], held.at[k, :, cols], sems.at[k, t]
+                data_ref.at[rows_of(own_ref, piece, quarter), cols], held.at[k, :, cols], sems.at[k, t]
             )
             copy.start()
             row.append(copy)
@@ -58,13 +62,16 @@
     return copies
 
 
-def sketch_kernel(pieces, quarter, first, own_ref, data_ref, omega_ref, *refs):
+def sketch_kernel(pieces, quarter, first, near, own_ref, data_ref, omega_ref, *refs):
     if first:
         refs, (omega_held, omega_sem) = refs[:-2], refs[-2:]
         omega_copy = pltpu.make_async_copy(omega_ref, omega_held, omega_sem)
         omega_copy.start()
-    outs, (held, sems) = refs[:-2], refs[-2:]
-    copies = start_copies(own_ref, data_ref, held, sems, pieces, quarter)
+    if near:
+        outs, copies = refs, None
+    else:
+        outs, (held, sems) = refs[:-2], refs[-2:]
+        copies = start_copies(own_ref, data_ref, held, sems, pieces, quarter)
     if first:
         width = omega_ref.shape[1]
         wide = outs[-1]
@@ -77,9 +84,13 @@
         width = omega_ref.shape[1] // 2
     for k in range(len(pieces)):
         both = more = None
-        for t, copy in enumerate(copies[k]):
-            copy.wait()
-            upper, rest = split(held[k, :, t * TILE : (t + 1) * TILE])
+        for t in range(data_ref.shape[1] // TILE):
+            if near:
+                value = data_ref[rows_of(own_ref, pieces[k], quarter), t * TILE : (t + 1) * TILE]
+            else:
+                copies[k][t].wait()
+                value = held[k, :, t * TILE : (t + 1) * TILE]
+            upper, rest = split(value)
             omega = wide[t * TILE : (t + 1) * TILE, :]
             one = jnp.dot(upper, omega, preferred_element_type=f32)
             two = jnp.dot(rest, omega[:, :width], preferred_element_type=f32)
@@ -90,7 +101,7 @@
         out[first_row : first_row + PIECE] = both[:, :width] + both[:, width:] + more
 
 
-def sketch(own, data, omega, places, first=False):
+def sketch(own, data, omega, places, first=False, near=False):
     pieces = [(place, row) for place in places for row in (0, PIECE)]
     cols = data.shape[1]
     width = omega.shape[1] if first else omega.shape[1] // 2
@@ -102,11 +113,13 @@
         pltpu.VMEM((len(pieces), PIECE, cols), f32),
         pltpu.SemaphoreType.DMA((len(pieces), cols // TILE)),
     ]
+    if near:
+        scratch = []
     if first:
         scratch += [pltpu.VMEM(omega.shape, f32), pltpu.SemaphoreType.DMA]
     return pl.pallas_call(
-        functools.partial(sketch_kernel, pieces, quarter, first),
-        in_specs=[SMEM, HBM, HBM if first else VMEM],
+        functools.partial(sketch_kernel, pieces, quarter, first, near),
+        in_specs=[SMEM, VMEM if near else HBM, HBM if first else VMEM],
         out_specs=[VMEM] * len(out),
         out_shape=out,
         scratch_shapes=scratch,
@@ -127,19 +140,15 @@
     count = len(pieces)
     parts, refs = refs[: count // 2], refs[count // 2 :]
     old, refs = (refs[0], refs[1:]) if before else (None, refs)
-    outs, (total, held, sems) = refs[:-3], refs[-3:]
-    if orders is None:
-        total = outs[0]
-    copies = start_copies(own_ref, data_ref, held, sems, pieces, quarter)
+    outs, total = (refs, refs[0]) if orders is None else (refs[:-1], refs[-1])
     for k in range(count):
         first = pieces[k][1]
         upper, rest = split(parts[k // 2][first : first + PIECE].T)
         stack = jnp.concatenate([upper, rest], 0)
         width = upper.shape[0]
-        for t, copy in enumerate(copies[k]):
-            copy.wait()
+        for t in range(data_ref.shape[1] // TILE):
             cols = slice(t * TILE, (t + 1) * TILE)
-            d_upper, d_rest = split(held[k, :, cols])
+            d_upper, d_rest = split(data_ref[rows_of(own_ref, pieces[k], quarter), cols])
             both = jnp.dot(stack, d_upper, preferred_element_type=f32)
             value = both[:width] + both[width:] + jnp.dot(upper, d_rest, preferred_element_type=f32)
             if k > 0:
@@ -170,14 +179,10 @@
         out = [jax.ShapeDtypeStruct((width // len(orders) // 2, cols), f32)] * (2 * len(orders))
     return pl.pallas_call(
         functools.partial(project_kernel, pieces, quarter, before is not None, orders),
-        in_specs=[SMEM, HBM] + [VMEM] * (len(args) - 2),
+        in_specs=[SMEM] + [VMEM] * (len(args) - 1),
         out_specs=[VMEM] * len(out),
         out_shape=out,
-        scratch_shapes=[
-            pltpu.VMEM((width, cols) if orders is not None else (8, 128), f32),
-            pltpu.VMEM((len(pieces), PIECE, cols), f32),
-            pltpu.SemaphoreType.DMA((len(pieces), cols // TILE)),
-        ],
+        scratch_shapes=[] if orders is None else [pltpu.VMEM((width, cols), f32)],
         compiler_params=params(),
         cost_estimate=cost(6 * len(pieces)),
         name="project",
@@ -241,7 +246,7 @@
         out_shape=jax.ShapeDtypeStruct((n, n if last else 2 * n), f32),
         scratch_shapes=[pltpu.VMEM((n, 2 * n), f32)] if last else [],
         compiler_params=params(),
-        cost_estimate=cost(32 / count),
+        cost_estimate=cost(0.01),
         name="factor",
     )(value)
 
@@ -288,59 +293,72 @@
     own = jnp.stack([lax.axis_index("col"), lax.axis_index("row") % 8]).astype(jnp.int32)
     bits = [1 << k for k in range(nrow.bit_length() - 1)]
 
+    near = pltpu.with_memory_space_constraint(data, pltpu.VMEM)
+    data = pltpu.with_memory_space_constraint(data, pltpu.HBM)
+
     part, wide = sketch(own, data, omega, [3], True)
     (pair,) = sketch(own, data, wide, [2])
     pair, wide = fence((pair + swap(part, "col", 1), wide))
     away = swap(pair, "col", 2)
-    part, here = sketch(own, data, wide, [1, 0])
-    part, away = fence((swap(part, "col", 1), away))
-    sketched = here + part + away
+    part, here = sketch(own, near, wide, [1, 0], near=True)
+    part_a, part_b, away = fence((swap(part[:PIECE], "col", 1), swap(part[PIECE:], "col", 1), away))
+    sketched = here + jnp.concatenate([part_a, part_b], 0) + away
 
     third = swap(sketched, "col", 2)
     second = swap(sketched, "col", 1)
     gram = dot(sketched, sketched, 0, 0)
-    gram = gram + swap(gram, "row", bits[0])
-    (acc,) = project(own, data, [0], [sketched])
-    gram, acc, second = fence((gram, acc, second))
-    gram = gram + swap(gram, "row", bits[1])
-    (acc,) = project(own, data, [1], [second], acc)
-    gram, acc = fence((gram, acc))
+    far = swap(gram, "row", bits[0])
+    (acc,) = project(own, near, [0], [sketched])
+    far, acc, second = fence((far, acc, second))
+    gram = gram + far
+    far = swap(gram, "row", bits[1])
+    (acc,) = project(own, near, [1], [second], acc)
+    far, acc = fence((far, acc))
+    gram = gram + far
     for bit in bits[2:]:
         gram = gram + swap(gram, "row", bit)
     gram = gram + swap(gram, "col", 1)
     third, gram, acc = fence((third, gram, acc))
     fourth = swap(third, "col", 1)
-    gram = gram + swap(gram, "col", 2)
-    (acc,) = project(own, data, [2], [third], acc)
-    gram, acc, fourth = fence((gram, acc, fourth))
+    far = swap(gram, "col", 2)
+    (acc,) = project(own, near, [2], [third], acc)
+    far, acc, fourth = fence((far, acc, fourth))
+    gram = gram + far
     cuts = [(1, 2, 4), (2, 4, 1)]
     orders = [order(cut) for cut in cuts]
-    sums = project(own, data, [3], [fourth], acc, orders)
+    sums = project(own, near, [3], [fourth], acc, orders)
 
     *sums, state = fence((*sums, gram))
     sends, keeps = sums[0::2], sums[1::2]
+
+    def exchange(values, step, beside):
+        got = [swap(v, "row", cut[step]) for v, cut in zip(values, cuts)]
+        *got, beside = fence((*got, beside))
+        return got, beside
+
     for k in range(3):
-        if k > 0:
+        got, state = exchange(sends, k, factor(k, 4, state))
+        keeps = [v + w for v, w in zip(keeps, got)]
+        if k < 2:
             half = keeps[0].shape[0] // 2
-            sends, keeps = [v[half:] for v in keeps], [v[:half] for v in keeps]
-        keeps = [v + swap(w, "row", cut[k]) for v, w, cut in zip(keeps, sends, cuts)]
-        state = factor(k, 4, state)
-        *keeps, state = fence((*keeps, state))
+            *cut_up, state = fence((*[v[half:] for v in keeps], *[v[:half] for v in keeps], state))
+            sends, keeps = cut_up[:2], cut_up[2:]
     for bit in bits[3:]:
         keeps = [v + swap(v, "row", bit) for v in keeps]
-    keeps = [jnp.concatenate([v, swap(v, "row", cut[2])], 0) for v, cut in zip(keeps, cuts)]
-    inverse = factor(3, 4, state)
+    *keeps, state = fence((*keeps, state))
+    got, inverse = exchange(keeps, 2, factor(3, 4, state))
+    keeps = [jnp.concatenate([v, w], 0) for v, w in zip(keeps, got)]
     *keeps, inverse = fence((*keeps, inverse))
-    keeps = [jnp.concatenate([v, swap(v, "row", cut[1])], 0) for v, cut in zip(keeps, cuts)]
-    basis = dot(sketched, inverse, 1, 1)
+    got, basis = exchange(keeps, 1, dot(sketched, inverse, 1, 1))
+    keeps = [jnp.concatenate([v, w], 0) for v, w in zip(keeps, got)]
     *keeps, basis = fence((*keeps, basis))
     parts = []
     for v, cut in zip(keeps, cuts):
         parts += [v, swap(v, "row", cut[0])]
 
     projected, small = finish(own, inverse, parts, orders)
-    small = small + swap(small, "col", 1)
-    small = small + swap(small, "col", 2)
+    across = [swap(small, "col", bit) for bit in (2, 3, 1)]
+    small = (small + across[2]) + (across[0] + across[1])
     return (basis, projected, small / total_rows)
 
 

time: 114 us -> 97.7 us (0.86)
  Pallas kernels: 41.9 us -> 29.3 us
  waiting for transfers between devices: 40.4 us -> 32.4 us
  starting transfers between devices: 26.5 us -> 30.3 us
    pallas_call x4, Pallas kernels: 16.5 us -> 6.85 us  [project(): pl.pallas_call(functools.partial(project_kernel, pieces, quarter, before...]
    ppermute x25 -> x27, waiting for transfers between devices: 40.4 us -> 32.4 us  [swap(): lax.ppermute(value, axis, [(i, i ^ bit) for i in range(lax.axis_size(axis...]
    ppermute x25 -> x27, starting transfers between devices: 26.5 us -> 30.3 us  [swap(): lax.ppermute(value, axis, [(i, i ^ bit) for i in range(lax.axis_size(axis...]
    pallas_call x3, Pallas kernels: 14.4 us -> 11.5 us  [sketch(): pl.pallas_call(functools.partial(sketch_kernel, pieces, quarter, first, n...]
  transfers between devices with their start and end apart: 25 -> 27, of which waited for: 15 -> 18; matrix products, arithmetic and copies ran while one was open for 2% -> 3% of each run, Pallas kernels for 22% -> 21%
where the time goes in v6:
time: 97.7 us; the launch traced here: 97.5 us
  waiting for transfers between devices  32.4 us (33%)
  starting transfers between devices  30.3 us (31%)
  Pallas kernels  29.3 us (30%)
  matrix products  2.38 us (2%)
  local copies, waits for them, and re-layouts  1.13 us (1%)
  other arithmetic  1.03 us (1%)
    ppermute x27, waiting for transfers between devices, swap(): lax.ppermute(value, axis, [(i, i ^ bit) for i in range(lax.axis_size(axis...  32.4 us
    ppermute x27, starting transfers between devices, swap(): lax.ppermute(value, axis, [(i, i ^ bit) for i in range(lax.axis_size(axis...  30.3 us
    pallas_call x3, Pallas kernels, sketch(): pl.pallas_call(functools.partial(sketch_kernel, pieces, quarter, first, n...  11.5 us
    pallas_call x4, Pallas kernels, factor(): pl.pallas_call(functools.partial(factor_kernel, index, count), in_specs=[...  8.69 us
    pallas_call x4, Pallas kernels, project(): pl.pallas_call(functools.partial(project_kernel, pieces, quarter, before...  6.85 us
    dot_general x2, matrix products, dot(): lax.dot_general(a, b, (((a_dim,), (b_dim,)), ((), ())), precision=precisi...  2.38 us
    pallas_call x1, Pallas kernels, finish(): pl.pallas_call(functools.partial(finish_kernel, orders), in_specs=[SMEM]...  2.3 us
  transfers between devices with their start and end apart: 27, of which 18 were waited for; matrix products, arithmetic and copies ran while one was open for 3% of the time, Pallas kernels for 21%

profile of v6, /device:TPU:0, one launch (start us, length us, event | category | flops | bytes accessed | tf_op | source)
XLA Modules:
  0.0 97.5 jit_solution(10771168373862333684)
XLA Ops:
  1.8 4.3 %partial_sketch.3 = (f32[1024,128]{1,0:T(8,128)S(1)}, bf16[1024,256]{1,0:T(8,128)(2,1)S(1)}) custom-call(s32[2]{0:T(128)S(1)} %pad_add_fusion.own_ref, f32[4096,1024]{1,0:T(8,128)} %data_ref.13, f32[1024,128]{1,0:T(8,128)S(1)} %copy-done), custom_call_target="tpu_custom_call" | custom-call | flops 1 | bytes 20971 | tf_op jit(solution)/shard_map/partial_sketch/pallas_call | solution.py:120
  6.6 4.3 %partial_sketch.4 = f32[1024,128]{1,0:T(8,128)S(1)} custom-call(s32[2]{0:T(128)S(1)} %pad_add_fusion.own_ref, f32[4096,1024]{1,0:T(8,128)} %data_ref.13, bf16[1024,256]{1,0:T(8,128)(2,1)S(1)} %get-tuple-element.70.omega_ref), custom_call_target="tpu_custom_call" | custom-call | flops 1 | bytes 20971 | tf_op jit(solution)/shard_map/partial_sketch/pallas_call | solution.py:120
  11.0 2.6 %collective-permute-start.3 = (f32[1024,128]{1,0:T(8,128)S(1)}, f32[1024,128]{1,0:T(8,128)S(1)}, u32[]{:S(2)}, u32[]{:S(2)}) collective-permute-start(f32[1024,128]{1,0:T(8,128)S(1)} %add.56), channel_id=1, source_target_pairs={{0,2},{1,3},{2,0},{3,1},{4,6},{5,7},{6,4},{7,5},{8,10},{9,11},{10,... | collective-permute-start | bytes 1572872 | tf_op jit(solution)/shard_map/ppermute | solution.py:31
  13.5 2.9 %partial_sketch.5 = (f32[1024,128]{1,0:T(8,128)S(1)}, f32[1024,128]{1,0:T(8,128)S(1)}) custom-call(s32[2]{0:T(128)S(1)} %pad_add_fusion.own_ref, f32[4096,1024]{1,0:T(8,128)S(1)} %bitcast.7, bf16[1024,256]{1,0:T(8,128)(2,1)S(1)} %get-tuple-element.70.omega_ref), custom_call_target="tpu_custom_call" | custom-call | flops 1 | bytes 41943 | tf_op jit(solution)/shard_map/partial_sketch/pallas_call | solution.py:120
  18.5 7.6 %collective-permute-done.3 = f32[1024,128]{1,0:T(8,128)S(1)} collective-permute-done((f32[1024,128]{1,0:T(8,128)S(1)}, f32[1024,128]{1,0:T(8,128)S(1)}, u32[]{:S(2)}, u32[]{:S(2)}) %collective-permute-start.3) | collective-permute-done | bytes 524320 | tf_op jit(solution)/shard_map/ppermute | solution.py:31
  26.3 1.8 %collective-permute-start.4 = (f32[1024,128]{1,0:T(8,128)S(1)}, f32[1024,128]{1,0:T(8,128)S(1)}, u32[]{:S(2)}, u32[]{:S(2)}) collective-permute-start(f32[1024,128]{1,0:T(8,128)S(1)} %fusion.refs_0_), channel_id=1, source_target_pairs={{0,2},{1,3},{2,0},{3,1},{4,6},{5,7},{6,4},{7,5},{8,10},{9,11},{10,... | collective-permute-start | bytes 1572872 | tf_op jit(solution)/shard_map/ppermute | solution.py:31
  29.1 1.6 %collective-permute-start.5 = (f32[128,128]{1,0:T(8,128)S(1)}, f32[128,128]{1,0:T(8,128)S(1)}, u32[]{:S(2)}, u32[]{:S(2)}) collective-permute-start(f32[128,128]{1,0:T(8,128)S(1)} %fusion.6), channel_id=1, source_target_pairs={{0,4},{4,0},{8,12},{12,8},{16,20},{20,16},{24,28},{28,24},{1,5},{5... | collective-permute-start | bytes 196616 | tf_op jit(solution)/shard_map/ppermute | solution.py:31
  30.7 1.7 %project.4.refs_1_ = f32[128,1024]{1,0:T(8,128)S(1)} custom-call(s32[2]{0:T(128)S(1)} %pad_add_fusion.own_ref, f32[4096,1024]{1,0:T(8,128)S(1)} %bitcast.7, f32[1024,128]{1,0:T(8,128)S(1)} %fusion.refs_0_), custom_call_target="tpu_custom_call" | custom-call | flops 1 | bytes 12582912 | tf_op jit(solution)/shard_map/project/pallas_call | solution.py:180
  33.5 1.6 %collective-permute-start.7 = (f32[128,128]{1,0:T(8,128)S(1)}, f32[128,128]{1,0:T(8,128)S(1)}, u32[]{:S(2)}, u32[]{:S(2)}) collective-permute-start(f32[128,128]{1,0:T(8,128)S(1)} %add.59), channel_id=1, source_target_pairs={{0,8},{4,12},{8,0},{12,4},{16,24},{20,28},{24,16},{28,20},{1,9},{5... | collective-permute-start | bytes 196616 | tf_op jit(solution)/shard_map/ppermute | solution.py:31
  35.1 1.7 %project.5.refs_1_ = f32[128,1024]{1,0:T(8,128)S(1)} custom-call(s32[2]{0:T(128)S(1)} %pad_add_fusion.own_ref, f32[4096,1024]{1,0:T(8,128)S(1)} %bitcast.7, f32[1024,128]{1,0:T(8,128)S(1)} %collective-permute-done.6.refs_0_, f32[128,1024]{1,0:T(8,128)S(1)} %project.4.refs_1_), custom_call_target="tpu_custom_call" | custom-call | flops 1 | bytes 12582912 | tf_op jit(solution)/shard_map/project/pallas_call | solution.py:180
  37.8 2.6 %collective-permute-start.8 = (f32[128,128]{1,0:T(8,128)S(1)}, f32[128,128]{1,0:T(8,128)S(1)}, u32[]{:S(2)}, u32[]{:S(2)}) collective-permute-start(f32[128,128]{1,0:T(8,128)S(1)} %add.60), channel_id=1, source_target_pairs={{0,16},{4,20},{8,24},{12,28},{16,0},{20,4},{24,8},{28,12},{1,17},{... | collective-permute-start | bytes 196616 | tf_op jit(solution)/shard_map/ppermute | solution.py:31
  40.5 2.6 %collective-permute-done.8 = f32[128,128]{1,0:T(8,128)S(1)} collective-permute-done((f32[128,128]{1,0:T(8,128)S(1)}, f32[128,128]{1,0:T(8,128)S(1)}, u32[]{:S(2)}, u32[]{:S(2)}) %collective-permute-start.8) | collective-permute-done | bytes 65568 | tf_op jit(solution)/shard_map/ppermute | solution.py:31
  44.9 1.7 %project.6.refs_1_ = f32[128,1024]{1,0:T(8,128)S(1)} custom-call(s32[2]{0:T(128)S(1)} %pad_add_fusion.own_ref, f32[4096,1024]{1,0:T(8,128)S(1)} %bitcast.7, f32[1024,128]{1,0:T(8,128)S(1)} %collective-permute-done.4.refs_0_, f32[128,1024]{1,0:T(8,128)S(1)} %project.5.refs_1_), custom_call_target="tpu_custom_call" | custom-call | flops 1 | bytes 12582912 | tf_op jit(solution)/shard_map/project/pallas_call | solution.py:180
  46.6 2.4 %collective-permute-done.10 = f32[128,128]{1,0:T(8,128)S(1)} collective-permute-done((f32[128,128]{1,0:T(8,128)S(1)}, f32[128,128]{1,0:T(8,128)S(1)}, u32[]{:S(2)}, u32[]{:S(2)}) %collective-permute-start.10) | collective-permute-done | bytes 65568 | tf_op jit(solution)/shard_map/ppermute | solution.py:31
  49.0 1.7 %project.7 = (f32[32,1024]{1,0:T(8,128)S(1)}, f32[32,1024]{1,0:T(8,128)S(1)}, f32[32,1024]{1,0:T(8,128)S(1)}, f32[32,1024]{1,0:T(8,128)S(1)}) custom-call(s32[2]{0:T(128)S(1)} %pad_add_fusion.own_ref, f32[4096,1024]{1,0:T(8,128)S(1)} %bitcast.7, f32[1024,128]{1,0:T(8,128)S(1)} %collective-permute-done.11.refs_0_, f32[128,1024]{1,0:T(8,128)S(1)} %project.6.refs_1_), custom_call_target="tpu_custom_call" | custom-call | flops 1 | bytes 12582912 | tf_op jit(solution)/shard_map/project/pallas_call | solution.py:180
  50.8 1.7 %collective-permute-start.12 = (f32[32,1024]{1,0:T(8,128)S(1)}, f32[32,1024]{1,0:T(8,128)S(1)}, u32[]{:S(2)}, u32[]{:S(2)}) collective-permute-start(f32[32,1024]{1,0:T(8,128)S(1)} %get-tuple-element.93), channel_id=1, source_target_pairs={{0,4},{4,0},{8,12},{12,8},{16,20},{20,16},{24,28},{28,24},{1,5},{5... | collective-permute-start | bytes 393224 | tf_op jit(solution)/shard_map/ppermute | solution.py:31
  52.5 1.6 %collective-permute-start.13 = (f32[32,1024]{1,0:T(8,128)S(1)}, f32[32,1024]{1,0:T(8,128)S(1)}, u32[]{:S(2)}, u32[]{:S(2)}) collective-permute-start(f32[32,1024]{1,0:T(8,128)S(1)} %get-tuple-element.94), channel_id=1, source_target_pairs={{0,8},{4,12},{8,0},{12,4},{16,24},{20,28},{24,16},{28,20},{1,9},{5... | collective-permute-start | bytes 393224 | tf_op jit(solution)/shard_map/ppermute | solution.py:31
  54.1 2.2 %factor.4.in_ref = f32[128,256]{1,0:T(8,128)S(1)} custom-call(f32[128,128]{1,0:T(8,128)S(1)} %add.63.in_ref), custom_call_target="tpu_custom_call" | custom-call | flops 1 | bytes 10485 | tf_op jit(solution)/shard_map/factor/pallas_call | solution.py:242
  57.5 1.6 %collective-permute-start.14 = (f32[16,1024]{1,0:T(8,128)S(1)}, f32[16,1024]{1,0:T(8,128)S(1)}, u32[]{:S(2)}, u32[]{:S(2)}) collective-permute-start(f32[16,1024]{1,0:T(8,128)S(1)} %get-tuple-element.101), channel_id=1, source_target_pairs={{0,8},{4,12},{8,0},{12,4},{16,24},{20,28},{24,16},{28,20},{1,9},{5... | collective-permute-start | bytes 196616 | tf_op jit(solution)/shard_map/ppermute | solution.py:31
  59.2 3.2 %collective-permute-start.15 = (f32[16,1024]{1,0:T(8,128)S(1)}, f32[16,1024]{1,0:T(8,128)S(1)}, u32[]{:S(2)}, u32[]{:S(2)}) collective-permute-start(f32[16,1024]{1,0:T(8,128)S(1)} %get-tuple-element.102), channel_id=1, source_target_pairs={{0,16},{4,20},{8,24},{12,28},{16,0},{20,4},{24,8},{28,12},{1,17},{... | collective-permute-start | bytes 196616 | tf_op jit(solution)/shard_map/ppermute | solution.py:31
  62.3 2.3 %factor.5.in_ref = f32[128,256]{1,0:T(8,128)S(1)} custom-call(f32[128,256]{1,0:T(8,128)S(1)} %factor.4.in_ref), custom_call_target="tpu_custom_call" | custom-call | flops 1 | bytes 10485 | tf_op jit(solution)/shard_map/factor/pallas_call | solution.py:242
  65.4 2.3 %collective-permute-start.16 = (f32[8,1024]{1,0:T(8,128)S(1)}, f32[8,1024]{1,0:T(8,128)S(1)}, u32[]{:S(2)}, u32[]{:S(2)}) collective-permute-start(f32[8,1024]{1,0:T(8,128)S(1)} %get-tuple-element.109), channel_id=1, source_target_pairs={{0,16},{4,20},{8,24},{12,28},{16,0},{20,4},{24,8},{28,12},{1,17},{... | collective-permute-start | bytes 98312 | tf_op jit(solution)/shard_map/ppermute | solution.py:31
  68.2 2.3 %factor.6.in_ref = f32[128,256]{1,0:T(8,128)S(1)} custom-call(f32[128,256]{1,0:T(8,128)S(1)} %factor.5.in_ref), custom_call_target="tpu_custom_call" | custom-call | flops 1 | bytes 10485 | tf_op jit(solution)/shard_map/factor/pallas_call | solution.py:242
  73.2 1.9 %factor.7.inverse_ref = f32[128,128]{1,0:T(8,128)S(1)} custom-call(f32[128,256]{1,0:T(8,128)S(1)} %factor.6.in_ref), custom_call_target="tpu_custom_call" | custom-call | flops 1 | bytes 10485 | tf_op jit(solution)/shard_map/factor/pallas_call | solution.py:242
  75.0 2.4 %collective-permute-done.18 = f32[8,1024]{1,0:T(8,128)S(1)} collective-permute-done((f32[8,1024]{1,0:T(8,128)S(1)}, f32[8,1024]{1,0:T(8,128)S(1)}, u32[]{:S(2)}, u32[]{:S(2)}) %collective-permute-start.18) | collective-permute-done | bytes 32800 | tf_op jit(solution)/shard_map/ppermute | solution.py:31
  78.8 1.4 %fusion.7 = f32[1024,128]{1,0:T(8,128)} fusion(f32[1024,128]{1,0:T(8,128)S(1)} %fusion.refs_0_, f32[128,128]{1,0:T(8,128)S(1)} %factor.7.inverse_ref), kind=kOutput, calls=%fused_computation.14 | convolution fusion | flops 201326592 | bytes 1114112 | tf_op jit(solution)/shard_map/dot_general | solution.py:35
  80.2 1.9 %collective-permute-done.20 = f32[16,1024]{1,0:T(8,128)S(1)} collective-permute-done((f32[16,1024]{1,0:T(8,128)S(1)}, f32[16,1024]{1,0:T(8,128)S(1)}, u32[]{:S(2)}, u32[]{:S(2)}) %collective-permute-start.20) | collective-permute-done | bytes 65568 | tf_op jit(solution)/shard_map/ppermute | solution.py:31
  84.1 1.5 %collective-permute-start.23 = (f32[32,1024]{1,0:T(8,128)S(1)}, f32[32,1024]{1,0:T(8,128)S(1)}, u32[]{:S(2)}, u32[]{:S(2)}) collective-permute-start(f32[32,1024]{1,0:T(8,128)S(1)} %pad_maximum_fusion.1.refs_2_), channel_id=1, source_target_pairs={{0,8},{4,12},{8,0},{12,4},{16,24},{20,28},{24,16},{28,20},{1,9},{5... | collective-permute-start | bytes 393224 | tf_op jit(solution)/shard_map/ppermute | solution.py:31
  85.6 2.3 %collective-permute-done.22.refs_1_ = f32[32,1024]{1,0:T(8,128)S(1)} collective-permute-done((f32[32,1024]{1,0:T(8,128)S(1)}, f32[32,1024]{1,0:T(8,128)S(1)}, u32[]{:S(2)}, u32[]{:S(2)}) %collective-permute-start.22) | collective-permute-done | bytes 131104 | tf_op jit(solution)/shard_map/ppermute | solution.py:31
  89.1 2.3 %finish.1 = (f32[128,1024]{1,0:T(8,128)}, f32[128,128]{1,0:T(8,128)S(1)}) custom-call(s32[2]{0:T(128)S(1)} %pad_add_fusion.own_ref, f32[128,128]{1,0:T(8,128)S(1)} %factor.7.inverse_ref, f32[32,1024]{1,0:T(8,128)S(1)} %pad_maximum_fusion.refs_0_, f32[32,1024]{1,0:T(8,128)S(1)} %collective-permute-done.22.refs_1_, f32[32,1024]{1,0:T(8,128)S(1)} %pad_maximum_fusion.1.refs_2_, ...), custom_call_target="tpu_custom_call" | custom-call | flops 1 | bytes 8388608 | tf_op jit(solution)/shard_map/finish/pallas_call | solution.py:273
  91.9 1.4 %collective-permute-start.26 = (f32[128,128]{1,0:T(8,128)S(1)}, f32[128,128]{1,0:T(8,128)S(1)}, u32[]{:S(2)}, u32[]{:S(2)}) collective-permute-start(f32[128,128]{1,0:T(8,128)S(1)} %get-tuple-element.132), channel_id=1, source_target_pairs={{0,3},{1,2},{2,1},{3,0},{4,7},{5,6},{6,5},{7,4},{8,11},{9,10},{10,... | collective-permute-start | bytes 196616 | tf_op jit(solution)/shard_map/ppermute | solution.py:31
  93.2 3.0 %collective-permute-done.25 = f32[128,128]{1,0:T(8,128)S(1)} collective-permute-done((f32[128,128]{1,0:T(8,128)S(1)}, f32[128,128]{1,0:T(8,128)S(1)}, u32[]{:S(2)}, u32[]{:S(2)}) %collective-permute-start.25) | collective-permute-done | bytes 65568 | tf_op jit(solution)/shard_map/ppermute | solution.py:31
  (70 shorter events, 20.1 us)
Async XLA Ops:
  0.7 1.0 %copy-start = (f32[1024,128]{1,0:T(8,128)S(1)}, f32[1024,128]{1,0:T(8,128)}, u32[]{:S(2)}) copy-start(f32[1024,128]{1,0:T(8,128)} %omega_ref.1) | copy-start | bytes 1572868
  1.8 11.8 %slice-start = ((s8[16777216]{0:T(1024)(128)(4,1)}), s8[4194304]{0:T(1024)(128)(4,1)S(1)}, s32[]{:S(2)}) async-start(s8[16777216]{0:T(1024)(128)(4,1)} %bitcast.6), calls=%async_computation | async-start | bytes 8388608
  1.8 11.8 %slice-start.1 = ((s8[16777216]{0:T(1024)(128)(4,1)}), s8[4194304]{0:T(1024)(128)(4,1)S(1)}, s32[]{:S(2)}) async-start(s8[16777216]{0:T(1024)(128)(4,1)} %bitcast.6), calls=%async_computation.1 | async-start | bytes 8388608
  6.1 4.8 %collective-permute-start = (f32[1024,128]{1,0:T(8,128)S(1)}, f32[1024,128]{1,0:T(8,128)S(1)}, u32[]{:S(2)}, u32[]{:S(2)}) collective-permute-start(f32[1024,128]{1,0:T(8,128)S(1)} %get-tuple-element.69), channel_id=1, source_target_pairs={{0,1},{1,0},{2,3},{3,2},{4,5},{5,4},{6,7},{7,6},{8,9},{9,8},{10,11... | collective-permute-start | bytes 1572872 | tf_op jit(solution)/shard_map/ppermute | solution.py:31
  6.6 6.9 %slice-start.2 = ((s8[16777216]{0:T(1024)(128)(4,1)}), s8[4194304]{0:T(1024)(128)(4,1)S(1)}, s32[]{:S(2)}) async-start(s8[16777216]{0:T(1024)(128)(4,1)} %bitcast.6), calls=%async_computation.2 | async-start | bytes 8388608
  6.6 6.9 %slice-start.3 = ((s8[16777216]{0:T(1024)(128)(4,1)}), s8[4194304]{0:T(1024)(128)(4,1)S(1)}, s32[]{:S(2)}) async-start(s8[16777216]{0:T(1024)(128)(4,1)} %bitcast.6), calls=%async_computation.3 | async-start | bytes 8388608
  11.0 15.2 %collective-permute-start.3 = (f32[1024,128]{1,0:T(8,128)S(1)}, f32[1024,128]{1,0:T(8,128)S(1)}, u32[]{:S(2)}, u32[]{:S(2)}) collective-permute-start(f32[1024,128]{1,0:T(8,128)S(1)} %add.56), channel_id=1, source_target_pairs={{0,2},{1,3},{2,0},{3,1},{4,6},{5,7},{6,4},{7,5},{8,10},{9,11},{10,... | collective-permute-start | bytes 1572872 | tf_op jit(solution)/shard_map/ppermute | solution.py:31
  16.5 1.6 %collective-permute-start.1 = (f32[512,128]{1,0:T(8,128)S(1)}, f32[512,128]{1,0:T(8,128)S(1)}, u32[]{:S(2)}, u32[]{:S(2)}) collective-permute-start(f32[512,128]{1,0:T(8,128)S(1)} %get-tuple-element.134), channel_id=1, source_target_pairs={{0,1},{1,0},{2,3},{3,2},{4,5},{5,4},{6,7},{7,6},{8,9},{9,8},{10,11... | collective-permute-start | bytes 786440 | tf_op jit(solution)/shard_map/ppermute | solution.py:31
  16.8 1.7 %collective-permute-start.2 = (f32[512,128]{1,0:T(8,128)S(1)}, f32[512,128]{1,0:T(8,128)S(1)}, u32[]{:S(2)}, u32[]{:S(2)}) collective-permute-start(f32[512,128]{1,0:T(8,128)S(1)} %get-tuple-element.133), channel_id=1, source_target_pairs={{0,1},{1,0},{2,3},{3,2},{4,5},{5,4},{6,7},{7,6},{8,9},{9,8},{10,11... | collective-permute-start | bytes 786440 | tf_op jit(solution)/shard_map/ppermute | solution.py:31
  26.2 7.2 %collective-permute-start.6 = (f32[1024,128]{1,0:T(8,128)S(1)}, f32[1024,128]{1,0:T(8,128)S(1)}, u32[]{:S(2)}, u32[]{:S(2)}) collective-permute-start(f32[1024,128]{1,0:T(8,128)S(1)} %fusion.refs_0_), channel_id=1, source_target_pairs={{0,1},{1,0},{2,3},{3,2},{4,5},{5,4},{6,7},{7,6},{8,9},{9,8},{10,11... | collective-permute-start | bytes 1572872 | tf_op jit(solution)/shard_map/ppermute | solution.py:31
  26.3 18.1 %collective-permute-start.4 = (f32[1024,128]{1,0:T(8,128)S(1)}, f32[1024,128]{1,0:T(8,128)S(1)}, u32[]{:S(2)}, u32[]{:S(2)}) collective-permute-start(f32[1024,128]{1,0:T(8,128)S(1)} %fusion.refs_0_), channel_id=1, source_target_pairs={{0,2},{1,3},{2,0},{3,1},{4,6},{5,7},{6,4},{7,5},{8,10},{9,11},{10,... | collective-permute-start | bytes 1572872 | tf_op jit(solution)/shard_map/ppermute | solution.py:31
  29.1 4.3 %collective-permute-start.5 = (f32[128,128]{1,0:T(8,128)S(1)}, f32[128,128]{1,0:T(8,128)S(1)}, u32[]{:S(2)}, u32[]{:S(2)}) collective-permute-start(f32[128,128]{1,0:T(8,128)S(1)} %fusion.6), channel_id=1, source_target_pairs={{0,4},{4,0},{8,12},{12,8},{16,20},{20,16},{24,28},{28,24},{1,5},{5... | collective-permute-start | bytes 196616 | tf_op jit(solution)/shard_map/ppermute | solution.py:31
  33.5 4.3 %collective-permute-start.7 = (f32[128,128]{1,0:T(8,128)S(1)}, f32[128,128]{1,0:T(8,128)S(1)}, u32[]{:S(2)}, u32[]{:S(2)}) collective-permute-start(f32[128,128]{1,0:T(8,128)S(1)} %add.59), channel_id=1, source_target_pairs={{0,8},{4,12},{8,0},{12,4},{16,24},{20,28},{24,16},{28,20},{1,9},{5... | collective-permute-start | bytes 196616 | tf_op jit(solution)/shard_map/ppermute | solution.py:31
  37.8 5.2 %collective-permute-start.8 = (f32[128,128]{1,0:T(8,128)S(1)}, f32[128,128]{1,0:T(8,128)S(1)}, u32[]{:S(2)}, u32[]{:S(2)}) collective-permute-start(f32[128,128]{1,0:T(8,128)S(1)} %add.60), channel_id=1, source_target_pairs={{0,16},{4,20},{8,24},{12,28},{16,0},{20,4},{24,8},{28,12},{1,17},{... | collective-permute-start | bytes 196616 | tf_op jit(solution)/shard_map/ppermute | solution.py:31
  43.1 1.3 %collective-permute-start.9 = (f32[128,128]{1,0:T(8,128)S(1)}, f32[128,128]{1,0:T(8,128)S(1)}, u32[]{:S(2)}, u32[]{:S(2)}) collective-permute-start(f32[128,128]{1,0:T(8,128)S(1)} %add.61), channel_id=1, source_target_pairs={{0,1},{1,0},{2,3},{3,2},{4,5},{5,4},{6,7},{7,6},{8,9},{9,8},{10,11... | collective-permute-start | bytes 196616 | tf_op jit(solution)/shard_map/ppermute | solution.py:31
  44.4 4.6 %collective-permute-start.11 = (f32[1024,128]{1,0:T(8,128)S(1)}, f32[1024,128]{1,0:T(8,128)S(1)}, u32[]{:S(2)}, u32[]{:S(2)}) collective-permute-start(f32[1024,128]{1,0:T(8,128)S(1)} %collective-permute-done.4.refs_0_), channel_id=1, source_target_pairs={{0,1},{1,0},{2,3},{3,2},{4,5},{5,4},{6,7},{7,6},{8,9},{9,8},{10,11... | collective-permute-start | bytes 1572872 | tf_op jit(solution)/shard_map/ppermute | solution.py:31
  44.6 4.4 %collective-permute-start.10 = (f32[128,128]{1,0:T(8,128)S(1)}, f32[128,128]{1,0:T(8,128)S(1)}, u32[]{:S(2)}, u32[]{:S(2)}) collective-permute-start(f32[128,128]{1,0:T(8,128)S(1)} %add.62), channel_id=1, source_target_pairs={{0,2},{1,3},{2,0},{3,1},{4,6},{5,7},{6,4},{7,5},{8,10},{9,11},{10,... | collective-permute-start | bytes 196616 | tf_op jit(solution)/shard_map/ppermute | solution.py:31
  50.8 5.6 %collective-permute-start.12 = (f32[32,1024]{1,0:T(8,128)S(1)}, f32[32,1024]{1,0:T(8,128)S(1)}, u32[]{:S(2)}, u32[]{:S(2)}) collective-permute-start(f32[32,1024]{1,0:T(8,128)S(1)} %get-tuple-element.93), channel_id=1, source_target_pairs={{0,4},{4,0},{8,12},{12,8},{16,20},{20,16},{24,28},{28,24},{1,5},{5... | collective-permute-start | bytes 393224 | tf_op jit(solution)/shard_map/ppermute | solution.py:31
  52.5 5.0 %collective-permute-start.13 = (f32[32,1024]{1,0:T(8,128)S(1)}, f32[32,1024]{1,0:T(8,128)S(1)}, u32[]{:S(2)}, u32[]{:S(2)}) collective-permute-start(f32[32,1024]{1,0:T(8,128)S(1)} %get-tuple-element.94), channel_id=1, source_target_pairs={{0,8},{4,12},{8,0},{12,4},{16,24},{20,28},{24,16},{28,20},{1,9},{5... | collective-permute-start | bytes 393224 | tf_op jit(solution)/shard_map/ppermute | solution.py:31
  57.5 7.1 %collective-permute-start.14 = (f32[16,1024]{1,0:T(8,128)S(1)}, f32[16,1024]{1,0:T(8,128)S(1)}, u32[]{:S(2)}, u32[]{:S(2)}) collective-permute-start(f32[16,1024]{1,0:T(8,128)S(1)} %get-tuple-element.101), channel_id=1, source_target_pairs={{0,8},{4,12},{8,0},{12,4},{16,24},{20,28},{24,16},{28,20},{1,9},{5... | collective-permute-start | bytes 196616 | tf_op jit(solution)/shard_map/ppermute | solution.py:31
  59.2 6.1 %collective-permute-start.15 = (f32[16,1024]{1,0:T(8,128)S(1)}, f32[16,1024]{1,0:T(8,128)S(1)}, u32[]{:S(2)}, u32[]{:S(2)}) collective-permute-start(f32[16,1024]{1,0:T(8,128)S(1)} %get-tuple-element.102), channel_id=1, source_target_pairs={{0,16},{4,20},{8,24},{12,28},{16,0},{20,4},{24,8},{28,12},{1,17},{... | collective-permute-start | bytes 196616 | tf_op jit(solution)/shard_map/ppermute | solution.py:31
  65.4 5.2 %collective-permute-start.16 = (f32[8,1024]{1,0:T(8,128)S(1)}, f32[8,1024]{1,0:T(8,128)S(1)}, u32[]{:S(2)}, u32[]{:S(2)}) collective-permute-start(f32[8,1024]{1,0:T(8,128)S(1)} %get-tuple-element.109), channel_id=1, source_target_pairs={{0,16},{4,20},{8,24},{12,28},{16,0},{20,4},{24,8},{28,12},{1,17},{... | collective-permute-start | bytes 98312 | tf_op jit(solution)/shard_map/ppermute | solution.py:31
  67.7 4.1 %collective-permute-start.17 = (f32[8,1024]{1,0:T(8,128)S(1)}, f32[8,1024]{1,0:T(8,128)S(1)}, u32[]{:S(2)}, u32[]{:S(2)}) collective-permute-start(f32[8,1024]{1,0:T(8,128)S(1)} %get-tuple-element.110), channel_id=1, source_target_pairs={{0,4},{4,0},{8,12},{12,8},{16,20},{20,16},{24,28},{28,24},{1,5},{5... | collective-permute-start | bytes 98312 | tf_op jit(solution)/shard_map/ppermute | solution.py:31
  71.8 5.7 %collective-permute-start.18 = (f32[8,1024]{1,0:T(8,128)S(1)}, f32[8,1024]{1,0:T(8,128)S(1)}, u32[]{:S(2)}, u32[]{:S(2)}) collective-permute-start(f32[8,1024]{1,0:T(8,128)S(1)} %add.68), channel_id=1, source_target_pairs={{0,16},{4,20},{8,24},{12,28},{16,0},{20,4},{24,8},{28,12},{1,17},{... | collective-permute-start | bytes 98312 | tf_op jit(solution)/shard_map/ppermute | solution.py:31
  72.9 4.6 %collective-permute-start.19 = (f32[8,1024]{1,0:T(8,128)S(1)}, f32[8,1024]{1,0:T(8,128)S(1)}, u32[]{:S(2)}, u32[]{:S(2)}) collective-permute-start(f32[8,1024]{1,0:T(8,128)S(1)} %add.69), channel_id=1, source_target_pairs={{0,4},{4,0},{8,12},{12,8},{16,20},{20,16},{24,28},{28,24},{1,5},{5... | collective-permute-start | bytes 98312 | tf_op jit(solution)/shard_map/ppermute | solution.py:31
  77.5 4.7 %collective-permute-start.20 = (f32[16,1024]{1,0:T(8,128)S(1)}, f32[16,1024]{1,0:T(8,128)S(1)}, u32[]{:S(2)}, u32[]{:S(2)}) collective-permute-start(f32[16,1024]{1,0:T(8,128)S(1)} %pad_maximum_fusion.2), channel_id=1, source_target_pairs={{0,8},{4,12},{8,0},{12,4},{16,24},{20,28},{24,16},{28,20},{1,9},{5... | collective-permute-start | bytes 196616 | tf_op jit(solution)/shard_map/ppermute | solution.py:31
  77.5 5.3 %collective-permute-start.21 = (f32[16,1024]{1,0:T(8,128)S(1)}, f32[16,1024]{1,0:T(8,128)S(1)}, u32[]{:S(2)}, u32[]{:S(2)}) collective-permute-start(f32[16,1024]{1,0:T(8,128)S(1)} %pad_maximum_fusion.3), channel_id=1, source_target_pairs={{0,16},{4,20},{8,24},{12,28},{16,0},{20,4},{24,8},{28,12},{1,17},{... | collective-permute-start | bytes 196616 | tf_op jit(solution)/shard_map/ppermute | solution.py:31
  82.9 5.0 %collective-permute-start.22 = (f32[32,1024]{1,0:T(8,128)S(1)}, f32[32,1024]{1,0:T(8,128)S(1)}, u32[]{:S(2)}, u32[]{:S(2)}) collective-permute-start(f32[32,1024]{1,0:T(8,128)S(1)} %pad_maximum_fusion.refs_0_), channel_id=1, source_target_pairs={{0,4},{4,0},{8,12},{12,8},{16,20},{20,16},{24,28},{28,24},{1,5},{5... | collective-permute-start | bytes 393224 | tf_op jit(solution)/shard_map/ppermute | solution.py:31
  84.1 5.0 %collective-permute-start.23 = (f32[32,1024]{1,0:T(8,128)S(1)}, f32[32,1024]{1,0:T(8,128)S(1)}, u32[]{:S(2)}, u32[]{:S(2)}) collective-permute-start(f32[32,1024]{1,0:T(8,128)S(1)} %pad_maximum_fusion.1.refs_2_), channel_id=1, source_target_pairs={{0,8},{4,12},{8,0},{12,4},{16,24},{20,28},{24,16},{28,20},{1,9},{5... | collective-permute-start | bytes 393224 | tf_op jit(solution)/shard_map/ppermute | solution.py:31
  91.4 1.9 %collective-permute-start.24 = (f32[128,128]{1,0:T(8,128)S(1)}, f32[128,128]{1,0:T(8,128)S(1)}, u32[]{:S(2)}, u32[]{:S(2)}) collective-permute-start(f32[128,128]{1,0:T(8,128)S(1)} %get-tuple-element.132), channel_id=1, source_target_pairs={{0,1},{1,0},{2,3},{3,2},{4,5},{5,4},{6,7},{7,6},{8,9},{9,8},{10,11... | collective-permute-start | bytes 196616 | tf_op jit(solution)/shard_map/ppermute | solution.py:31
  91.4 4.9 %collective-permute-start.25 = (f32[128,128]{1,0:T(8,128)S(1)}, f32[128,128]{1,0:T(8,128)S(1)}, u32[]{:S(2)}, u32[]{:S(2)}) collective-permute-start(f32[128,128]{1,0:T(8,128)S(1)} %get-tuple-element.132), channel_id=1, source_target_pairs={{0,2},{1,3},{2,0},{3,1},{4,6},{5,7},{6,4},{7,5},{8,10},{9,11},{10,... | collective-permute-start | bytes 196616 | tf_op jit(solution)/shard_map/ppermute | solution.py:31
  91.9 5.0 %collective-permute-start.26 = (f32[128,128]{1,0:T(8,128)S(1)}, f32[128,128]{1,0:T(8,128)S(1)}, u32[]{:S(2)}, u32[]{:S(2)}) collective-permute-start(f32[128,128]{1,0:T(8,128)S(1)} %get-tuple-element.132), channel_id=1, source_target_pairs={{0,3},{1,2},{2,1},{3,0},{4,7},{5,6},{6,5},{7,4},{8,11},{9,10},{10,... | collective-permute-start | bytes 196616 | tf_op jit(solution)/shard_map/ppermute | solution.py:31

commit v7 on v6

v7 whole, which is shorter than its diff:
```python
import functools

import jax
import jax.numpy as jnp
from jax import lax
from jax.experimental import pallas as pl
from jax.experimental.pallas import tpu as pltpu
from jax.sharding import PartitionSpec as P

full = lax.Precision.HIGHEST
f32 = jnp.float32
bf16 = jnp.bfloat16

PIECE = 512
TILE = 256
SMEM = pl.BlockSpec(memory_space=pltpu.SMEM)
VMEM = pl.BlockSpec(memory_space=pltpu.VMEM)
HBM = pl.BlockSpec(memory_space=pltpu.HBM)
fence = lax.optimization_barrier


def cost(mib):
    return pl.CostEstimate(flops=1, bytes_accessed=int(mib * 2**20), transcendentals=0)


def params():
    return pltpu.CompilerParams(vmem_limit_bytes=16 * 1024 * 1024)


def swap(value, axis, bit):
    return lax.ppermute(value, axis, [(i, i ^ bit) for i in range(lax.axis_size(axis))])


def dot(a, b, a_dim, b_dim, precision=full):
    return lax.dot_general(
        a, b, (((a_dim,), (b_dim,)), ((), ())), precision=precision, preferred_element_type=f32
    )


def split(value):
    upper = value.astype(bf16)
    return upper, (value - upper.astype(f32)).astype(bf16)


def sketch_kernel(places, first, own_ref, data_ref, omega_ref, *refs):
    count = len(places)
    if first:
        refs, (omega_held, omega_sem) = refs[:-2], refs[-2:]
        omega_copy = pltpu.make_async_copy(omega_ref, omega_held, omega_sem)
        omega_copy.start()
    outs, held, sems = refs[:count], refs[count : 2 * count], refs[-1]
    quarter, cols = held[0].shape
    copies = {}
    for k, place in enumerate(places):
        for row in range(0, quarter, PIECE):
            at = pl.multiple_of((own_ref[0] ^ place) * quarter + row, PIECE)
            for t in range(cols // TILE):
                tile = pl.ds(t * TILE, TILE)
                copy = pltpu.make_async_copy(
                    data_ref.at[pl.ds(at, PIECE), tile],
                    held[k].at[pl.ds(row, PIECE), tile],
                    sems.at[k, row // PIECE, t],
                )
                copy.start()
                copies[k, row, t] = copy
    if first:
        width = omega_ref.shape[1]
        wide = refs[2 * count]
        omega_copy.wait()
        upper, rest = split(omega_held[...])
        wide[:, :width] = upper
        wide[:, width:] = rest
    else:
        wide = omega_ref
        width = omega_ref.shape[1] // 2
    for (k, row, t), copy in copies.items():
        tile = slice(t * TILE, (t + 1) * TILE)
        copy.wait()
        upper, rest = split(held[k][row : row + PIECE, tile])
        one = jnp.dot(upper, wide[tile, :], preferred_element_type=f32)
        two = jnp.dot(rest, wide[tile, :width], preferred_element_type=f32)
        both, more = (one, two) if t == 0 else (both + one, more + two)
        if t == cols // TILE - 1:
            outs[k][row : row + PIECE] = both[:, :width] + both[:, width:] + more


def sketch(own, data, omega, places, first=False):
    cols = data.shape[1]
    width = omega.shape[1] if first else omega.shape[1] // 2
    quarter = data.shape[0] // lax.axis_size("col")
    count = len(places)
    out = [jax.ShapeDtypeStruct((quarter, width), f32)] * count
    out += [pltpu.VMEM((quarter, cols), f32)] * count
    scratch = [pltpu.SemaphoreType.DMA((count, quarter // PIECE, cols // TILE))]
    if first:
        out.append(jax.ShapeDtypeStruct((cols, 2 * width), bf16))
        scratch += [pltpu.VMEM(omega.shape, f32), pltpu.SemaphoreType.DMA]
    return pl.pallas_call(
        functools.partial(sketch_kernel, places, first),
        in_specs=[SMEM, HBM, HBM if first else VMEM],
        out_specs=[VMEM] * len(out),
        out_shape=out,
        scratch_shapes=scratch,
        compiler_params=params(),
        cost_estimate=cost(0.01),
        name="partial_sketch",
    )(own, data, omega)


def project_kernel(before, slices, own_ref, rows_ref, part_ref, *refs):
    old, refs = (refs[0], refs[1:]) if before else (None, refs)
    outs, total = (refs[:-1], refs[-1]) if slices else (refs, refs[0])
    quarter, cols = rows_ref.shape
    for row in range(0, quarter, PIECE):
        upper, rest = split(part_ref[row : row + PIECE].T)
        stack = jnp.concatenate([upper, rest], 0)
        width = upper.shape[0]
        for t in range(cols // TILE):
            tile = slice(t * TILE, (t + 1) * TILE)
            d_upper, d_rest = split(rows_ref[row : row + PIECE, tile])
            both = jnp.dot(stack, d_upper, preferred_element_type=f32)
            value = both[:width] + both[width:] + jnp.dot(upper, d_rest, preferred_element_type=f32)
            if row > 0:
                value += total[:, tile]
            elif before:
                value += old[:, tile]
            total[:, tile] = value
    if slices:
        step = outs[0].shape[0]
        for place, ref in enumerate(outs):
            at = pl.multiple_of((place ^ own_ref[1]) * step, step)
            ref[...] = total[pl.ds(at, step)]


def project(own, rows, part, before=None, slices=0):
    cols = rows.shape[1]
    width = part.shape[1]
    args = [own, rows, part] + ([] if before is None else [before])
    if slices:
        out = [jax.ShapeDtypeStruct((width // slices, cols), f32)] * slices
    else:
        out = [jax.ShapeDtypeStruct((width, cols), f32)]
    return pl.pallas_call(
        functools.partial(project_kernel, before is not None, slices),
        in_specs=[SMEM] + [VMEM] * (len(args) - 1),
        out_specs=[VMEM] * len(out),
        out_shape=out,
        scratch_shapes=[pltpu.VMEM((width, cols), f32)] if slices else [],
        compiler_params=params(),
        cost_estimate=cost(6),
        name="project",
    )(*args)


def factor_kernel(index, count, in_ref, out_ref, *scratch):
    n = in_ref.shape[0]
    last = index == count - 1
    work = scratch[0] if last else out_ref
    if index == 0:
        row = lax.broadcasted_iota(jnp.int32, (n, n), 0)
        col = lax.broadcasted_iota(jnp.int32, (n, n), 1)
        work[:, :n] = in_ref[...]
        work[:, n:] = jnp.where(row == col, 1.0, 0.0).astype(f32)
    else:
        work[...] = in_ref[...]
    sub = lax.broadcasted_iota(jnp.int32, (8, n), 0)
    panels = n // 8
    for b in range(panels * index // count, panels * (index + 1) // count):
        top = slice(8 * b, 8 * b + 8)
        panel = work[top, :]
        spread = [jnp.broadcast_to(panel[:, 8 * b + j : 8 * b + j + 1], (8, n)) for j in range(8)]
        e = [
            [jnp.broadcast_to(spread[j][i : i + 1, :], (8, n)) for j in range(i + 1)]
            for i in range(8)
        ]
        left = [jnp.broadcast_to(panel[i : i + 1, :n], (8, n)) for i in range(8)]
        right = [jnp.broadcast_to(panel[i : i + 1, n:], (8, n)) for i in range(8)]
        for j in range(8):
            scale = lax.rsqrt(e[j][j])
            left[j] = left[j] * scale
            right[j] = right[j] * scale
            low = {i: e[i][j] * scale for i in range(j + 1, 8)}
            for i in range(j + 1, 8):
                for k in range(j + 1, i + 1):
                    e[i][k] = e[i][k] - low[i] * low[k]
                left[i] = left[i] - low[i] * left[j]
                right[i] = right[i] - low[i] * right[j]
        l_panel, r_panel = left[0], right[0]
        for i in range(1, 8):
            l_panel = jnp.where(sub == i, left[i], l_panel)
            r_panel = jnp.where(sub == i, right[i], r_panel)
        work[top, n:] = r_panel
        if b < panels - 1:
            done = jnp.concatenate([l_panel, r_panel], 1)
            change = dot(l_panel, done, 0, 0)
            below = slice(8 * b + 8, n)
            work[below, :] = work[below, :] - change[8 * b + 8 :, :]
    if last:
        out_ref[...] = work[:, n:]


def factor(index, count, value):
    n = value.shape[0]
    last = index == count - 1
    return pl.pallas_call(
        functools.partial(factor_kernel, index, count),
        in_specs=[VMEM],
        out_specs=VMEM,
        out_shape=jax.ShapeDtypeStruct((n, n if last else 2 * n), f32),
        scratch_shapes=[pltpu.VMEM((n, 2 * n), f32)] if last else [],
        compiler_params=params(),
        cost_estimate=cost(0.01),
        name="factor",
    )(value)


def finish_kernel(own_ref, inverse_ref, *refs):
    parts, (out_ref, gram_ref, total) = refs[:-3], refs[-3:]
    step = parts[0].shape[0]
    for place, ref in enumerate(parts):
        at = pl.multiple_of((place ^ own_ref[1]) * step, step)
        total[pl.ds(at, step)] = ref[...]
    value = jnp.dot(inverse_ref[...], total[...], precision=full, preferred_element_type=f32)
    out_ref[...] = value
    gram_ref[...] = dot(value, value, 1, 1)


def finish(own, inverse, parts):
    width = inverse.shape[0]
    cols = parts[0].shape[1]
    return pl.pallas_call(
        finish_kernel,
        in_specs=[SMEM] + [VMEM] * (1 + len(parts)),
        out_specs=[VMEM] * 2,
        out_shape=[
            jax.ShapeDtypeStruct((width, cols), f32),
            jax.ShapeDtypeStruct((width, width), f32),
        ],
        scratch_shapes=[pltpu.VMEM((width, cols), f32)],
        compiler_params=params(),
        cost_estimate=cost(8),
        name="finish",
    )(own, inverse, *parts)


def per_device(data, omega):
    nrow, ncol = lax.axis_size("row"), lax.axis_size("col")
    quarter = data.shape[0] // ncol
    assert ncol == 4 and quarter == 2 * PIECE and nrow >= 8
    total_rows = data.shape[0] * nrow
    own = jnp.stack([lax.axis_index("col"), lax.axis_index("row") % 8]).astype(jnp.int32)
    bits = [1 << k for k in range(nrow.bit_length() - 1)]

    data = pltpu.with_memory_space_constraint(data, pltpu.HBM)
    omega = pltpu.with_memory_space_constraint(omega, pltpu.HBM)

    part, rows3, wide = sketch(own, data, omega, [3], True)
    pair, rows2 = sketch(own, data, wide, [2])
    pair, wide = fence((pair + swap(part, "col", 1), wide))
    away = swap(pair, "col", 2)
    part, here, rows1, rows0 = sketch(own, data, wide, [1, 0])
    part_a, part_b, away = fence((swap(part[:PIECE], "col", 1), swap(part[PIECE:], "col", 1), away))
    sketched = here + jnp.concatenate([part_a, part_b], 0) + away

    third = swap(sketched, "col", 2)
    second = swap(sketched, "col", 1)
    gram = dot(sketched, sketched, 0, 0)
    far = swap(gram, "row", bits[0])
    (acc,) = project(own, rows0, sketched)
    far, acc, second = fence((far, acc, second))
    gram = gram + far
    far = swap(gram, "row", bits[1])
    (acc,) = project(own, rows1, second, acc)
    far, acc = fence((far, acc))
    gram = gram + far
    far = swap(gram, "row", bits[2])
    third, acc = fence((third, acc))
    fourth = swap(third, "col", 1)
    (acc,) = project(own, rows2, third, acc)
    far, acc, fourth = fence((far, acc, fourth))
    gram = gram + far
    for bit in bits[3:]:
        gram = gram + swap(gram, "row", bit)
    far = swap(gram, "col", 1)
    slices = project(own, rows3, fourth, acc, 8)
    far, *slices = fence((far, *slices))
    gram = gram + far

    state = factor(0, 2, gram + swap(gram, "col", 2))
    got = [swap(slices[q], "row", q) for q in range(1, 8)]
    *got, state = fence((*got, state))
    mine = ((slices[0] + got[0]) + (got[1] + got[2])) + ((got[3] + got[4]) + (got[5] + got[6]))
    for bit in bits[3:]:
        mine = mine + swap(mine, "row", bit)
    mine, state = fence((mine, state))
    inverse = factor(1, 2, state)
    got = [swap(mine, "row", q) for q in range(1, 8)]
    *got, inverse = fence((*got, inverse))
    projected, small = finish(own, inverse, [mine, *got])

    across = [swap(small, "col", bit) for bit in (2, 3, 1)]
    *across, basis = fence((*across, dot(sketched, inverse, 1, 1)))
    small = (small + across[2]) + (across[0] + across[1])
    return (basis, projected, small / total_rows)


def solution(mesh):
    placed = (P("row", "col"), P("col", None))
    return jax.shard_map(
        per_device,
        mesh=mesh,
        in_specs=placed,
        out_specs=(P(("row", "col"), None), P(None, "col"), P()),
        check_vma=False,
    )
```

time: 97.7 us -> 94.5 us (0.967)
  waiting for transfers between devices: 32.4 us -> 17.3 us
  starting transfers between devices: 30.3 us -> 39.2 us
  Pallas kernels: 29.3 us -> 33.6 us
  local copies, waits for them, and re-layouts: 1.13 us -> 0.04 us
    ppermute x27 -> x29, waiting for transfers between devices: 32.4 us -> 17.3 us  [swap(): lax.ppermute(value, axis, [(i, i ^ bit) for i in range(lax.axis_size(axis...]
    ppermute x27 -> x29, starting transfers between devices: 30.3 us -> 39.2 us  [swap(): lax.ppermute(value, axis, [(i, i ^ bit) for i in range(lax.axis_size(axis...]
    pallas_call x8, Pallas kernels: 20.6 us -> 24.9 us  [the longest x3 15.6 us: sketch(): pl.pallas_call(functools.partial(sketch_kernel, places, first), in_specs=...]
    unnamed x10 -> x0, local copies, waits for them, and re-layouts: 1.06 us -> none
    pallas_call x4 -> x2, Pallas kernels: 8.69 us -> 8.71 us  [factor(): pl.pallas_call(functools.partial(factor_kernel, index, count), in_specs=[...]
  transfers between devices with their start and end apart: 27 -> 29, of which waited for: 18 -> 11; matrix products, arithmetic and copies ran while one was open for 3% -> 3% of each run, Pallas kernels for 21% -> 28%
where the time goes in v7:
time: 94.5 us; the launch traced here: 94.3 us
  starting transfers between devices  39.2 us (41%)
  Pallas kernels  33.6 us (36%)
  waiting for transfers between devices  17.3 us (18%)
  matrix products  2.4 us (3%)
    ppermute x29, starting transfers between devices, swap(): lax.ppermute(value, axis, [(i, i ^ bit) for i in range(lax.axis_size(axis...  39.2 us
    ppermute x29, waiting for transfers between devices, swap(): lax.ppermute(value, axis, [(i, i ^ bit) for i in range(lax.axis_size(axis...  17.3 us
    pallas_call x3, Pallas kernels, sketch(): pl.pallas_call(functools.partial(sketch_kernel, places, first), in_specs=...  15.6 us
    pallas_call x2, Pallas kernels, factor(): pl.pallas_call(functools.partial(factor_kernel, index, count), in_specs=[...  8.71 us
    pallas_call x4, Pallas kernels, project(): pl.pallas_call(functools.partial(project_kernel, before is not None, slic...  7.02 us
    dot_general x2, matrix products, dot(): lax.dot_general(a, b, (((a_dim,), (b_dim,)), ((), ())), precision=precisi...  2.4 us
    pallas_call x1, Pallas kernels, finish(): pl.pallas_call(finish_kernel, in_specs=[SMEM] + [VMEM] * (1 + len(parts))...  2.3 us
  transfers between devices with their start and end apart: 29, of which 11 were waited for; matrix products, arithmetic and copies ran while one was open for 3% of the time, Pallas kernels for 28%

profile of v7, /device:TPU:0, one launch (start us, length us, event | category | flops | bytes accessed | tf_op | source)
XLA Modules:
  0.0 94.3 jit_solution(249051895100967123)
XLA Ops:
  0.7 5.2 %partial_sketch.3 = (f32[1024,128]{1,0:T(8,128)S(1)}, f32[1024,1024]{1,0:T(8,128)S(1)}, bf16[1024,256]{1,0:T(8,128)(2,1)S(1)}) custom-call(s32[2]{0:T(128)S(1)} %pad_add_fusion.own_ref, f32[4096,1024]{1,0:T(8,128)} %data_ref.5, f32[1024,128]{1,0:T(8,128)} %omega_ref.1), custom_call_target="tpu_custom_call" | custom-call | flops 1 | bytes 10485 | tf_op jit(solution)/shard_map/partial_sketch/pallas_call | solution.py:98
  6.5 4.0 %partial_sketch.4 = (f32[1024,128]{1,0:T(8,128)S(1)}, f32[1024,1024]{1,0:T(8,128)S(1)}) custom-call(s32[2]{0:T(128)S(1)} %pad_add_fusion.own_ref, f32[4096,1024]{1,0:T(8,128)} %data_ref.5, bf16[1024,256]{1,0:T(8,128)(2,1)S(1)} %get-tuple-element.71.omega_ref), custom_call_target="tpu_custom_call" | custom-call | flops 1 | bytes 10485 | tf_op jit(solution)/shard_map/partial_sketch/pallas_call | solution.py:98
  10.6 2.6 %collective-permute-start.3 = (f32[1024,128]{1,0:T(8,128)S(1)}, f32[1024,128]{1,0:T(8,128)S(1)}, u32[]{:S(2)}, u32[]{:S(2)}) collective-permute-start(f32[1024,128]{1,0:T(8,128)S(1)} %add.59), channel_id=1, source_target_pairs={{0,2},{1,3},{2,0},{3,1},{4,6},{5,7},{6,4},{7,5},{8,10},{9,11},{10,... | collective-permute-start | bytes 1572872 | tf_op jit(solution)/shard_map/ppermute | solution.py:31
  13.1 6.4 %partial_sketch.5 = (f32[1024,128]{1,0:T(8,128)S(1)}, f32[1024,128]{1,0:T(8,128)S(1)}, f32[1024,1024]{1,0:T(8,128)S(1)}, f32[1024,1024]{1,0:T(8,128)S(1)}) custom-call(s32[2]{0:T(128)S(1)} %pad_add_fusion.own_ref, f32[4096,1024]{1,0:T(8,128)} %data_ref.5, bf16[1024,256]{1,0:T(8,128)(2,1)S(1)} %get-tuple-element.71.omega_ref), custom_call_target="tpu_custom_call" | custom-call | flops 1 | bytes 10485 | tf_op jit(solution)/shard_map/partial_sketch/pallas_call | solution.py:98
  21.5 4.2 %collective-permute-done.3 = f32[1024,128]{1,0:T(8,128)S(1)} collective-permute-done((f32[1024,128]{1,0:T(8,128)S(1)}, f32[1024,128]{1,0:T(8,128)S(1)}, u32[]{:S(2)}, u32[]{:S(2)}) %collective-permute-start.3) | collective-permute-done | bytes 524320 | tf_op jit(solution)/shard_map/ppermute | solution.py:31
  25.9 1.8 %collective-permute-start.8 = (f32[1024,128]{1,0:T(8,128)S(1)}, f32[1024,128]{1,0:T(8,128)S(1)}, u32[]{:S(2)}, u32[]{:S(2)}) collective-permute-start(f32[1024,128]{1,0:T(8,128)S(1)} %fusion.part_ref), channel_id=1, source_target_pairs={{0,2},{1,3},{2,0},{3,1},{4,6},{5,7},{6,4},{7,5},{8,10},{9,11},{10,... | collective-permute-start | bytes 1572872 | tf_op jit(solution)/shard_map/ppermute | solution.py:31
  28.7 1.6 %collective-permute-start.4 = (f32[128,128]{1,0:T(8,128)S(1)}, f32[128,128]{1,0:T(8,128)S(1)}, u32[]{:S(2)}, u32[]{:S(2)}) collective-permute-start(f32[128,128]{1,0:T(8,128)S(1)} %fusion.2), channel_id=1, source_target_pairs={{0,4},{4,0},{8,12},{12,8},{16,20},{20,16},{24,28},{28,24},{1,5},{5... | collective-permute-start | bytes 196616 | tf_op jit(solution)/shard_map/ppermute | solution.py:31
  30.3 1.7 %project.4.refs_0_ = f32[128,1024]{1,0:T(8,128)S(1)} custom-call(s32[2]{0:T(128)S(1)} %pad_add_fusion.own_ref, f32[1024,1024]{1,0:T(8,128)S(1)} %get-tuple-element.78.rows_ref, f32[1024,128]{1,0:T(8,128)S(1)} %fusion.part_ref), custom_call_target="tpu_custom_call" | custom-call | flops 1 | bytes 6291456 | tf_op jit(solution)/shard_map/project/pallas_call | solution.py:143
  33.1 1.6 %collective-permute-start.6 = (f32[128,128]{1,0:T(8,128)S(1)}, f32[128,128]{1,0:T(8,128)S(1)}, u32[]{:S(2)}, u32[]{:S(2)}) collective-permute-start(f32[128,128]{1,0:T(8,128)S(1)} %add.62), channel_id=1, source_target_pairs={{0,8},{4,12},{8,0},{12,4},{16,24},{20,28},{24,16},{28,20},{1,9},{5... | collective-permute-start | bytes 196616 | tf_op jit(solution)/shard_map/ppermute | solution.py:31
  34.7 1.7 %project.5.refs_0_ = f32[128,1024]{1,0:T(8,128)S(1)} custom-call(s32[2]{0:T(128)S(1)} %pad_add_fusion.own_ref, f32[1024,1024]{1,0:T(8,128)S(1)} %get-tuple-element.80.rows_ref, f32[1024,128]{1,0:T(8,128)S(1)} %collective-permute-done.5.part_ref, f32[128,1024]{1,0:T(8,128)S(1)} %project.4.refs_0_), custom_call_target="tpu_custom_call" | custom-call | flops 1 | bytes 6291456 | tf_op jit(solution)/shard_map/project/pallas_call | solution.py:143
  37.4 2.8 %collective-permute-done.8.part_ref = f32[1024,128]{1,0:T(8,128)S(1)} collective-permute-done((f32[1024,128]{1,0:T(8,128)S(1)}, f32[1024,128]{1,0:T(8,128)S(1)}, u32[]{:S(2)}, u32[]{:S(2)}) %collective-permute-start.8) | collective-permute-done | bytes 524320 | tf_op jit(solution)/shard_map/ppermute | solution.py:31
  40.2 2.9 %collective-permute-start.7 = (f32[128,128]{1,0:T(8,128)S(1)}, f32[128,128]{1,0:T(8,128)S(1)}, u32[]{:S(2)}, u32[]{:S(2)}) collective-permute-start(f32[128,128]{1,0:T(8,128)S(1)} %add.63), channel_id=1, source_target_pairs={{0,16},{4,20},{8,24},{12,28},{16,0},{20,4},{24,8},{28,12},{1,17},{... | collective-permute-start | bytes 196616 | tf_op jit(solution)/shard_map/ppermute | solution.py:31
  43.1 1.9 %project.6.refs_0_ = f32[128,1024]{1,0:T(8,128)S(1)} custom-call(s32[2]{0:T(128)S(1)} %pad_add_fusion.own_ref, f32[1024,1024]{1,0:T(8,128)S(1)} %get-tuple-element.84.rows_ref, f32[1024,128]{1,0:T(8,128)S(1)} %collective-permute-done.8.part_ref, f32[128,1024]{1,0:T(8,128)S(1)} %project.5.refs_0_), custom_call_target="tpu_custom_call" | custom-call | flops 1 | bytes 6291456 | tf_op jit(solution)/shard_map/project/pallas_call | solution.py:143
  45.0 2.3 %collective-permute-done.7 = f32[128,128]{1,0:T(8,128)S(1)} collective-permute-done((f32[128,128]{1,0:T(8,128)S(1)}, f32[128,128]{1,0:T(8,128)S(1)}, u32[]{:S(2)}, u32[]{:S(2)}) %collective-permute-start.7) | collective-permute-done | bytes 65568 | tf_op jit(solution)/shard_map/ppermute | solution.py:31
  47.4 1.7 %project.7 = (f32[16,1024]{1,0:T(8,128)S(1)}, f32[16,1024]{1,0:T(8,128)S(1)}, f32[16,1024]{1,0:T(8,128)S(1)}, f32[16,1024]{1,0:T(8,128)S(1)}, f32[16,1024]{1,0:T...) custom-call(s32[2]{0:T(128)S(1)} %pad_add_fusion.own_ref, ...), custom_call_target="tpu_custom_call" | custom-call | flops 1 | bytes 6291456 | tf_op jit(solution)/shard_map/project/pallas_call | solution.py:143
  49.1 1.6 %collective-permute-start.11 = (f32[16,1024]{1,0:T(8,128)S(1)}, f32[16,1024]{1,0:T(8,128)S(1)}, u32[]{:S(2)}, u32[]{:S(2)}) collective-permute-start(f32[16,1024]{1,0:T(8,128)S(1)} %get-tuple-element.101), channel_id=1, source_target_pairs={{0,4},{4,0},{8,12},{12,8},{16,20},{20,16},{24,28},{28,24},{1,5},{5... | collective-permute-start | bytes 196616 | tf_op jit(solution)/shard_map/ppermute | solution.py:31
  51.5 1.6 %collective-permute-start.18 = (f32[128,128]{1,0:T(8,128)S(1)}, f32[128,128]{1,0:T(8,128)S(1)}, u32[]{:S(2)}, u32[]{:S(2)}) collective-permute-start(f32[128,128]{1,0:T(8,128)S(1)} %add.65), channel_id=1, source_target_pairs={{0,2},{1,3},{2,0},{3,1},{4,6},{5,7},{6,4},{7,5},{8,10},{9,11},{10,... | collective-permute-start | bytes 196616 | tf_op jit(solution)/shard_map/ppermute | solution.py:31
  54.3 2.1 %collective-permute-start.14 = (f32[16,1024]{1,0:T(8,128)S(1)}, f32[16,1024]{1,0:T(8,128)S(1)}, u32[]{:S(2)}, u32[]{:S(2)}) collective-permute-start(f32[16,1024]{1,0:T(8,128)S(1)} %get-tuple-element.104), channel_id=1, source_target_pairs={{0,16},{4,20},{8,24},{12,28},{16,0},{20,4},{24,8},{28,12},{1,17},{... | collective-permute-start | bytes 196616 | tf_op jit(solution)/shard_map/ppermute | solution.py:31
  56.5 1.7 %collective-permute-start.15 = (f32[16,1024]{1,0:T(8,128)S(1)}, f32[16,1024]{1,0:T(8,128)S(1)}, u32[]{:S(2)}, u32[]{:S(2)}) collective-permute-start(f32[16,1024]{1,0:T(8,128)S(1)} %get-tuple-element.105), channel_id=1, source_target_pairs={{0,20},{4,16},{8,28},{12,24},{16,4},{20,0},{24,12},{28,8},{1,21},{... | collective-permute-start | bytes 196616 | tf_op jit(solution)/shard_map/ppermute | solution.py:31
  58.2 3.5 %collective-permute-start.16 = (f32[16,1024]{1,0:T(8,128)S(1)}, f32[16,1024]{1,0:T(8,128)S(1)}, u32[]{:S(2)}, u32[]{:S(2)}) collective-permute-start(f32[16,1024]{1,0:T(8,128)S(1)} %get-tuple-element.106), channel_id=1, source_target_pairs={{0,24},{4,28},{8,16},{12,20},{16,8},{20,12},{24,0},{28,4},{1,25},{... | collective-permute-start | bytes 196616 | tf_op jit(solution)/shard_map/ppermute | solution.py:31
  62.0 4.5 %factor.2.in_ref = f32[128,256]{1,0:T(8,128)S(1)} custom-call(f32[128,128]{1,0:T(8,128)S(1)} %add.66.in_ref), custom_call_target="tpu_custom_call" | custom-call | flops 1 | bytes 10485 | tf_op jit(solution)/shard_map/factor/pallas_call | solution.py:205
  67.4 1.4 %collective-permute-done.17 = f32[16,1024]{1,0:T(8,128)S(1)} collective-permute-done((f32[16,1024]{1,0:T(8,128)S(1)}, f32[16,1024]{1,0:T(8,128)S(1)}, u32[]{:S(2)}, u32[]{:S(2)}) %collective-permute-start.17) | collective-permute-done | bytes 65568 | tf_op jit(solution)/shard_map/ppermute | solution.py:31
  68.8 2.3 %collective-permute-start.25 = (f32[16,1024]{1,0:T(8,128)S(1)}, f32[16,1024]{1,0:T(8,128)S(1)}, u32[]{:S(2)}, u32[]{:S(2)}) collective-permute-start(f32[16,1024]{1,0:T(8,128)S(1)} %add_add_fusion.refs_0_), channel_id=1, source_target_pairs={{0,28},{4,24},{8,20},{12,16},{16,12},{20,8},{24,4},{28,0},{1,29},{... | collective-permute-start | bytes 196616 | tf_op jit(solution)/shard_map/ppermute | solution.py:31
  71.2 1.5 %collective-permute-start.24 = (f32[16,1024]{1,0:T(8,128)S(1)}, f32[16,1024]{1,0:T(8,128)S(1)}, u32[]{:S(2)}, u32[]{:S(2)}) collective-permute-start(f32[16,1024]{1,0:T(8,128)S(1)} %add_add_fusion.refs_0_), channel_id=1, source_target_pairs={{0,24},{4,28},{8,16},{12,20},{16,8},{20,12},{24,0},{28,4},{1,25},{... | collective-permute-start | bytes 196616 | tf_op jit(solution)/shard_map/ppermute | solution.py:31
  72.7 2.0 %collective-permute-start.23 = (f32[16,1024]{1,0:T(8,128)S(1)}, f32[16,1024]{1,0:T(8,128)S(1)}, u32[]{:S(2)}, u32[]{:S(2)}) collective-permute-start(f32[16,1024]{1,0:T(8,128)S(1)} %add_add_fusion.refs_0_), channel_id=1, source_target_pairs={{0,20},{4,16},{8,28},{12,24},{16,4},{20,0},{24,12},{28,8},{1,21},{... | collective-permute-start | bytes 196616 | tf_op jit(solution)/shard_map/ppermute | solution.py:31
  74.7 1.8 %collective-permute-start.22 = (f32[16,1024]{1,0:T(8,128)S(1)}, f32[16,1024]{1,0:T(8,128)S(1)}, u32[]{:S(2)}, u32[]{:S(2)}) collective-permute-start(f32[16,1024]{1,0:T(8,128)S(1)} %add_add_fusion.refs_0_), channel_id=1, source_target_pairs={{0,16},{4,20},{8,24},{12,28},{16,0},{20,4},{24,8},{28,12},{1,17},{... | collective-permute-start | bytes 196616 | tf_op jit(solution)/shard_map/ppermute | solution.py:31
  76.7 4.0 %collective-permute-start.20 = (f32[16,1024]{1,0:T(8,128)S(1)}, f32[16,1024]{1,0:T(8,128)S(1)}, u32[]{:S(2)}, u32[]{:S(2)}) collective-permute-start(f32[16,1024]{1,0:T(8,128)S(1)} %add_add_fusion.refs_0_), channel_id=1, source_target_pairs={{0,8},{4,12},{8,0},{12,4},{16,24},{20,28},{24,16},{28,20},{1,9},{5... | collective-permute-start | bytes 196616 | tf_op jit(solution)/shard_map/ppermute | solution.py:31
  81.3 4.2 %factor.3.inverse_ref = f32[128,128]{1,0:T(8,128)S(1)} custom-call(f32[128,256]{1,0:T(8,128)S(1)} %factor.2.in_ref), custom_call_target="tpu_custom_call" | custom-call | flops 1 | bytes 10485 | tf_op jit(solution)/shard_map/factor/pallas_call | solution.py:205
  85.6 2.3 %finish.1 = (f32[128,1024]{1,0:T(8,128)}, f32[128,128]{1,0:T(8,128)S(1)}) custom-call(s32[2]{0:T(128)S(1)} %pad_add_fusion.own_ref, f32[128,128]{1,0:T(8,128)S(1)} %factor.3.inverse_ref, f32[16,1024]{1,0:T(8,128)S(1)} %add_add_fusion.refs_0_, f32[16,1024]{1,0:T(8,128)S(1)} %collective-permute-done.19.refs_1_, ...), custom_call_target="tpu_custom_call" | custom-call | flops 1 | bytes 8388608 | tf_op jit(solution)/shard_map/finish/pallas_call | solution.py:231
  88.5 1.5 %collective-permute-start.26 = (f32[128,128]{1,0:T(8,128)S(1)}, f32[128,128]{1,0:T(8,128)S(1)}, u32[]{:S(2)}, u32[]{:S(2)}) collective-permute-start(f32[128,128]{1,0:T(8,128)S(1)} %get-tuple-element.127), channel_id=1, source_target_pairs={{0,2},{1,3},{2,0},{3,1},{4,6},{5,7},{6,4},{7,5},{8,10},{9,11},{10,... | collective-permute-start | bytes 196616 | tf_op jit(solution)/shard_map/ppermute | solution.py:31
  90.0 1.4 %fusion.3 = f32[1024,128]{1,0:T(8,128)} fusion(f32[1024,128]{1,0:T(8,128)S(1)} %fusion.part_ref, f32[128,128]{1,0:T(8,128)S(1)} %factor.3.inverse_ref), kind=kOutput, calls=%fused_computation.7 | convolution fusion | flops 201326592 | bytes 1114112 | tf_op jit(solution)/shard_map/dot_general | solution.py:35
  91.6 2.1 %collective-permute-done.26 = f32[128,128]{1,0:T(8,128)S(1)} collective-permute-done((f32[128,128]{1,0:T(8,128)S(1)}, f32[128,128]{1,0:T(8,128)S(1)}, u32[]{:S(2)}, u32[]{:S(2)}) %collective-permute-start.26) | collective-permute-done | bytes 65568 | tf_op jit(solution)/shard_map/ppermute | solution.py:31
  (49 shorter events, 11.4 us)
Async XLA Ops:
  5.9 4.5 %collective-permute-start = (f32[1024,128]{1,0:T(8,128)S(1)}, f32[1024,128]{1,0:T(8,128)S(1)}, u32[]{:S(2)}, u32[]{:S(2)}) collective-permute-start(f32[1024,128]{1,0:T(8,128)S(1)} %get-tuple-element.70), channel_id=1, source_target_pairs={{0,1},{1,0},{2,3},{3,2},{4,5},{5,4},{6,7},{7,6},{8,9},{9,8},{10,11... | collective-permute-start | bytes 1572872 | tf_op jit(solution)/shard_map/ppermute | solution.py:31
  10.6 15.2 %collective-permute-start.3 = (f32[1024,128]{1,0:T(8,128)S(1)}, f32[1024,128]{1,0:T(8,128)S(1)}, u32[]{:S(2)}, u32[]{:S(2)}) collective-permute-start(f32[1024,128]{1,0:T(8,128)S(1)} %add.59), channel_id=1, source_target_pairs={{0,2},{1,3},{2,0},{3,1},{4,6},{5,7},{6,4},{7,5},{8,10},{9,11},{10,... | collective-permute-start | bytes 1572872 | tf_op jit(solution)/shard_map/ppermute | solution.py:31
  19.6 1.6 %collective-permute-start.2 = (f32[512,128]{1,0:T(8,128)S(1)}, f32[512,128]{1,0:T(8,128)S(1)}, u32[]{:S(2)}, u32[]{:S(2)}) collective-permute-start(f32[512,128]{1,0:T(8,128)S(1)} %get-tuple-element.133), channel_id=1, source_target_pairs={{0,1},{1,0},{2,3},{3,2},{4,5},{5,4},{6,7},{7,6},{8,9},{9,8},{10,11... | collective-permute-start | bytes 786440 | tf_op jit(solution)/shard_map/ppermute | solution.py:31
  19.8 1.7 %collective-permute-start.1 = (f32[512,128]{1,0:T(8,128)S(1)}, f32[512,128]{1,0:T(8,128)S(1)}, u32[]{:S(2)}, u32[]{:S(2)}) collective-permute-start(f32[512,128]{1,0:T(8,128)S(1)} %get-tuple-element.134), channel_id=1, source_target_pairs={{0,1},{1,0},{2,3},{3,2},{4,5},{5,4},{6,7},{7,6},{8,9},{9,8},{10,11... | collective-permute-start | bytes 786440 | tf_op jit(solution)/shard_map/ppermute | solution.py:31
  25.8 7.2 %collective-permute-start.5 = (f32[1024,128]{1,0:T(8,128)S(1)}, f32[1024,128]{1,0:T(8,128)S(1)}, u32[]{:S(2)}, u32[]{:S(2)}) collective-permute-start(f32[1024,128]{1,0:T(8,128)S(1)} %fusion.part_ref), channel_id=1, source_target_pairs={{0,1},{1,0},{2,3},{3,2},{4,5},{5,4},{6,7},{7,6},{8,9},{9,8},{10,11... | collective-permute-start | bytes 1572872 | tf_op jit(solution)/shard_map/ppermute | solution.py:31
  25.9 14.3 %collective-permute-start.8 = (f32[1024,128]{1,0:T(8,128)S(1)}, f32[1024,128]{1,0:T(8,128)S(1)}, u32[]{:S(2)}, u32[]{:S(2)}) collective-permute-start(f32[1024,128]{1,0:T(8,128)S(1)} %fusion.part_ref), channel_id=1, source_target_pairs={{0,2},{1,3},{2,0},{3,1},{4,6},{5,7},{6,4},{7,5},{8,10},{9,11},{10,... | collective-permute-start | bytes 1572872 | tf_op jit(solution)/shard_map/ppermute | solution.py:31
  28.7 4.3 %collective-permute-start.4 = (f32[128,128]{1,0:T(8,128)S(1)}, f32[128,128]{1,0:T(8,128)S(1)}, u32[]{:S(2)}, u32[]{:S(2)}) collective-permute-start(f32[128,128]{1,0:T(8,128)S(1)} %fusion.2), channel_id=1, source_target_pairs={{0,4},{4,0},{8,12},{12,8},{16,20},{20,16},{24,28},{28,24},{1,5},{5... | collective-permute-start | bytes 196616 | tf_op jit(solution)/shard_map/ppermute | solution.py:31
  33.1 4.3 %collective-permute-start.6 = (f32[128,128]{1,0:T(8,128)S(1)}, f32[128,128]{1,0:T(8,128)S(1)}, u32[]{:S(2)}, u32[]{:S(2)}) collective-permute-start(f32[128,128]{1,0:T(8,128)S(1)} %add.62), channel_id=1, source_target_pairs={{0,8},{4,12},{8,0},{12,4},{16,24},{20,28},{24,16},{28,20},{1,9},{5... | collective-permute-start | bytes 196616 | tf_op jit(solution)/shard_map/ppermute | solution.py:31
  40.2 7.1 %collective-permute-start.9 = (f32[1024,128]{1,0:T(8,128)S(1)}, f32[1024,128]{1,0:T(8,128)S(1)}, u32[]{:S(2)}, u32[]{:S(2)}) collective-permute-start(f32[1024,128]{1,0:T(8,128)S(1)} %collective-permute-done.8.part_ref), channel_id=1, source_target_pairs={{0,1},{1,0},{2,3},{3,2},{4,5},{5,4},{6,7},{7,6},{8,9},{9,8},{10,11... | collective-permute-start | bytes 1572872 | tf_op jit(solution)/shard_map/ppermute | solution.py:31
  40.2 7.0 %collective-permute-start.7 = (f32[128,128]{1,0:T(8,128)S(1)}, f32[128,128]{1,0:T(8,128)S(1)}, u32[]{:S(2)}, u32[]{:S(2)}) collective-permute-start(f32[128,128]{1,0:T(8,128)S(1)} %add.63), channel_id=1, source_target_pairs={{0,16},{4,20},{8,24},{12,28},{16,0},{20,4},{24,8},{28,12},{1,17},{... | collective-permute-start | bytes 196616 | tf_op jit(solution)/shard_map/ppermute | solution.py:31
  47.3 1.8 %collective-permute-start.10 = (f32[128,128]{1,0:T(8,128)S(1)}, f32[128,128]{1,0:T(8,128)S(1)}, u32[]{:S(2)}, u32[]{:S(2)}) collective-permute-start(f32[128,128]{1,0:T(8,128)S(1)} %add.64), channel_id=1, source_target_pairs={{0,1},{1,0},{2,3},{3,2},{4,5},{5,4},{6,7},{7,6},{8,9},{9,8},{10,11... | collective-permute-start | bytes 196616 | tf_op jit(solution)/shard_map/ppermute | solution.py:31
  49.1 7.3 %collective-permute-start.11 = (f32[16,1024]{1,0:T(8,128)S(1)}, f32[16,1024]{1,0:T(8,128)S(1)}, u32[]{:S(2)}, u32[]{:S(2)}) collective-permute-start(f32[16,1024]{1,0:T(8,128)S(1)} %get-tuple-element.101), channel_id=1, source_target_pairs={{0,4},{4,0},{8,12},{12,8},{16,20},{20,16},{24,28},{28,24},{1,5},{5... | collective-permute-start | bytes 196616 | tf_op jit(solution)/shard_map/ppermute | solution.py:31
  50.7 7.5 %collective-permute-start.12 = (f32[16,1024]{1,0:T(8,128)S(1)}, f32[16,1024]{1,0:T(8,128)S(1)}, u32[]{:S(2)}, u32[]{:S(2)}) collective-permute-start(f32[16,1024]{1,0:T(8,128)S(1)} %get-tuple-element.102), channel_id=1, source_target_pairs={{0,8},{4,12},{8,0},{12,4},{16,24},{20,28},{24,16},{28,20},{1,9},{5... | collective-permute-start | bytes 196616 | tf_op jit(solution)/shard_map/ppermute | solution.py:31
  51.5 10.3 %collective-permute-start.18 = (f32[128,128]{1,0:T(8,128)S(1)}, f32[128,128]{1,0:T(8,128)S(1)}, u32[]{:S(2)}, u32[]{:S(2)}) collective-permute-start(f32[128,128]{1,0:T(8,128)S(1)} %add.65), channel_id=1, source_target_pairs={{0,2},{1,3},{2,0},{3,1},{4,6},{5,7},{6,4},{7,5},{8,10},{9,11},{10,... | collective-permute-start | bytes 196616 | tf_op jit(solution)/shard_map/ppermute | solution.py:31
  53.1 13.5 %collective-permute-start.13 = (f32[16,1024]{1,0:T(8,128)S(1)}, f32[16,1024]{1,0:T(8,128)S(1)}, u32[]{:S(2)}, u32[]{:S(2)}) collective-permute-start(f32[16,1024]{1,0:T(8,128)S(1)} %get-tuple-element.103), channel_id=1, source_target_pairs={{0,12},{4,8},{8,4},{12,0},{16,28},{20,24},{24,20},{28,16},{1,13},{... | collective-permute-start | bytes 196616 | tf_op jit(solution)/shard_map/ppermute | solution.py:31
  54.3 12.2 %collective-permute-start.14 = (f32[16,1024]{1,0:T(8,128)S(1)}, f32[16,1024]{1,0:T(8,128)S(1)}, u32[]{:S(2)}, u32[]{:S(2)}) collective-permute-start(f32[16,1024]{1,0:T(8,128)S(1)} %get-tuple-element.104), channel_id=1, source_target_pairs={{0,16},{4,20},{8,24},{12,28},{16,0},{20,4},{24,8},{28,12},{1,17},{... | collective-permute-start | bytes 196616 | tf_op jit(solution)/shard_map/ppermute | solution.py:31
  56.5 10.9 %collective-permute-start.15 = (f32[16,1024]{1,0:T(8,128)S(1)}, f32[16,1024]{1,0:T(8,128)S(1)}, u32[]{:S(2)}, u32[]{:S(2)}) collective-permute-start(f32[16,1024]{1,0:T(8,128)S(1)} %get-tuple-element.105), channel_id=1, source_target_pairs={{0,20},{4,16},{8,28},{12,24},{16,4},{20,0},{24,12},{28,8},{1,21},{... | collective-permute-start | bytes 196616 | tf_op jit(solution)/shard_map/ppermute | solution.py:31
  58.2 9.2 %collective-permute-start.16 = (f32[16,1024]{1,0:T(8,128)S(1)}, f32[16,1024]{1,0:T(8,128)S(1)}, u32[]{:S(2)}, u32[]{:S(2)}) collective-permute-start(f32[16,1024]{1,0:T(8,128)S(1)} %get-tuple-element.106), channel_id=1, source_target_pairs={{0,24},{4,28},{8,16},{12,20},{16,8},{20,12},{24,0},{28,4},{1,25},{... | collective-permute-start | bytes 196616 | tf_op jit(solution)/shard_map/ppermute | solution.py:31
  61.7 7.1 %collective-permute-start.17 = (f32[16,1024]{1,0:T(8,128)S(1)}, f32[16,1024]{1,0:T(8,128)S(1)}, u32[]{:S(2)}, u32[]{:S(2)}) collective-permute-start(f32[16,1024]{1,0:T(8,128)S(1)} %get-tuple-element.107), channel_id=1, source_target_pairs={{0,28},{4,24},{8,20},{12,16},{16,12},{20,8},{24,4},{28,0},{1,29},{... | collective-permute-start | bytes 196616 | tf_op jit(solution)/shard_map/ppermute | solution.py:31
  68.8 7.9 %collective-permute-start.25 = (f32[16,1024]{1,0:T(8,128)S(1)}, f32[16,1024]{1,0:T(8,128)S(1)}, u32[]{:S(2)}, u32[]{:S(2)}) collective-permute-start(f32[16,1024]{1,0:T(8,128)S(1)} %add_add_fusion.refs_0_), channel_id=1, source_target_pairs={{0,28},{4,24},{8,20},{12,16},{16,12},{20,8},{24,4},{28,0},{1,29},{... | collective-permute-start | bytes 196616 | tf_op jit(solution)/shard_map/ppermute | solution.py:31
  71.2 9.6 %collective-permute-start.24 = (f32[16,1024]{1,0:T(8,128)S(1)}, f32[16,1024]{1,0:T(8,128)S(1)}, u32[]{:S(2)}, u32[]{:S(2)}) collective-permute-start(f32[16,1024]{1,0:T(8,128)S(1)} %add_add_fusion.refs_0_), channel_id=1, source_target_pairs={{0,24},{4,28},{8,16},{12,20},{16,8},{20,12},{24,0},{28,4},{1,25},{... | collective-permute-start | bytes 196616 | tf_op jit(solution)/shard_map/ppermute | solution.py:31
  72.7 12.8 %collective-permute-start.23 = (f32[16,1024]{1,0:T(8,128)S(1)}, f32[16,1024]{1,0:T(8,128)S(1)}, u32[]{:S(2)}, u32[]{:S(2)}) collective-permute-start(f32[16,1024]{1,0:T(8,128)S(1)} %add_add_fusion.refs_0_), channel_id=1, source_target_pairs={{0,20},{4,16},{8,28},{12,24},{16,4},{20,0},{24,12},{28,8},{1,21},{... | collective-permute-start | bytes 196616 | tf_op jit(solution)/shard_map/ppermute | solution.py:31
  74.7 10.8 %collective-permute-start.22 = (f32[16,1024]{1,0:T(8,128)S(1)}, f32[16,1024]{1,0:T(8,128)S(1)}, u32[]{:S(2)}, u32[]{:S(2)}) collective-permute-start(f32[16,1024]{1,0:T(8,128)S(1)} %add_add_fusion.refs_0_), channel_id=1, source_target_pairs={{0,16},{4,20},{8,24},{12,28},{16,0},{20,4},{24,8},{28,12},{1,17},{... | collective-permute-start | bytes 196616 | tf_op jit(solution)/shard_map/ppermute | solution.py:31
  76.6 9.0 %collective-permute-start.21 = (f32[16,1024]{1,0:T(8,128)S(1)}, f32[16,1024]{1,0:T(8,128)S(1)}, u32[]{:S(2)}, u32[]{:S(2)}) collective-permute-start(f32[16,1024]{1,0:T(8,128)S(1)} %add_add_fusion.refs_0_), channel_id=1, source_target_pairs={{0,12},{4,8},{8,4},{12,0},{16,28},{20,24},{24,20},{28,16},{1,13},{... | collective-permute-start | bytes 196616 | tf_op jit(solution)/shard_map/ppermute | solution.py:31
  76.7 8.9 %collective-permute-start.20 = (f32[16,1024]{1,0:T(8,128)S(1)}, f32[16,1024]{1,0:T(8,128)S(1)}, u32[]{:S(2)}, u32[]{:S(2)}) collective-permute-start(f32[16,1024]{1,0:T(8,128)S(1)} %add_add_fusion.refs_0_), channel_id=1, source_target_pairs={{0,8},{4,12},{8,0},{12,4},{16,24},{20,28},{24,16},{28,20},{1,9},{5... | collective-permute-start | bytes 196616 | tf_op jit(solution)/shard_map/ppermute | solution.py:31
  80.7 4.8 %collective-permute-start.19 = (f32[16,1024]{1,0:T(8,128)S(1)}, f32[16,1024]{1,0:T(8,128)S(1)}, u32[]{:S(2)}, u32[]{:S(2)}) collective-permute-start(f32[16,1024]{1,0:T(8,128)S(1)} %add_add_fusion.refs_0_), channel_id=1, source_target_pairs={{0,4},{4,0},{8,12},{12,8},{16,20},{20,16},{24,28},{28,24},{1,5},{5... | collective-permute-start | bytes 196616 | tf_op jit(solution)/shard_map/ppermute | solution.py:31
  87.9 3.5 %collective-permute-start.28 = (f32[128,128]{1,0:T(8,128)S(1)}, f32[128,128]{1,0:T(8,128)S(1)}, u32[]{:S(2)}, u32[]{:S(2)}) collective-permute-start(f32[128,128]{1,0:T(8,128)S(1)} %get-tuple-element.127), channel_id=1, source_target_pairs={{0,1},{1,0},{2,3},{3,2},{4,5},{5,4},{6,7},{7,6},{8,9},{9,8},{10,11... | collective-permute-start | bytes 196616 | tf_op jit(solution)/shard_map/ppermute | solution.py:31
  87.9 3.7 %collective-permute-start.27 = (f32[128,128]{1,0:T(8,128)S(1)}, f32[128,128]{1,0:T(8,128)S(1)}, u32[]{:S(2)}, u32[]{:S(2)}) collective-permute-start(f32[128,128]{1,0:T(8,128)S(1)} %get-tuple-element.127), channel_id=1, source_target_pairs={{0,3},{1,2},{2,1},{3,0},{4,7},{5,6},{6,5},{7,4},{8,11},{9,10},{10,... | collective-permute-start | bytes 196616 | tf_op jit(solution)/shard_map/ppermute | solution.py:31
  88.5 5.2 %collective-permute-start.26 = (f32[128,128]{1,0:T(8,128)S(1)}, f32[128,128]{1,0:T(8,128)S(1)}, u32[]{:S(2)}, u32[]{:S(2)}) collective-permute-start(f32[128,128]{1,0:T(8,128)S(1)} %get-tuple-element.127), channel_id=1, source_target_pairs={{0,2},{1,3},{2,0},{3,1},{4,6},{5,7},{6,4},{7,5},{8,10},{9,11},{10,... | collective-permute-start | bytes 196616 | tf_op jit(solution)/shard_map/ppermute | solution.py:31

commit v8 on v7

--- a/solution.py
+++ b/solution.py
@@ -13,6 +13,8 @@
 
 PIECE = 512
 TILE = 256
+RUN = 128
+SLICES = 8
 SMEM = pl.BlockSpec(memory_space=pltpu.SMEM)
 VMEM = pl.BlockSpec(memory_space=pltpu.VMEM)
 HBM = pl.BlockSpec(memory_space=pltpu.HBM)
@@ -52,17 +54,13 @@
     quarter, cols = held[0].shape
     copies = {}
     for k, place in enumerate(places):
-        for row in range(0, quarter, PIECE):
-            at = pl.multiple_of((own_ref[0] ^ place) * quarter + row, PIECE)
-            for t in range(cols // TILE):
-                tile = pl.ds(t * TILE, TILE)
-                copy = pltpu.make_async_copy(
-                    data_ref.at[pl.ds(at, PIECE), tile],
-                    held[k].at[pl.ds(row, PIECE), tile],
-                    sems.at[k, row // PIECE, t],
-                )
-                copy.start()
-                copies[k, row, t] = copy
+        for row in range(0, quarter, RUN):
+            at = pl.multiple_of((own_ref[0] ^ place) * quarter + row, RUN)
+            copy = pltpu.make_async_copy(
+                data_ref.at[pl.ds(at, RUN)], held[k].at[pl.ds(row, RUN)], sems.at[k, row // RUN]
+            )
+            copy.start()
+            copies[k, row] = copy
     if first:
         width = omega_ref.shape[1]
         wide = refs[2 * count]
@@ -73,14 +71,16 @@
     else:
         wide = omega_ref
         width = omega_ref.shape[1] // 2
-    for (k, row, t), copy in copies.items():
-        tile = slice(t * TILE, (t + 1) * TILE)
-        copy.wait()
-        upper, rest = split(held[k][row : row + PIECE, tile])
-        one = jnp.dot(upper, wide[tile, :], preferred_element_type=f32)
-        two = jnp.dot(rest, wide[tile, :width], preferred_element_type=f32)
-        both, more = (one, two) if t == 0 else (both + one, more + two)
-        if t == cols // TILE - 1:
+    for k in range(count):
+        for row in range(0, quarter, PIECE):
+            for run in range(row, row + PIECE, RUN):
+                copies[k, run].wait()
+            for t in range(cols // TILE):
+                tile = slice(t * TILE, (t + 1) * TILE)
+                upper, rest = split(held[k][row : row + PIECE, tile])
+                one = jnp.dot(upper, wide[tile, :], preferred_element_type=f32)
+                two = jnp.dot(rest, wide[tile, :width], preferred_element_type=f32)
+                both, more = (one, two) if t == 0 else (both + one, more + two)
             outs[k][row : row + PIECE] = both[:, :width] + both[:, width:] + more
 
 
@@ -91,7 +91,7 @@
     count = len(places)
     out = [jax.ShapeDtypeStruct((quarter, width), f32)] * count
     out += [pltpu.VMEM((quarter, cols), f32)] * count
-    scratch = [pltpu.SemaphoreType.DMA((count, quarter // PIECE, cols // TILE))]
+    scratch = [pltpu.SemaphoreType.DMA((count, quarter // RUN))]
     if first:
         out.append(jax.ShapeDtypeStruct((cols, 2 * width), bf16))
         scratch += [pltpu.VMEM(omega.shape, f32), pltpu.SemaphoreType.DMA]
@@ -126,10 +126,11 @@
                 value += old[:, tile]
             total[:, tile] = value
     if slices:
-        step = outs[0].shape[0]
-        for place, ref in enumerate(outs):
+        step = total.shape[0] // slices
+        for place in range(slices):
             at = pl.multiple_of((place ^ own_ref[1]) * step, step)
-            ref[...] = total[pl.ds(at, step)]
+            row = place // 2 * step
+            outs[1 - place % 2][row : row + step] = total[pl.ds(at, step)]
 
 
 def project(own, rows, part, before=None, slices=0):
@@ -137,7 +138,7 @@
     width = part.shape[1]
     args = [own, rows, part] + ([] if before is None else [before])
     if slices:
-        out = [jax.ShapeDtypeStruct((width // slices, cols), f32)] * slices
+        out = [jax.ShapeDtypeStruct((width // 2, cols), f32)] * 2
     else:
         out = [jax.ShapeDtypeStruct((width, cols), f32)]
     return pl.pallas_call(
@@ -191,10 +192,20 @@
             r_panel = jnp.where(sub == i, right[i], r_panel)
         work[top, n:] = r_panel
         if b < panels - 1:
+            rows = slice(8 * b + 8, 8 * b + 16)
+            l_next, r_next = work[rows, :n], work[rows, n:]
+            column = l_panel.T[rows, :]
+            for j in range(8):
+                factors = jnp.broadcast_to(column[:, j : j + 1], (8, n))
+                l_next = l_next - factors * left[j]
+                r_next = r_next - factors * right[j]
+            work[rows, :n] = l_next
+            work[rows, n:] = r_next
+        if b < panels - 2:
             done = jnp.concatenate([l_panel, r_panel], 1)
             change = dot(l_panel, done, 0, 0)
-            below = slice(8 * b + 8, n)
-            work[below, :] = work[below, :] - change[8 * b + 8 :, :]
+            below = slice(8 * b + 16, n)
+            work[below, :] = work[below, :] - change[8 * b + 16 :, :]
     if last:
         out_ref[...] = work[:, n:]
 
@@ -216,10 +227,11 @@
 
 def finish_kernel(own_ref, inverse_ref, *refs):
     parts, (out_ref, gram_ref, total) = refs[:-3], refs[-3:]
-    step = parts[0].shape[0]
-    for place, ref in enumerate(parts):
+    step = total.shape[0] // SLICES
+    for place in range(SLICES):
         at = pl.multiple_of((place ^ own_ref[1]) * step, step)
-        total[pl.ds(at, step)] = ref[...]
+        row = place // 2 * step
+        total[pl.ds(at, step)] = parts[place % 2][row : row + step]
     value = jnp.dot(inverse_ref[...], total[...], precision=full, preferred_element_type=f32)
     out_ref[...] = value
     gram_ref[...] = dot(value, value, 1, 1)
@@ -274,32 +286,36 @@
     far, acc = fence((far, acc))
     gram = gram + far
     far = swap(gram, "row", bits[2])
-    third, acc = fence((third, acc))
+    third, acc, far = fence((third, acc, far))
     fourth = swap(third, "col", 1)
     (acc,) = project(own, rows2, third, acc)
-    far, acc, fourth = fence((far, acc, fourth))
+    acc, fourth = fence((acc, fourth))
     gram = gram + far
     for bit in bits[3:]:
         gram = gram + swap(gram, "row", bit)
     far = swap(gram, "col", 1)
-    slices = project(own, rows3, fourth, acc, 8)
-    far, *slices = fence((far, *slices))
+    send, keep = project(own, rows3, fourth, acc, SLICES)
+    far, send, keep = fence((far, send, keep))
     gram = gram + far
 
-    state = factor(0, 2, gram + swap(gram, "col", 2))
-    got = [swap(slices[q], "row", q) for q in range(1, 8)]
-    *got, state = fence((*got, state))
-    mine = ((slices[0] + got[0]) + (got[1] + got[2])) + ((got[3] + got[4]) + (got[5] + got[6]))
+    got, state = fence((swap(send, "row", 1), factor(0, 3, gram + swap(gram, "col", 2))))
+    step = keep.shape[0] // 4
+    quads = [keep[i * step : (i + 1) * step] + got[i * step : (i + 1) * step] for i in range(4)]
+    *quads, state = fence((*quads, state))
+    got = [swap(quads[i], "row", 2 * i) for i in (1, 2, 3)]
+    *got, state = fence((*got, factor(1, 3, state)))
+    mine = (quads[0] + got[0]) + (got[1] + got[2])
     for bit in bits[3:]:
         mine = mine + swap(mine, "row", bit)
     mine, state = fence((mine, state))
-    inverse = factor(1, 2, state)
-    got = [swap(mine, "row", q) for q in range(1, 8)]
-    *got, inverse = fence((*got, inverse))
-    projected, small = finish(own, inverse, [mine, *got])
+    got = [swap(mine, "row", 2 * i) for i in (1, 2, 3)]
+    *got, inverse = fence((*got, factor(2, 3, state)))
+    keep = jnp.concatenate([mine, *got], 0)
+    keep, inverse = fence((keep, inverse))
+    got, basis = fence((swap(keep, "row", 1), dot(sketched, inverse, 1, 1)))
+    projected, small = finish(own, inverse, [keep, got])
 
     across = [swap(small, "col", bit) for bit in (2, 3, 1)]
-    *across, basis = fence((*across, dot(sketched, inverse, 1, 1)))
     small = (small + across[2]) + (across[0] + across[1])
     return (basis, projected, small / total_rows)
 

time: 94.5 us -> 86.8 us (0.919)
  starting transfers between devices: 39.2 us -> 26.8 us
  waiting for transfers between devices: 17.3 us -> 27.1 us
  Pallas kernels: 33.6 us -> 28.5 us
    ppermute x29 -> x23, starting transfers between devices: 39.2 us -> 26.8 us  [swap(): lax.ppermute(value, axis, [(i, i ^ bit) for i in range(lax.axis_size(axis...]
    ppermute x29 -> x23, waiting for transfers between devices: 17.3 us -> 27.1 us  [swap(): lax.ppermute(value, axis, [(i, i ^ bit) for i in range(lax.axis_size(axis...]
    pallas_call x3, Pallas kernels: 15.6 us -> 13 us  [sketch(): pl.pallas_call(functools.partial(sketch_kernel, places, first), in_specs=...]
    pallas_call x2 -> x3, Pallas kernels: 8.71 us -> 6.38 us  [factor(): pl.pallas_call(functools.partial(factor_kernel, index, count), in_specs=[...]
  transfers between devices with their start and end apart: 29 -> 23, of which waited for: 11 -> 15; matrix products, arithmetic and copies ran while one was open for 3% -> 3% of each run, Pallas kernels for 28% -> 25%
where the time goes in v8:
time: 86.8 us; the launch traced here: 86.6 us
  Pallas kernels  28.5 us (33%)
  waiting for transfers between devices  27.1 us (31%)
  starting transfers between devices  26.8 us (31%)
  matrix products  2.4 us (3%)
  other arithmetic  0.98 us (1%)
    ppermute x23, waiting for transfers between devices, swap(): lax.ppermute(value, axis, [(i, i ^ bit) for i in range(lax.axis_size(axis...  27.1 us
    ppermute x23, starting transfers between devices, swap(): lax.ppermute(value, axis, [(i, i ^ bit) for i in range(lax.axis_size(axis...  26.8 us
    pallas_call x3, Pallas kernels, sketch(): pl.pallas_call(functools.partial(sketch_kernel, places, first), in_specs=...  13 us
    pallas_call x4, Pallas kernels, project(): pl.pallas_call(functools.partial(project_kernel, before is not None, slic...  6.82 us
    pallas_call x3, Pallas kernels, factor(): pl.pallas_call(functools.partial(factor_kernel, index, count), in_specs=[...  6.38 us
    dot_general x2, matrix products, dot(): lax.dot_general(a, b, (((a_dim,), (b_dim,)), ((), ())), precision=precisi...  2.4 us
    pallas_call x1, Pallas kernels, finish(): pl.pallas_call(finish_kernel, in_specs=[SMEM] + [VMEM] * (1 + len(parts))...  2.3 us
  transfers between devices with their start and end apart: 23, of which 15 were waited for; matrix products, arithmetic and copies ran while one was open for 3% of the time, Pallas kernels for 25%

profile of v8, /device:TPU:0, one launch (start us, length us, event | category | flops | bytes accessed | tf_op | source)
XLA Modules:
  0.0 86.6 jit_solution(13358160327548870086)
XLA Ops:
  0.7 4.3 %partial_sketch.3 = (f32[1024,128]{1,0:T(8,128)S(1)}, f32[1024,1024]{1,0:T(8,128)S(1)}, bf16[1024,256]{1,0:T(8,128)(2,1)S(1)}) custom-call(s32[2]{0:T(128)S(1)} %pad_add_fusion.own_ref, f32[4096,1024]{1,0:T(8,128)} %data_ref.5, f32[1024,128]{1,0:T(8,128)} %omega_ref.1), custom_call_target="tpu_custom_call" | custom-call | flops 1 | bytes 10485 | tf_op jit(solution)/shard_map/partial_sketch/pallas_call | solution.py:98
  5.6 3.6 %partial_sketch.4 = (f32[1024,128]{1,0:T(8,128)S(1)}, f32[1024,1024]{1,0:T(8,128)S(1)}) custom-call(s32[2]{0:T(128)S(1)} %pad_add_fusion.own_ref, f32[4096,1024]{1,0:T(8,128)} %data_ref.5, bf16[1024,256]{1,0:T(8,128)(2,1)S(1)} %get-tuple-element.58.omega_ref), custom_call_target="tpu_custom_call" | custom-call | flops 1 | bytes 10485 | tf_op jit(solution)/shard_map/partial_sketch/pallas_call | solution.py:98
  9.2 2.6 %collective-permute-start.3 = (f32[1024,128]{1,0:T(8,128)S(1)}, f32[1024,128]{1,0:T(8,128)S(1)}, u32[]{:S(2)}, u32[]{:S(2)}) collective-permute-start(f32[1024,128]{1,0:T(8,128)S(1)} %add.59), channel_id=1, source_target_pairs={{0,2},{1,3},{2,0},{3,1},{4,6},{5,7},{6,4},{7,5},{8,10},{9,11},{10,... | collective-permute-start | bytes 1572872 | tf_op jit(solution)/shard_map/ppermute | solution.py:33
  11.8 5.1 %partial_sketch.5 = (f32[1024,128]{1,0:T(8,128)S(1)}, f32[1024,128]{1,0:T(8,128)S(1)}, f32[1024,1024]{1,0:T(8,128)S(1)}, f32[1024,1024]{1,0:T(8,128)S(1)}) custom-call(s32[2]{0:T(128)S(1)} %pad_add_fusion.own_ref, f32[4096,1024]{1,0:T(8,128)} %data_ref.5, bf16[1024,256]{1,0:T(8,128)(2,1)S(1)} %get-tuple-element.58.omega_ref), custom_call_target="tpu_custom_call" | custom-call | flops 1 | bytes 10485 | tf_op jit(solution)/shard_map/partial_sketch/pallas_call | solution.py:98
  19.0 5.4 %collective-permute-done.3 = f32[1024,128]{1,0:T(8,128)S(1)} collective-permute-done((f32[1024,128]{1,0:T(8,128)S(1)}, f32[1024,128]{1,0:T(8,128)S(1)}, u32[]{:S(2)}, u32[]{:S(2)}) %collective-permute-start.3) | collective-permute-done | bytes 524320 | tf_op jit(solution)/shard_map/ppermute | solution.py:33
  24.6 1.8 %collective-permute-start.7 = (f32[1024,128]{1,0:T(8,128)S(1)}, f32[1024,128]{1,0:T(8,128)S(1)}, u32[]{:S(2)}, u32[]{:S(2)}) collective-permute-start(f32[1024,128]{1,0:T(8,128)S(1)} %fusion.part_ref), channel_id=1, source_target_pairs={{0,2},{1,3},{2,0},{3,1},{4,6},{5,7},{6,4},{7,5},{8,10},{9,11},{10,... | collective-permute-start | bytes 1572872 | tf_op jit(solution)/shard_map/ppermute | solution.py:33
  27.4 1.6 %collective-permute-start.4 = (f32[128,128]{1,0:T(8,128)S(1)}, f32[128,128]{1,0:T(8,128)S(1)}, u32[]{:S(2)}, u32[]{:S(2)}) collective-permute-start(f32[128,128]{1,0:T(8,128)S(1)} %fusion.2), channel_id=1, source_target_pairs={{0,4},{4,0},{8,12},{12,8},{16,20},{20,16},{24,28},{28,24},{1,5},{5... | collective-permute-start | bytes 196616 | tf_op jit(solution)/shard_map/ppermute | solution.py:33
  29.0 1.7 %project.4.refs_0_ = f32[128,1024]{1,0:T(8,128)S(1)} custom-call(s32[2]{0:T(128)S(1)} %pad_add_fusion.own_ref, f32[1024,1024]{1,0:T(8,128)S(1)} %get-tuple-element.65.rows_ref, f32[1024,128]{1,0:T(8,128)S(1)} %fusion.part_ref), custom_call_target="tpu_custom_call" | custom-call | flops 1 | bytes 6291456 | tf_op jit(solution)/shard_map/project/pallas_call | solution.py:144
  30.7 1.1 %collective-permute-done.4 = f32[128,128]{1,0:T(8,128)S(1)} collective-permute-done((f32[128,128]{1,0:T(8,128)S(1)}, f32[128,128]{1,0:T(8,128)S(1)}, u32[]{:S(2)}, u32[]{:S(2)}) %collective-permute-start.4) | collective-permute-done | bytes 65568 | tf_op jit(solution)/shard_map/ppermute | solution.py:33
  31.8 1.6 %collective-permute-start.6 = (f32[128,128]{1,0:T(8,128)S(1)}, f32[128,128]{1,0:T(8,128)S(1)}, u32[]{:S(2)}, u32[]{:S(2)}) collective-permute-start(f32[128,128]{1,0:T(8,128)S(1)} %add.62), channel_id=1, source_target_pairs={{0,8},{4,12},{8,0},{12,4},{16,24},{20,28},{24,16},{28,20},{1,9},{5... | collective-permute-start | bytes 196616 | tf_op jit(solution)/shard_map/ppermute | solution.py:33
  33.4 1.7 %project.5.refs_0_ = f32[128,1024]{1,0:T(8,128)S(1)} custom-call(s32[2]{0:T(128)S(1)} %pad_add_fusion.own_ref, f32[1024,1024]{1,0:T(8,128)S(1)} %get-tuple-element.67.rows_ref, f32[1024,128]{1,0:T(8,128)S(1)} %collective-permute-done.5.part_ref, f32[128,1024]{1,0:T(8,128)S(1)} %project.4.refs_0_), custom_call_target="tpu_custom_call" | custom-call | flops 1 | bytes 6291456 | tf_op jit(solution)/shard_map/project/pallas_call | solution.py:144
  36.1 2.7 %collective-permute-start.8 = (f32[128,128]{1,0:T(8,128)S(1)}, f32[128,128]{1,0:T(8,128)S(1)}, u32[]{:S(2)}, u32[]{:S(2)}) collective-permute-start(f32[128,128]{1,0:T(8,128)S(1)} %add.63), channel_id=1, source_target_pairs={{0,16},{4,20},{8,24},{12,28},{16,0},{20,4},{24,8},{28,12},{1,17},{... | collective-permute-start | bytes 196616 | tf_op jit(solution)/shard_map/ppermute | solution.py:33
  38.9 2.4 %collective-permute-done.8 = f32[128,128]{1,0:T(8,128)S(1)} collective-permute-done((f32[128,128]{1,0:T(8,128)S(1)}, f32[128,128]{1,0:T(8,128)S(1)}, u32[]{:S(2)}, u32[]{:S(2)}) %collective-permute-start.8) | collective-permute-done | bytes 65568 | tf_op jit(solution)/shard_map/ppermute | solution.py:33
  41.9 1.7 %project.6.refs_0_ = f32[128,1024]{1,0:T(8,128)S(1)} custom-call(s32[2]{0:T(128)S(1)} %pad_add_fusion.own_ref, f32[1024,1024]{1,0:T(8,128)S(1)} %get-tuple-element.74.rows_ref, f32[1024,128]{1,0:T(8,128)S(1)} %collective-permute-done.7.part_ref, f32[128,1024]{1,0:T(8,128)S(1)} %project.5.refs_0_), custom_call_target="tpu_custom_call" | custom-call | flops 1 | bytes 6291456 | tf_op jit(solution)/shard_map/project/pallas_call | solution.py:144
  43.6 1.7 %project.7 = (f32[64,1024]{1,0:T(8,128)S(1)}, f32[64,1024]{1,0:T(8,128)S(1)}) custom-call(s32[2]{0:T(128)S(1)} %pad_add_fusion.own_ref, f32[1024,1024]{1,0:T(8,128)S(1)} %get-tuple-element.73.rows_ref, f32[1024,128]{1,0:T(8,128)S(1)} %collective-permute-done.10.part_ref, f32[128,1024]{1,0:T(8,128)S(1)} %project.6.refs_0_), custom_call_target="tpu_custom_call" | custom-call | flops 1 | bytes 6291456 | tf_op jit(solution)/shard_map/project/pallas_call | solution.py:144
  45.4 1.6 %collective-permute-start.11 = (f32[64,1024]{1,0:T(8,128)S(1)}, f32[64,1024]{1,0:T(8,128)S(1)}, u32[]{:S(2)}, u32[]{:S(2)}) collective-permute-start(f32[64,1024]{1,0:T(8,128)S(1)} %get-tuple-element.82), channel_id=1, source_target_pairs={{0,4},{4,0},{8,12},{12,8},{16,20},{20,16},{24,28},{28,24},{1,5},{5... | collective-permute-start | bytes 786440 | tf_op jit(solution)/shard_map/ppermute | solution.py:33
  47.5 3.8 %collective-permute-done.12 = f32[128,128]{1,0:T(8,128)S(1)} collective-permute-done((f32[128,128]{1,0:T(8,128)S(1)}, f32[128,128]{1,0:T(8,128)S(1)}, u32[]{:S(2)}, u32[]{:S(2)}) %collective-permute-start.12) | collective-permute-done | bytes 65568 | tf_op jit(solution)/shard_map/ppermute | solution.py:33
  51.3 2.2 %factor.3.in_ref = f32[128,256]{1,0:T(8,128)S(1)} custom-call(f32[128,128]{1,0:T(8,128)S(1)} %add.66.in_ref), custom_call_target="tpu_custom_call" | custom-call | flops 1 | bytes 10485 | tf_op jit(solution)/shard_map/factor/pallas_call | solution.py:216
  53.7 1.6 %collective-permute-start.13 = (f32[16,1024]{1,0:T(8,128)S(1)}, f32[16,1024]{1,0:T(8,128)S(1)}, u32[]{:S(2)}, u32[]{:S(2)}) collective-permute-start(f32[16,1024]{1,0:T(8,128)S(1)} %get-tuple-element.87), channel_id=1, source_target_pairs={{0,8},{4,12},{8,0},{12,4},{16,24},{20,28},{24,16},{28,20},{1,9},{5... | collective-permute-start | bytes 196616 | tf_op jit(solution)/shard_map/ppermute | solution.py:33
  55.4 3.2 %collective-permute-start.14 = (f32[16,1024]{1,0:T(8,128)S(1)}, f32[16,1024]{1,0:T(8,128)S(1)}, u32[]{:S(2)}, u32[]{:S(2)}) collective-permute-start(f32[16,1024]{1,0:T(8,128)S(1)} %get-tuple-element.88), channel_id=1, source_target_pairs={{0,16},{4,20},{8,24},{12,28},{16,0},{20,4},{24,8},{28,12},{1,17},{... | collective-permute-start | bytes 196616 | tf_op jit(solution)/shard_map/ppermute | solution.py:33
  58.6 2.1 %factor.4.in_ref = f32[128,256]{1,0:T(8,128)S(1)} custom-call(f32[128,256]{1,0:T(8,128)S(1)} %factor.3.in_ref), custom_call_target="tpu_custom_call" | custom-call | flops 1 | bytes 10485 | tf_op jit(solution)/shard_map/factor/pallas_call | solution.py:216
  60.6 1.9 %collective-permute-done.14 = f32[16,1024]{1,0:T(8,128)S(1)} collective-permute-done((f32[16,1024]{1,0:T(8,128)S(1)}, f32[16,1024]{1,0:T(8,128)S(1)}, u32[]{:S(2)}, u32[]{:S(2)}) %collective-permute-start.14) | collective-permute-done | bytes 65568 | tf_op jit(solution)/shard_map/ppermute | solution.py:33
  62.5 2.2 %collective-permute-done.15 = f32[16,1024]{1,0:T(8,128)S(1)} collective-permute-done((f32[16,1024]{1,0:T(8,128)S(1)}, f32[16,1024]{1,0:T(8,128)S(1)}, u32[]{:S(2)}, u32[]{:S(2)}) %collective-permute-start.15) | collective-permute-done | bytes 65568 | tf_op jit(solution)/shard_map/ppermute | solution.py:33
  65.7 3.5 %collective-permute-start.16 = (f32[16,1024]{1,0:T(8,128)S(1)}, f32[16,1024]{1,0:T(8,128)S(1)}, u32[]{:S(2)}, u32[]{:S(2)}) collective-permute-start(f32[16,1024]{1,0:T(8,128)S(1)} %add_add_fusion), channel_id=1, source_target_pairs={{0,8},{4,12},{8,0},{12,4},{16,24},{20,28},{24,16},{28,20},{1,9},{5... | collective-permute-start | bytes 196616 | tf_op jit(solution)/shard_map/ppermute | solution.py:33
  69.2 2.1 %factor.5.inverse_ref = f32[128,128]{1,0:T(8,128)S(1)} custom-call(f32[128,256]{1,0:T(8,128)S(1)} %factor.4.in_ref), custom_call_target="tpu_custom_call" | custom-call | flops 1 | bytes 10485 | tf_op jit(solution)/shard_map/factor/pallas_call | solution.py:216
  72.3 1.6 %collective-permute-start.19 = (f32[64,1024]{1,0:T(8,128)S(1)}, f32[64,1024]{1,0:T(8,128)S(1)}, u32[]{:S(2)}, u32[]{:S(2)}) collective-permute-start(f32[64,1024]{1,0:T(8,128)S(1)} %pad_maximum_fusion.refs_0_), channel_id=1, source_target_pairs={{0,4},{4,0},{8,12},{12,8},{16,20},{20,16},{24,28},{28,24},{1,5},{5... | collective-permute-start | bytes 786440 | tf_op jit(solution)/shard_map/ppermute | solution.py:33
  73.9 1.4 %fusion.3 = f32[1024,128]{1,0:T(8,128)} fusion(f32[1024,128]{1,0:T(8,128)S(1)} %fusion.part_ref, f32[128,128]{1,0:T(8,128)S(1)} %factor.5.inverse_ref), kind=kOutput, calls=%fused_computation.12 | convolution fusion | flops 201326592 | bytes 1114112 | tf_op jit(solution)/shard_map/dot_general | solution.py:37
  75.2 3.5 %collective-permute-done.19.refs_1_ = f32[64,1024]{1,0:T(8,128)S(1)} collective-permute-done((f32[64,1024]{1,0:T(8,128)S(1)}, f32[64,1024]{1,0:T(8,128)S(1)}, u32[]{:S(2)}, u32[]{:S(2)}) %collective-permute-start.19) | collective-permute-done | bytes 262176 | tf_op jit(solution)/shard_map/ppermute | solution.py:33
  78.7 2.3 %finish.1 = (f32[128,1024]{1,0:T(8,128)}, f32[128,128]{1,0:T(8,128)S(1)}) custom-call(s32[2]{0:T(128)S(1)} %pad_add_fusion.own_ref, f32[128,128]{1,0:T(8,128)S(1)} %factor.5.inverse_ref, f32[64,1024]{1,0:T(8,128)S(1)} %pad_maximum_fusion.refs_0_, f32[64,1024]{1,0:T(8,128)S(1)} %collective-permute-done.19.refs_1_), custom_call_target="tpu_custom_call" | custom-call | flops 1 | bytes 8388608 | tf_op jit(solution)/shard_map/finish/pallas_call | solution.py:243
  81.6 1.3 %collective-permute-start.20 = (f32[128,128]{1,0:T(8,128)S(1)}, f32[128,128]{1,0:T(8,128)S(1)}, u32[]{:S(2)}, u32[]{:S(2)}) collective-permute-start(f32[128,128]{1,0:T(8,128)S(1)} %get-tuple-element.106), channel_id=1, source_target_pairs={{0,1},{1,0},{2,3},{3,2},{4,5},{5,4},{6,7},{7,6},{8,9},{9,8},{10,11... | collective-permute-start | bytes 196616 | tf_op jit(solution)/shard_map/ppermute | solution.py:33
  82.9 2.0 %collective-permute-done.22 = f32[128,128]{1,0:T(8,128)S(1)} collective-permute-done((f32[128,128]{1,0:T(8,128)S(1)}, f32[128,128]{1,0:T(8,128)S(1)}, u32[]{:S(2)}, u32[]{:S(2)}) %collective-permute-start.22) | collective-permute-done | bytes 65568 | tf_op jit(solution)/shard_map/ppermute | solution.py:33
  84.9 1.1 %collective-permute-done.21 = f32[128,128]{1,0:T(8,128)S(1)} collective-permute-done((f32[128,128]{1,0:T(8,128)S(1)}, f32[128,128]{1,0:T(8,128)S(1)}, u32[]{:S(2)}, u32[]{:S(2)}) %collective-permute-start.21) | collective-permute-done | bytes 65568 | tf_op jit(solution)/shard_map/ppermute | solution.py:33
  (40 shorter events, 9.6 us)
Async XLA Ops:
  5.1 4.1 %collective-permute-start = (f32[1024,128]{1,0:T(8,128)S(1)}, f32[1024,128]{1,0:T(8,128)S(1)}, u32[]{:S(2)}, u32[]{:S(2)}) collective-permute-start(f32[1024,128]{1,0:T(8,128)S(1)} %get-tuple-element.57), channel_id=1, source_target_pairs={{0,1},{1,0},{2,3},{3,2},{4,5},{5,4},{6,7},{7,6},{8,9},{9,8},{10,11... | collective-permute-start | bytes 1572872 | tf_op jit(solution)/shard_map/ppermute | solution.py:33
  9.2 15.2 %collective-permute-start.3 = (f32[1024,128]{1,0:T(8,128)S(1)}, f32[1024,128]{1,0:T(8,128)S(1)}, u32[]{:S(2)}, u32[]{:S(2)}) collective-permute-start(f32[1024,128]{1,0:T(8,128)S(1)} %add.59), channel_id=1, source_target_pairs={{0,2},{1,3},{2,0},{3,1},{4,6},{5,7},{6,4},{7,5},{8,10},{9,11},{10,... | collective-permute-start | bytes 1572872 | tf_op jit(solution)/shard_map/ppermute | solution.py:33
  17.0 1.6 %collective-permute-start.2 = (f32[512,128]{1,0:T(8,128)S(1)}, f32[512,128]{1,0:T(8,128)S(1)}, u32[]{:S(2)}, u32[]{:S(2)}) collective-permute-start(f32[512,128]{1,0:T(8,128)S(1)} %get-tuple-element.111), channel_id=1, source_target_pairs={{0,1},{1,0},{2,3},{3,2},{4,5},{5,4},{6,7},{7,6},{8,9},{9,8},{10,11... | collective-permute-start | bytes 786440 | tf_op jit(solution)/shard_map/ppermute | solution.py:33
  17.3 1.7 %collective-permute-start.1 = (f32[512,128]{1,0:T(8,128)S(1)}, f32[512,128]{1,0:T(8,128)S(1)}, u32[]{:S(2)}, u32[]{:S(2)}) collective-permute-start(f32[512,128]{1,0:T(8,128)S(1)} %get-tuple-element.112), channel_id=1, source_target_pairs={{0,1},{1,0},{2,3},{3,2},{4,5},{5,4},{6,7},{7,6},{8,9},{9,8},{10,11... | collective-permute-start | bytes 786440 | tf_op jit(solution)/shard_map/ppermute | solution.py:33
  24.5 7.2 %collective-permute-start.5 = (f32[1024,128]{1,0:T(8,128)S(1)}, f32[1024,128]{1,0:T(8,128)S(1)}, u32[]{:S(2)}, u32[]{:S(2)}) collective-permute-start(f32[1024,128]{1,0:T(8,128)S(1)} %fusion.part_ref), channel_id=1, source_target_pairs={{0,1},{1,0},{2,3},{3,2},{4,5},{5,4},{6,7},{7,6},{8,9},{9,8},{10,11... | collective-permute-start | bytes 1572872 | tf_op jit(solution)/shard_map/ppermute | solution.py:33
  24.6 14.3 %collective-permute-start.7 = (f32[1024,128]{1,0:T(8,128)S(1)}, f32[1024,128]{1,0:T(8,128)S(1)}, u32[]{:S(2)}, u32[]{:S(2)}) collective-permute-start(f32[1024,128]{1,0:T(8,128)S(1)} %fusion.part_ref), channel_id=1, source_target_pairs={{0,2},{1,3},{2,0},{3,1},{4,6},{5,7},{6,4},{7,5},{8,10},{9,11},{10,... | collective-permute-start | bytes 1572872 | tf_op jit(solution)/shard_map/ppermute | solution.py:33
  27.4 4.3 %collective-permute-start.4 = (f32[128,128]{1,0:T(8,128)S(1)}, f32[128,128]{1,0:T(8,128)S(1)}, u32[]{:S(2)}, u32[]{:S(2)}) collective-permute-start(f32[128,128]{1,0:T(8,128)S(1)} %fusion.2), channel_id=1, source_target_pairs={{0,4},{4,0},{8,12},{12,8},{16,20},{20,16},{24,28},{28,24},{1,5},{5... | collective-permute-start | bytes 196616 | tf_op jit(solution)/shard_map/ppermute | solution.py:33
  31.8 4.3 %collective-permute-start.6 = (f32[128,128]{1,0:T(8,128)S(1)}, f32[128,128]{1,0:T(8,128)S(1)}, u32[]{:S(2)}, u32[]{:S(2)}) collective-permute-start(f32[128,128]{1,0:T(8,128)S(1)} %add.62), channel_id=1, source_target_pairs={{0,8},{4,12},{8,0},{12,4},{16,24},{20,28},{24,16},{28,20},{1,9},{5... | collective-permute-start | bytes 196616 | tf_op jit(solution)/shard_map/ppermute | solution.py:33
  36.1 5.2 %collective-permute-start.8 = (f32[128,128]{1,0:T(8,128)S(1)}, f32[128,128]{1,0:T(8,128)S(1)}, u32[]{:S(2)}, u32[]{:S(2)}) collective-permute-start(f32[128,128]{1,0:T(8,128)S(1)} %add.63), channel_id=1, source_target_pairs={{0,16},{4,20},{8,24},{12,28},{16,0},{20,4},{24,8},{28,12},{1,17},{... | collective-permute-start | bytes 196616 | tf_op jit(solution)/shard_map/ppermute | solution.py:33
  41.3 2.3 %collective-permute-start.10 = (f32[1024,128]{1,0:T(8,128)S(1)}, f32[1024,128]{1,0:T(8,128)S(1)}, u32[]{:S(2)}, u32[]{:S(2)}) collective-permute-start(f32[1024,128]{1,0:T(8,128)S(1)} %collective-permute-done.7.part_ref), channel_id=1, source_target_pairs={{0,1},{1,0},{2,3},{3,2},{4,5},{5,4},{6,7},{7,6},{8,9},{9,8},{10,11... | collective-permute-start | bytes 1572872 | tf_op jit(solution)/shard_map/ppermute | solution.py:33
  41.4 4.0 %collective-permute-start.9 = (f32[128,128]{1,0:T(8,128)S(1)}, f32[128,128]{1,0:T(8,128)S(1)}, u32[]{:S(2)}, u32[]{:S(2)}) collective-permute-start(f32[128,128]{1,0:T(8,128)S(1)} %add.64), channel_id=1, source_target_pairs={{0,1},{1,0},{2,3},{3,2},{4,5},{5,4},{6,7},{7,6},{8,9},{9,8},{10,11... | collective-permute-start | bytes 196616 | tf_op jit(solution)/shard_map/ppermute | solution.py:33
  45.4 8.3 %collective-permute-start.11 = (f32[64,1024]{1,0:T(8,128)S(1)}, f32[64,1024]{1,0:T(8,128)S(1)}, u32[]{:S(2)}, u32[]{:S(2)}) collective-permute-start(f32[64,1024]{1,0:T(8,128)S(1)} %get-tuple-element.82), channel_id=1, source_target_pairs={{0,4},{4,0},{8,12},{12,8},{16,20},{20,16},{24,28},{28,24},{1,5},{5... | collective-permute-start | bytes 786440 | tf_op jit(solution)/shard_map/ppermute | solution.py:33
  47.0 4.3 %collective-permute-start.12 = (f32[128,128]{1,0:T(8,128)S(1)}, f32[128,128]{1,0:T(8,128)S(1)}, u32[]{:S(2)}, u32[]{:S(2)}) collective-permute-start(f32[128,128]{1,0:T(8,128)S(1)} %add.65), channel_id=1, source_target_pairs={{0,2},{1,3},{2,0},{3,1},{4,6},{5,7},{6,4},{7,5},{8,10},{9,11},{10,... | collective-permute-start | bytes 196616 | tf_op jit(solution)/shard_map/ppermute | solution.py:33
  53.7 6.9 %collective-permute-start.13 = (f32[16,1024]{1,0:T(8,128)S(1)}, f32[16,1024]{1,0:T(8,128)S(1)}, u32[]{:S(2)}, u32[]{:S(2)}) collective-permute-start(f32[16,1024]{1,0:T(8,128)S(1)} %get-tuple-element.87), channel_id=1, source_target_pairs={{0,8},{4,12},{8,0},{12,4},{16,24},{20,28},{24,16},{28,20},{1,9},{5... | collective-permute-start | bytes 196616 | tf_op jit(solution)/shard_map/ppermute | solution.py:33
  55.4 7.1 %collective-permute-start.14 = (f32[16,1024]{1,0:T(8,128)S(1)}, f32[16,1024]{1,0:T(8,128)S(1)}, u32[]{:S(2)}, u32[]{:S(2)}) collective-permute-start(f32[16,1024]{1,0:T(8,128)S(1)} %get-tuple-element.88), channel_id=1, source_target_pairs={{0,16},{4,20},{8,24},{12,28},{16,0},{20,4},{24,8},{28,12},{1,17},{... | collective-permute-start | bytes 196616 | tf_op jit(solution)/shard_map/ppermute | solution.py:33
  58.5 6.2 %collective-permute-start.15 = (f32[16,1024]{1,0:T(8,128)S(1)}, f32[16,1024]{1,0:T(8,128)S(1)}, u32[]{:S(2)}, u32[]{:S(2)}) collective-permute-start(f32[16,1024]{1,0:T(8,128)S(1)} %get-tuple-element.89), channel_id=1, source_target_pairs={{0,24},{4,28},{8,16},{12,20},{16,8},{20,12},{24,0},{28,4},{1,25},{... | collective-permute-start | bytes 196616 | tf_op jit(solution)/shard_map/ppermute | solution.py:33
  64.7 6.5 %collective-permute-start.18 = (f32[16,1024]{1,0:T(8,128)S(1)}, f32[16,1024]{1,0:T(8,128)S(1)}, u32[]{:S(2)}, u32[]{:S(2)}) collective-permute-start(f32[16,1024]{1,0:T(8,128)S(1)} %add_add_fusion), channel_id=1, source_target_pairs={{0,24},{4,28},{8,16},{12,20},{16,8},{20,12},{24,0},{28,4},{1,25},{... | collective-permute-start | bytes 196616 | tf_op jit(solution)/shard_map/ppermute | solution.py:33
  65.7 6.5 %collective-permute-start.17 = (f32[16,1024]{1,0:T(8,128)S(1)}, f32[16,1024]{1,0:T(8,128)S(1)}, u32[]{:S(2)}, u32[]{:S(2)}) collective-permute-start(f32[16,1024]{1,0:T(8,128)S(1)} %add_add_fusion), channel_id=1, source_target_pairs={{0,16},{4,20},{8,24},{12,28},{16,0},{20,4},{24,8},{28,12},{1,17},{... | collective-permute-start | bytes 196616 | tf_op jit(solution)/shard_map/ppermute | solution.py:33
  65.7 6.5 %collective-permute-start.16 = (f32[16,1024]{1,0:T(8,128)S(1)}, f32[16,1024]{1,0:T(8,128)S(1)}, u32[]{:S(2)}, u32[]{:S(2)}) collective-permute-start(f32[16,1024]{1,0:T(8,128)S(1)} %add_add_fusion), channel_id=1, source_target_pairs={{0,8},{4,12},{8,0},{12,4},{16,24},{20,28},{24,16},{28,20},{1,9},{5... | collective-permute-start | bytes 196616 | tf_op jit(solution)/shard_map/ppermute | solution.py:33
  72.3 6.4 %collective-permute-start.19 = (f32[64,1024]{1,0:T(8,128)S(1)}, f32[64,1024]{1,0:T(8,128)S(1)}, u32[]{:S(2)}, u32[]{:S(2)}) collective-permute-start(f32[64,1024]{1,0:T(8,128)S(1)} %pad_maximum_fusion.refs_0_), channel_id=1, source_target_pairs={{0,4},{4,0},{8,12},{12,8},{16,20},{20,16},{24,28},{28,24},{1,5},{5... | collective-permute-start | bytes 786440 | tf_op jit(solution)/shard_map/ppermute | solution.py:33
  81.0 3.8 %collective-permute-start.22 = (f32[128,128]{1,0:T(8,128)S(1)}, f32[128,128]{1,0:T(8,128)S(1)}, u32[]{:S(2)}, u32[]{:S(2)}) collective-permute-start(f32[128,128]{1,0:T(8,128)S(1)} %get-tuple-element.106), channel_id=1, source_target_pairs={{0,3},{1,2},{2,1},{3,0},{4,7},{5,6},{6,5},{7,4},{8,11},{9,10},{10,... | collective-permute-start | bytes 196616 | tf_op jit(solution)/shard_map/ppermute | solution.py:33
  81.0 4.9 %collective-permute-start.21 = (f32[128,128]{1,0:T(8,128)S(1)}, f32[128,128]{1,0:T(8,128)S(1)}, u32[]{:S(2)}, u32[]{:S(2)}) collective-permute-start(f32[128,128]{1,0:T(8,128)S(1)} %get-tuple-element.106), channel_id=1, source_target_pairs={{0,2},{1,3},{2,0},{3,1},{4,6},{5,7},{6,4},{7,5},{8,10},{9,11},{10,... | collective-permute-start | bytes 196616 | tf_op jit(solution)/shard_map/ppermute | solution.py:33
  81.6 4.4 %collective-permute-start.20 = (f32[128,128]{1,0:T(8,128)S(1)}, f32[128,128]{1,0:T(8,128)S(1)}, u32[]{:S(2)}, u32[]{:S(2)}) collective-permute-start(f32[128,128]{1,0:T(8,128)S(1)} %get-tuple-element.106), channel_id=1, source_target_pairs={{0,1},{1,0},{2,3},{3,2},{4,5},{5,4},{6,7},{7,6},{8,9},{9,8},{10,11... | collective-permute-start | bytes 196616 | tf_op jit(solution)/shard_map/ppermute | solution.py:33

commit v9 on v8

--- a/solution.py
+++ b/solution.py
@@ -44,16 +44,30 @@
     return upper, (value - upper.astype(f32)).astype(bf16)
 
 
-def sketch_kernel(places, first, own_ref, data_ref, omega_ref, *refs):
-    count = len(places)
+def multiply(held, wide, out):
+    quarter, cols = held.shape
+    width = out.shape[1]
+    for row in range(0, quarter, PIECE):
+        yield row
+        for t in range(cols // TILE):
+            tile = slice(t * TILE, (t + 1) * TILE)
+            upper, rest = split(held[row : row + PIECE, tile])
+            one = jnp.dot(upper, wide[tile, :], preferred_element_type=f32)
+            two = jnp.dot(rest, wide[tile, :width], preferred_element_type=f32)
+            both, more = (one, two) if t == 0 else (both + one, more + two)
+        out[row : row + PIECE] = both[:, :width] + both[:, width:] + more
+
+
+def sketch_kernel(places, ahead, first, own_ref, data_ref, omega_ref, *refs):
+    count, total = len(places), len(places) + len(ahead)
     if first:
         refs, (omega_held, omega_sem) = refs[:-2], refs[-2:]
         omega_copy = pltpu.make_async_copy(omega_ref, omega_held, omega_sem)
         omega_copy.start()
-    outs, held, sems = refs[:count], refs[count : 2 * count], refs[-1]
-    quarter, cols = held[0].shape
+    outs, held, sems = refs[:count], refs[count : count + total], refs[-1]
+    quarter = held[0].shape[0]
     copies = {}
-    for k, place in enumerate(places):
+    for k, place in enumerate(places + ahead):
         for row in range(0, quarter, RUN):
             at = pl.multiple_of((own_ref[0] ^ place) * quarter + row, RUN)
             copy = pltpu.make_async_copy(
@@ -63,40 +77,35 @@
             copies[k, row] = copy
     if first:
         width = omega_ref.shape[1]
-        wide = refs[2 * count]
+        wide = refs[count + total]
         omega_copy.wait()
         upper, rest = split(omega_held[...])
         wide[:, :width] = upper
         wide[:, width:] = rest
     else:
         wide = omega_ref
-        width = omega_ref.shape[1] // 2
     for k in range(count):
-        for row in range(0, quarter, PIECE):
+        for row in multiply(held[k], wide, outs[k]):
             for run in range(row, row + PIECE, RUN):
                 copies[k, run].wait()
-            for t in range(cols // TILE):
-                tile = slice(t * TILE, (t + 1) * TILE)
-                upper, rest = split(held[k][row : row + PIECE, tile])
-                one = jnp.dot(upper, wide[tile, :], preferred_element_type=f32)
-                two = jnp.dot(rest, wide[tile, :width], preferred_element_type=f32)
-                both, more = (one, two) if t == 0 else (both + one, more + two)
-            outs[k][row : row + PIECE] = both[:, :width] + both[:, width:] + more
-
-
-def sketch(own, data, omega, places, first=False):
+    for k in range(count, total):
+        for row in range(0, quarter, RUN):
+            copies[k, row].wait()
+
+
+def sketch(own, data, omega, places, ahead=(), first=False):
     cols = data.shape[1]
     width = omega.shape[1] if first else omega.shape[1] // 2
     quarter = data.shape[0] // lax.axis_size("col")
-    count = len(places)
-    out = [jax.ShapeDtypeStruct((quarter, width), f32)] * count
-    out += [pltpu.VMEM((quarter, cols), f32)] * count
-    scratch = [pltpu.SemaphoreType.DMA((count, quarter // RUN))]
+    total = len(places) + len(ahead)
+    out = [jax.ShapeDtypeStruct((quarter, width), f32)] * len(places)
+    out += [pltpu.VMEM((quarter, cols), f32)] * total
+    scratch = [pltpu.SemaphoreType.DMA((total, quarter // RUN))]
     if first:
         out.append(jax.ShapeDtypeStruct((cols, 2 * width), bf16))
         scratch += [pltpu.VMEM(omega.shape, f32), pltpu.SemaphoreType.DMA]
     return pl.pallas_call(
-        functools.partial(sketch_kernel, places, first),
+        functools.partial(sketch_kernel, places, ahead, first),
         in_specs=[SMEM, HBM, HBM if first else VMEM],
         out_specs=[VMEM] * len(out),
         out_shape=out,
@@ -107,17 +116,34 @@
     )(own, data, omega)
 
 
-def project_kernel(before, slices, own_ref, rows_ref, part_ref, *refs):
+def held_kernel(rows_ref, wide_ref, out_ref):
+    for _ in multiply(rows_ref, wide_ref, out_ref):
+        pass
+
+
+def sketch_held(rows, wide):
+    return pl.pallas_call(
+        held_kernel,
+        in_specs=[VMEM] * 2,
+        out_specs=VMEM,
+        out_shape=jax.ShapeDtypeStruct((rows.shape[0], wide.shape[1] // 2), f32),
+        compiler_params=params(),
+        cost_estimate=cost(0.01),
+        name="partial_sketch_held",
+    )(rows, wide)
+
+
+def project_kernel(start, before, slices, own_ref, rows_ref, part_ref, *refs):
     old, refs = (refs[0], refs[1:]) if before else (None, refs)
     outs, total = (refs[:-1], refs[-1]) if slices else (refs, refs[0])
-    quarter, cols = rows_ref.shape
-    for row in range(0, quarter, PIECE):
+    cols = rows_ref.shape[1]
+    for row in range(0, part_ref.shape[0], PIECE):
         upper, rest = split(part_ref[row : row + PIECE].T)
         stack = jnp.concatenate([upper, rest], 0)
         width = upper.shape[0]
         for t in range(cols // TILE):
             tile = slice(t * TILE, (t + 1) * TILE)
-            d_upper, d_rest = split(rows_ref[row : row + PIECE, tile])
+            d_upper, d_rest = split(rows_ref[start + row : start + row + PIECE, tile])
             both = jnp.dot(stack, d_upper, preferred_element_type=f32)
             value = both[:width] + both[width:] + jnp.dot(upper, d_rest, preferred_element_type=f32)
             if row > 0:
@@ -133,7 +159,7 @@
             outs[1 - place % 2][row : row + step] = total[pl.ds(at, step)]
 
 
-def project(own, rows, part, before=None, slices=0):
+def project(own, rows, part, before=None, slices=0, start=0):
     cols = rows.shape[1]
     width = part.shape[1]
     args = [own, rows, part] + ([] if before is None else [before])
@@ -142,13 +168,13 @@
     else:
         out = [jax.ShapeDtypeStruct((width, cols), f32)]
     return pl.pallas_call(
-        functools.partial(project_kernel, before is not None, slices),
+        functools.partial(project_kernel, start, before is not None, slices),
         in_specs=[SMEM] + [VMEM] * (len(args) - 1),
         out_specs=[VMEM] * len(out),
         out_shape=out,
         scratch_shapes=[pltpu.VMEM((width, cols), f32)] if slices else [],
         compiler_params=params(),
-        cost_estimate=cost(6),
+        cost_estimate=cost(6 * part.shape[0] / rows.shape[0]),
         name="project",
     )(*args)
 
@@ -232,9 +258,25 @@
         at = pl.multiple_of((place ^ own_ref[1]) * step, step)
         row = place // 2 * step
         total[pl.ds(at, step)] = parts[place % 2][row : row + step]
-    value = jnp.dot(inverse_ref[...], total[...], precision=full, preferred_element_type=f32)
-    out_ref[...] = value
-    gram_ref[...] = dot(value, value, 1, 1)
+    upper, rest = split(inverse_ref[...])
+    stack = jnp.concatenate([upper, rest], 0)
+    width = upper.shape[0]
+    gram = jnp.zeros((2 * width, width), f32)
+    for t in range(total.shape[1] // TILE):
+        tile = slice(t * TILE, (t + 1) * TILE)
+        t_upper, t_rest = split(total[:, tile])
+        both = jnp.dot(stack, t_upper, preferred_element_type=f32)
+        value = both[:width] + both[width:] + jnp.dot(upper, t_rest, preferred_element_type=f32)
+        out_ref[:, tile] = value
+        v_upper, v_rest = split(value)
+        gram += lax.dot_general(
+            jnp.concatenate([v_upper, v_rest], 0),
+            v_upper,
+            (((1,), (1,)), ((), ())),
+            preferred_element_type=f32,
+        )
+    cross = gram[width:]
+    gram_ref[...] = gram[:width] + (cross + cross.T)
 
 
 def finish(own, inverse, parts):
@@ -266,11 +308,10 @@
     data = pltpu.with_memory_space_constraint(data, pltpu.HBM)
     omega = pltpu.with_memory_space_constraint(omega, pltpu.HBM)
 
-    part, rows3, wide = sketch(own, data, omega, [3], True)
-    pair, rows2 = sketch(own, data, wide, [2])
-    pair, wide = fence((pair + swap(part, "col", 1), wide))
+    part, rows3, rows2, wide = sketch(own, data, omega, (3,), (2,), True)
+    pair, wide = fence((sketch_held(rows2, wide) + swap(part, "col", 1), wide))
     away = swap(pair, "col", 2)
-    part, here, rows1, rows0 = sketch(own, data, wide, [1, 0])
+    part, here, rows1, rows0 = sketch(own, data, wide, (1, 0))
     part_a, part_b, away = fence((swap(part[:PIECE], "col", 1), swap(part[PIECE:], "col", 1), away))
     sketched = here + jnp.concatenate([part_a, part_b], 0) + away
 
@@ -283,39 +324,37 @@
     gram = gram + far
     far = swap(gram, "row", bits[1])
     (acc,) = project(own, rows1, second, acc)
-    far, acc = fence((far, acc))
+    far, acc, third = fence((far, acc, third))
     gram = gram + far
-    far = swap(gram, "row", bits[2])
-    third, acc, far = fence((third, acc, far))
     fourth = swap(third, "col", 1)
     (acc,) = project(own, rows2, third, acc)
-    acc, fourth = fence((acc, fourth))
-    gram = gram + far
-    for bit in bits[3:]:
+    fourth, acc = fence((fourth, acc))
+    send, keep = project(own, rows3, fourth, acc, SLICES)
+    send, keep, gram = fence((send, keep, gram))
+
+    got = swap(send, "row", 1)
+    for bit in bits[2:]:
         gram = gram + swap(gram, "row", bit)
-    far = swap(gram, "col", 1)
-    send, keep = project(own, rows3, fourth, acc, SLICES)
-    far, send, keep = fence((far, send, keep))
-    gram = gram + far
-
-    got, state = fence((swap(send, "row", 1), factor(0, 3, gram + swap(gram, "col", 2))))
+    gram = gram + swap(gram, "col", 1)
+    got, state = fence((got, gram + swap(gram, "col", 2)))
     step = keep.shape[0] // 4
     quads = [keep[i * step : (i + 1) * step] + got[i * step : (i + 1) * step] for i in range(4)]
     *quads, state = fence((*quads, state))
-    got = [swap(quads[i], "row", 2 * i) for i in (1, 2, 3)]
-    *got, state = fence((*got, factor(1, 3, state)))
+    got = [swap(quads[i], "row", 2 * i) for i in (3, 2, 1)]
+    *got, state = fence((*got, factor(0, 3, state)))
     mine = (quads[0] + got[0]) + (got[1] + got[2])
     for bit in bits[3:]:
         mine = mine + swap(mine, "row", bit)
     mine, state = fence((mine, state))
     got = [swap(mine, "row", 2 * i) for i in (1, 2, 3)]
-    *got, inverse = fence((*got, factor(2, 3, state)))
+    *got, state = fence((*got, factor(1, 3, state)))
     keep = jnp.concatenate([mine, *got], 0)
-    keep, inverse = fence((keep, inverse))
-    got, basis = fence((swap(keep, "row", 1), dot(sketched, inverse, 1, 1)))
+    keep, state = fence((keep, state))
+    got, inverse = fence((swap(keep, "row", 1), factor(2, 3, state)))
     projected, small = finish(own, inverse, [keep, got])
 
     across = [swap(small, "col", bit) for bit in (2, 3, 1)]
+    *across, basis = fence((*across, dot(sketched, inverse, 1, 1)))
     small = (small + across[2]) + (across[0] + across[1])
     return (basis, projected, small / total_rows)
 

time: 86.8 us -> 88.7 us (1.022)
  waiting for transfers between devices: 27.1 us -> 30.6 us
  Pallas kernels: 28.5 us -> 27.1 us
    ppermute x23, waiting for transfers between devices: 27.1 us -> 30.6 us  [swap(): lax.ppermute(value, axis, [(i, i ^ bit) for i in range(lax.axis_size(axis...]
    pallas_call x7, Pallas kernels: 19.8 us -> 18.8 us  [the longest x2 10.7 us: sketch(): pl.pallas_call(functools.partial(sketch_kernel, places, ahead, first), in...]
  transfers between devices with their start and end apart: 23 -> 23, of which waited for: 15 -> 16; matrix products, arithmetic and copies ran while one was open for 3% -> 3% of each run, Pallas kernels for 25% -> 20%
where the time goes in v9:
time: 88.7 us; the launch traced here: 88.5 us
  waiting for transfers between devices  30.6 us (34%)
  Pallas kernels  27.1 us (31%)
  starting transfers between devices  26.6 us (30%)
  matrix products  2.4 us (3%)
  other arithmetic  1 us (1%)
    ppermute x23, waiting for transfers between devices, swap(): lax.ppermute(value, axis, [(i, i ^ bit) for i in range(lax.axis_size(axis...  30.6 us
    ppermute x23, starting transfers between devices, swap(): lax.ppermute(value, axis, [(i, i ^ bit) for i in range(lax.axis_size(axis...  26.6 us
    pallas_call x2, Pallas kernels, sketch(): pl.pallas_call(functools.partial(sketch_kernel, places, ahead, first), in...  10.7 us
    pallas_call x4, Pallas kernels, project(): pl.pallas_call(functools.partial(project_kernel, start, before is not Non...  6.82 us
    pallas_call x3, Pallas kernels, factor(): pl.pallas_call(functools.partial(factor_kernel, index, count), in_specs=[...  6.39 us
    dot_general x2, matrix products, dot(): lax.dot_general(a, b, (((a_dim,), (b_dim,)), ((), ())), precision=precisi...  2.4 us
    pallas_call x1, Pallas kernels, finish(): pl.pallas_call(finish_kernel, in_specs=[SMEM] + [VMEM] * (1 + len(parts))...  1.87 us
  transfers between devices with their start and end apart: 23, of which 16 were waited for; matrix products, arithmetic and copies ran while one was open for 3% of the time, Pallas kernels for 20%

profile of v9, /device:TPU:0, one launch (start us, length us, event | category | flops | bytes accessed | tf_op | source)
XLA Modules:
  0.0 88.5 jit_solution(14480577949939981213)
XLA Ops:
  0.7 5.6 %partial_sketch.2 = (f32[1024,128]{1,0:T(8,128)S(1)}, f32[1024,1024]{1,0:T(8,128)S(1)}, f32[1024,1024]{1,0:T(8,128)S(1)}, bf16[1024,256]{1,0:T(8,128)(2,1)S(1)}) custom-call(s32[2]{0:T(128)S(1)} %pad_add_fusion.own_ref, f32[4096,1024]{1,0:T(8,128)} %data_ref.3, f32[1024,128]{1,0:T(8,128)} %omega_ref.1), custom_call_target="tpu_custom_call" | custom-call | flops 1 | bytes 10485 | tf_op jit(solution)/shard_map/partial_sketch/pallas_call | solution.py:107
  6.9 1.3 %partial_sketch_held.1 = f32[1024,128]{1,0:T(8,128)S(1)} custom-call(f32[1024,1024]{1,0:T(8,128)S(1)} %get-tuple-element.57.rows_ref, bf16[1024,256]{1,0:T(8,128)(2,1)S(1)} %get-tuple-element.60.wide_ref.omega_ref), custom_call_target="tpu_custom_call" | custom-call | flops 1 | bytes 10485 | tf_op jit(solution)/shard_map/partial_sketch_held/pallas_call | solution.py:125
  8.5 3.0 %collective-permute-start.3 = (f32[1024,128]{1,0:T(8,128)S(1)}, f32[1024,128]{1,0:T(8,128)S(1)}, u32[]{:S(2)}, u32[]{:S(2)}) collective-permute-start(f32[1024,128]{1,0:T(8,128)S(1)} %add.59), channel_id=1, source_target_pairs={{0,2},{1,3},{2,0},{3,1},{4,6},{5,7},{6,4},{7,5},{8,10},{9,11},{10,... | collective-permute-start | bytes 1572872 | tf_op jit(solution)/shard_map/ppermute | solution.py:33
  11.5 5.1 %partial_sketch.3 = (f32[1024,128]{1,0:T(8,128)S(1)}, f32[1024,128]{1,0:T(8,128)S(1)}, f32[1024,1024]{1,0:T(8,128)S(1)}, f32[1024,1024]{1,0:T(8,128)S(1)}) custom-call(s32[2]{0:T(128)S(1)} %pad_add_fusion.own_ref, f32[4096,1024]{1,0:T(8,128)} %data_ref.3, bf16[1024,256]{1,0:T(8,128)(2,1)S(1)} %get-tuple-element.60.wide_ref.omega_ref), custom_call_target="tpu_custom_call" | custom-call | flops 1 | bytes 10485 | tf_op jit(solution)/shard_map/partial_sketch/pallas_call | solution.py:107
  18.6 5.1 %collective-permute-done.3 = f32[1024,128]{1,0:T(8,128)S(1)} collective-permute-done((f32[1024,128]{1,0:T(8,128)S(1)}, f32[1024,128]{1,0:T(8,128)S(1)}, u32[]{:S(2)}, u32[]{:S(2)}) %collective-permute-start.3) | collective-permute-done | bytes 524320 | tf_op jit(solution)/shard_map/ppermute | solution.py:33
  23.8 1.8 %collective-permute-start.7 = (f32[1024,128]{1,0:T(8,128)S(1)}, f32[1024,128]{1,0:T(8,128)S(1)}, u32[]{:S(2)}, u32[]{:S(2)}) collective-permute-start(f32[1024,128]{1,0:T(8,128)S(1)} %fusion.part_ref), channel_id=1, source_target_pairs={{0,2},{1,3},{2,0},{3,1},{4,6},{5,7},{6,4},{7,5},{8,10},{9,11},{10,... | collective-permute-start | bytes 1572872 | tf_op jit(solution)/shard_map/ppermute | solution.py:33
  26.7 1.6 %collective-permute-start.4 = (f32[128,128]{1,0:T(8,128)S(1)}, f32[128,128]{1,0:T(8,128)S(1)}, u32[]{:S(2)}, u32[]{:S(2)}) collective-permute-start(f32[128,128]{1,0:T(8,128)S(1)} %fusion.2), channel_id=1, source_target_pairs={{0,4},{4,0},{8,12},{12,8},{16,20},{20,16},{24,28},{28,24},{1,5},{5... | collective-permute-start | bytes 196616 | tf_op jit(solution)/shard_map/ppermute | solution.py:33
  28.2 1.7 %project.4.refs_0_ = f32[128,1024]{1,0:T(8,128)S(1)} custom-call(s32[2]{0:T(128)S(1)} %pad_add_fusion.own_ref, f32[1024,1024]{1,0:T(8,128)S(1)} %get-tuple-element.67.rows_ref, f32[1024,128]{1,0:T(8,128)S(1)} %fusion.part_ref), custom_call_target="tpu_custom_call" | custom-call | flops 1 | bytes 6291456 | tf_op jit(solution)/shard_map/project/pallas_call | solution.py:170
  31.0 1.6 %collective-permute-start.6 = (f32[128,128]{1,0:T(8,128)S(1)}, f32[128,128]{1,0:T(8,128)S(1)}, u32[]{:S(2)}, u32[]{:S(2)}) collective-permute-start(f32[128,128]{1,0:T(8,128)S(1)} %add.62), channel_id=1, source_target_pairs={{0,8},{4,12},{8,0},{12,4},{16,24},{20,28},{24,16},{28,20},{1,9},{5... | collective-permute-start | bytes 196616 | tf_op jit(solution)/shard_map/ppermute | solution.py:33
  32.7 1.7 %project.5.refs_0_ = f32[128,1024]{1,0:T(8,128)S(1)} custom-call(s32[2]{0:T(128)S(1)} %pad_add_fusion.own_ref, f32[1024,1024]{1,0:T(8,128)S(1)} %get-tuple-element.69.rows_ref, f32[1024,128]{1,0:T(8,128)S(1)} %collective-permute-done.5.part_ref, f32[128,1024]{1,0:T(8,128)S(1)} %project.4.refs_0_), custom_call_target="tpu_custom_call" | custom-call | flops 1 | bytes 6291456 | tf_op jit(solution)/shard_map/project/pallas_call | solution.py:170
  34.4 3.8 %collective-permute-done.7.part_ref = f32[1024,128]{1,0:T(8,128)S(1)} collective-permute-done((f32[1024,128]{1,0:T(8,128)S(1)}, f32[1024,128]{1,0:T(8,128)S(1)}, u32[]{:S(2)}, u32[]{:S(2)}) %collective-permute-start.7) | collective-permute-done | bytes 524320 | tf_op jit(solution)/shard_map/ppermute | solution.py:33
  38.2 1.7 %project.6.refs_0_ = f32[128,1024]{1,0:T(8,128)S(1)} custom-call(s32[2]{0:T(128)S(1)} %pad_add_fusion.own_ref, f32[1024,1024]{1,0:T(8,128)S(1)} %get-tuple-element.57.rows_ref, f32[1024,128]{1,0:T(8,128)S(1)} %collective-permute-done.7.part_ref, f32[128,1024]{1,0:T(8,128)S(1)} %project.5.refs_0_), custom_call_target="tpu_custom_call" | custom-call | flops 1 | bytes 6291456 | tf_op jit(solution)/shard_map/project/pallas_call | solution.py:170
  40.1 1.7 %project.7 = (f32[64,1024]{1,0:T(8,128)S(1)}, f32[64,1024]{1,0:T(8,128)S(1)}) custom-call(s32[2]{0:T(128)S(1)} %pad_add_fusion.own_ref, f32[1024,1024]{1,0:T(8,128)S(1)} %get-tuple-element.56.rows_ref, f32[1024,128]{1,0:T(8,128)S(1)} %collective-permute-done.8.part_ref, f32[128,1024]{1,0:T(8,128)S(1)} %project.6.refs_0_), custom_call_target="tpu_custom_call" | custom-call | flops 1 | bytes 6291456 | tf_op jit(solution)/shard_map/project/pallas_call | solution.py:170
  41.8 1.8 %collective-permute-start.9 = (f32[64,1024]{1,0:T(8,128)S(1)}, f32[64,1024]{1,0:T(8,128)S(1)}, u32[]{:S(2)}, u32[]{:S(2)}) collective-permute-start(f32[64,1024]{1,0:T(8,128)S(1)} %get-tuple-element.80), channel_id=1, source_target_pairs={{0,4},{4,0},{8,12},{12,8},{16,20},{20,16},{24,28},{28,24},{1,5},{5... | collective-permute-start | bytes 786440 | tf_op jit(solution)/shard_map/ppermute | solution.py:33
  43.6 2.6 %collective-permute-start.10 = (f32[128,128]{1,0:T(8,128)S(1)}, f32[128,128]{1,0:T(8,128)S(1)}, u32[]{:S(2)}, u32[]{:S(2)}) collective-permute-start(f32[128,128]{1,0:T(8,128)S(1)} %add.63), channel_id=1, source_target_pairs={{0,16},{4,20},{8,24},{12,28},{16,0},{20,4},{24,8},{28,12},{1,17},{... | collective-permute-start | bytes 196616 | tf_op jit(solution)/shard_map/ppermute | solution.py:33
  46.2 4.0 %collective-permute-done.10 = f32[128,128]{1,0:T(8,128)S(1)} collective-permute-done((f32[128,128]{1,0:T(8,128)S(1)}, f32[128,128]{1,0:T(8,128)S(1)}, u32[]{:S(2)}, u32[]{:S(2)}) %collective-permute-start.10) | collective-permute-done | bytes 65568 | tf_op jit(solution)/shard_map/ppermute | solution.py:33
  50.3 1.2 %collective-permute-done.11 = f32[128,128]{1,0:T(8,128)S(1)} collective-permute-done((f32[128,128]{1,0:T(8,128)S(1)}, f32[128,128]{1,0:T(8,128)S(1)}, u32[]{:S(2)}, u32[]{:S(2)}) %collective-permute-start.11) | collective-permute-done | bytes 65568 | tf_op jit(solution)/shard_map/ppermute | solution.py:33
  51.5 1.6 %collective-permute-start.12 = (f32[128,128]{1,0:T(8,128)S(1)}, f32[128,128]{1,0:T(8,128)S(1)}, u32[]{:S(2)}, u32[]{:S(2)}) collective-permute-start(f32[128,128]{1,0:T(8,128)S(1)} %add.65), channel_id=1, source_target_pairs={{0,2},{1,3},{2,0},{3,1},{4,6},{5,7},{6,4},{7,5},{8,10},{9,11},{10,... | collective-permute-start | bytes 196616 | tf_op jit(solution)/shard_map/ppermute | solution.py:33
  53.1 2.7 %collective-permute-done.12 = f32[128,128]{1,0:T(8,128)S(1)} collective-permute-done((f32[128,128]{1,0:T(8,128)S(1)}, f32[128,128]{1,0:T(8,128)S(1)}, u32[]{:S(2)}, u32[]{:S(2)}) %collective-permute-start.12) | collective-permute-done | bytes 65568 | tf_op jit(solution)/shard_map/ppermute | solution.py:33
  55.9 3.4 %collective-permute-start.13 = (f32[16,1024]{1,0:T(8,128)S(1)}, f32[16,1024]{1,0:T(8,128)S(1)}, u32[]{:S(2)}, u32[]{:S(2)}) collective-permute-start(f32[16,1024]{1,0:T(8,128)S(1)} %get-tuple-element.85), channel_id=1, source_target_pairs={{0,24},{4,28},{8,16},{12,20},{16,8},{20,12},{24,0},{28,4},{1,25},{... | collective-permute-start | bytes 196616 | tf_op jit(solution)/shard_map/ppermute | solution.py:33
  60.4 2.2 %factor.3.in_ref = f32[128,256]{1,0:T(8,128)S(1)} custom-call(f32[128,128]{1,0:T(8,128)S(1)} %add.66.in_ref), custom_call_target="tpu_custom_call" | custom-call | flops 1 | bytes 10485 | tf_op jit(solution)/shard_map/factor/pallas_call | solution.py:242
  62.6 1.9 %collective-permute-done.14 = f32[16,1024]{1,0:T(8,128)S(1)} collective-permute-done((f32[16,1024]{1,0:T(8,128)S(1)}, f32[16,1024]{1,0:T(8,128)S(1)}, u32[]{:S(2)}, u32[]{:S(2)}) %collective-permute-start.14) | collective-permute-done | bytes 65568 | tf_op jit(solution)/shard_map/ppermute | solution.py:33
  65.0 1.7 %collective-permute-start.18 = (f32[16,1024]{1,0:T(8,128)S(1)}, f32[16,1024]{1,0:T(8,128)S(1)}, u32[]{:S(2)}, u32[]{:S(2)}) collective-permute-start(f32[16,1024]{1,0:T(8,128)S(1)} %add_add_fusion), channel_id=1, source_target_pairs={{0,24},{4,28},{8,16},{12,20},{16,8},{20,12},{24,0},{28,4},{1,25},{... | collective-permute-start | bytes 196616 | tf_op jit(solution)/shard_map/ppermute | solution.py:33
  66.7 2.7 %collective-permute-start.16 = (f32[16,1024]{1,0:T(8,128)S(1)}, f32[16,1024]{1,0:T(8,128)S(1)}, u32[]{:S(2)}, u32[]{:S(2)}) collective-permute-start(f32[16,1024]{1,0:T(8,128)S(1)} %add_add_fusion), channel_id=1, source_target_pairs={{0,8},{4,12},{8,0},{12,4},{16,24},{20,28},{24,16},{28,20},{1,9},{5... | collective-permute-start | bytes 196616 | tf_op jit(solution)/shard_map/ppermute | solution.py:33
  69.4 2.1 %factor.4.in_ref = f32[128,256]{1,0:T(8,128)S(1)} custom-call(f32[128,256]{1,0:T(8,128)S(1)} %factor.3.in_ref), custom_call_target="tpu_custom_call" | custom-call | flops 1 | bytes 10485 | tf_op jit(solution)/shard_map/factor/pallas_call | solution.py:242
  71.5 1.4 %collective-permute-done.17 = f32[16,1024]{1,0:T(8,128)S(1)} collective-permute-done((f32[16,1024]{1,0:T(8,128)S(1)}, f32[16,1024]{1,0:T(8,128)S(1)}, u32[]{:S(2)}, u32[]{:S(2)}) %collective-permute-start.17) | collective-permute-done | bytes 65568 | tf_op jit(solution)/shard_map/ppermute | solution.py:33
  73.3 2.1 %factor.5.inverse_ref = f32[128,128]{1,0:T(8,128)S(1)} custom-call(f32[128,256]{1,0:T(8,128)S(1)} %factor.4.in_ref), custom_call_target="tpu_custom_call" | custom-call | flops 1 | bytes 10485 | tf_op jit(solution)/shard_map/factor/pallas_call | solution.py:242
  75.4 4.8 %collective-permute-done.19.refs_1_ = f32[64,1024]{1,0:T(8,128)S(1)} collective-permute-done((f32[64,1024]{1,0:T(8,128)S(1)}, f32[64,1024]{1,0:T(8,128)S(1)}, u32[]{:S(2)}, u32[]{:S(2)}) %collective-permute-start.19) | collective-permute-done | bytes 262176 | tf_op jit(solution)/shard_map/ppermute | solution.py:33
  80.2 1.9 %finish.1 = (f32[128,1024]{1,0:T(8,128)}, f32[128,128]{1,0:T(8,128)S(1)}) custom-call(s32[2]{0:T(128)S(1)} %pad_add_fusion.own_ref, f32[128,128]{1,0:T(8,128)S(1)} %factor.5.inverse_ref, f32[64,1024]{1,0:T(8,128)S(1)} %pad_maximum_fusion.refs_0_, f32[64,1024]{1,0:T(8,128)S(1)} %collective-permute-done.19.refs_1_), custom_call_target="tpu_custom_call" | custom-call | flops 1 | bytes 8388608 | tf_op jit(solution)/shard_map/finish/pallas_call | solution.py:285
  82.0 1.6 %collective-permute-start.21 = (f32[128,128]{1,0:T(8,128)S(1)}, f32[128,128]{1,0:T(8,128)S(1)}, u32[]{:S(2)}, u32[]{:S(2)}) collective-permute-start(f32[128,128]{1,0:T(8,128)S(1)} %get-tuple-element.103), channel_id=1, source_target_pairs={{0,3},{1,2},{2,1},{3,0},{4,7},{5,6},{6,5},{7,4},{8,11},{9,10},{10,... | collective-permute-start | bytes 196616 | tf_op jit(solution)/shard_map/ppermute | solution.py:33
  84.2 1.4 %fusion.3 = f32[1024,128]{1,0:T(8,128)} fusion(f32[1024,128]{1,0:T(8,128)S(1)} %fusion.part_ref, f32[128,128]{1,0:T(8,128)S(1)} %factor.5.inverse_ref), kind=kOutput, calls=%fused_computation.12 | convolution fusion | flops 201326592 | bytes 1114112 | tf_op jit(solution)/shard_map/dot_general | solution.py:37
  86.1 1.8 %collective-permute-done.20 = f32[128,128]{1,0:T(8,128)S(1)} collective-permute-done((f32[128,128]{1,0:T(8,128)S(1)}, f32[128,128]{1,0:T(8,128)S(1)}, u32[]{:S(2)}, u32[]{:S(2)}) %collective-permute-start.20) | collective-permute-done | bytes 65568 | tf_op jit(solution)/shard_map/ppermute | solution.py:33
  (40 shorter events, 9.3 us)
Async XLA Ops:
  6.4 2.1 %collective-permute-start = (f32[1024,128]{1,0:T(8,128)S(1)}, f32[1024,128]{1,0:T(8,128)S(1)}, u32[]{:S(2)}, u32[]{:S(2)}) collective-permute-start(f32[1024,128]{1,0:T(8,128)S(1)} %get-tuple-element.59), channel_id=1, source_target_pairs={{0,1},{1,0},{2,3},{3,2},{4,5},{5,4},{6,7},{7,6},{8,9},{9,8},{10,11... | collective-permute-start | bytes 1572872 | tf_op jit(solution)/shard_map/ppermute | solution.py:33
  8.5 15.2 %collective-permute-start.3 = (f32[1024,128]{1,0:T(8,128)S(1)}, f32[1024,128]{1,0:T(8,128)S(1)}, u32[]{:S(2)}, u32[]{:S(2)}) collective-permute-start(f32[1024,128]{1,0:T(8,128)S(1)} %add.59), channel_id=1, source_target_pairs={{0,2},{1,3},{2,0},{3,1},{4,6},{5,7},{6,4},{7,5},{8,10},{9,11},{10,... | collective-permute-start | bytes 1572872 | tf_op jit(solution)/shard_map/ppermute | solution.py:33
  16.6 1.6 %collective-permute-start.2 = (f32[512,128]{1,0:T(8,128)S(1)}, f32[512,128]{1,0:T(8,128)S(1)}, u32[]{:S(2)}, u32[]{:S(2)}) collective-permute-start(f32[512,128]{1,0:T(8,128)S(1)} %get-tuple-element.113), channel_id=1, source_target_pairs={{0,1},{1,0},{2,3},{3,2},{4,5},{5,4},{6,7},{7,6},{8,9},{9,8},{10,11... | collective-permute-start | bytes 786440 | tf_op jit(solution)/shard_map/ppermute | solution.py:33
  16.7 1.9 %collective-permute-start.1 = (f32[512,128]{1,0:T(8,128)S(1)}, f32[512,128]{1,0:T(8,128)S(1)}, u32[]{:S(2)}, u32[]{:S(2)}) collective-permute-start(f32[512,128]{1,0:T(8,128)S(1)} %get-tuple-element.114), channel_id=1, source_target_pairs={{0,1},{1,0},{2,3},{3,2},{4,5},{5,4},{6,7},{7,6},{8,9},{9,8},{10,11... | collective-permute-start | bytes 786440 | tf_op jit(solution)/shard_map/ppermute | solution.py:33
  23.8 7.2 %collective-permute-start.5 = (f32[1024,128]{1,0:T(8,128)S(1)}, f32[1024,128]{1,0:T(8,128)S(1)}, u32[]{:S(2)}, u32[]{:S(2)}) collective-permute-start(f32[1024,128]{1,0:T(8,128)S(1)} %fusion.part_ref), channel_id=1, source_target_pairs={{0,1},{1,0},{2,3},{3,2},{4,5},{5,4},{6,7},{7,6},{8,9},{9,8},{10,11... | collective-permute-start | bytes 1572872 | tf_op jit(solution)/shard_map/ppermute | solution.py:33
  23.8 14.3 %collective-permute-start.7 = (f32[1024,128]{1,0:T(8,128)S(1)}, f32[1024,128]{1,0:T(8,128)S(1)}, u32[]{:S(2)}, u32[]{:S(2)}) collective-permute-start(f32[1024,128]{1,0:T(8,128)S(1)} %fusion.part_ref), channel_id=1, source_target_pairs={{0,2},{1,3},{2,0},{3,1},{4,6},{5,7},{6,4},{7,5},{8,10},{9,11},{10,... | collective-permute-start | bytes 1572872 | tf_op jit(solution)/shard_map/ppermute | solution.py:33
  26.7 4.3 %collective-permute-start.4 = (f32[128,128]{1,0:T(8,128)S(1)}, f32[128,128]{1,0:T(8,128)S(1)}, u32[]{:S(2)}, u32[]{:S(2)}) collective-permute-start(f32[128,128]{1,0:T(8,128)S(1)} %fusion.2), channel_id=1, source_target_pairs={{0,4},{4,0},{8,12},{12,8},{16,20},{20,16},{24,28},{28,24},{1,5},{5... | collective-permute-start | bytes 196616 | tf_op jit(solution)/shard_map/ppermute | solution.py:33
  31.0 7.2 %collective-permute-start.6 = (f32[128,128]{1,0:T(8,128)S(1)}, f32[128,128]{1,0:T(8,128)S(1)}, u32[]{:S(2)}, u32[]{:S(2)}) collective-permute-start(f32[128,128]{1,0:T(8,128)S(1)} %add.62), channel_id=1, source_target_pairs={{0,8},{4,12},{8,0},{12,4},{16,24},{20,28},{24,16},{28,20},{1,9},{5... | collective-permute-start | bytes 196616 | tf_op jit(solution)/shard_map/ppermute | solution.py:33
  38.2 1.9 %collective-permute-start.8 = (f32[1024,128]{1,0:T(8,128)S(1)}, f32[1024,128]{1,0:T(8,128)S(1)}, u32[]{:S(2)}, u32[]{:S(2)}) collective-permute-start(f32[1024,128]{1,0:T(8,128)S(1)} %collective-permute-done.7.part_ref), channel_id=1, source_target_pairs={{0,1},{1,0},{2,3},{3,2},{4,5},{5,4},{6,7},{7,6},{8,9},{9,8},{10,11... | collective-permute-start | bytes 1572872 | tf_op jit(solution)/shard_map/ppermute | solution.py:33
  41.8 14.0 %collective-permute-start.9 = (f32[64,1024]{1,0:T(8,128)S(1)}, f32[64,1024]{1,0:T(8,128)S(1)}, u32[]{:S(2)}, u32[]{:S(2)}) collective-permute-start(f32[64,1024]{1,0:T(8,128)S(1)} %get-tuple-element.80), channel_id=1, source_target_pairs={{0,4},{4,0},{8,12},{12,8},{16,20},{20,16},{24,28},{28,24},{1,5},{5... | collective-permute-start | bytes 786440 | tf_op jit(solution)/shard_map/ppermute | solution.py:33
  43.6 6.6 %collective-permute-start.10 = (f32[128,128]{1,0:T(8,128)S(1)}, f32[128,128]{1,0:T(8,128)S(1)}, u32[]{:S(2)}, u32[]{:S(2)}) collective-permute-start(f32[128,128]{1,0:T(8,128)S(1)} %add.63), channel_id=1, source_target_pairs={{0,16},{4,20},{8,24},{12,28},{16,0},{20,4},{24,8},{28,12},{1,17},{... | collective-permute-start | bytes 196616 | tf_op jit(solution)/shard_map/ppermute | solution.py:33
  50.2 1.3 %collective-permute-start.11 = (f32[128,128]{1,0:T(8,128)S(1)}, f32[128,128]{1,0:T(8,128)S(1)}, u32[]{:S(2)}, u32[]{:S(2)}) collective-permute-start(f32[128,128]{1,0:T(8,128)S(1)} %add.64), channel_id=1, source_target_pairs={{0,1},{1,0},{2,3},{3,2},{4,5},{5,4},{6,7},{7,6},{8,9},{9,8},{10,11... | collective-permute-start | bytes 196616 | tf_op jit(solution)/shard_map/ppermute | solution.py:33
  51.5 4.3 %collective-permute-start.12 = (f32[128,128]{1,0:T(8,128)S(1)}, f32[128,128]{1,0:T(8,128)S(1)}, u32[]{:S(2)}, u32[]{:S(2)}) collective-permute-start(f32[128,128]{1,0:T(8,128)S(1)} %add.65), channel_id=1, source_target_pairs={{0,2},{1,3},{2,0},{3,1},{4,6},{5,7},{6,4},{7,5},{8,10},{9,11},{10,... | collective-permute-start | bytes 196616 | tf_op jit(solution)/shard_map/ppermute | solution.py:33
  55.9 6.7 %collective-permute-start.13 = (f32[16,1024]{1,0:T(8,128)S(1)}, f32[16,1024]{1,0:T(8,128)S(1)}, u32[]{:S(2)}, u32[]{:S(2)}) collective-permute-start(f32[16,1024]{1,0:T(8,128)S(1)} %get-tuple-element.85), channel_id=1, source_target_pairs={{0,24},{4,28},{8,16},{12,20},{16,8},{20,12},{24,0},{28,4},{1,25},{... | collective-permute-start | bytes 196616 | tf_op jit(solution)/shard_map/ppermute | solution.py:33
  59.3 5.2 %collective-permute-start.14 = (f32[16,1024]{1,0:T(8,128)S(1)}, f32[16,1024]{1,0:T(8,128)S(1)}, u32[]{:S(2)}, u32[]{:S(2)}) collective-permute-start(f32[16,1024]{1,0:T(8,128)S(1)} %get-tuple-element.86), channel_id=1, source_target_pairs={{0,16},{4,20},{8,24},{12,28},{16,0},{20,4},{24,8},{28,12},{1,17},{... | collective-permute-start | bytes 196616 | tf_op jit(solution)/shard_map/ppermute | solution.py:33
  59.3 5.7 %collective-permute-start.15 = (f32[16,1024]{1,0:T(8,128)S(1)}, f32[16,1024]{1,0:T(8,128)S(1)}, u32[]{:S(2)}, u32[]{:S(2)}) collective-permute-start(f32[16,1024]{1,0:T(8,128)S(1)} %get-tuple-element.87), channel_id=1, source_target_pairs={{0,8},{4,12},{8,0},{12,4},{16,24},{20,28},{24,16},{28,20},{1,9},{5... | collective-permute-start | bytes 196616 | tf_op jit(solution)/shard_map/ppermute | solution.py:33
  65.0 6.5 %collective-permute-start.18 = (f32[16,1024]{1,0:T(8,128)S(1)}, f32[16,1024]{1,0:T(8,128)S(1)}, u32[]{:S(2)}, u32[]{:S(2)}) collective-permute-start(f32[16,1024]{1,0:T(8,128)S(1)} %add_add_fusion), channel_id=1, source_target_pairs={{0,24},{4,28},{8,16},{12,20},{16,8},{20,12},{24,0},{28,4},{1,25},{... | collective-permute-start | bytes 196616 | tf_op jit(solution)/shard_map/ppermute | solution.py:33
  66.6 6.2 %collective-permute-start.17 = (f32[16,1024]{1,0:T(8,128)S(1)}, f32[16,1024]{1,0:T(8,128)S(1)}, u32[]{:S(2)}, u32[]{:S(2)}) collective-permute-start(f32[16,1024]{1,0:T(8,128)S(1)} %add_add_fusion), channel_id=1, source_target_pairs={{0,16},{4,20},{8,24},{12,28},{16,0},{20,4},{24,8},{28,12},{1,17},{... | collective-permute-start | bytes 196616 | tf_op jit(solution)/shard_map/ppermute | solution.py:33
  66.7 6.2 %collective-permute-start.16 = (f32[16,1024]{1,0:T(8,128)S(1)}, f32[16,1024]{1,0:T(8,128)S(1)}, u32[]{:S(2)}, u32[]{:S(2)}) collective-permute-start(f32[16,1024]{1,0:T(8,128)S(1)} %add_add_fusion), channel_id=1, source_target_pairs={{0,8},{4,12},{8,0},{12,4},{16,24},{20,28},{24,16},{28,20},{1,9},{5... | collective-permute-start | bytes 196616 | tf_op jit(solution)/shard_map/ppermute | solution.py:33
  72.9 7.3 %collective-permute-start.19 = (f32[64,1024]{1,0:T(8,128)S(1)}, f32[64,1024]{1,0:T(8,128)S(1)}, u32[]{:S(2)}, u32[]{:S(2)}) collective-permute-start(f32[64,1024]{1,0:T(8,128)S(1)} %pad_maximum_fusion.refs_0_), channel_id=1, source_target_pairs={{0,4},{4,0},{8,12},{12,8},{16,20},{20,16},{24,28},{28,24},{1,5},{5... | collective-permute-start | bytes 786440 | tf_op jit(solution)/shard_map/ppermute | solution.py:33
  82.0 3.5 %collective-permute-start.22 = (f32[128,128]{1,0:T(8,128)S(1)}, f32[128,128]{1,0:T(8,128)S(1)}, u32[]{:S(2)}, u32[]{:S(2)}) collective-permute-start(f32[128,128]{1,0:T(8,128)S(1)} %get-tuple-element.103), channel_id=1, source_target_pairs={{0,1},{1,0},{2,3},{3,2},{4,5},{5,4},{6,7},{7,6},{8,9},{9,8},{10,11... | collective-permute-start | bytes 196616 | tf_op jit(solution)/shard_map/ppermute | solution.py:33
  82.0 4.0 %collective-permute-start.21 = (f32[128,128]{1,0:T(8,128)S(1)}, f32[128,128]{1,0:T(8,128)S(1)}, u32[]{:S(2)}, u32[]{:S(2)}) collective-permute-start(f32[128,128]{1,0:T(8,128)S(1)} %get-tuple-element.103), channel_id=1, source_target_pairs={{0,3},{1,2},{2,1},{3,0},{4,7},{5,6},{6,5},{7,4},{8,11},{9,10},{10,... | collective-permute-start | bytes 196616 | tf_op jit(solution)/shard_map/ppermute | solution.py:33
  83.6 4.3 %collective-permute-start.20 = (f32[128,128]{1,0:T(8,128)S(1)}, f32[128,128]{1,0:T(8,128)S(1)}, u32[]{:S(2)}, u32[]{:S(2)}) collective-permute-start(f32[128,128]{1,0:T(8,128)S(1)} %get-tuple-element.103), channel_id=1, source_target_pairs={{0,2},{1,3},{2,0},{3,1},{4,6},{5,7},{6,4},{7,5},{8,10},{9,11},{10,... | collective-permute-start | bytes 196616 | tf_op jit(solution)/shard_map/ppermute | solution.py:33

commit v10 on v9

--- a/solution.py
+++ b/solution.py
@@ -15,6 +15,7 @@
 TILE = 256
 RUN = 128
 SLICES = 8
+CUTS = ((1, 2, 4), (2, 4, 1))
 SMEM = pl.BlockSpec(memory_space=pltpu.SMEM)
 VMEM = pl.BlockSpec(memory_space=pltpu.VMEM)
 HBM = pl.BlockSpec(memory_space=pltpu.HBM)
@@ -31,6 +32,27 @@
 
 def swap(value, axis, bit):
     return lax.ppermute(value, axis, [(i, i ^ bit) for i in range(lax.axis_size(axis))])
+
+
+def stage(value, step):
+    nrow, ncol = lax.axis_size("row"), lax.axis_size("col")
+    pairs = [
+        (r * ncol + c, (r ^ CUTS[c % 2][step]) * ncol + c) for r in range(nrow) for c in range(ncol)
+    ]
+    return lax.ppermute(value, ("row", "col"), pairs)
+
+
+def slice_rows(own_ref, index, step):
+    even, odd = [order(cut)[index] for cut in CUTS]
+    place = jnp.where(own_ref[0] % 2 == 0, even, odd)
+    return pl.ds(pl.multiple_of((place ^ own_ref[1]) * step, step), step)
+
+
+def order(bits):
+    places = [0]
+    for bit in reversed(bits):
+        places = places + [place ^ bit for place in places]
+    return places
 
 
 def dot(a, b, a_dim, b_dim, precision=full):
@@ -153,10 +175,10 @@
             total[:, tile] = value
     if slices:
         step = total.shape[0] // slices
-        for place in range(slices):
-            at = pl.multiple_of((place ^ own_ref[1]) * step, step)
-            row = place // 2 * step
-            outs[1 - place % 2][row : row + step] = total[pl.ds(at, step)]
+        for index in range(slices):
+            row = index % (slices // 2) * step
+            keep = index < slices // 2
+            outs[1 if keep else 0][row : row + step] = total[slice_rows(own_ref, index, step)]
 
 
 def project(own, rows, part, before=None, slices=0, start=0):
@@ -254,10 +276,10 @@
 def finish_kernel(own_ref, inverse_ref, *refs):
     parts, (out_ref, gram_ref, total) = refs[:-3], refs[-3:]
     step = total.shape[0] // SLICES
-    for place in range(SLICES):
-        at = pl.multiple_of((place ^ own_ref[1]) * step, step)
-        row = place // 2 * step
-        total[pl.ds(at, step)] = parts[place % 2][row : row + step]
+    for index in range(SLICES):
+        row = index % (SLICES // 2) * step
+        half = index // (SLICES // 2)
+        total[slice_rows(own_ref, index, step)] = parts[half][row : row + step]
     upper, rest = split(inverse_ref[...])
     stack = jnp.concatenate([upper, rest], 0)
     width = upper.shape[0]
@@ -318,43 +340,45 @@
     third = swap(sketched, "col", 2)
     second = swap(sketched, "col", 1)
     gram = dot(sketched, sketched, 0, 0)
-    far = swap(gram, "row", bits[0])
+    far = swap(gram, "row", bits[2])
     (acc,) = project(own, rows0, sketched)
     far, acc, second = fence((far, acc, second))
     gram = gram + far
     far = swap(gram, "row", bits[1])
     (acc,) = project(own, rows1, second, acc)
-    far, acc, third = fence((far, acc, third))
+    far, acc = fence((far, acc))
+    gram = gram + far
+    for bit in bits[3:]:
+        gram = gram + swap(gram, "row", bit)
+    far = swap(gram, "row", bits[0])
+    third, acc, far = fence((third, acc, far))
     gram = gram + far
     fourth = swap(third, "col", 1)
     (acc,) = project(own, rows2, third, acc)
     fourth, acc = fence((fourth, acc))
+    far = swap(gram, "col", 1)
     send, keep = project(own, rows3, fourth, acc, SLICES)
-    send, keep, gram = fence((send, keep, gram))
-
-    got = swap(send, "row", 1)
-    for bit in bits[2:]:
-        gram = gram + swap(gram, "row", bit)
-    gram = gram + swap(gram, "col", 1)
-    got, state = fence((got, gram + swap(gram, "col", 2)))
-    step = keep.shape[0] // 4
-    quads = [keep[i * step : (i + 1) * step] + got[i * step : (i + 1) * step] for i in range(4)]
-    *quads, state = fence((*quads, state))
-    got = [swap(quads[i], "row", 2 * i) for i in (3, 2, 1)]
-    *got, state = fence((*got, factor(0, 3, state)))
-    mine = (quads[0] + got[0]) + (got[1] + got[2])
+    far, send, keep = fence((far, send, keep))
+    gram = gram + far
+
+    got, state = fence((stage(send, 0), gram + swap(gram, "col", 2)))
+    keep = keep + got
+    for step in (1, 2):
+        half = keep.shape[0] // 2
+        keep, send, state = fence((keep[:half], keep[half:], state))
+        got, state = fence((stage(send, step), factor(step - 1, 3, state)))
+        keep = keep + got
     for bit in bits[3:]:
-        mine = mine + swap(mine, "row", bit)
-    mine, state = fence((mine, state))
-    got = [swap(mine, "row", 2 * i) for i in (1, 2, 3)]
-    *got, state = fence((*got, factor(1, 3, state)))
-    keep = jnp.concatenate([mine, *got], 0)
+        keep = keep + swap(keep, "row", bit)
     keep, state = fence((keep, state))
-    got, inverse = fence((swap(keep, "row", 1), factor(2, 3, state)))
+    got, inverse = fence((stage(keep, 2), factor(2, 3, state)))
+    keep, inverse = fence((jnp.concatenate([keep, got], 0), inverse))
+    got, basis = fence((stage(keep, 1), dot(sketched, inverse, 1, 1)))
+    keep, inverse = fence((jnp.concatenate([keep, got], 0), inverse))
+    got = stage(keep, 0)
     projected, small = finish(own, inverse, [keep, got])
 
     across = [swap(small, "col", bit) for bit in (2, 3, 1)]
-    *across, basis = fence((*across, dot(sketched, inverse, 1, 1)))
     small = (small + across[2]) + (across[0] + across[1])
     return (basis, projected, small / total_rows)
 

time: 88.7 us -> 90 us (1.015)
  waiting for transfers between devices: 30.6 us -> 32 us
    ppermute x23 -> x15, starting transfers between devices: 26.6 us -> 13.8 us  [swap(): lax.ppermute(value, axis, [(i, i ^ bit) for i in range(lax.axis_size(axis...]
    ppermute x0 -> x6, starting transfers between devices: none -> 12.2 us  [stage(): return lax.ppermute(value, ('row', 'col'), pairs)]
    ppermute x0 -> x6, waiting for transfers between devices: none -> 11.4 us  [stage(): return lax.ppermute(value, ('row', 'col'), pairs)]
    ppermute x23 -> x15, waiting for transfers between devices: 30.6 us -> 20.7 us  [swap(): lax.ppermute(value, axis, [(i, i ^ bit) for i in range(lax.axis_size(axis...]
  transfers between devices with their start and end apart: 23 -> 21, of which waited for: 16 -> 16; matrix products, arithmetic and copies ran while one was open for 3% -> 3% of each run, Pallas kernels for 20% -> 22%
where the time goes in v10:
time: 90 us; the launch traced here: 89.4 us
  waiting for transfers between devices  32 us (36%)
  Pallas kernels  27.1 us (30%)
  starting transfers between devices  25.9 us (29%)
  matrix products  2.4 us (3%)
  other arithmetic  1.01 us (1%)
    ppermute x15, waiting for transfers between devices, swap(): lax.ppermute(value, axis, [(i, i ^ bit) for i in range(lax.axis_size(axis...  20.7 us
    ppermute x15, starting transfers between devices, swap(): lax.ppermute(value, axis, [(i, i ^ bit) for i in range(lax.axis_size(axis...  13.8 us
    ppermute x6, starting transfers between devices, stage(): return lax.ppermute(value, ('row', 'col'), pairs)  12.2 us
    ppermute x6, waiting for transfers between devices, stage(): return lax.ppermute(value, ('row', 'col'), pairs)  11.4 us
    pallas_call x2, Pallas kernels, sketch(): pl.pallas_call(functools.partial(sketch_kernel, places, ahead, first), in...  10.7 us
    pallas_call x4, Pallas kernels, project(): pl.pallas_call(functools.partial(project_kernel, start, before is not Non...  6.82 us
    pallas_call x3, Pallas kernels, factor(): pl.pallas_call(functools.partial(factor_kernel, index, count), in_specs=[...  6.37 us
    dot_general x2, matrix products, dot(): lax.dot_general(a, b, (((a_dim,), (b_dim,)), ((), ())), precision=precisi...  2.4 us
  transfers between devices with their start and end apart: 21, of which 16 were waited for; matrix products, arithmetic and copies ran while one was open for 3% of the time, Pallas kernels for 22%

profile of v10, /device:TPU:0, one launch (start us, length us, event | category | flops | bytes accessed | tf_op | source)
XLA Modules:
  0.0 89.4 jit_solution(1127051995103917928)
XLA Ops:
  0.7 5.6 %partial_sketch.2 = (f32[1024,128]{1,0:T(8,128)S(1)}, f32[1024,1024]{1,0:T(8,128)S(1)}, f32[1024,1024]{1,0:T(8,128)S(1)}, bf16[1024,256]{1,0:T(8,128)(2,1)S(1)}) custom-call(s32[2]{0:T(128)S(1)} %pad_add_fusion.own_ref, f32[4096,1024]{1,0:T(8,128)} %data_ref.3, f32[1024,128]{1,0:T(8,128)} %omega_ref.1), custom_call_target="tpu_custom_call" | custom-call | flops 1 | bytes 10485 | tf_op jit(solution)/shard_map/partial_sketch/pallas_call | solution.py:129
  6.9 1.3 %partial_sketch_held.1 = f32[1024,128]{1,0:T(8,128)S(1)} custom-call(f32[1024,1024]{1,0:T(8,128)S(1)} %get-tuple-element.55.rows_ref, bf16[1024,256]{1,0:T(8,128)(2,1)S(1)} %get-tuple-element.58.wide_ref.omega_ref), custom_call_target="tpu_custom_call" | custom-call | flops 1 | bytes 10485 | tf_op jit(solution)/shard_map/partial_sketch_held/pallas_call | solution.py:147
  8.5 3.0 %collective-permute-start.3 = (f32[1024,128]{1,0:T(8,128)S(1)}, f32[1024,128]{1,0:T(8,128)S(1)}, u32[]{:S(2)}, u32[]{:S(2)}) collective-permute-start(f32[1024,128]{1,0:T(8,128)S(1)} %add.47), channel_id=1, source_target_pairs={{0,2},{1,3},{2,0},{3,1},{4,6},{5,7},{6,4},{7,5},{8,10},{9,11},{10,... | collective-permute-start | bytes 1572872 | tf_op jit(solution)/shard_map/ppermute | solution.py:34
  11.5 5.1 %partial_sketch.3 = (f32[1024,128]{1,0:T(8,128)S(1)}, f32[1024,128]{1,0:T(8,128)S(1)}, f32[1024,1024]{1,0:T(8,128)S(1)}, f32[1024,1024]{1,0:T(8,128)S(1)}) custom-call(s32[2]{0:T(128)S(1)} %pad_add_fusion.own_ref, f32[4096,1024]{1,0:T(8,128)} %data_ref.3, bf16[1024,256]{1,0:T(8,128)(2,1)S(1)} %get-tuple-element.58.wide_ref.omega_ref), custom_call_target="tpu_custom_call" | custom-call | flops 1 | bytes 10485 | tf_op jit(solution)/shard_map/partial_sketch/pallas_call | solution.py:129
  18.6 5.1 %collective-permute-done.3 = f32[1024,128]{1,0:T(8,128)S(1)} collective-permute-done((f32[1024,128]{1,0:T(8,128)S(1)}, f32[1024,128]{1,0:T(8,128)S(1)}, u32[]{:S(2)}, u32[]{:S(2)}) %collective-permute-start.3) | collective-permute-done | bytes 524320 | tf_op jit(solution)/shard_map/ppermute | solution.py:34
  23.8 1.8 %collective-permute-start.7 = (f32[1024,128]{1,0:T(8,128)S(1)}, f32[1024,128]{1,0:T(8,128)S(1)}, u32[]{:S(2)}, u32[]{:S(2)}) collective-permute-start(f32[1024,128]{1,0:T(8,128)S(1)} %fusion.part_ref), channel_id=1, source_target_pairs={{0,2},{1,3},{2,0},{3,1},{4,6},{5,7},{6,4},{7,5},{8,10},{9,11},{10,... | collective-permute-start | bytes 1572872 | tf_op jit(solution)/shard_map/ppermute | solution.py:34
  26.7 2.7 %collective-permute-start.4 = (f32[128,128]{1,0:T(8,128)S(1)}, f32[128,128]{1,0:T(8,128)S(1)}, u32[]{:S(2)}, u32[]{:S(2)}) collective-permute-start(f32[128,128]{1,0:T(8,128)S(1)} %fusion.4), channel_id=1, source_target_pairs={{0,16},{4,20},{8,24},{12,28},{16,0},{20,4},{24,8},{28,12},{1,17},{... | collective-permute-start | bytes 196616 | tf_op jit(solution)/shard_map/ppermute | solution.py:34
  29.3 1.7 %project.4.refs_0_ = f32[128,1024]{1,0:T(8,128)S(1)} custom-call(s32[2]{0:T(128)S(1)} %pad_add_fusion.own_ref, f32[1024,1024]{1,0:T(8,128)S(1)} %get-tuple-element.65.rows_ref, f32[1024,128]{1,0:T(8,128)S(1)} %fusion.part_ref), custom_call_target="tpu_custom_call" | custom-call | flops 1 | bytes 6291456 | tf_op jit(solution)/shard_map/project/pallas_call | solution.py:192
  31.0 2.3 %collective-permute-done.4 = f32[128,128]{1,0:T(8,128)S(1)} collective-permute-done((f32[128,128]{1,0:T(8,128)S(1)}, f32[128,128]{1,0:T(8,128)S(1)}, u32[]{:S(2)}, u32[]{:S(2)}) %collective-permute-start.4) | collective-permute-done | bytes 65568 | tf_op jit(solution)/shard_map/ppermute | solution.py:34
  34.0 1.7 %project.5.refs_0_ = f32[128,1024]{1,0:T(8,128)S(1)} custom-call(s32[2]{0:T(128)S(1)} %pad_add_fusion.own_ref, f32[1024,1024]{1,0:T(8,128)S(1)} %get-tuple-element.67.rows_ref, f32[1024,128]{1,0:T(8,128)S(1)} %collective-permute-done.5.part_ref, f32[128,1024]{1,0:T(8,128)S(1)} %project.4.refs_0_), custom_call_target="tpu_custom_call" | custom-call | flops 1 | bytes 6291456 | tf_op jit(solution)/shard_map/project/pallas_call | solution.py:192
  35.7 2.0 %collective-permute-done.6 = f32[128,128]{1,0:T(8,128)S(1)} collective-permute-done((f32[128,128]{1,0:T(8,128)S(1)}, f32[128,128]{1,0:T(8,128)S(1)}, u32[]{:S(2)}, u32[]{:S(2)}) %collective-permute-start.6) | collective-permute-done | bytes 65568 | tf_op jit(solution)/shard_map/ppermute | solution.py:34
  37.7 1.6 %collective-permute-start.8 = (f32[128,128]{1,0:T(8,128)S(1)}, f32[128,128]{1,0:T(8,128)S(1)}, u32[]{:S(2)}, u32[]{:S(2)}) collective-permute-start(f32[128,128]{1,0:T(8,128)S(1)} %add.51), channel_id=1, source_target_pairs={{0,4},{4,0},{8,12},{12,8},{16,20},{20,16},{24,28},{28,24},{1,5},{5... | collective-permute-start | bytes 196616 | tf_op jit(solution)/shard_map/ppermute | solution.py:34
  39.2 2.8 %collective-permute-done.8 = f32[128,128]{1,0:T(8,128)S(1)} collective-permute-done((f32[128,128]{1,0:T(8,128)S(1)}, f32[128,128]{1,0:T(8,128)S(1)}, u32[]{:S(2)}, u32[]{:S(2)}) %collective-permute-start.8) | collective-permute-done | bytes 65568 | tf_op jit(solution)/shard_map/ppermute | solution.py:34
  42.6 1.7 %project.6.refs_0_ = f32[128,1024]{1,0:T(8,128)S(1)} custom-call(s32[2]{0:T(128)S(1)} %pad_add_fusion.own_ref, f32[1024,1024]{1,0:T(8,128)S(1)} %get-tuple-element.55.rows_ref, f32[1024,128]{1,0:T(8,128)S(1)} %collective-permute-done.7.part_ref, f32[128,1024]{1,0:T(8,128)S(1)} %project.5.refs_0_), custom_call_target="tpu_custom_call" | custom-call | flops 1 | bytes 6291456 | tf_op jit(solution)/shard_map/project/pallas_call | solution.py:192
  44.3 1.7 %project.7 = (f32[64,1024]{1,0:T(8,128)S(1)}, f32[64,1024]{1,0:T(8,128)S(1)}) custom-call(s32[2]{0:T(128)S(1)} %pad_add_fusion.own_ref, f32[1024,1024]{1,0:T(8,128)S(1)} %get-tuple-element.73.rows_ref, f32[1024,128]{1,0:T(8,128)S(1)} %collective-permute-done.10.part_ref, f32[128,1024]{1,0:T(8,128)S(1)} %project.6.refs_0_), custom_call_target="tpu_custom_call" | custom-call | flops 1 | bytes 6291456 | tf_op jit(solution)/shard_map/project/pallas_call | solution.py:192
  46.1 1.6 %collective-permute-start.11 = (f32[64,1024]{1,0:T(8,128)S(1)}, f32[64,1024]{1,0:T(8,128)S(1)}, u32[]{:S(2)}, u32[]{:S(2)}) collective-permute-start(f32[64,1024]{1,0:T(8,128)S(1)} %get-tuple-element.81), channel_id=1, source_target_pairs={{0,4},{1,9},{2,6},{3,11},{4,0},{5,13},{6,2},{7,15},{8,12},{9,1},{1... | collective-permute-start | bytes 786440 | tf_op jit(solution)/shard_map/ppermute | solution.py:42
  48.2 3.8 %collective-permute-done.12 = f32[128,128]{1,0:T(8,128)S(1)} collective-permute-done((f32[128,128]{1,0:T(8,128)S(1)}, f32[128,128]{1,0:T(8,128)S(1)}, u32[]{:S(2)}, u32[]{:S(2)}) %collective-permute-start.12) | collective-permute-done | bytes 65568 | tf_op jit(solution)/shard_map/ppermute | solution.py:34
  53.2 2.2 %factor.3.in_ref = f32[128,256]{1,0:T(8,128)S(1)} custom-call(f32[128,128]{1,0:T(8,128)S(1)} %add.54.in_ref), custom_call_target="tpu_custom_call" | custom-call | flops 1 | bytes 10485 | tf_op jit(solution)/shard_map/factor/pallas_call | solution.py:264
  55.4 2.2 %collective-permute-done.13 = f32[32,1024]{1,0:T(8,128)S(1)} collective-permute-done((f32[32,1024]{1,0:T(8,128)S(1)}, f32[32,1024]{1,0:T(8,128)S(1)}, u32[]{:S(2)}, u32[]{:S(2)}) %collective-permute-start.13) | collective-permute-done | bytes 131104 | tf_op jit(solution)/shard_map/ppermute | solution.py:42
  57.7 2.5 %collective-permute-start.14 = (f32[16,1024]{1,0:T(8,128)S(1)}, f32[16,1024]{1,0:T(8,128)S(1)}, u32[]{:S(2)}, u32[]{:S(2)}) collective-permute-start(f32[16,1024]{1,0:T(8,128)S(1)} %get-tuple-element.91), channel_id=1, source_target_pairs={{0,16},{1,5},{2,18},{3,7},{4,20},{5,1},{6,22},{7,3},{8,24},{9,13},... | collective-permute-start | bytes 196616 | tf_op jit(solution)/shard_map/ppermute | solution.py:42
  60.2 2.1 %factor.4.in_ref = f32[128,256]{1,0:T(8,128)S(1)} custom-call(f32[128,256]{1,0:T(8,128)S(1)} %factor.3.in_ref), custom_call_target="tpu_custom_call" | custom-call | flops 1 | bytes 10485 | tf_op jit(solution)/shard_map/factor/pallas_call | solution.py:264
  62.9 2.5 %collective-permute-start.15 = (f32[16,1024]{1,0:T(8,128)S(1)}, f32[16,1024]{1,0:T(8,128)S(1)}, u32[]{:S(2)}, u32[]{:S(2)}) collective-permute-start(f32[16,1024]{1,0:T(8,128)S(1)} %add.57), channel_id=1, source_target_pairs={{0,16},{1,5},{2,18},{3,7},{4,20},{5,1},{6,22},{7,3},{8,24},{9,13},... | collective-permute-start | bytes 196616 | tf_op jit(solution)/shard_map/ppermute | solution.py:42
  65.4 2.1 %factor.5.inverse_ref = f32[128,128]{1,0:T(8,128)S(1)} custom-call(f32[128,256]{1,0:T(8,128)S(1)} %factor.4.in_ref), custom_call_target="tpu_custom_call" | custom-call | flops 1 | bytes 10485 | tf_op jit(solution)/shard_map/factor/pallas_call | solution.py:264
  68.1 3.4 %collective-permute-start.16 = (f32[32,1024]{1,0:T(8,128)S(1)}, f32[32,1024]{1,0:T(8,128)S(1)}, u32[]{:S(2)}, u32[]{:S(2)}) collective-permute-start(f32[32,1024]{1,0:T(8,128)S(1)} %pad_maximum_fusion.1), channel_id=1, source_target_pairs={{0,8},{1,17},{2,10},{3,19},{4,12},{5,21},{6,14},{7,23},{8,0},{9,25... | collective-permute-start | bytes 393224 | tf_op jit(solution)/shard_map/ppermute | solution.py:42
  71.6 1.4 %fusion.5 = f32[1024,128]{1,0:T(8,128)} fusion(f32[1024,128]{1,0:T(8,128)S(1)} %fusion.part_ref, f32[128,128]{1,0:T(8,128)S(1)} %factor.5.inverse_ref), kind=kOutput, calls=%fused_computation.10 | convolution fusion | flops 201326592 | bytes 1114112 | tf_op jit(solution)/shard_map/dot_general | solution.py:59
  72.9 2.5 %collective-permute-done.16 = f32[32,1024]{1,0:T(8,128)S(1)} collective-permute-done((f32[32,1024]{1,0:T(8,128)S(1)}, f32[32,1024]{1,0:T(8,128)S(1)}, u32[]{:S(2)}, u32[]{:S(2)}) %collective-permute-start.16) | collective-permute-done | bytes 131104 | tf_op jit(solution)/shard_map/ppermute | solution.py:42
  75.5 1.6 %collective-permute-start.17 = (f32[64,1024]{1,0:T(8,128)S(1)}, f32[64,1024]{1,0:T(8,128)S(1)}, u32[]{:S(2)}, u32[]{:S(2)}) collective-permute-start(f32[64,1024]{1,0:T(8,128)S(1)} %pad_maximum_fusion.refs_0_), channel_id=1, source_target_pairs={{0,4},{1,9},{2,6},{3,11},{4,0},{5,13},{6,2},{7,15},{8,12},{9,1},{1... | collective-permute-start | bytes 786440 | tf_op jit(solution)/shard_map/ppermute | solution.py:42
  77.1 4.9 %collective-permute-done.17.refs_1_ = f32[64,1024]{1,0:T(8,128)S(1)} collective-permute-done((f32[64,1024]{1,0:T(8,128)S(1)}, f32[64,1024]{1,0:T(8,128)S(1)}, u32[]{:S(2)}, u32[]{:S(2)}) %collective-permute-start.17) | collective-permute-done | bytes 262176 | tf_op jit(solution)/shard_map/ppermute | solution.py:42
  81.9 1.9 %finish.1 = (f32[128,1024]{1,0:T(8,128)}, f32[128,128]{1,0:T(8,128)S(1)}) custom-call(s32[2]{0:T(128)S(1)} %pad_add_fusion.own_ref, f32[128,128]{1,0:T(8,128)S(1)} %factor.5.inverse_ref, f32[64,1024]{1,0:T(8,128)S(1)} %pad_maximum_fusion.refs_0_, f32[64,1024]{1,0:T(8,128)S(1)} %collective-permute-done.17.refs_1_), custom_call_target="tpu_custom_call" | custom-call | flops 1 | bytes 8388608 | tf_op jit(solution)/shard_map/finish/pallas_call | solution.py:307
  84.3 1.3 %collective-permute-start.18 = (f32[128,128]{1,0:T(8,128)S(1)}, f32[128,128]{1,0:T(8,128)S(1)}, u32[]{:S(2)}, u32[]{:S(2)}) collective-permute-start(f32[128,128]{1,0:T(8,128)S(1)} %get-tuple-element.106), channel_id=1, source_target_pairs={{0,1},{1,0},{2,3},{3,2},{4,5},{5,4},{6,7},{7,6},{8,9},{9,8},{10,11... | collective-permute-start | bytes 196616 | tf_op jit(solution)/shard_map/ppermute | solution.py:34
  85.6 2.0 %collective-permute-done.20 = f32[128,128]{1,0:T(8,128)S(1)} collective-permute-done((f32[128,128]{1,0:T(8,128)S(1)}, f32[128,128]{1,0:T(8,128)S(1)}, u32[]{:S(2)}, u32[]{:S(2)}) %collective-permute-start.20) | collective-permute-done | bytes 65568 | tf_op jit(solution)/shard_map/ppermute | solution.py:34
  87.6 1.1 %collective-permute-done.19 = f32[128,128]{1,0:T(8,128)S(1)} collective-permute-done((f32[128,128]{1,0:T(8,128)S(1)}, f32[128,128]{1,0:T(8,128)S(1)}, u32[]{:S(2)}, u32[]{:S(2)}) %collective-permute-start.19) | collective-permute-done | bytes 65568 | tf_op jit(solution)/shard_map/ppermute | solution.py:34
  (40 shorter events, 9.7 us)
Async XLA Ops:
  6.4 2.1 %collective-permute-start = (f32[1024,128]{1,0:T(8,128)S(1)}, f32[1024,128]{1,0:T(8,128)S(1)}, u32[]{:S(2)}, u32[]{:S(2)}) collective-permute-start(f32[1024,128]{1,0:T(8,128)S(1)} %get-tuple-element.57), channel_id=1, source_target_pairs={{0,1},{1,0},{2,3},{3,2},{4,5},{5,4},{6,7},{7,6},{8,9},{9,8},{10,11... | collective-permute-start | bytes 1572872 | tf_op jit(solution)/shard_map/ppermute | solution.py:34
  8.5 15.2 %collective-permute-start.3 = (f32[1024,128]{1,0:T(8,128)S(1)}, f32[1024,128]{1,0:T(8,128)S(1)}, u32[]{:S(2)}, u32[]{:S(2)}) collective-permute-start(f32[1024,128]{1,0:T(8,128)S(1)} %add.47), channel_id=1, source_target_pairs={{0,2},{1,3},{2,0},{3,1},{4,6},{5,7},{6,4},{7,5},{8,10},{9,11},{10,... | collective-permute-start | bytes 1572872 | tf_op jit(solution)/shard_map/ppermute | solution.py:34
  16.6 1.6 %collective-permute-start.2 = (f32[512,128]{1,0:T(8,128)S(1)}, f32[512,128]{1,0:T(8,128)S(1)}, u32[]{:S(2)}, u32[]{:S(2)}) collective-permute-start(f32[512,128]{1,0:T(8,128)S(1)} %get-tuple-element.107), channel_id=1, source_target_pairs={{0,1},{1,0},{2,3},{3,2},{4,5},{5,4},{6,7},{7,6},{8,9},{9,8},{10,11... | collective-permute-start | bytes 786440 | tf_op jit(solution)/shard_map/ppermute | solution.py:34
  16.7 1.9 %collective-permute-start.1 = (f32[512,128]{1,0:T(8,128)S(1)}, f32[512,128]{1,0:T(8,128)S(1)}, u32[]{:S(2)}, u32[]{:S(2)}) collective-permute-start(f32[512,128]{1,0:T(8,128)S(1)} %get-tuple-element.108), channel_id=1, source_target_pairs={{0,1},{1,0},{2,3},{3,2},{4,5},{5,4},{6,7},{7,6},{8,9},{9,8},{10,11... | collective-permute-start | bytes 786440 | tf_op jit(solution)/shard_map/ppermute | solution.py:34
  23.8 9.6 %collective-permute-start.5 = (f32[1024,128]{1,0:T(8,128)S(1)}, f32[1024,128]{1,0:T(8,128)S(1)}, u32[]{:S(2)}, u32[]{:S(2)}) collective-permute-start(f32[1024,128]{1,0:T(8,128)S(1)} %fusion.part_ref), channel_id=1, source_target_pairs={{0,1},{1,0},{2,3},{3,2},{4,5},{5,4},{6,7},{7,6},{8,9},{9,8},{10,11... | collective-permute-start | bytes 1572872 | tf_op jit(solution)/shard_map/ppermute | solution.py:34
  23.8 15.4 %collective-permute-start.7 = (f32[1024,128]{1,0:T(8,128)S(1)}, f32[1024,128]{1,0:T(8,128)S(1)}, u32[]{:S(2)}, u32[]{:S(2)}) collective-permute-start(f32[1024,128]{1,0:T(8,128)S(1)} %fusion.part_ref), channel_id=1, source_target_pairs={{0,2},{1,3},{2,0},{3,1},{4,6},{5,7},{6,4},{7,5},{8,10},{9,11},{10,... | collective-permute-start | bytes 1572872 | tf_op jit(solution)/shard_map/ppermute | solution.py:34
  26.7 6.6 %collective-permute-start.4 = (f32[128,128]{1,0:T(8,128)S(1)}, f32[128,128]{1,0:T(8,128)S(1)}, u32[]{:S(2)}, u32[]{:S(2)}) collective-permute-start(f32[128,128]{1,0:T(8,128)S(1)} %fusion.4), channel_id=1, source_target_pairs={{0,16},{4,20},{8,24},{12,28},{16,0},{20,4},{24,8},{28,12},{1,17},{... | collective-permute-start | bytes 196616 | tf_op jit(solution)/shard_map/ppermute | solution.py:34
  33.3 4.3 %collective-permute-start.6 = (f32[128,128]{1,0:T(8,128)S(1)}, f32[128,128]{1,0:T(8,128)S(1)}, u32[]{:S(2)}, u32[]{:S(2)}) collective-permute-start(f32[128,128]{1,0:T(8,128)S(1)} %add.50), channel_id=1, source_target_pairs={{0,8},{4,12},{8,0},{12,4},{16,24},{20,28},{24,16},{28,20},{1,9},{5... | collective-permute-start | bytes 196616 | tf_op jit(solution)/shard_map/ppermute | solution.py:34
  37.7 4.3 %collective-permute-start.8 = (f32[128,128]{1,0:T(8,128)S(1)}, f32[128,128]{1,0:T(8,128)S(1)}, u32[]{:S(2)}, u32[]{:S(2)}) collective-permute-start(f32[128,128]{1,0:T(8,128)S(1)} %add.51), channel_id=1, source_target_pairs={{0,4},{4,0},{8,12},{12,8},{16,20},{20,16},{24,28},{28,24},{1,5},{5... | collective-permute-start | bytes 196616 | tf_op jit(solution)/shard_map/ppermute | solution.py:34
  42.0 2.3 %collective-permute-start.10 = (f32[1024,128]{1,0:T(8,128)S(1)}, f32[1024,128]{1,0:T(8,128)S(1)}, u32[]{:S(2)}, u32[]{:S(2)}) collective-permute-start(f32[1024,128]{1,0:T(8,128)S(1)} %collective-permute-done.7.part_ref), channel_id=1, source_target_pairs={{0,1},{1,0},{2,3},{3,2},{4,5},{5,4},{6,7},{7,6},{8,9},{9,8},{10,11... | collective-permute-start | bytes 1572872 | tf_op jit(solution)/shard_map/ppermute | solution.py:34
  42.0 4.0 %collective-permute-start.9 = (f32[128,128]{1,0:T(8,128)S(1)}, f32[128,128]{1,0:T(8,128)S(1)}, u32[]{:S(2)}, u32[]{:S(2)}) collective-permute-start(f32[128,128]{1,0:T(8,128)S(1)} %add.52), channel_id=1, source_target_pairs={{0,1},{1,0},{2,3},{3,2},{4,5},{5,4},{6,7},{7,6},{8,9},{9,8},{10,11... | collective-permute-start | bytes 196616 | tf_op jit(solution)/shard_map/ppermute | solution.py:34
  46.1 6.4 %collective-permute-start.11 = (f32[64,1024]{1,0:T(8,128)S(1)}, f32[64,1024]{1,0:T(8,128)S(1)}, u32[]{:S(2)}, u32[]{:S(2)}) collective-permute-start(f32[64,1024]{1,0:T(8,128)S(1)} %get-tuple-element.81), channel_id=1, source_target_pairs={{0,4},{1,9},{2,6},{3,11},{4,0},{5,13},{6,2},{7,15},{8,12},{9,1},{1... | collective-permute-start | bytes 786440 | tf_op jit(solution)/shard_map/ppermute | solution.py:42
  47.6 4.3 %collective-permute-start.12 = (f32[128,128]{1,0:T(8,128)S(1)}, f32[128,128]{1,0:T(8,128)S(1)}, u32[]{:S(2)}, u32[]{:S(2)}) collective-permute-start(f32[128,128]{1,0:T(8,128)S(1)} %add.53), channel_id=1, source_target_pairs={{0,2},{1,3},{2,0},{3,1},{4,6},{5,7},{6,4},{7,5},{8,10},{9,11},{10,... | collective-permute-start | bytes 196616 | tf_op jit(solution)/shard_map/ppermute | solution.py:34
  52.6 5.0 %collective-permute-start.13 = (f32[32,1024]{1,0:T(8,128)S(1)}, f32[32,1024]{1,0:T(8,128)S(1)}, u32[]{:S(2)}, u32[]{:S(2)}) collective-permute-start(f32[32,1024]{1,0:T(8,128)S(1)} %get-tuple-element.86), channel_id=1, source_target_pairs={{0,8},{1,17},{2,10},{3,19},{4,12},{5,21},{6,14},{7,23},{8,0},{9,25... | collective-permute-start | bytes 393224 | tf_op jit(solution)/shard_map/ppermute | solution.py:42
  57.7 5.2 %collective-permute-start.14 = (f32[16,1024]{1,0:T(8,128)S(1)}, f32[16,1024]{1,0:T(8,128)S(1)}, u32[]{:S(2)}, u32[]{:S(2)}) collective-permute-start(f32[16,1024]{1,0:T(8,128)S(1)} %get-tuple-element.91), channel_id=1, source_target_pairs={{0,16},{1,5},{2,18},{3,7},{4,20},{5,1},{6,22},{7,3},{8,24},{9,13},... | collective-permute-start | bytes 196616 | tf_op jit(solution)/shard_map/ppermute | solution.py:42
  62.9 5.2 %collective-permute-start.15 = (f32[16,1024]{1,0:T(8,128)S(1)}, f32[16,1024]{1,0:T(8,128)S(1)}, u32[]{:S(2)}, u32[]{:S(2)}) collective-permute-start(f32[16,1024]{1,0:T(8,128)S(1)} %add.57), channel_id=1, source_target_pairs={{0,16},{1,5},{2,18},{3,7},{4,20},{5,1},{6,22},{7,3},{8,24},{9,13},... | collective-permute-start | bytes 196616 | tf_op jit(solution)/shard_map/ppermute | solution.py:42
  68.1 7.3 %collective-permute-start.16 = (f32[32,1024]{1,0:T(8,128)S(1)}, f32[32,1024]{1,0:T(8,128)S(1)}, u32[]{:S(2)}, u32[]{:S(2)}) collective-permute-start(f32[32,1024]{1,0:T(8,128)S(1)} %pad_maximum_fusion.1), channel_id=1, source_target_pairs={{0,8},{1,17},{2,10},{3,19},{4,12},{5,21},{6,14},{7,23},{8,0},{9,25... | collective-permute-start | bytes 393224 | tf_op jit(solution)/shard_map/ppermute | solution.py:42
  75.5 6.4 %collective-permute-start.17 = (f32[64,1024]{1,0:T(8,128)S(1)}, f32[64,1024]{1,0:T(8,128)S(1)}, u32[]{:S(2)}, u32[]{:S(2)}) collective-permute-start(f32[64,1024]{1,0:T(8,128)S(1)} %pad_maximum_fusion.refs_0_), channel_id=1, source_target_pairs={{0,4},{1,9},{2,6},{3,11},{4,0},{5,13},{6,2},{7,15},{8,12},{9,1},{1... | collective-permute-start | bytes 786440 | tf_op jit(solution)/shard_map/ppermute | solution.py:42
  83.8 3.8 %collective-permute-start.20 = (f32[128,128]{1,0:T(8,128)S(1)}, f32[128,128]{1,0:T(8,128)S(1)}, u32[]{:S(2)}, u32[]{:S(2)}) collective-permute-start(f32[128,128]{1,0:T(8,128)S(1)} %get-tuple-element.106), channel_id=1, source_target_pairs={{0,3},{1,2},{2,1},{3,0},{4,7},{5,6},{6,5},{7,4},{8,11},{9,10},{10,... | collective-permute-start | bytes 196616 | tf_op jit(solution)/shard_map/ppermute | solution.py:34
  83.8 4.9 %collective-permute-start.19 = (f32[128,128]{1,0:T(8,128)S(1)}, f32[128,128]{1,0:T(8,128)S(1)}, u32[]{:S(2)}, u32[]{:S(2)}) collective-permute-start(f32[128,128]{1,0:T(8,128)S(1)} %get-tuple-element.106), channel_id=1, source_target_pairs={{0,2},{1,3},{2,0},{3,1},{4,6},{5,7},{6,4},{7,5},{8,10},{9,11},{10,... | collective-permute-start | bytes 196616 | tf_op jit(solution)/shard_map/ppermute | solution.py:34
  84.3 4.4 %collective-permute-start.18 = (f32[128,128]{1,0:T(8,128)S(1)}, f32[128,128]{1,0:T(8,128)S(1)}, u32[]{:S(2)}, u32[]{:S(2)}) collective-permute-start(f32[128,128]{1,0:T(8,128)S(1)} %get-tuple-element.106), channel_id=1, source_target_pairs={{0,1},{1,0},{2,3},{3,2},{4,5},{5,4},{6,7},{7,6},{8,9},{9,8},{10,11... | collective-permute-start | bytes 196616 | tf_op jit(solution)/shard_map/ppermute | solution.py:34

commit v11 on v9

--- a/solution.py
+++ b/solution.py
@@ -155,8 +155,8 @@
         step = total.shape[0] // slices
         for place in range(slices):
             at = pl.multiple_of((place ^ own_ref[1]) * step, step)
-            row = place // 2 * step
-            outs[1 - place % 2][row : row + step] = total[pl.ds(at, step)]
+            group, row = ((0, 0), (1, 0), (1, step), (0, step))[place // 2]
+            outs[2 * (place % 2) + group][row : row + step] = total[pl.ds(at, step)]
 
 
 def project(own, rows, part, before=None, slices=0, start=0):
@@ -164,7 +164,7 @@
     width = part.shape[1]
     args = [own, rows, part] + ([] if before is None else [before])
     if slices:
-        out = [jax.ShapeDtypeStruct((width // 2, cols), f32)] * 2
+        out = [jax.ShapeDtypeStruct((width // 4, cols), f32)] * 4
     else:
         out = [jax.ShapeDtypeStruct((width, cols), f32)]
     return pl.pallas_call(
@@ -324,32 +324,39 @@
     gram = gram + far
     far = swap(gram, "row", bits[1])
     (acc,) = project(own, rows1, second, acc)
-    far, acc, third = fence((far, acc, third))
+    far, acc = fence((far, acc))
     gram = gram + far
+    far = swap(gram, "row", bits[2])
+    third, acc, far = fence((third, acc, far))
+    gram = gram + far
+    for bit in bits[3:]:
+        gram = gram + swap(gram, "row", bit)
     fourth = swap(third, "col", 1)
     (acc,) = project(own, rows2, third, acc)
     fourth, acc = fence((fourth, acc))
-    send, keep = project(own, rows3, fourth, acc, SLICES)
-    send, keep, gram = fence((send, keep, gram))
-
-    got = swap(send, "row", 1)
-    for bit in bits[2:]:
-        gram = gram + swap(gram, "row", bit)
-    gram = gram + swap(gram, "col", 1)
-    got, state = fence((got, gram + swap(gram, "col", 2)))
-    step = keep.shape[0] // 4
-    quads = [keep[i * step : (i + 1) * step] + got[i * step : (i + 1) * step] for i in range(4)]
-    *quads, state = fence((*quads, state))
-    got = [swap(quads[i], "row", 2 * i) for i in (3, 2, 1)]
-    *got, state = fence((*got, factor(0, 3, state)))
-    mine = (quads[0] + got[0]) + (got[1] + got[2])
+    far = swap(gram, "col", 1)
+    outer_keep, inner_keep, outer_send, inner_send = project(own, rows3, fourth, acc, SLICES)
+    far, outer_keep, inner_keep, outer_send, inner_send = fence(
+        (far, outer_keep, inner_keep, outer_send, inner_send)
+    )
+    gram = gram + far
+
+    step = outer_keep.shape[0] // 2
+    outer_got, state = fence((swap(outer_send, "row", 1), gram + swap(gram, "col", 2)))
+    zero, six = outer_keep[:step] + outer_got[:step], outer_keep[step:] + outer_got[step:]
+    zero, six, state = fence((zero, six, state))
+    six = swap(six, "row", 6)
+    inner_got = swap(inner_send, "row", 1)
+    two, four = inner_keep[:step] + inner_got[:step], inner_keep[step:] + inner_got[step:]
+    four, two = swap(four, "row", 4), swap(two, "row", 2)
+    six, four, two, state = fence((six, four, two, factor(0, 3, state)))
+    zero = (zero + two) + (four + six)
     for bit in bits[3:]:
-        mine = mine + swap(mine, "row", bit)
-    mine, state = fence((mine, state))
-    got = [swap(mine, "row", 2 * i) for i in (1, 2, 3)]
+        zero = zero + swap(zero, "row", bit)
+    zero, state = fence((zero, state))
+    got = [swap(zero, "row", q) for q in (2, 4, 6)]
     *got, state = fence((*got, factor(1, 3, state)))
-    keep = jnp.concatenate([mine, *got], 0)
-    keep, state = fence((keep, state))
+    keep, state = fence((jnp.concatenate([zero, *got], 0), state))
     got, inverse = fence((swap(keep, "row", 1), factor(2, 3, state)))
     projected, small = finish(own, inverse, [keep, got])
 

time: 88.7 us -> 83.8 us (0.945)
  waiting for transfers between devices: 30.6 us -> 22.7 us
  starting transfers between devices: 26.6 us -> 29.6 us
    ppermute x23 -> x24, waiting for transfers between devices: 30.6 us -> 22.7 us  [swap(): lax.ppermute(value, axis, [(i, i ^ bit) for i in range(lax.axis_size(axis...]
    ppermute x23 -> x24, starting transfers between devices: 26.6 us -> 29.6 us  [swap(): lax.ppermute(value, axis, [(i, i ^ bit) for i in range(lax.axis_size(axis...]
  transfers between devices with their start and end apart: 23 -> 24, of which waited for: 16 -> 15; matrix products, arithmetic and copies ran while one was open for 3% -> 3% of each run, Pallas kernels for 20% -> 23%
where the time goes in v11:
time: 83.8 us; the launch traced here: 83.7 us
  starting transfers between devices  29.6 us (35%)
  Pallas kernels  27.1 us (32%)
  waiting for transfers between devices  22.7 us (27%)
  matrix products  2.4 us (3%)
  other arithmetic  1 us (1%)
  between operations  0.84 us (1%)
    ppermute x24, starting transfers between devices, swap(): lax.ppermute(value, axis, [(i, i ^ bit) for i in range(lax.axis_size(axis...  29.6 us
    ppermute x24, waiting for transfers between devices, swap(): lax.ppermute(value, axis, [(i, i ^ bit) for i in range(lax.axis_size(axis...  22.7 us
    pallas_call x2, Pallas kernels, sketch(): pl.pallas_call(functools.partial(sketch_kernel, places, ahead, first), in...  10.7 us
    pallas_call x4, Pallas kernels, project(): pl.pallas_call(functools.partial(project_kernel, start, before is not Non...  6.82 us
    pallas_call x3, Pallas kernels, factor(): pl.pallas_call(functools.partial(factor_kernel, index, count), in_specs=[...  6.38 us
    dot_general x2, matrix products, dot(): lax.dot_general(a, b, (((a_dim,), (b_dim,)), ((), ())), precision=precisi...  2.4 us
    pallas_call x1, Pallas kernels, finish(): pl.pallas_call(finish_kernel, in_specs=[SMEM] + [VMEM] * (1 + len(parts))...  1.87 us
  transfers between devices with their start and end apart: 24, of which 15 were waited for; matrix products, arithmetic and copies ran while one was open for 3% of the time, Pallas kernels for 23%

profile of v11, /device:TPU:0, one launch (start us, length us, event | category | flops | bytes accessed | tf_op | source)
XLA Modules:
  0.0 83.7 jit_solution(3451591466165517899)
XLA Ops:
  0.7 5.6 %partial_sketch.2 = (f32[1024,128]{1,0:T(8,128)S(1)}, f32[1024,1024]{1,0:T(8,128)S(1)}, f32[1024,1024]{1,0:T(8,128)S(1)}, bf16[1024,256]{1,0:T(8,128)(2,1)S(1)}) custom-call(s32[2]{0:T(128)S(1)} %pad_add_fusion.own_ref, f32[4096,1024]{1,0:T(8,128)} %data_ref.3, f32[1024,128]{1,0:T(8,128)} %omega_ref.1), custom_call_target="tpu_custom_call" | custom-call | flops 1 | bytes 10485 | tf_op jit(solution)/shard_map/partial_sketch/pallas_call | solution.py:107
  6.9 1.3 %partial_sketch_held.1 = f32[1024,128]{1,0:T(8,128)S(1)} custom-call(f32[1024,1024]{1,0:T(8,128)S(1)} %get-tuple-element.60.rows_ref, bf16[1024,256]{1,0:T(8,128)(2,1)S(1)} %get-tuple-element.63.wide_ref.omega_ref), custom_call_target="tpu_custom_call" | custom-call | flops 1 | bytes 10485 | tf_op jit(solution)/shard_map/partial_sketch_held/pallas_call | solution.py:125
  8.5 3.0 %collective-permute-start.3 = (f32[1024,128]{1,0:T(8,128)S(1)}, f32[1024,128]{1,0:T(8,128)S(1)}, u32[]{:S(2)}, u32[]{:S(2)}) collective-permute-start(f32[1024,128]{1,0:T(8,128)S(1)} %add.59), channel_id=1, source_target_pairs={{0,2},{1,3},{2,0},{3,1},{4,6},{5,7},{6,4},{7,5},{8,10},{9,11},{10,... | collective-permute-start | bytes 1572872 | tf_op jit(solution)/shard_map/ppermute | solution.py:33
  11.5 5.1 %partial_sketch.3 = (f32[1024,128]{1,0:T(8,128)S(1)}, f32[1024,128]{1,0:T(8,128)S(1)}, f32[1024,1024]{1,0:T(8,128)S(1)}, f32[1024,1024]{1,0:T(8,128)S(1)}) custom-call(s32[2]{0:T(128)S(1)} %pad_add_fusion.own_ref, f32[4096,1024]{1,0:T(8,128)} %data_ref.3, bf16[1024,256]{1,0:T(8,128)(2,1)S(1)} %get-tuple-element.63.wide_ref.omega_ref), custom_call_target="tpu_custom_call" | custom-call | flops 1 | bytes 10485 | tf_op jit(solution)/shard_map/partial_sketch/pallas_call | solution.py:107
  18.6 5.1 %collective-permute-done.3 = f32[1024,128]{1,0:T(8,128)S(1)} collective-permute-done((f32[1024,128]{1,0:T(8,128)S(1)}, f32[1024,128]{1,0:T(8,128)S(1)}, u32[]{:S(2)}, u32[]{:S(2)}) %collective-permute-start.3) | collective-permute-done | bytes 524320 | tf_op jit(solution)/shard_map/ppermute | solution.py:33
  23.8 1.8 %collective-permute-start.7 = (f32[1024,128]{1,0:T(8,128)S(1)}, f32[1024,128]{1,0:T(8,128)S(1)}, u32[]{:S(2)}, u32[]{:S(2)}) collective-permute-start(f32[1024,128]{1,0:T(8,128)S(1)} %fusion.part_ref), channel_id=1, source_target_pairs={{0,2},{1,3},{2,0},{3,1},{4,6},{5,7},{6,4},{7,5},{8,10},{9,11},{10,... | collective-permute-start | bytes 1572872 | tf_op jit(solution)/shard_map/ppermute | solution.py:33
  25.6 1.0 %fusion.2 = f32[128,128]{1,0:T(8,128)S(1)} fusion(f32[1024,128]{1,0:T(8,128)S(1)} %fusion.part_ref), kind=kOutput, calls=%fused_computation.11 | convolution fusion | flops 201326592 | bytes 589824 | tf_op jit(solution)/shard_map/dot_general | solution.py:37
  26.7 1.6 %collective-permute-start.4 = (f32[128,128]{1,0:T(8,128)S(1)}, f32[128,128]{1,0:T(8,128)S(1)}, u32[]{:S(2)}, u32[]{:S(2)}) collective-permute-start(f32[128,128]{1,0:T(8,128)S(1)} %fusion.2), channel_id=1, source_target_pairs={{0,4},{4,0},{8,12},{12,8},{16,20},{20,16},{24,28},{28,24},{1,5},{5... | collective-permute-start | bytes 196616 | tf_op jit(solution)/shard_map/ppermute | solution.py:33
  28.2 1.7 %project.4.refs_0_ = f32[128,1024]{1,0:T(8,128)S(1)} custom-call(s32[2]{0:T(128)S(1)} %pad_add_fusion.own_ref, f32[1024,1024]{1,0:T(8,128)S(1)} %get-tuple-element.70.rows_ref, f32[1024,128]{1,0:T(8,128)S(1)} %fusion.part_ref), custom_call_target="tpu_custom_call" | custom-call | flops 1 | bytes 6291456 | tf_op jit(solution)/shard_map/project/pallas_call | solution.py:170
  29.9 1.1 %collective-permute-done.4 = f32[128,128]{1,0:T(8,128)S(1)} collective-permute-done((f32[128,128]{1,0:T(8,128)S(1)}, f32[128,128]{1,0:T(8,128)S(1)}, u32[]{:S(2)}, u32[]{:S(2)}) %collective-permute-start.4) | collective-permute-done | bytes 65568 | tf_op jit(solution)/shard_map/ppermute | solution.py:33
  31.0 1.6 %collective-permute-start.6 = (f32[128,128]{1,0:T(8,128)S(1)}, f32[128,128]{1,0:T(8,128)S(1)}, u32[]{:S(2)}, u32[]{:S(2)}) collective-permute-start(f32[128,128]{1,0:T(8,128)S(1)} %add.62), channel_id=1, source_target_pairs={{0,8},{4,12},{8,0},{12,4},{16,24},{20,28},{24,16},{28,20},{1,9},{5... | collective-permute-start | bytes 196616 | tf_op jit(solution)/shard_map/ppermute | solution.py:33
  32.7 1.7 %project.5.refs_0_ = f32[128,1024]{1,0:T(8,128)S(1)} custom-call(s32[2]{0:T(128)S(1)} %pad_add_fusion.own_ref, f32[1024,1024]{1,0:T(8,128)S(1)} %get-tuple-element.72.rows_ref, f32[1024,128]{1,0:T(8,128)S(1)} %collective-permute-done.5.part_ref, f32[128,1024]{1,0:T(8,128)S(1)} %project.4.refs_0_), custom_call_target="tpu_custom_call" | custom-call | flops 1 | bytes 6291456 | tf_op jit(solution)/shard_map/project/pallas_call | solution.py:170
  35.4 2.7 %collective-permute-start.8 = (f32[128,128]{1,0:T(8,128)S(1)}, f32[128,128]{1,0:T(8,128)S(1)}, u32[]{:S(2)}, u32[]{:S(2)}) collective-permute-start(f32[128,128]{1,0:T(8,128)S(1)} %add.63), channel_id=1, source_target_pairs={{0,16},{4,20},{8,24},{12,28},{16,0},{20,4},{24,8},{28,12},{1,17},{... | collective-permute-start | bytes 196616 | tf_op jit(solution)/shard_map/ppermute | solution.py:33
  38.2 2.4 %collective-permute-done.8 = f32[128,128]{1,0:T(8,128)S(1)} collective-permute-done((f32[128,128]{1,0:T(8,128)S(1)}, f32[128,128]{1,0:T(8,128)S(1)}, u32[]{:S(2)}, u32[]{:S(2)}) %collective-permute-start.8) | collective-permute-done | bytes 65568 | tf_op jit(solution)/shard_map/ppermute | solution.py:33
  41.2 1.7 %project.6.refs_0_ = f32[128,1024]{1,0:T(8,128)S(1)} custom-call(s32[2]{0:T(128)S(1)} %pad_add_fusion.own_ref, f32[1024,1024]{1,0:T(8,128)S(1)} %get-tuple-element.60.rows_ref, f32[1024,128]{1,0:T(8,128)S(1)} %collective-permute-done.7.part_ref, f32[128,1024]{1,0:T(8,128)S(1)} %project.5.refs_0_), custom_call_target="tpu_custom_call" | custom-call | flops 1 | bytes 6291456 | tf_op jit(solution)/shard_map/project/pallas_call | solution.py:170
  42.9 1.7 %project.7 = (f32[32,1024]{1,0:T(8,128)S(1)}, f32[32,1024]{1,0:T(8,128)S(1)}, f32[32,1024]{1,0:T(8,128)S(1)}, f32[32,1024]{1,0:T(8,128)S(1)}) custom-call(s32[2]{0:T(128)S(1)} %pad_add_fusion.own_ref, f32[1024,1024]{1,0:T(8,128)S(1)} %get-tuple-element.78.rows_ref, f32[1024,128]{1,0:T(8,128)S(1)} %collective-permute-done.10.part_ref, ...), custom_call_target="tpu_custom_call" | custom-call | flops 1 | bytes 6291456 | tf_op jit(solution)/shard_map/project/pallas_call | solution.py:170
  44.7 1.6 %collective-permute-start.11 = (f32[32,1024]{1,0:T(8,128)S(1)}, f32[32,1024]{1,0:T(8,128)S(1)}, u32[]{:S(2)}, u32[]{:S(2)}) collective-permute-start(f32[32,1024]{1,0:T(8,128)S(1)} %get-tuple-element.88), channel_id=1, source_target_pairs={{0,4},{4,0},{8,12},{12,8},{16,20},{20,16},{24,28},{28,24},{1,5},{5... | collective-permute-start | bytes 393224 | tf_op jit(solution)/shard_map/ppermute | solution.py:33
  47.1 3.4 %collective-permute-done.12 = f32[128,128]{1,0:T(8,128)S(1)} collective-permute-done((f32[128,128]{1,0:T(8,128)S(1)}, f32[128,128]{1,0:T(8,128)S(1)}, u32[]{:S(2)}, u32[]{:S(2)}) %collective-permute-start.12) | collective-permute-done | bytes 65568 | tf_op jit(solution)/shard_map/ppermute | solution.py:33
  51.1 4.2 %collective-permute-start.13 = (f32[16,1024]{1,0:T(8,128)S(1)}, f32[16,1024]{1,0:T(8,128)S(1)}, u32[]{:S(2)}, u32[]{:S(2)}) collective-permute-start(f32[16,1024]{1,0:T(8,128)S(1)} %get-tuple-element.93), channel_id=1, source_target_pairs={{0,24},{4,28},{8,16},{12,20},{16,8},{20,12},{24,0},{28,4},{1,25},{... | collective-permute-start | bytes 196616 | tf_op jit(solution)/shard_map/ppermute | solution.py:33
  55.5 2.3 %collective-permute-start.15 = (f32[16,1024]{1,0:T(8,128)S(1)}, f32[16,1024]{1,0:T(8,128)S(1)}, u32[]{:S(2)}, u32[]{:S(2)}) collective-permute-start(f32[16,1024]{1,0:T(8,128)S(1)} %get-tuple-element.120), channel_id=1, source_target_pairs={{0,16},{4,20},{8,24},{12,28},{16,0},{20,4},{24,8},{28,12},{1,17},{... | collective-permute-start | bytes 196616 | tf_op jit(solution)/shard_map/ppermute | solution.py:33
  57.8 2.2 %factor.3.in_ref = f32[128,256]{1,0:T(8,128)S(1)} custom-call(f32[128,128]{1,0:T(8,128)S(1)} %add.66.in_ref), custom_call_target="tpu_custom_call" | custom-call | flops 1 | bytes 10485 | tf_op jit(solution)/shard_map/factor/pallas_call | solution.py:242
  60.7 2.2 %collective-permute-start.19 = (f32[16,1024]{1,0:T(8,128)S(1)}, f32[16,1024]{1,0:T(8,128)S(1)}, u32[]{:S(2)}, u32[]{:S(2)}) collective-permute-start(f32[16,1024]{1,0:T(8,128)S(1)} %add_add_fusion), channel_id=1, source_target_pairs={{0,24},{4,28},{8,16},{12,20},{16,8},{20,12},{24,0},{28,4},{1,25},{... | collective-permute-start | bytes 196616 | tf_op jit(solution)/shard_map/ppermute | solution.py:33
  62.9 1.3 %collective-permute-start.18 = (f32[16,1024]{1,0:T(8,128)S(1)}, f32[16,1024]{1,0:T(8,128)S(1)}, u32[]{:S(2)}, u32[]{:S(2)}) collective-permute-start(f32[16,1024]{1,0:T(8,128)S(1)} %add_add_fusion), channel_id=1, source_target_pairs={{0,16},{4,20},{8,24},{12,28},{16,0},{20,4},{24,8},{28,12},{1,17},{... | collective-permute-start | bytes 196616 | tf_op jit(solution)/shard_map/ppermute | solution.py:33
  65.2 2.1 %factor.4.in_ref = f32[128,256]{1,0:T(8,128)S(1)} custom-call(f32[128,256]{1,0:T(8,128)S(1)} %factor.3.in_ref), custom_call_target="tpu_custom_call" | custom-call | flops 1 | bytes 10485 | tf_op jit(solution)/shard_map/factor/pallas_call | solution.py:242
  67.3 1.6 %collective-permute-done.18 = f32[16,1024]{1,0:T(8,128)S(1)} collective-permute-done((f32[16,1024]{1,0:T(8,128)S(1)}, f32[16,1024]{1,0:T(8,128)S(1)}, u32[]{:S(2)}, u32[]{:S(2)}) %collective-permute-start.18) | collective-permute-done | bytes 65568 | tf_op jit(solution)/shard_map/ppermute | solution.py:33
  68.9 1.6 %collective-permute-start.20 = (f32[64,1024]{1,0:T(8,128)S(1)}, f32[64,1024]{1,0:T(8,128)S(1)}, u32[]{:S(2)}, u32[]{:S(2)}) collective-permute-start(f32[64,1024]{1,0:T(8,128)S(1)} %pad_maximum_fusion.refs_0_), channel_id=1, source_target_pairs={{0,4},{4,0},{8,12},{12,8},{16,20},{20,16},{24,28},{28,24},{1,5},{5... | collective-permute-start | bytes 786440 | tf_op jit(solution)/shard_map/ppermute | solution.py:33
  70.5 2.1 %factor.5.inverse_ref = f32[128,128]{1,0:T(8,128)S(1)} custom-call(f32[128,256]{1,0:T(8,128)S(1)} %factor.4.in_ref), custom_call_target="tpu_custom_call" | custom-call | flops 1 | bytes 10485 | tf_op jit(solution)/shard_map/factor/pallas_call | solution.py:242
  72.6 2.8 %collective-permute-done.20.refs_1_ = f32[64,1024]{1,0:T(8,128)S(1)} collective-permute-done((f32[64,1024]{1,0:T(8,128)S(1)}, f32[64,1024]{1,0:T(8,128)S(1)}, u32[]{:S(2)}, u32[]{:S(2)}) %collective-permute-start.20) | collective-permute-done | bytes 262176 | tf_op jit(solution)/shard_map/ppermute | solution.py:33
  75.4 1.9 %finish.1 = (f32[128,1024]{1,0:T(8,128)}, f32[128,128]{1,0:T(8,128)S(1)}) custom-call(s32[2]{0:T(128)S(1)} %pad_add_fusion.own_ref, f32[128,128]{1,0:T(8,128)S(1)} %factor.5.inverse_ref, f32[64,1024]{1,0:T(8,128)S(1)} %pad_maximum_fusion.refs_0_, f32[64,1024]{1,0:T(8,128)S(1)} %collective-permute-done.20.refs_1_), custom_call_target="tpu_custom_call" | custom-call | flops 1 | bytes 8388608 | tf_op jit(solution)/shard_map/finish/pallas_call | solution.py:285
  77.5 1.9 %collective-permute-start.21 = (f32[128,128]{1,0:T(8,128)S(1)}, f32[128,128]{1,0:T(8,128)S(1)}, u32[]{:S(2)}, u32[]{:S(2)}) collective-permute-start(f32[128,128]{1,0:T(8,128)S(1)} %get-tuple-element.111), channel_id=1, source_target_pairs={{0,2},{1,3},{2,0},{3,1},{4,6},{5,7},{6,4},{7,5},{8,10},{9,11},{10,... | collective-permute-start | bytes 196616 | tf_op jit(solution)/shard_map/ppermute | solution.py:33
  79.4 1.4 %fusion.3 = f32[1024,128]{1,0:T(8,128)} fusion(f32[1024,128]{1,0:T(8,128)S(1)} %fusion.part_ref, f32[128,128]{1,0:T(8,128)S(1)} %factor.5.inverse_ref), kind=kOutput, calls=%fused_computation.12 | convolution fusion | flops 201326592 | bytes 1114112 | tf_op jit(solution)/shard_map/dot_general | solution.py:37
  81.0 2.1 %collective-permute-done.21 = f32[128,128]{1,0:T(8,128)S(1)} collective-permute-done((f32[128,128]{1,0:T(8,128)S(1)}, f32[128,128]{1,0:T(8,128)S(1)}, u32[]{:S(2)}, u32[]{:S(2)}) %collective-permute-start.21) | collective-permute-done | bytes 65568 | tf_op jit(solution)/shard_map/ppermute | solution.py:33
  (43 shorter events, 9.2 us)
Async XLA Ops:
  6.4 2.1 %collective-permute-start = (f32[1024,128]{1,0:T(8,128)S(1)}, f32[1024,128]{1,0:T(8,128)S(1)}, u32[]{:S(2)}, u32[]{:S(2)}) collective-permute-start(f32[1024,128]{1,0:T(8,128)S(1)} %get-tuple-element.62), channel_id=1, source_target_pairs={{0,1},{1,0},{2,3},{3,2},{4,5},{5,4},{6,7},{7,6},{8,9},{9,8},{10,11... | collective-permute-start | bytes 1572872 | tf_op jit(solution)/shard_map/ppermute | solution.py:33
  8.5 15.2 %collective-permute-start.3 = (f32[1024,128]{1,0:T(8,128)S(1)}, f32[1024,128]{1,0:T(8,128)S(1)}, u32[]{:S(2)}, u32[]{:S(2)}) collective-permute-start(f32[1024,128]{1,0:T(8,128)S(1)} %add.59), channel_id=1, source_target_pairs={{0,2},{1,3},{2,0},{3,1},{4,6},{5,7},{6,4},{7,5},{8,10},{9,11},{10,... | collective-permute-start | bytes 1572872 | tf_op jit(solution)/shard_map/ppermute | solution.py:33
  16.6 1.6 %collective-permute-start.2 = (f32[512,128]{1,0:T(8,128)S(1)}, f32[512,128]{1,0:T(8,128)S(1)}, u32[]{:S(2)}, u32[]{:S(2)}) collective-permute-start(f32[512,128]{1,0:T(8,128)S(1)} %get-tuple-element.117), channel_id=1, source_target_pairs={{0,1},{1,0},{2,3},{3,2},{4,5},{5,4},{6,7},{7,6},{8,9},{9,8},{10,11... | collective-permute-start | bytes 786440 | tf_op jit(solution)/shard_map/ppermute | solution.py:33
  16.7 1.9 %collective-permute-start.1 = (f32[512,128]{1,0:T(8,128)S(1)}, f32[512,128]{1,0:T(8,128)S(1)}, u32[]{:S(2)}, u32[]{:S(2)}) collective-permute-start(f32[512,128]{1,0:T(8,128)S(1)} %get-tuple-element.118), channel_id=1, source_target_pairs={{0,1},{1,0},{2,3},{3,2},{4,5},{5,4},{6,7},{7,6},{8,9},{9,8},{10,11... | collective-permute-start | bytes 786440 | tf_op jit(solution)/shard_map/ppermute | solution.py:33
  23.8 7.2 %collective-permute-start.5 = (f32[1024,128]{1,0:T(8,128)S(1)}, f32[1024,128]{1,0:T(8,128)S(1)}, u32[]{:S(2)}, u32[]{:S(2)}) collective-permute-start(f32[1024,128]{1,0:T(8,128)S(1)} %fusion.part_ref), channel_id=1, source_target_pairs={{0,1},{1,0},{2,3},{3,2},{4,5},{5,4},{6,7},{7,6},{8,9},{9,8},{10,11... | collective-permute-start | bytes 1572872 | tf_op jit(solution)/shard_map/ppermute | solution.py:33
  23.8 14.3 %collective-permute-start.7 = (f32[1024,128]{1,0:T(8,128)S(1)}, f32[1024,128]{1,0:T(8,128)S(1)}, u32[]{:S(2)}, u32[]{:S(2)}) collective-permute-start(f32[1024,128]{1,0:T(8,128)S(1)} %fusion.part_ref), channel_id=1, source_target_pairs={{0,2},{1,3},{2,0},{3,1},{4,6},{5,7},{6,4},{7,5},{8,10},{9,11},{10,... | collective-permute-start | bytes 1572872 | tf_op jit(solution)/shard_map/ppermute | solution.py:33
  26.7 4.3 %collective-permute-start.4 = (f32[128,128]{1,0:T(8,128)S(1)}, f32[128,128]{1,0:T(8,128)S(1)}, u32[]{:S(2)}, u32[]{:S(2)}) collective-permute-start(f32[128,128]{1,0:T(8,128)S(1)} %fusion.2), channel_id=1, source_target_pairs={{0,4},{4,0},{8,12},{12,8},{16,20},{20,16},{24,28},{28,24},{1,5},{5... | collective-permute-start | bytes 196616 | tf_op jit(solution)/shard_map/ppermute | solution.py:33
  31.0 4.3 %collective-permute-start.6 = (f32[128,128]{1,0:T(8,128)S(1)}, f32[128,128]{1,0:T(8,128)S(1)}, u32[]{:S(2)}, u32[]{:S(2)}) collective-permute-start(f32[128,128]{1,0:T(8,128)S(1)} %add.62), channel_id=1, source_target_pairs={{0,8},{4,12},{8,0},{12,4},{16,24},{20,28},{24,16},{28,20},{1,9},{5... | collective-permute-start | bytes 196616 | tf_op jit(solution)/shard_map/ppermute | solution.py:33
  35.4 5.2 %collective-permute-start.8 = (f32[128,128]{1,0:T(8,128)S(1)}, f32[128,128]{1,0:T(8,128)S(1)}, u32[]{:S(2)}, u32[]{:S(2)}) collective-permute-start(f32[128,128]{1,0:T(8,128)S(1)} %add.63), channel_id=1, source_target_pairs={{0,16},{4,20},{8,24},{12,28},{16,0},{20,4},{24,8},{28,12},{1,17},{... | collective-permute-start | bytes 196616 | tf_op jit(solution)/shard_map/ppermute | solution.py:33
  40.6 2.3 %collective-permute-start.10 = (f32[1024,128]{1,0:T(8,128)S(1)}, f32[1024,128]{1,0:T(8,128)S(1)}, u32[]{:S(2)}, u32[]{:S(2)}) collective-permute-start(f32[1024,128]{1,0:T(8,128)S(1)} %collective-permute-done.7.part_ref), channel_id=1, source_target_pairs={{0,1},{1,0},{2,3},{3,2},{4,5},{5,4},{6,7},{7,6},{8,9},{9,8},{10,11... | collective-permute-start | bytes 1572872 | tf_op jit(solution)/shard_map/ppermute | solution.py:33
  40.6 4.0 %collective-permute-start.9 = (f32[128,128]{1,0:T(8,128)S(1)}, f32[128,128]{1,0:T(8,128)S(1)}, u32[]{:S(2)}, u32[]{:S(2)}) collective-permute-start(f32[128,128]{1,0:T(8,128)S(1)} %add.64), channel_id=1, source_target_pairs={{0,1},{1,0},{2,3},{3,2},{4,5},{5,4},{6,7},{7,6},{8,9},{9,8},{10,11... | collective-permute-start | bytes 196616 | tf_op jit(solution)/shard_map/ppermute | solution.py:33
  44.7 6.4 %collective-permute-start.11 = (f32[32,1024]{1,0:T(8,128)S(1)}, f32[32,1024]{1,0:T(8,128)S(1)}, u32[]{:S(2)}, u32[]{:S(2)}) collective-permute-start(f32[32,1024]{1,0:T(8,128)S(1)} %get-tuple-element.88), channel_id=1, source_target_pairs={{0,4},{4,0},{8,12},{12,8},{16,20},{20,16},{24,28},{28,24},{1,5},{5... | collective-permute-start | bytes 393224 | tf_op jit(solution)/shard_map/ppermute | solution.py:33
  46.2 4.3 %collective-permute-start.12 = (f32[128,128]{1,0:T(8,128)S(1)}, f32[128,128]{1,0:T(8,128)S(1)}, u32[]{:S(2)}, u32[]{:S(2)}) collective-permute-start(f32[128,128]{1,0:T(8,128)S(1)} %add.65), channel_id=1, source_target_pairs={{0,2},{1,3},{2,0},{3,1},{4,6},{5,7},{6,4},{7,5},{8,10},{9,11},{10,... | collective-permute-start | bytes 196616 | tf_op jit(solution)/shard_map/ppermute | solution.py:33
  46.8 8.6 %collective-permute-start.14 = (f32[32,1024]{1,0:T(8,128)S(1)}, f32[32,1024]{1,0:T(8,128)S(1)}, u32[]{:S(2)}, u32[]{:S(2)}) collective-permute-start(f32[32,1024]{1,0:T(8,128)S(1)} %get-tuple-element.95), channel_id=1, source_target_pairs={{0,4},{4,0},{8,12},{12,8},{16,20},{20,16},{24,28},{28,24},{1,5},{5... | collective-permute-start | bytes 393224 | tf_op jit(solution)/shard_map/ppermute | solution.py:33
  51.1 8.9 %collective-permute-start.13 = (f32[16,1024]{1,0:T(8,128)S(1)}, f32[16,1024]{1,0:T(8,128)S(1)}, u32[]{:S(2)}, u32[]{:S(2)}) collective-permute-start(f32[16,1024]{1,0:T(8,128)S(1)} %get-tuple-element.93), channel_id=1, source_target_pairs={{0,24},{4,28},{8,16},{12,20},{16,8},{20,12},{24,0},{28,4},{1,25},{... | collective-permute-start | bytes 196616 | tf_op jit(solution)/shard_map/ppermute | solution.py:33
  55.4 4.7 %collective-permute-start.16 = (f32[16,1024]{1,0:T(8,128)S(1)}, f32[16,1024]{1,0:T(8,128)S(1)}, u32[]{:S(2)}, u32[]{:S(2)}) collective-permute-start(f32[16,1024]{1,0:T(8,128)S(1)} %get-tuple-element.119), channel_id=1, source_target_pairs={{0,8},{4,12},{8,0},{12,4},{16,24},{20,28},{24,16},{28,20},{1,9},{5... | collective-permute-start | bytes 196616 | tf_op jit(solution)/shard_map/ppermute | solution.py:33
  55.5 5.2 %collective-permute-start.15 = (f32[16,1024]{1,0:T(8,128)S(1)}, f32[16,1024]{1,0:T(8,128)S(1)}, u32[]{:S(2)}, u32[]{:S(2)}) collective-permute-start(f32[16,1024]{1,0:T(8,128)S(1)} %get-tuple-element.120), channel_id=1, source_target_pairs={{0,16},{4,20},{8,24},{12,28},{16,0},{20,4},{24,8},{28,12},{1,17},{... | collective-permute-start | bytes 196616 | tf_op jit(solution)/shard_map/ppermute | solution.py:33
  60.7 6.5 %collective-permute-start.19 = (f32[16,1024]{1,0:T(8,128)S(1)}, f32[16,1024]{1,0:T(8,128)S(1)}, u32[]{:S(2)}, u32[]{:S(2)}) collective-permute-start(f32[16,1024]{1,0:T(8,128)S(1)} %add_add_fusion), channel_id=1, source_target_pairs={{0,24},{4,28},{8,16},{12,20},{16,8},{20,12},{24,0},{28,4},{1,25},{... | collective-permute-start | bytes 196616 | tf_op jit(solution)/shard_map/ppermute | solution.py:33
  62.9 6.0 %collective-permute-start.18 = (f32[16,1024]{1,0:T(8,128)S(1)}, f32[16,1024]{1,0:T(8,128)S(1)}, u32[]{:S(2)}, u32[]{:S(2)}) collective-permute-start(f32[16,1024]{1,0:T(8,128)S(1)} %add_add_fusion), channel_id=1, source_target_pairs={{0,16},{4,20},{8,24},{12,28},{16,0},{20,4},{24,8},{28,12},{1,17},{... | collective-permute-start | bytes 196616 | tf_op jit(solution)/shard_map/ppermute | solution.py:33
  64.2 4.7 %collective-permute-start.17 = (f32[16,1024]{1,0:T(8,128)S(1)}, f32[16,1024]{1,0:T(8,128)S(1)}, u32[]{:S(2)}, u32[]{:S(2)}) collective-permute-start(f32[16,1024]{1,0:T(8,128)S(1)} %add_add_fusion), channel_id=1, source_target_pairs={{0,8},{4,12},{8,0},{12,4},{16,24},{20,28},{24,16},{28,20},{1,9},{5... | collective-permute-start | bytes 196616 | tf_op jit(solution)/shard_map/ppermute | solution.py:33
  68.9 6.4 %collective-permute-start.20 = (f32[64,1024]{1,0:T(8,128)S(1)}, f32[64,1024]{1,0:T(8,128)S(1)}, u32[]{:S(2)}, u32[]{:S(2)}) collective-permute-start(f32[64,1024]{1,0:T(8,128)S(1)} %pad_maximum_fusion.refs_0_), channel_id=1, source_target_pairs={{0,4},{4,0},{8,12},{12,8},{16,20},{20,16},{24,28},{28,24},{1,5},{5... | collective-permute-start | bytes 786440 | tf_op jit(solution)/shard_map/ppermute | solution.py:33
  77.2 3.5 %collective-permute-start.23 = (f32[128,128]{1,0:T(8,128)S(1)}, f32[128,128]{1,0:T(8,128)S(1)}, u32[]{:S(2)}, u32[]{:S(2)}) collective-permute-start(f32[128,128]{1,0:T(8,128)S(1)} %get-tuple-element.111), channel_id=1, source_target_pairs={{0,1},{1,0},{2,3},{3,2},{4,5},{5,4},{6,7},{7,6},{8,9},{9,8},{10,11... | collective-permute-start | bytes 196616 | tf_op jit(solution)/shard_map/ppermute | solution.py:33
  77.2 3.7 %collective-permute-start.22 = (f32[128,128]{1,0:T(8,128)S(1)}, f32[128,128]{1,0:T(8,128)S(1)}, u32[]{:S(2)}, u32[]{:S(2)}) collective-permute-start(f32[128,128]{1,0:T(8,128)S(1)} %get-tuple-element.111), channel_id=1, source_target_pairs={{0,3},{1,2},{2,1},{3,0},{4,7},{5,6},{6,5},{7,4},{8,11},{9,10},{10,... | collective-permute-start | bytes 196616 | tf_op jit(solution)/shard_map/ppermute | solution.py:33
  77.5 5.5 %collective-permute-start.21 = (f32[128,128]{1,0:T(8,128)S(1)}, f32[128,128]{1,0:T(8,128)S(1)}, u32[]{:S(2)}, u32[]{:S(2)}) collective-permute-start(f32[128,128]{1,0:T(8,128)S(1)} %get-tuple-element.111), channel_id=1, source_target_pairs={{0,2},{1,3},{2,0},{3,1},{4,6},{5,7},{6,4},{7,5},{8,10},{9,11},{10,... | collective-permute-start | bytes 196616 | tf_op jit(solution)/shard_map/ppermute | solution.py:33

commit v12 on v11

--- a/solution.py
+++ b/solution.py
@@ -13,7 +13,7 @@
 
 PIECE = 512
 TILE = 256
-RUN = 128
+RUN = 512
 SLICES = 8
 SMEM = pl.BlockSpec(memory_space=pltpu.SMEM)
 VMEM = pl.BlockSpec(memory_space=pltpu.VMEM)
@@ -179,11 +179,12 @@
     )(*args)
 
 
-def factor_kernel(index, count, in_ref, out_ref, *scratch):
+def factor_kernel(first, end, in_ref, out_ref, *scratch):
     n = in_ref.shape[0]
-    last = index == count - 1
+    panels = n // 8
+    last = end == panels
     work = scratch[0] if last else out_ref
-    if index == 0:
+    if first == 0:
         row = lax.broadcasted_iota(jnp.int32, (n, n), 0)
         col = lax.broadcasted_iota(jnp.int32, (n, n), 1)
         work[:, :n] = in_ref[...]
@@ -191,8 +192,7 @@
     else:
         work[...] = in_ref[...]
     sub = lax.broadcasted_iota(jnp.int32, (8, n), 0)
-    panels = n // 8
-    for b in range(panels * index // count, panels * (index + 1) // count):
+    for b in range(first, end):
         top = slice(8 * b, 8 * b + 8)
         panel = work[top, :]
         spread = [jnp.broadcast_to(panel[:, 8 * b + j : 8 * b + j + 1], (8, n)) for j in range(8)]
@@ -236,11 +236,11 @@
         out_ref[...] = work[:, n:]
 
 
-def factor(index, count, value):
+def factor(first, end, value):
     n = value.shape[0]
-    last = index == count - 1
-    return pl.pallas_call(
-        functools.partial(factor_kernel, index, count),
+    last = end == n // 8
+    return pl.pallas_call(
+        functools.partial(factor_kernel, first, end),
         in_specs=[VMEM],
         out_specs=VMEM,
         out_shape=jax.ShapeDtypeStruct((n, n if last else 2 * n), f32),
@@ -324,13 +324,8 @@
     gram = gram + far
     far = swap(gram, "row", bits[1])
     (acc,) = project(own, rows1, second, acc)
-    far, acc = fence((far, acc))
+    far, acc, third = fence((far, acc, third))
     gram = gram + far
-    far = swap(gram, "row", bits[2])
-    third, acc, far = fence((third, acc, far))
-    gram = gram + far
-    for bit in bits[3:]:
-        gram = gram + swap(gram, "row", bit)
     fourth = swap(third, "col", 1)
     (acc,) = project(own, rows2, third, acc)
     fourth, acc = fence((fourth, acc))
@@ -342,22 +337,25 @@
     gram = gram + far
 
     step = outer_keep.shape[0] // 2
-    outer_got, state = fence((swap(outer_send, "row", 1), gram + swap(gram, "col", 2)))
+    outer_got = swap(outer_send, "row", 1)
     zero, six = outer_keep[:step] + outer_got[:step], outer_keep[step:] + outer_got[step:]
-    zero, six, state = fence((zero, six, state))
+    zero, six = fence((zero, six))
     six = swap(six, "row", 6)
-    inner_got = swap(inner_send, "row", 1)
+    inner_got, far = fence((swap(inner_send, "row", 1), swap(gram, "col", 2)))
+    gram = gram + far
     two, four = inner_keep[:step] + inner_got[:step], inner_keep[step:] + inner_got[step:]
     four, two = swap(four, "row", 4), swap(two, "row", 2)
-    six, four, two, state = fence((six, four, two, factor(0, 3, state)))
+    for bit in bits[2:]:
+        gram = gram + swap(gram, "row", bit)
+    six, four, two, state = fence((six, four, two, gram))
     zero = (zero + two) + (four + six)
     for bit in bits[3:]:
         zero = zero + swap(zero, "row", bit)
     zero, state = fence((zero, state))
     got = [swap(zero, "row", q) for q in (2, 4, 6)]
-    *got, state = fence((*got, factor(1, 3, state)))
+    *got, state = fence((*got, factor(0, 6, state)))
     keep, state = fence((jnp.concatenate([zero, *got], 0), state))
-    got, inverse = fence((swap(keep, "row", 1), factor(2, 3, state)))
+    got, inverse = fence((swap(keep, "row", 1), factor(6, 16, state)))
     projected, small = finish(own, inverse, [keep, got])
 
     across = [swap(small, "col", bit) for bit in (2, 3, 1)]

time: 83.8 us -> 83.8 us (level)
  waiting for transfers between devices: 22.7 us -> 25 us
  Pallas kernels: 27.1 us -> 25.2 us
    ppermute x24, waiting for transfers between devices: 22.7 us -> 25 us  [swap(): lax.ppermute(value, axis, [(i, i ^ bit) for i in range(lax.axis_size(axis...]
    pallas_call x2, Pallas kernels: 10.7 us -> 9.28 us  [sketch(): pl.pallas_call(functools.partial(sketch_kernel, places, ahead, first), in...]
    pallas_call x3 -> x2, Pallas kernels: 6.38 us -> 5.95 us  [factor(): pl.pallas_call(functools.partial(factor_kernel, first, end), in_specs=[VM...]
  transfers between devices with their start and end apart: 24 -> 24, of which waited for: 15 -> 13; matrix products, arithmetic and copies ran while one was open for 3% -> 3% of each run, Pallas kernels for 23% -> 23%
where the time goes in v12:
time: 83.8 us; the launch traced here: 83.7 us
  starting transfers between devices  29.2 us (35%)
  Pallas kernels  25.2 us (30%)
  waiting for transfers between devices  25 us (30%)
  matrix products  2.4 us (3%)
  other arithmetic  1 us (1%)
    ppermute x24, starting transfers between devices, swap(): lax.ppermute(value, axis, [(i, i ^ bit) for i in range(lax.axis_size(axis...  29.2 us
    ppermute x24, waiting for transfers between devices, swap(): lax.ppermute(value, axis, [(i, i ^ bit) for i in range(lax.axis_size(axis...  25 us
    pallas_call x2, Pallas kernels, sketch(): pl.pallas_call(functools.partial(sketch_kernel, places, ahead, first), in...  9.28 us
    pallas_call x4, Pallas kernels, project(): pl.pallas_call(functools.partial(project_kernel, start, before is not Non...  6.82 us
    pallas_call x2, Pallas kernels, factor(): pl.pallas_call(functools.partial(factor_kernel, first, end), in_specs=[VM...  5.95 us
    dot_general x2, matrix products, dot(): lax.dot_general(a, b, (((a_dim,), (b_dim,)), ((), ())), precision=precisi...  2.4 us
    pallas_call x1, Pallas kernels, finish(): pl.pallas_call(finish_kernel, in_specs=[SMEM] + [VMEM] * (1 + len(parts))...  1.87 us
  transfers between devices with their start and end apart: 24, of which 13 were waited for; matrix products, arithmetic and copies ran while one was open for 3% of the time, Pallas kernels for 23%

profile of v12, /device:TPU:0, one launch (start us, length us, event | category | flops | bytes accessed | tf_op | source)
XLA Modules:
  0.0 83.7 jit_solution(8462422290128295799)
XLA Ops:
  0.7 4.2 %partial_sketch.2 = (f32[1024,128]{1,0:T(8,128)S(1)}, f32[1024,1024]{1,0:T(8,128)S(1)}, f32[1024,1024]{1,0:T(8,128)S(1)}, bf16[1024,256]{1,0:T(8,128)(2,1)S(1)}) custom-call(s32[2]{0:T(128)S(1)} %pad_add_fusion.own_ref, f32[4096,1024]{1,0:T(8,128)} %data_ref.3, f32[1024,128]{1,0:T(8,128)} %omega_ref.1), custom_call_target="tpu_custom_call" | custom-call | flops 1 | bytes 10485 | tf_op jit(solution)/shard_map/partial_sketch/pallas_call | solution.py:107
  5.5 1.3 %partial_sketch_held.1 = f32[1024,128]{1,0:T(8,128)S(1)} custom-call(f32[1024,1024]{1,0:T(8,128)S(1)} %get-tuple-element.57.rows_ref, bf16[1024,256]{1,0:T(8,128)(2,1)S(1)} %get-tuple-element.60.wide_ref.omega_ref), custom_call_target="tpu_custom_call" | custom-call | flops 1 | bytes 10485 | tf_op jit(solution)/shard_map/partial_sketch_held/pallas_call | solution.py:125
  7.1 3.0 %collective-permute-start.3 = (f32[1024,128]{1,0:T(8,128)S(1)}, f32[1024,128]{1,0:T(8,128)S(1)}, u32[]{:S(2)}, u32[]{:S(2)}) collective-permute-start(f32[1024,128]{1,0:T(8,128)S(1)} %add.59), channel_id=1, source_target_pairs={{0,2},{1,3},{2,0},{3,1},{4,6},{5,7},{6,4},{7,5},{8,10},{9,11},{10,... | collective-permute-start | bytes 1572872 | tf_op jit(solution)/shard_map/ppermute | solution.py:33
  10.0 5.1 %partial_sketch.3 = (f32[1024,128]{1,0:T(8,128)S(1)}, f32[1024,128]{1,0:T(8,128)S(1)}, f32[1024,1024]{1,0:T(8,128)S(1)}, f32[1024,1024]{1,0:T(8,128)S(1)}) custom-call(s32[2]{0:T(128)S(1)} %pad_add_fusion.own_ref, f32[4096,1024]{1,0:T(8,128)} %data_ref.3, bf16[1024,256]{1,0:T(8,128)(2,1)S(1)} %get-tuple-element.60.wide_ref.omega_ref), custom_call_target="tpu_custom_call" | custom-call | flops 1 | bytes 10485 | tf_op jit(solution)/shard_map/partial_sketch/pallas_call | solution.py:107
  17.1 5.1 %collective-permute-done.3 = f32[1024,128]{1,0:T(8,128)S(1)} collective-permute-done((f32[1024,128]{1,0:T(8,128)S(1)}, f32[1024,128]{1,0:T(8,128)S(1)}, u32[]{:S(2)}, u32[]{:S(2)}) %collective-permute-start.3) | collective-permute-done | bytes 524320 | tf_op jit(solution)/shard_map/ppermute | solution.py:33
  22.4 1.8 %collective-permute-start.7 = (f32[1024,128]{1,0:T(8,128)S(1)}, f32[1024,128]{1,0:T(8,128)S(1)}, u32[]{:S(2)}, u32[]{:S(2)}) collective-permute-start(f32[1024,128]{1,0:T(8,128)S(1)} %fusion.part_ref), channel_id=1, source_target_pairs={{0,2},{1,3},{2,0},{3,1},{4,6},{5,7},{6,4},{7,5},{8,10},{9,11},{10,... | collective-permute-start | bytes 1572872 | tf_op jit(solution)/shard_map/ppermute | solution.py:33
  25.3 1.6 %collective-permute-start.4 = (f32[128,128]{1,0:T(8,128)S(1)}, f32[128,128]{1,0:T(8,128)S(1)}, u32[]{:S(2)}, u32[]{:S(2)}) collective-permute-start(f32[128,128]{1,0:T(8,128)S(1)} %fusion.2), channel_id=1, source_target_pairs={{0,4},{4,0},{8,12},{12,8},{16,20},{20,16},{24,28},{28,24},{1,5},{5... | collective-permute-start | bytes 196616 | tf_op jit(solution)/shard_map/ppermute | solution.py:33
  26.8 1.7 %project.4.refs_0_ = f32[128,1024]{1,0:T(8,128)S(1)} custom-call(s32[2]{0:T(128)S(1)} %pad_add_fusion.own_ref, f32[1024,1024]{1,0:T(8,128)S(1)} %get-tuple-element.67.rows_ref, f32[1024,128]{1,0:T(8,128)S(1)} %fusion.part_ref), custom_call_target="tpu_custom_call" | custom-call | flops 1 | bytes 6291456 | tf_op jit(solution)/shard_map/project/pallas_call | solution.py:170
  29.6 1.6 %collective-permute-start.6 = (f32[128,128]{1,0:T(8,128)S(1)}, f32[128,128]{1,0:T(8,128)S(1)}, u32[]{:S(2)}, u32[]{:S(2)}) collective-permute-start(f32[128,128]{1,0:T(8,128)S(1)} %add.62), channel_id=1, source_target_pairs={{0,8},{4,12},{8,0},{12,4},{16,24},{20,28},{24,16},{28,20},{1,9},{5... | collective-permute-start | bytes 196616 | tf_op jit(solution)/shard_map/ppermute | solution.py:33
  31.2 1.7 %project.5.refs_0_ = f32[128,1024]{1,0:T(8,128)S(1)} custom-call(s32[2]{0:T(128)S(1)} %pad_add_fusion.own_ref, f32[1024,1024]{1,0:T(8,128)S(1)} %get-tuple-element.69.rows_ref, f32[1024,128]{1,0:T(8,128)S(1)} %collective-permute-done.5.part_ref, f32[128,1024]{1,0:T(8,128)S(1)} %project.4.refs_0_), custom_call_target="tpu_custom_call" | custom-call | flops 1 | bytes 6291456 | tf_op jit(solution)/shard_map/project/pallas_call | solution.py:170
  33.0 3.8 %collective-permute-done.7.part_ref = f32[1024,128]{1,0:T(8,128)S(1)} collective-permute-done((f32[1024,128]{1,0:T(8,128)S(1)}, f32[1024,128]{1,0:T(8,128)S(1)}, u32[]{:S(2)}, u32[]{:S(2)}) %collective-permute-start.7) | collective-permute-done | bytes 524320 | tf_op jit(solution)/shard_map/ppermute | solution.py:33
  37.4 1.7 %project.6.refs_0_ = f32[128,1024]{1,0:T(8,128)S(1)} custom-call(s32[2]{0:T(128)S(1)} %pad_add_fusion.own_ref, f32[1024,1024]{1,0:T(8,128)S(1)} %get-tuple-element.57.rows_ref, f32[1024,128]{1,0:T(8,128)S(1)} %collective-permute-done.7.part_ref, f32[128,1024]{1,0:T(8,128)S(1)} %project.5.refs_0_), custom_call_target="tpu_custom_call" | custom-call | flops 1 | bytes 6291456 | tf_op jit(solution)/shard_map/project/pallas_call | solution.py:170
  39.1 1.7 %project.7 = (f32[32,1024]{1,0:T(8,128)S(1)}, f32[32,1024]{1,0:T(8,128)S(1)}, f32[32,1024]{1,0:T(8,128)S(1)}, f32[32,1024]{1,0:T(8,128)S(1)}) custom-call(s32[2]{0:T(128)S(1)} %pad_add_fusion.own_ref, f32[1024,1024]{1,0:T(8,128)S(1)} %get-tuple-element.73.rows_ref, f32[1024,128]{1,0:T(8,128)S(1)} %collective-permute-done.9.part_ref, ...), custom_call_target="tpu_custom_call" | custom-call | flops 1 | bytes 6291456 | tf_op jit(solution)/shard_map/project/pallas_call | solution.py:170
  40.8 1.8 %collective-permute-start.10 = (f32[32,1024]{1,0:T(8,128)S(1)}, f32[32,1024]{1,0:T(8,128)S(1)}, u32[]{:S(2)}, u32[]{:S(2)}) collective-permute-start(f32[32,1024]{1,0:T(8,128)S(1)} %get-tuple-element.83), channel_id=1, source_target_pairs={{0,4},{4,0},{8,12},{12,8},{16,20},{20,16},{24,28},{28,24},{1,5},{5... | collective-permute-start | bytes 393224 | tf_op jit(solution)/shard_map/ppermute | solution.py:33
  42.6 1.6 %collective-permute-start.13 = (f32[128,128]{1,0:T(8,128)S(1)}, f32[128,128]{1,0:T(8,128)S(1)}, u32[]{:S(2)}, u32[]{:S(2)}) collective-permute-start(f32[128,128]{1,0:T(8,128)S(1)} %add.66), channel_id=1, source_target_pairs={{0,2},{1,3},{2,0},{3,1},{4,6},{5,7},{6,4},{7,5},{8,10},{9,11},{10,... | collective-permute-start | bytes 196616 | tf_op jit(solution)/shard_map/ppermute | solution.py:33
  44.7 1.8 %collective-permute-done.10 = f32[32,1024]{1,0:T(8,128)S(1)} collective-permute-done((f32[32,1024]{1,0:T(8,128)S(1)}, f32[32,1024]{1,0:T(8,128)S(1)}, u32[]{:S(2)}, u32[]{:S(2)}) %collective-permute-start.10) | collective-permute-done | bytes 131104 | tf_op jit(solution)/shard_map/ppermute | solution.py:33
  46.5 3.9 %collective-permute-start.11 = (f32[16,1024]{1,0:T(8,128)S(1)}, f32[16,1024]{1,0:T(8,128)S(1)}, u32[]{:S(2)}, u32[]{:S(2)}) collective-permute-start(f32[16,1024]{1,0:T(8,128)S(1)} %get-tuple-element.85), channel_id=1, source_target_pairs={{0,24},{4,28},{8,16},{12,20},{16,8},{20,12},{24,0},{28,4},{1,25},{... | collective-permute-start | bytes 196616 | tf_op jit(solution)/shard_map/ppermute | solution.py:33
  50.4 1.6 %collective-permute-start.16 = (f32[128,128]{1,0:T(8,128)S(1)}, f32[128,128]{1,0:T(8,128)S(1)}, u32[]{:S(2)}, u32[]{:S(2)}) collective-permute-start(f32[128,128]{1,0:T(8,128)S(1)} %add.69), channel_id=1, source_target_pairs={{0,16},{4,20},{8,24},{12,28},{16,0},{20,4},{24,8},{28,12},{1,17},{... | collective-permute-start | bytes 196616 | tf_op jit(solution)/shard_map/ppermute | solution.py:33
  52.0 1.6 %collective-permute-start.15 = (f32[16,1024]{1,0:T(8,128)S(1)}, f32[16,1024]{1,0:T(8,128)S(1)}, u32[]{:S(2)}, u32[]{:S(2)}) collective-permute-start(f32[16,1024]{1,0:T(8,128)S(1)} %get-tuple-element.113), channel_id=1, source_target_pairs={{0,8},{4,12},{8,0},{12,4},{16,24},{20,28},{24,16},{28,20},{1,9},{5... | collective-permute-start | bytes 196616 | tf_op jit(solution)/shard_map/ppermute | solution.py:33
  54.0 3.7 %collective-permute-done.16 = f32[128,128]{1,0:T(8,128)S(1)} collective-permute-done((f32[128,128]{1,0:T(8,128)S(1)}, f32[128,128]{1,0:T(8,128)S(1)}, u32[]{:S(2)}, u32[]{:S(2)}) %collective-permute-start.16) | collective-permute-done | bytes 65568 | tf_op jit(solution)/shard_map/ppermute | solution.py:33
  57.7 1.8 %collective-permute-done.14 = f32[16,1024]{1,0:T(8,128)S(1)} collective-permute-done((f32[16,1024]{1,0:T(8,128)S(1)}, f32[16,1024]{1,0:T(8,128)S(1)}, u32[]{:S(2)}, u32[]{:S(2)}) %collective-permute-start.14) | collective-permute-done | bytes 65568 | tf_op jit(solution)/shard_map/ppermute | solution.py:33
  59.5 2.1 %collective-permute-start.19 = (f32[16,1024]{1,0:T(8,128)S(1)}, f32[16,1024]{1,0:T(8,128)S(1)}, u32[]{:S(2)}, u32[]{:S(2)}) collective-permute-start(f32[16,1024]{1,0:T(8,128)S(1)} %add_add_fusion), channel_id=1, source_target_pairs={{0,24},{4,28},{8,16},{12,20},{16,8},{20,12},{24,0},{28,4},{1,25},{... | collective-permute-start | bytes 196616 | tf_op jit(solution)/shard_map/ppermute | solution.py:33
  61.6 2.3 %collective-permute-start.17 = (f32[16,1024]{1,0:T(8,128)S(1)}, f32[16,1024]{1,0:T(8,128)S(1)}, u32[]{:S(2)}, u32[]{:S(2)}) collective-permute-start(f32[16,1024]{1,0:T(8,128)S(1)} %add_add_fusion), channel_id=1, source_target_pairs={{0,8},{4,12},{8,0},{12,4},{16,24},{20,28},{24,16},{28,20},{1,9},{5... | collective-permute-start | bytes 196616 | tf_op jit(solution)/shard_map/ppermute | solution.py:33
  63.9 2.4 %factor.2.in_ref = f32[128,256]{1,0:T(8,128)S(1)} custom-call(f32[128,128]{1,0:T(8,128)S(1)} %add.70.in_ref), custom_call_target="tpu_custom_call" | custom-call | flops 1 | bytes 10485 | tf_op jit(solution)/shard_map/factor/pallas_call | solution.py:242
  66.3 1.1 %collective-permute-done.18 = f32[16,1024]{1,0:T(8,128)S(1)} collective-permute-done((f32[16,1024]{1,0:T(8,128)S(1)}, f32[16,1024]{1,0:T(8,128)S(1)}, u32[]{:S(2)}, u32[]{:S(2)}) %collective-permute-start.18) | collective-permute-done | bytes 65568 | tf_op jit(solution)/shard_map/ppermute | solution.py:33
  67.5 1.6 %collective-permute-start.20 = (f32[64,1024]{1,0:T(8,128)S(1)}, f32[64,1024]{1,0:T(8,128)S(1)}, u32[]{:S(2)}, u32[]{:S(2)}) collective-permute-start(f32[64,1024]{1,0:T(8,128)S(1)} %pad_maximum_fusion.refs_0_), channel_id=1, source_target_pairs={{0,4},{4,0},{8,12},{12,8},{16,20},{20,16},{24,28},{28,24},{1,5},{5... | collective-permute-start | bytes 786440 | tf_op jit(solution)/shard_map/ppermute | solution.py:33
  69.1 3.6 %factor.3.inverse_ref = f32[128,128]{1,0:T(8,128)S(1)} custom-call(f32[128,256]{1,0:T(8,128)S(1)} %factor.2.in_ref), custom_call_target="tpu_custom_call" | custom-call | flops 1 | bytes 10485 | tf_op jit(solution)/shard_map/factor/pallas_call | solution.py:242
  72.6 2.4 %collective-permute-done.20.refs_1_ = f32[64,1024]{1,0:T(8,128)S(1)} collective-permute-done((f32[64,1024]{1,0:T(8,128)S(1)}, f32[64,1024]{1,0:T(8,128)S(1)}, u32[]{:S(2)}, u32[]{:S(2)}) %collective-permute-start.20) | collective-permute-done | bytes 262176 | tf_op jit(solution)/shard_map/ppermute | solution.py:33
  75.1 1.9 %finish.1 = (f32[128,1024]{1,0:T(8,128)}, f32[128,128]{1,0:T(8,128)S(1)}) custom-call(s32[2]{0:T(128)S(1)} %pad_add_fusion.own_ref, f32[128,128]{1,0:T(8,128)S(1)} %factor.3.inverse_ref, f32[64,1024]{1,0:T(8,128)S(1)} %pad_maximum_fusion.refs_0_, f32[64,1024]{1,0:T(8,128)S(1)} %collective-permute-done.20.refs_1_), custom_call_target="tpu_custom_call" | custom-call | flops 1 | bytes 8388608 | tf_op jit(solution)/shard_map/finish/pallas_call | solution.py:285
  76.9 1.8 %collective-permute-start.22 = (f32[128,128]{1,0:T(8,128)S(1)}, f32[128,128]{1,0:T(8,128)S(1)}, u32[]{:S(2)}, u32[]{:S(2)}) collective-permute-start(f32[128,128]{1,0:T(8,128)S(1)} %get-tuple-element.105), channel_id=1, source_target_pairs={{0,3},{1,2},{2,1},{3,0},{4,7},{5,6},{6,5},{7,4},{8,11},{9,10},{10,... | collective-permute-start | bytes 196616 | tf_op jit(solution)/shard_map/ppermute | solution.py:33
  79.1 1.4 %fusion.3 = f32[1024,128]{1,0:T(8,128)} fusion(f32[1024,128]{1,0:T(8,128)S(1)} %fusion.part_ref, f32[128,128]{1,0:T(8,128)S(1)} %factor.3.inverse_ref), kind=kOutput, calls=%fused_computation.12 | convolution fusion | flops 201326592 | bytes 1114112 | tf_op jit(solution)/shard_map/dot_general | solution.py:37
  81.2 1.8 %collective-permute-done.21 = f32[128,128]{1,0:T(8,128)S(1)} collective-permute-done((f32[128,128]{1,0:T(8,128)S(1)}, f32[128,128]{1,0:T(8,128)S(1)}, u32[]{:S(2)}, u32[]{:S(2)}) %collective-permute-start.21) | collective-permute-done | bytes 65568 | tf_op jit(solution)/shard_map/ppermute | solution.py:33
  (42 shorter events, 8.5 us)
Async XLA Ops:
  4.9 2.1 %collective-permute-start = (f32[1024,128]{1,0:T(8,128)S(1)}, f32[1024,128]{1,0:T(8,128)S(1)}, u32[]{:S(2)}, u32[]{:S(2)}) collective-permute-start(f32[1024,128]{1,0:T(8,128)S(1)} %get-tuple-element.59), channel_id=1, source_target_pairs={{0,1},{1,0},{2,3},{3,2},{4,5},{5,4},{6,7},{7,6},{8,9},{9,8},{10,11... | collective-permute-start | bytes 1572872 | tf_op jit(solution)/shard_map/ppermute | solution.py:33
  7.1 15.2 %collective-permute-start.3 = (f32[1024,128]{1,0:T(8,128)S(1)}, f32[1024,128]{1,0:T(8,128)S(1)}, u32[]{:S(2)}, u32[]{:S(2)}) collective-permute-start(f32[1024,128]{1,0:T(8,128)S(1)} %add.59), channel_id=1, source_target_pairs={{0,2},{1,3},{2,0},{3,1},{4,6},{5,7},{6,4},{7,5},{8,10},{9,11},{10,... | collective-permute-start | bytes 1572872 | tf_op jit(solution)/shard_map/ppermute | solution.py:33
  15.1 1.6 %collective-permute-start.2 = (f32[512,128]{1,0:T(8,128)S(1)}, f32[512,128]{1,0:T(8,128)S(1)}, u32[]{:S(2)}, u32[]{:S(2)}) collective-permute-start(f32[512,128]{1,0:T(8,128)S(1)} %get-tuple-element.111), channel_id=1, source_target_pairs={{0,1},{1,0},{2,3},{3,2},{4,5},{5,4},{6,7},{7,6},{8,9},{9,8},{10,11... | collective-permute-start | bytes 786440 | tf_op jit(solution)/shard_map/ppermute | solution.py:33
  15.2 1.9 %collective-permute-start.1 = (f32[512,128]{1,0:T(8,128)S(1)}, f32[512,128]{1,0:T(8,128)S(1)}, u32[]{:S(2)}, u32[]{:S(2)}) collective-permute-start(f32[512,128]{1,0:T(8,128)S(1)} %get-tuple-element.112), channel_id=1, source_target_pairs={{0,1},{1,0},{2,3},{3,2},{4,5},{5,4},{6,7},{7,6},{8,9},{9,8},{10,11... | collective-permute-start | bytes 786440 | tf_op jit(solution)/shard_map/ppermute | solution.py:33
  22.3 7.2 %collective-permute-start.5 = (f32[1024,128]{1,0:T(8,128)S(1)}, f32[1024,128]{1,0:T(8,128)S(1)}, u32[]{:S(2)}, u32[]{:S(2)}) collective-permute-start(f32[1024,128]{1,0:T(8,128)S(1)} %fusion.part_ref), channel_id=1, source_target_pairs={{0,1},{1,0},{2,3},{3,2},{4,5},{5,4},{6,7},{7,6},{8,9},{9,8},{10,11... | collective-permute-start | bytes 1572872 | tf_op jit(solution)/shard_map/ppermute | solution.py:33
  22.4 14.3 %collective-permute-start.7 = (f32[1024,128]{1,0:T(8,128)S(1)}, f32[1024,128]{1,0:T(8,128)S(1)}, u32[]{:S(2)}, u32[]{:S(2)}) collective-permute-start(f32[1024,128]{1,0:T(8,128)S(1)} %fusion.part_ref), channel_id=1, source_target_pairs={{0,2},{1,3},{2,0},{3,1},{4,6},{5,7},{6,4},{7,5},{8,10},{9,11},{10,... | collective-permute-start | bytes 1572872 | tf_op jit(solution)/shard_map/ppermute | solution.py:33
  25.3 4.3 %collective-permute-start.4 = (f32[128,128]{1,0:T(8,128)S(1)}, f32[128,128]{1,0:T(8,128)S(1)}, u32[]{:S(2)}, u32[]{:S(2)}) collective-permute-start(f32[128,128]{1,0:T(8,128)S(1)} %fusion.2), channel_id=1, source_target_pairs={{0,4},{4,0},{8,12},{12,8},{16,20},{20,16},{24,28},{28,24},{1,5},{5... | collective-permute-start | bytes 196616 | tf_op jit(solution)/shard_map/ppermute | solution.py:33
  29.6 7.2 %collective-permute-start.6 = (f32[128,128]{1,0:T(8,128)S(1)}, f32[128,128]{1,0:T(8,128)S(1)}, u32[]{:S(2)}, u32[]{:S(2)}) collective-permute-start(f32[128,128]{1,0:T(8,128)S(1)} %add.62), channel_id=1, source_target_pairs={{0,8},{4,12},{8,0},{12,4},{16,24},{20,28},{24,16},{28,20},{1,9},{5... | collective-permute-start | bytes 196616 | tf_op jit(solution)/shard_map/ppermute | solution.py:33
  36.8 2.3 %collective-permute-start.9 = (f32[1024,128]{1,0:T(8,128)S(1)}, f32[1024,128]{1,0:T(8,128)S(1)}, u32[]{:S(2)}, u32[]{:S(2)}) collective-permute-start(f32[1024,128]{1,0:T(8,128)S(1)} %collective-permute-done.7.part_ref), channel_id=1, source_target_pairs={{0,1},{1,0},{2,3},{3,2},{4,5},{5,4},{6,7},{7,6},{8,9},{9,8},{10,11... | collective-permute-start | bytes 1572872 | tf_op jit(solution)/shard_map/ppermute | solution.py:33
  36.8 4.0 %collective-permute-start.8 = (f32[128,128]{1,0:T(8,128)S(1)}, f32[128,128]{1,0:T(8,128)S(1)}, u32[]{:S(2)}, u32[]{:S(2)}) collective-permute-start(f32[128,128]{1,0:T(8,128)S(1)} %add.63), channel_id=1, source_target_pairs={{0,1},{1,0},{2,3},{3,2},{4,5},{5,4},{6,7},{7,6},{8,9},{9,8},{10,11... | collective-permute-start | bytes 196616 | tf_op jit(solution)/shard_map/ppermute | solution.py:33
  40.8 5.7 %collective-permute-start.10 = (f32[32,1024]{1,0:T(8,128)S(1)}, f32[32,1024]{1,0:T(8,128)S(1)}, u32[]{:S(2)}, u32[]{:S(2)}) collective-permute-start(f32[32,1024]{1,0:T(8,128)S(1)} %get-tuple-element.83), channel_id=1, source_target_pairs={{0,4},{4,0},{8,12},{12,8},{16,20},{20,16},{24,28},{28,24},{1,5},{5... | collective-permute-start | bytes 393224 | tf_op jit(solution)/shard_map/ppermute | solution.py:33
  42.6 7.8 %collective-permute-start.13 = (f32[128,128]{1,0:T(8,128)S(1)}, f32[128,128]{1,0:T(8,128)S(1)}, u32[]{:S(2)}, u32[]{:S(2)}) collective-permute-start(f32[128,128]{1,0:T(8,128)S(1)} %add.66), channel_id=1, source_target_pairs={{0,2},{1,3},{2,0},{3,1},{4,6},{5,7},{6,4},{7,5},{8,10},{9,11},{10,... | collective-permute-start | bytes 196616 | tf_op jit(solution)/shard_map/ppermute | solution.py:33
  44.2 6.2 %collective-permute-start.12 = (f32[32,1024]{1,0:T(8,128)S(1)}, f32[32,1024]{1,0:T(8,128)S(1)}, u32[]{:S(2)}, u32[]{:S(2)}) collective-permute-start(f32[32,1024]{1,0:T(8,128)S(1)} %get-tuple-element.87), channel_id=1, source_target_pairs={{0,4},{4,0},{8,12},{12,8},{16,20},{20,16},{24,28},{28,24},{1,5},{5... | collective-permute-start | bytes 393224 | tf_op jit(solution)/shard_map/ppermute | solution.py:33
  46.5 11.2 %collective-permute-start.11 = (f32[16,1024]{1,0:T(8,128)S(1)}, f32[16,1024]{1,0:T(8,128)S(1)}, u32[]{:S(2)}, u32[]{:S(2)}) collective-permute-start(f32[16,1024]{1,0:T(8,128)S(1)} %get-tuple-element.85), channel_id=1, source_target_pairs={{0,24},{4,28},{8,16},{12,20},{16,8},{20,12},{24,0},{28,4},{1,25},{... | collective-permute-start | bytes 196616 | tf_op jit(solution)/shard_map/ppermute | solution.py:33
  50.4 7.2 %collective-permute-start.16 = (f32[128,128]{1,0:T(8,128)S(1)}, f32[128,128]{1,0:T(8,128)S(1)}, u32[]{:S(2)}, u32[]{:S(2)}) collective-permute-start(f32[128,128]{1,0:T(8,128)S(1)} %add.69), channel_id=1, source_target_pairs={{0,16},{4,20},{8,24},{12,28},{16,0},{20,4},{24,8},{28,12},{1,17},{... | collective-permute-start | bytes 196616 | tf_op jit(solution)/shard_map/ppermute | solution.py:33
  52.0 5.7 %collective-permute-start.15 = (f32[16,1024]{1,0:T(8,128)S(1)}, f32[16,1024]{1,0:T(8,128)S(1)}, u32[]{:S(2)}, u32[]{:S(2)}) collective-permute-start(f32[16,1024]{1,0:T(8,128)S(1)} %get-tuple-element.113), channel_id=1, source_target_pairs={{0,8},{4,12},{8,0},{12,4},{16,24},{20,28},{24,16},{28,20},{1,9},{5... | collective-permute-start | bytes 196616 | tf_op jit(solution)/shard_map/ppermute | solution.py:33
  53.7 5.8 %collective-permute-start.14 = (f32[16,1024]{1,0:T(8,128)S(1)}, f32[16,1024]{1,0:T(8,128)S(1)}, u32[]{:S(2)}, u32[]{:S(2)}) collective-permute-start(f32[16,1024]{1,0:T(8,128)S(1)} %get-tuple-element.114), channel_id=1, source_target_pairs={{0,16},{4,20},{8,24},{12,28},{16,0},{20,4},{24,8},{28,12},{1,17},{... | collective-permute-start | bytes 196616 | tf_op jit(solution)/shard_map/ppermute | solution.py:33
  59.5 6.9 %collective-permute-start.19 = (f32[16,1024]{1,0:T(8,128)S(1)}, f32[16,1024]{1,0:T(8,128)S(1)}, u32[]{:S(2)}, u32[]{:S(2)}) collective-permute-start(f32[16,1024]{1,0:T(8,128)S(1)} %add_add_fusion), channel_id=1, source_target_pairs={{0,24},{4,28},{8,16},{12,20},{16,8},{20,12},{24,0},{28,4},{1,25},{... | collective-permute-start | bytes 196616 | tf_op jit(solution)/shard_map/ppermute | solution.py:33
  61.6 5.8 %collective-permute-start.18 = (f32[16,1024]{1,0:T(8,128)S(1)}, f32[16,1024]{1,0:T(8,128)S(1)}, u32[]{:S(2)}, u32[]{:S(2)}) collective-permute-start(f32[16,1024]{1,0:T(8,128)S(1)} %add_add_fusion), channel_id=1, source_target_pairs={{0,16},{4,20},{8,24},{12,28},{16,0},{20,4},{24,8},{28,12},{1,17},{... | collective-permute-start | bytes 196616 | tf_op jit(solution)/shard_map/ppermute | solution.py:33
  61.6 5.8 %collective-permute-start.17 = (f32[16,1024]{1,0:T(8,128)S(1)}, f32[16,1024]{1,0:T(8,128)S(1)}, u32[]{:S(2)}, u32[]{:S(2)}) collective-permute-start(f32[16,1024]{1,0:T(8,128)S(1)} %add_add_fusion), channel_id=1, source_target_pairs={{0,8},{4,12},{8,0},{12,4},{16,24},{20,28},{24,16},{28,20},{1,9},{5... | collective-permute-start | bytes 196616 | tf_op jit(solution)/shard_map/ppermute | solution.py:33
  67.5 7.6 %collective-permute-start.20 = (f32[64,1024]{1,0:T(8,128)S(1)}, f32[64,1024]{1,0:T(8,128)S(1)}, u32[]{:S(2)}, u32[]{:S(2)}) collective-permute-start(f32[64,1024]{1,0:T(8,128)S(1)} %pad_maximum_fusion.refs_0_), channel_id=1, source_target_pairs={{0,4},{4,0},{8,12},{12,8},{16,20},{20,16},{24,28},{28,24},{1,5},{5... | collective-permute-start | bytes 786440 | tf_op jit(solution)/shard_map/ppermute | solution.py:33
  76.9 3.5 %collective-permute-start.23 = (f32[128,128]{1,0:T(8,128)S(1)}, f32[128,128]{1,0:T(8,128)S(1)}, u32[]{:S(2)}, u32[]{:S(2)}) collective-permute-start(f32[128,128]{1,0:T(8,128)S(1)} %get-tuple-element.105), channel_id=1, source_target_pairs={{0,1},{1,0},{2,3},{3,2},{4,5},{5,4},{6,7},{7,6},{8,9},{9,8},{10,11... | collective-permute-start | bytes 196616 | tf_op jit(solution)/shard_map/ppermute | solution.py:33
  76.9 4.2 %collective-permute-start.22 = (f32[128,128]{1,0:T(8,128)S(1)}, f32[128,128]{1,0:T(8,128)S(1)}, u32[]{:S(2)}, u32[]{:S(2)}) collective-permute-start(f32[128,128]{1,0:T(8,128)S(1)} %get-tuple-element.105), channel_id=1, source_target_pairs={{0,3},{1,2},{2,1},{3,0},{4,7},{5,6},{6,5},{7,4},{8,11},{9,10},{10,... | collective-permute-start | bytes 196616 | tf_op jit(solution)/shard_map/ppermute | solution.py:33
  78.7 4.3 %collective-permute-start.21 = (f32[128,128]{1,0:T(8,128)S(1)}, f32[128,128]{1,0:T(8,128)S(1)}, u32[]{:S(2)}, u32[]{:S(2)}) collective-permute-start(f32[128,128]{1,0:T(8,128)S(1)} %get-tuple-element.105), channel_id=1, source_target_pairs={{0,2},{1,3},{2,0},{3,1},{4,6},{5,7},{6,4},{7,5},{8,10},{9,11},{10,... | collective-permute-start | bytes 196616 | tf_op jit(solution)/shard_map/ppermute | solution.py:33

commit v13 on v11

--- a/solution.py
+++ b/solution.py
@@ -13,7 +13,7 @@
 
 PIECE = 512
 TILE = 256
-RUN = 128
+RUN = 512
 SLICES = 8
 SMEM = pl.BlockSpec(memory_space=pltpu.SMEM)
 VMEM = pl.BlockSpec(memory_space=pltpu.VMEM)
@@ -256,8 +256,8 @@
     step = total.shape[0] // SLICES
     for place in range(SLICES):
         at = pl.multiple_of((place ^ own_ref[1]) * step, step)
-        row = place // 2 * step
-        total[pl.ds(at, step)] = parts[place % 2][row : row + step]
+        group, row = (1, place // 2 * step - step) if place > 1 else (0, 0)
+        total[pl.ds(at, step)] = parts[2 * (place % 2) + group][row : row + step]
     upper, rest = split(inverse_ref[...])
     stack = jnp.concatenate([upper, rest], 0)
     width = upper.shape[0]
@@ -354,11 +354,11 @@
     for bit in bits[3:]:
         zero = zero + swap(zero, "row", bit)
     zero, state = fence((zero, state))
-    got = [swap(zero, "row", q) for q in (2, 4, 6)]
+    got = [swap(zero, "row", q) for q in (2, 4, 6, 1)]
     *got, state = fence((*got, factor(1, 3, state)))
-    keep, state = fence((jnp.concatenate([zero, *got], 0), state))
-    got, inverse = fence((swap(keep, "row", 1), factor(2, 3, state)))
-    projected, small = finish(own, inverse, [keep, got])
+    others, state = fence((jnp.concatenate(got[:3], 0), state))
+    far, inverse = fence((swap(others, "row", 1), factor(2, 3, state)))
+    projected, small = finish(own, inverse, [zero, others, got[3], far])
 
     across = [swap(small, "col", bit) for bit in (2, 3, 1)]
     *across, basis = fence((*across, dot(sketched, inverse, 1, 1)))

time: 83.8 us -> 83.2 us (level)
  Pallas kernels: 27.1 us -> 25.6 us
    pallas_call x2, Pallas kernels: 10.7 us -> 9.28 us  [sketch(): pl.pallas_call(functools.partial(sketch_kernel, places, ahead, first), in...]
    ppermute x24 -> x25, starting transfers between devices: 29.6 us -> 30.1 us  [swap(): lax.ppermute(value, axis, [(i, i ^ bit) for i in range(lax.axis_size(axis...]
    ppermute x24 -> x25, waiting for transfers between devices: 22.7 us -> 23.1 us  [swap(): lax.ppermute(value, axis, [(i, i ^ bit) for i in range(lax.axis_size(axis...]
  transfers between devices with their start and end apart: 24 -> 25, of which waited for: 15 -> 15; matrix products, arithmetic and copies ran while one was open for 3% -> 3% of each run, Pallas kernels for 23% -> 23%
where the time goes in v13:
time: 83.2 us; the launch traced here: 83 us
  starting transfers between devices  30.1 us (36%)
  Pallas kernels  25.6 us (31%)
  waiting for transfers between devices  23.1 us (28%)
  matrix products  2.4 us (3%)
  other arithmetic  0.99 us (1%)
  between operations  0.85 us (1%)
    ppermute x25, starting transfers between devices, swap(): lax.ppermute(value, axis, [(i, i ^ bit) for i in range(lax.axis_size(axis...  30.1 us
    ppermute x25, waiting for transfers between devices, swap(): lax.ppermute(value, axis, [(i, i ^ bit) for i in range(lax.axis_size(axis...  23.1 us
    pallas_call x2, Pallas kernels, sketch(): pl.pallas_call(functools.partial(sketch_kernel, places, ahead, first), in...  9.28 us
    pallas_call x4, Pallas kernels, project(): pl.pallas_call(functools.partial(project_kernel, start, before is not Non...  6.82 us
    pallas_call x3, Pallas kernels, factor(): pl.pallas_call(functools.partial(factor_kernel, index, count), in_specs=[...  6.36 us
    dot_general x2, matrix products, dot(): lax.dot_general(a, b, (((a_dim,), (b_dim,)), ((), ())), precision=precisi...  2.4 us
    pallas_call x1, Pallas kernels, finish(): pl.pallas_call(finish_kernel, in_specs=[SMEM] + [VMEM] * (1 + len(parts))...  1.86 us
  transfers between devices with their start and end apart: 25, of which 15 were waited for; matrix products, arithmetic and copies ran while one was open for 3% of the time, Pallas kernels for 23%

profile of v13, /device:TPU:0, one launch (start us, length us, event | category | flops | bytes accessed | tf_op | source)
XLA Modules:
  0.0 83.0 jit_solution(1485465260223397782)
XLA Ops:
  0.7 4.2 %partial_sketch.2 = (f32[1024,128]{1,0:T(8,128)S(1)}, f32[1024,1024]{1,0:T(8,128)S(1)}, f32[1024,1024]{1,0:T(8,128)S(1)}, bf16[1024,256]{1,0:T(8,128)(2,1)S(1)}) custom-call(s32[2]{0:T(128)S(1)} %pad_add_fusion.own_ref, f32[4096,1024]{1,0:T(8,128)} %data_ref.3, f32[1024,128]{1,0:T(8,128)} %omega_ref.1), custom_call_target="tpu_custom_call" | custom-call | flops 1 | bytes 10485 | tf_op jit(solution)/shard_map/partial_sketch/pallas_call | solution.py:107
  5.5 1.3 %partial_sketch_held.1 = f32[1024,128]{1,0:T(8,128)S(1)} custom-call(f32[1024,1024]{1,0:T(8,128)S(1)} %get-tuple-element.61.rows_ref, bf16[1024,256]{1,0:T(8,128)(2,1)S(1)} %get-tuple-element.64.wide_ref.omega_ref), custom_call_target="tpu_custom_call" | custom-call | flops 1 | bytes 10485 | tf_op jit(solution)/shard_map/partial_sketch_held/pallas_call | solution.py:125
  7.1 3.0 %collective-permute-start.3 = (f32[1024,128]{1,0:T(8,128)S(1)}, f32[1024,128]{1,0:T(8,128)S(1)}, u32[]{:S(2)}, u32[]{:S(2)}) collective-permute-start(f32[1024,128]{1,0:T(8,128)S(1)} %add.59), channel_id=1, source_target_pairs={{0,2},{1,3},{2,0},{3,1},{4,6},{5,7},{6,4},{7,5},{8,10},{9,11},{10,... | collective-permute-start | bytes 1572872 | tf_op jit(solution)/shard_map/ppermute | solution.py:33
  10.0 5.1 %partial_sketch.3 = (f32[1024,128]{1,0:T(8,128)S(1)}, f32[1024,128]{1,0:T(8,128)S(1)}, f32[1024,1024]{1,0:T(8,128)S(1)}, f32[1024,1024]{1,0:T(8,128)S(1)}) custom-call(s32[2]{0:T(128)S(1)} %pad_add_fusion.own_ref, f32[4096,1024]{1,0:T(8,128)} %data_ref.3, bf16[1024,256]{1,0:T(8,128)(2,1)S(1)} %get-tuple-element.64.wide_ref.omega_ref), custom_call_target="tpu_custom_call" | custom-call | flops 1 | bytes 10485 | tf_op jit(solution)/shard_map/partial_sketch/pallas_call | solution.py:107
  17.1 5.1 %collective-permute-done.3 = f32[1024,128]{1,0:T(8,128)S(1)} collective-permute-done((f32[1024,128]{1,0:T(8,128)S(1)}, f32[1024,128]{1,0:T(8,128)S(1)}, u32[]{:S(2)}, u32[]{:S(2)}) %collective-permute-start.3) | collective-permute-done | bytes 524320 | tf_op jit(solution)/shard_map/ppermute | solution.py:33
  22.4 1.8 %collective-permute-start.7 = (f32[1024,128]{1,0:T(8,128)S(1)}, f32[1024,128]{1,0:T(8,128)S(1)}, u32[]{:S(2)}, u32[]{:S(2)}) collective-permute-start(f32[1024,128]{1,0:T(8,128)S(1)} %fusion.part_ref), channel_id=1, source_target_pairs={{0,2},{1,3},{2,0},{3,1},{4,6},{5,7},{6,4},{7,5},{8,10},{9,11},{10,... | collective-permute-start | bytes 1572872 | tf_op jit(solution)/shard_map/ppermute | solution.py:33
  24.2 1.0 %fusion.2 = f32[128,128]{1,0:T(8,128)S(1)} fusion(f32[1024,128]{1,0:T(8,128)S(1)} %fusion.part_ref), kind=kOutput, calls=%fused_computation.11 | convolution fusion | flops 201326592 | bytes 589824 | tf_op jit(solution)/shard_map/dot_general | solution.py:37
  25.3 1.6 %collective-permute-start.4 = (f32[128,128]{1,0:T(8,128)S(1)}, f32[128,128]{1,0:T(8,128)S(1)}, u32[]{:S(2)}, u32[]{:S(2)}) collective-permute-start(f32[128,128]{1,0:T(8,128)S(1)} %fusion.2), channel_id=1, source_target_pairs={{0,4},{4,0},{8,12},{12,8},{16,20},{20,16},{24,28},{28,24},{1,5},{5... | collective-permute-start | bytes 196616 | tf_op jit(solution)/shard_map/ppermute | solution.py:33
  26.8 1.7 %project.4.refs_0_ = f32[128,1024]{1,0:T(8,128)S(1)} custom-call(s32[2]{0:T(128)S(1)} %pad_add_fusion.own_ref, f32[1024,1024]{1,0:T(8,128)S(1)} %get-tuple-element.71.rows_ref, f32[1024,128]{1,0:T(8,128)S(1)} %fusion.part_ref), custom_call_target="tpu_custom_call" | custom-call | flops 1 | bytes 6291456 | tf_op jit(solution)/shard_map/project/pallas_call | solution.py:170
  28.5 1.1 %collective-permute-done.4 = f32[128,128]{1,0:T(8,128)S(1)} collective-permute-done((f32[128,128]{1,0:T(8,128)S(1)}, f32[128,128]{1,0:T(8,128)S(1)}, u32[]{:S(2)}, u32[]{:S(2)}) %collective-permute-start.4) | collective-permute-done | bytes 65568 | tf_op jit(solution)/shard_map/ppermute | solution.py:33
  29.6 1.6 %collective-permute-start.6 = (f32[128,128]{1,0:T(8,128)S(1)}, f32[128,128]{1,0:T(8,128)S(1)}, u32[]{:S(2)}, u32[]{:S(2)}) collective-permute-start(f32[128,128]{1,0:T(8,128)S(1)} %add.62), channel_id=1, source_target_pairs={{0,8},{4,12},{8,0},{12,4},{16,24},{20,28},{24,16},{28,20},{1,9},{5... | collective-permute-start | bytes 196616 | tf_op jit(solution)/shard_map/ppermute | solution.py:33
  31.2 1.7 %project.5.refs_0_ = f32[128,1024]{1,0:T(8,128)S(1)} custom-call(s32[2]{0:T(128)S(1)} %pad_add_fusion.own_ref, f32[1024,1024]{1,0:T(8,128)S(1)} %get-tuple-element.73.rows_ref, f32[1024,128]{1,0:T(8,128)S(1)} %collective-permute-done.5.part_ref, f32[128,1024]{1,0:T(8,128)S(1)} %project.4.refs_0_), custom_call_target="tpu_custom_call" | custom-call | flops 1 | bytes 6291456 | tf_op jit(solution)/shard_map/project/pallas_call | solution.py:170
  33.9 2.7 %collective-permute-start.8 = (f32[128,128]{1,0:T(8,128)S(1)}, f32[128,128]{1,0:T(8,128)S(1)}, u32[]{:S(2)}, u32[]{:S(2)}) collective-permute-start(f32[128,128]{1,0:T(8,128)S(1)} %add.63), channel_id=1, source_target_pairs={{0,16},{4,20},{8,24},{12,28},{16,0},{20,4},{24,8},{28,12},{1,17},{... | collective-permute-start | bytes 196616 | tf_op jit(solution)/shard_map/ppermute | solution.py:33
  36.8 2.4 %collective-permute-done.8 = f32[128,128]{1,0:T(8,128)S(1)} collective-permute-done((f32[128,128]{1,0:T(8,128)S(1)}, f32[128,128]{1,0:T(8,128)S(1)}, u32[]{:S(2)}, u32[]{:S(2)}) %collective-permute-start.8) | collective-permute-done | bytes 65568 | tf_op jit(solution)/shard_map/ppermute | solution.py:33
  39.8 1.7 %project.6.refs_0_ = f32[128,1024]{1,0:T(8,128)S(1)} custom-call(s32[2]{0:T(128)S(1)} %pad_add_fusion.own_ref, f32[1024,1024]{1,0:T(8,128)S(1)} %get-tuple-element.61.rows_ref, f32[1024,128]{1,0:T(8,128)S(1)} %collective-permute-done.7.part_ref, f32[128,1024]{1,0:T(8,128)S(1)} %project.5.refs_0_), custom_call_target="tpu_custom_call" | custom-call | flops 1 | bytes 6291456 | tf_op jit(solution)/shard_map/project/pallas_call | solution.py:170
  41.5 1.7 %project.7 = (f32[32,1024]{1,0:T(8,128)S(1)}, f32[32,1024]{1,0:T(8,128)S(1)}, f32[32,1024]{1,0:T(8,128)S(1)}, f32[32,1024]{1,0:T(8,128)S(1)}) custom-call(s32[2]{0:T(128)S(1)} %pad_add_fusion.own_ref, f32[1024,1024]{1,0:T(8,128)S(1)} %get-tuple-element.79.rows_ref, f32[1024,128]{1,0:T(8,128)S(1)} %collective-permute-done.10.part_ref, ...), custom_call_target="tpu_custom_call" | custom-call | flops 1 | bytes 6291456 | tf_op jit(solution)/shard_map/project/pallas_call | solution.py:170
  43.2 1.6 %collective-permute-start.11 = (f32[32,1024]{1,0:T(8,128)S(1)}, f32[32,1024]{1,0:T(8,128)S(1)}, u32[]{:S(2)}, u32[]{:S(2)}) collective-permute-start(f32[32,1024]{1,0:T(8,128)S(1)} %get-tuple-element.89), channel_id=1, source_target_pairs={{0,4},{4,0},{8,12},{12,8},{16,20},{20,16},{24,28},{28,24},{1,5},{5... | collective-permute-start | bytes 393224 | tf_op jit(solution)/shard_map/ppermute | solution.py:33
  45.7 3.4 %collective-permute-done.12 = f32[128,128]{1,0:T(8,128)S(1)} collective-permute-done((f32[128,128]{1,0:T(8,128)S(1)}, f32[128,128]{1,0:T(8,128)S(1)}, u32[]{:S(2)}, u32[]{:S(2)}) %collective-permute-start.12) | collective-permute-done | bytes 65568 | tf_op jit(solution)/shard_map/ppermute | solution.py:33
  49.7 4.2 %collective-permute-start.13 = (f32[16,1024]{1,0:T(8,128)S(1)}, f32[16,1024]{1,0:T(8,128)S(1)}, u32[]{:S(2)}, u32[]{:S(2)}) collective-permute-start(f32[16,1024]{1,0:T(8,128)S(1)} %get-tuple-element.94), channel_id=1, source_target_pairs={{0,24},{4,28},{8,16},{12,20},{16,8},{20,12},{24,0},{28,4},{1,25},{... | collective-permute-start | bytes 196616 | tf_op jit(solution)/shard_map/ppermute | solution.py:33
  54.0 2.3 %collective-permute-start.15 = (f32[16,1024]{1,0:T(8,128)S(1)}, f32[16,1024]{1,0:T(8,128)S(1)}, u32[]{:S(2)}, u32[]{:S(2)}) collective-permute-start(f32[16,1024]{1,0:T(8,128)S(1)} %get-tuple-element.122), channel_id=1, source_target_pairs={{0,16},{4,20},{8,24},{12,28},{16,0},{20,4},{24,8},{28,12},{1,17},{... | collective-permute-start | bytes 196616 | tf_op jit(solution)/shard_map/ppermute | solution.py:33
  56.4 2.2 %factor.3.in_ref = f32[128,256]{1,0:T(8,128)S(1)} custom-call(f32[128,128]{1,0:T(8,128)S(1)} %add.66.in_ref), custom_call_target="tpu_custom_call" | custom-call | flops 1 | bytes 10485 | tf_op jit(solution)/shard_map/factor/pallas_call | solution.py:242
  59.3 1.6 %collective-permute-start.20 = (f32[16,1024]{1,0:T(8,128)S(1)}, f32[16,1024]{1,0:T(8,128)S(1)}, u32[]{:S(2)}, u32[]{:S(2)}) collective-permute-start(f32[16,1024]{1,0:T(8,128)S(1)} %add_add_fusion.refs_0_), channel_id=1, source_target_pairs={{0,4},{4,0},{8,12},{12,8},{16,20},{20,16},{24,28},{28,24},{1,5},{5... | collective-permute-start | bytes 196616 | tf_op jit(solution)/shard_map/ppermute | solution.py:33
  60.8 2.1 %collective-permute-start.19 = (f32[16,1024]{1,0:T(8,128)S(1)}, f32[16,1024]{1,0:T(8,128)S(1)}, u32[]{:S(2)}, u32[]{:S(2)}) collective-permute-start(f32[16,1024]{1,0:T(8,128)S(1)} %add_add_fusion.refs_0_), channel_id=1, source_target_pairs={{0,24},{4,28},{8,16},{12,20},{16,8},{20,12},{24,0},{28,4},{1,25},{... | collective-permute-start | bytes 196616 | tf_op jit(solution)/shard_map/ppermute | solution.py:33
  63.0 1.3 %collective-permute-start.18 = (f32[16,1024]{1,0:T(8,128)S(1)}, f32[16,1024]{1,0:T(8,128)S(1)}, u32[]{:S(2)}, u32[]{:S(2)}) collective-permute-start(f32[16,1024]{1,0:T(8,128)S(1)} %add_add_fusion.refs_0_), channel_id=1, source_target_pairs={{0,16},{4,20},{8,24},{12,28},{16,0},{20,4},{24,8},{28,12},{1,17},{... | collective-permute-start | bytes 196616 | tf_op jit(solution)/shard_map/ppermute | solution.py:33
  65.2 2.1 %factor.4.in_ref = f32[128,256]{1,0:T(8,128)S(1)} custom-call(f32[128,256]{1,0:T(8,128)S(1)} %factor.3.in_ref), custom_call_target="tpu_custom_call" | custom-call | flops 1 | bytes 10485 | tf_op jit(solution)/shard_map/factor/pallas_call | solution.py:242
  67.3 1.6 %collective-permute-done.18 = f32[16,1024]{1,0:T(8,128)S(1)} collective-permute-done((f32[16,1024]{1,0:T(8,128)S(1)}, f32[16,1024]{1,0:T(8,128)S(1)}, u32[]{:S(2)}, u32[]{:S(2)}) %collective-permute-start.18) | collective-permute-done | bytes 65568 | tf_op jit(solution)/shard_map/ppermute | solution.py:33
  69.6 2.1 %factor.5.inverse_ref = f32[128,128]{1,0:T(8,128)S(1)} custom-call(f32[128,256]{1,0:T(8,128)S(1)} %factor.4.in_ref), custom_call_target="tpu_custom_call" | custom-call | flops 1 | bytes 10485 | tf_op jit(solution)/shard_map/factor/pallas_call | solution.py:242
  71.7 3.1 %collective-permute-done.21.refs_3_ = f32[48,1024]{1,0:T(8,128)S(1)} collective-permute-done((f32[48,1024]{1,0:T(8,128)S(1)}, f32[48,1024]{1,0:T(8,128)S(1)}, u32[]{:S(2)}, u32[]{:S(2)}) %collective-permute-start.21) | collective-permute-done | bytes 196640 | tf_op jit(solution)/shard_map/ppermute | solution.py:33
  74.7 1.9 %finish.1 = (f32[128,1024]{1,0:T(8,128)}, f32[128,128]{1,0:T(8,128)S(1)}) custom-call(s32[2]{0:T(128)S(1)} %pad_add_fusion.own_ref, f32[128,128]{1,0:T(8,128)S(1)} %factor.5.inverse_ref, f32[16,1024]{1,0:T(8,128)S(1)} %add_add_fusion.refs_0_, f32[48,1024]{1,0:T(8,128)S(1)} %pad_maximum_fusion.refs_1_, f32[16,1024]{1,0:T(8,128)S(1)} %collective-permute-done.20.refs_2_, ...), custom_call_target="tpu_custom_call" | custom-call | flops 1 | bytes 8388608 | tf_op jit(solution)/shard_map/finish/pallas_call | solution.py:285
  77.2 1.5 %collective-permute-start.22 = (f32[128,128]{1,0:T(8,128)S(1)}, f32[128,128]{1,0:T(8,128)S(1)}, u32[]{:S(2)}, u32[]{:S(2)}) collective-permute-start(f32[128,128]{1,0:T(8,128)S(1)} %get-tuple-element.113), channel_id=1, source_target_pairs={{0,2},{1,3},{2,0},{3,1},{4,6},{5,7},{6,4},{7,5},{8,10},{9,11},{10,... | collective-permute-start | bytes 196616 | tf_op jit(solution)/shard_map/ppermute | solution.py:33
  78.7 1.4 %fusion.3 = f32[1024,128]{1,0:T(8,128)} fusion(f32[1024,128]{1,0:T(8,128)S(1)} %fusion.part_ref, f32[128,128]{1,0:T(8,128)S(1)} %factor.5.inverse_ref), kind=kOutput, calls=%fused_computation.12 | convolution fusion | flops 201326592 | bytes 1114112 | tf_op jit(solution)/shard_map/dot_general | solution.py:37
  80.3 2.1 %collective-permute-done.22 = f32[128,128]{1,0:T(8,128)S(1)} collective-permute-done((f32[128,128]{1,0:T(8,128)S(1)}, f32[128,128]{1,0:T(8,128)S(1)}, u32[]{:S(2)}, u32[]{:S(2)}) %collective-permute-start.22) | collective-permute-done | bytes 65568 | tf_op jit(solution)/shard_map/ppermute | solution.py:33
  (45 shorter events, 10.2 us)
Async XLA Ops:
  4.9 2.1 %collective-permute-start = (f32[1024,128]{1,0:T(8,128)S(1)}, f32[1024,128]{1,0:T(8,128)S(1)}, u32[]{:S(2)}, u32[]{:S(2)}) collective-permute-start(f32[1024,128]{1,0:T(8,128)S(1)} %get-tuple-element.63), channel_id=1, source_target_pairs={{0,1},{1,0},{2,3},{3,2},{4,5},{5,4},{6,7},{7,6},{8,9},{9,8},{10,11... | collective-permute-start | bytes 1572872 | tf_op jit(solution)/shard_map/ppermute | solution.py:33
  7.1 15.2 %collective-permute-start.3 = (f32[1024,128]{1,0:T(8,128)S(1)}, f32[1024,128]{1,0:T(8,128)S(1)}, u32[]{:S(2)}, u32[]{:S(2)}) collective-permute-start(f32[1024,128]{1,0:T(8,128)S(1)} %add.59), channel_id=1, source_target_pairs={{0,2},{1,3},{2,0},{3,1},{4,6},{5,7},{6,4},{7,5},{8,10},{9,11},{10,... | collective-permute-start | bytes 1572872 | tf_op jit(solution)/shard_map/ppermute | solution.py:33
  15.1 1.6 %collective-permute-start.2 = (f32[512,128]{1,0:T(8,128)S(1)}, f32[512,128]{1,0:T(8,128)S(1)}, u32[]{:S(2)}, u32[]{:S(2)}) collective-permute-start(f32[512,128]{1,0:T(8,128)S(1)} %get-tuple-element.119), channel_id=1, source_target_pairs={{0,1},{1,0},{2,3},{3,2},{4,5},{5,4},{6,7},{7,6},{8,9},{9,8},{10,11... | collective-permute-start | bytes 786440 | tf_op jit(solution)/shard_map/ppermute | solution.py:33
  15.2 1.9 %collective-permute-start.1 = (f32[512,128]{1,0:T(8,128)S(1)}, f32[512,128]{1,0:T(8,128)S(1)}, u32[]{:S(2)}, u32[]{:S(2)}) collective-permute-start(f32[512,128]{1,0:T(8,128)S(1)} %get-tuple-element.120), channel_id=1, source_target_pairs={{0,1},{1,0},{2,3},{3,2},{4,5},{5,4},{6,7},{7,6},{8,9},{9,8},{10,11... | collective-permute-start | bytes 786440 | tf_op jit(solution)/shard_map/ppermute | solution.py:33
  22.3 7.2 %collective-permute-start.5 = (f32[1024,128]{1,0:T(8,128)S(1)}, f32[1024,128]{1,0:T(8,128)S(1)}, u32[]{:S(2)}, u32[]{:S(2)}) collective-permute-start(f32[1024,128]{1,0:T(8,128)S(1)} %fusion.part_ref), channel_id=1, source_target_pairs={{0,1},{1,0},{2,3},{3,2},{4,5},{5,4},{6,7},{7,6},{8,9},{9,8},{10,11... | collective-permute-start | bytes 1572872 | tf_op jit(solution)/shard_map/ppermute | solution.py:33
  22.4 14.3 %collective-permute-start.7 = (f32[1024,128]{1,0:T(8,128)S(1)}, f32[1024,128]{1,0:T(8,128)S(1)}, u32[]{:S(2)}, u32[]{:S(2)}) collective-permute-start(f32[1024,128]{1,0:T(8,128)S(1)} %fusion.part_ref), channel_id=1, source_target_pairs={{0,2},{1,3},{2,0},{3,1},{4,6},{5,7},{6,4},{7,5},{8,10},{9,11},{10,... | collective-permute-start | bytes 1572872 | tf_op jit(solution)/shard_map/ppermute | solution.py:33
  25.3 4.3 %collective-permute-start.4 = (f32[128,128]{1,0:T(8,128)S(1)}, f32[128,128]{1,0:T(8,128)S(1)}, u32[]{:S(2)}, u32[]{:S(2)}) collective-permute-start(f32[128,128]{1,0:T(8,128)S(1)} %fusion.2), channel_id=1, source_target_pairs={{0,4},{4,0},{8,12},{12,8},{16,20},{20,16},{24,28},{28,24},{1,5},{5... | collective-permute-start | bytes 196616 | tf_op jit(solution)/shard_map/ppermute | solution.py:33
  29.6 4.3 %collective-permute-start.6 = (f32[128,128]{1,0:T(8,128)S(1)}, f32[128,128]{1,0:T(8,128)S(1)}, u32[]{:S(2)}, u32[]{:S(2)}) collective-permute-start(f32[128,128]{1,0:T(8,128)S(1)} %add.62), channel_id=1, source_target_pairs={{0,8},{4,12},{8,0},{12,4},{16,24},{20,28},{24,16},{28,20},{1,9},{5... | collective-permute-start | bytes 196616 | tf_op jit(solution)/shard_map/ppermute | solution.py:33
  33.9 5.2 %collective-permute-start.8 = (f32[128,128]{1,0:T(8,128)S(1)}, f32[128,128]{1,0:T(8,128)S(1)}, u32[]{:S(2)}, u32[]{:S(2)}) collective-permute-start(f32[128,128]{1,0:T(8,128)S(1)} %add.63), channel_id=1, source_target_pairs={{0,16},{4,20},{8,24},{12,28},{16,0},{20,4},{24,8},{28,12},{1,17},{... | collective-permute-start | bytes 196616 | tf_op jit(solution)/shard_map/ppermute | solution.py:33
  39.2 2.3 %collective-permute-start.10 = (f32[1024,128]{1,0:T(8,128)S(1)}, f32[1024,128]{1,0:T(8,128)S(1)}, u32[]{:S(2)}, u32[]{:S(2)}) collective-permute-start(f32[1024,128]{1,0:T(8,128)S(1)} %collective-permute-done.7.part_ref), channel_id=1, source_target_pairs={{0,1},{1,0},{2,3},{3,2},{4,5},{5,4},{6,7},{7,6},{8,9},{9,8},{10,11... | collective-permute-start | bytes 1572872 | tf_op jit(solution)/shard_map/ppermute | solution.py:33
  39.2 4.0 %collective-permute-start.9 = (f32[128,128]{1,0:T(8,128)S(1)}, f32[128,128]{1,0:T(8,128)S(1)}, u32[]{:S(2)}, u32[]{:S(2)}) collective-permute-start(f32[128,128]{1,0:T(8,128)S(1)} %add.64), channel_id=1, source_target_pairs={{0,1},{1,0},{2,3},{3,2},{4,5},{5,4},{6,7},{7,6},{8,9},{9,8},{10,11... | collective-permute-start | bytes 196616 | tf_op jit(solution)/shard_map/ppermute | solution.py:33
  43.2 6.4 %collective-permute-start.11 = (f32[32,1024]{1,0:T(8,128)S(1)}, f32[32,1024]{1,0:T(8,128)S(1)}, u32[]{:S(2)}, u32[]{:S(2)}) collective-permute-start(f32[32,1024]{1,0:T(8,128)S(1)} %get-tuple-element.89), channel_id=1, source_target_pairs={{0,4},{4,0},{8,12},{12,8},{16,20},{20,16},{24,28},{28,24},{1,5},{5... | collective-permute-start | bytes 393224 | tf_op jit(solution)/shard_map/ppermute | solution.py:33
  44.8 4.3 %collective-permute-start.12 = (f32[128,128]{1,0:T(8,128)S(1)}, f32[128,128]{1,0:T(8,128)S(1)}, u32[]{:S(2)}, u32[]{:S(2)}) collective-permute-start(f32[128,128]{1,0:T(8,128)S(1)} %add.65), channel_id=1, source_target_pairs={{0,2},{1,3},{2,0},{3,1},{4,6},{5,7},{6,4},{7,5},{8,10},{9,11},{10,... | collective-permute-start | bytes 196616 | tf_op jit(solution)/shard_map/ppermute | solution.py:33
  45.4 8.6 %collective-permute-start.14 = (f32[32,1024]{1,0:T(8,128)S(1)}, f32[32,1024]{1,0:T(8,128)S(1)}, u32[]{:S(2)}, u32[]{:S(2)}) collective-permute-start(f32[32,1024]{1,0:T(8,128)S(1)} %get-tuple-element.96), channel_id=1, source_target_pairs={{0,4},{4,0},{8,12},{12,8},{16,20},{20,16},{24,28},{28,24},{1,5},{5... | collective-permute-start | bytes 393224 | tf_op jit(solution)/shard_map/ppermute | solution.py:33
  49.7 8.9 %collective-permute-start.13 = (f32[16,1024]{1,0:T(8,128)S(1)}, f32[16,1024]{1,0:T(8,128)S(1)}, u32[]{:S(2)}, u32[]{:S(2)}) collective-permute-start(f32[16,1024]{1,0:T(8,128)S(1)} %get-tuple-element.94), channel_id=1, source_target_pairs={{0,24},{4,28},{8,16},{12,20},{16,8},{20,12},{24,0},{28,4},{1,25},{... | collective-permute-start | bytes 196616 | tf_op jit(solution)/shard_map/ppermute | solution.py:33
  54.0 4.6 %collective-permute-start.16 = (f32[16,1024]{1,0:T(8,128)S(1)}, f32[16,1024]{1,0:T(8,128)S(1)}, u32[]{:S(2)}, u32[]{:S(2)}) collective-permute-start(f32[16,1024]{1,0:T(8,128)S(1)} %get-tuple-element.121), channel_id=1, source_target_pairs={{0,8},{4,12},{8,0},{12,4},{16,24},{20,28},{24,16},{28,20},{1,9},{5... | collective-permute-start | bytes 196616 | tf_op jit(solution)/shard_map/ppermute | solution.py:33
  54.0 5.2 %collective-permute-start.15 = (f32[16,1024]{1,0:T(8,128)S(1)}, f32[16,1024]{1,0:T(8,128)S(1)}, u32[]{:S(2)}, u32[]{:S(2)}) collective-permute-start(f32[16,1024]{1,0:T(8,128)S(1)} %get-tuple-element.122), channel_id=1, source_target_pairs={{0,16},{4,20},{8,24},{12,28},{16,0},{20,4},{24,8},{28,12},{1,17},{... | collective-permute-start | bytes 196616 | tf_op jit(solution)/shard_map/ppermute | solution.py:33
  59.3 8.0 %collective-permute-start.20 = (f32[16,1024]{1,0:T(8,128)S(1)}, f32[16,1024]{1,0:T(8,128)S(1)}, u32[]{:S(2)}, u32[]{:S(2)}) collective-permute-start(f32[16,1024]{1,0:T(8,128)S(1)} %add_add_fusion.refs_0_), channel_id=1, source_target_pairs={{0,4},{4,0},{8,12},{12,8},{16,20},{20,16},{24,28},{28,24},{1,5},{5... | collective-permute-start | bytes 196616 | tf_op jit(solution)/shard_map/ppermute | solution.py:33
  60.8 6.5 %collective-permute-start.19 = (f32[16,1024]{1,0:T(8,128)S(1)}, f32[16,1024]{1,0:T(8,128)S(1)}, u32[]{:S(2)}, u32[]{:S(2)}) collective-permute-start(f32[16,1024]{1,0:T(8,128)S(1)} %add_add_fusion.refs_0_), channel_id=1, source_target_pairs={{0,24},{4,28},{8,16},{12,20},{16,8},{20,12},{24,0},{28,4},{1,25},{... | collective-permute-start | bytes 196616 | tf_op jit(solution)/shard_map/ppermute | solution.py:33
  63.0 6.0 %collective-permute-start.18 = (f32[16,1024]{1,0:T(8,128)S(1)}, f32[16,1024]{1,0:T(8,128)S(1)}, u32[]{:S(2)}, u32[]{:S(2)}) collective-permute-start(f32[16,1024]{1,0:T(8,128)S(1)} %add_add_fusion.refs_0_), channel_id=1, source_target_pairs={{0,16},{4,20},{8,24},{12,28},{16,0},{20,4},{24,8},{28,12},{1,17},{... | collective-permute-start | bytes 196616 | tf_op jit(solution)/shard_map/ppermute | solution.py:33
  64.3 4.7 %collective-permute-start.17 = (f32[16,1024]{1,0:T(8,128)S(1)}, f32[16,1024]{1,0:T(8,128)S(1)}, u32[]{:S(2)}, u32[]{:S(2)}) collective-permute-start(f32[16,1024]{1,0:T(8,128)S(1)} %add_add_fusion.refs_0_), channel_id=1, source_target_pairs={{0,8},{4,12},{8,0},{12,4},{16,24},{20,28},{24,16},{28,20},{1,9},{5... | collective-permute-start | bytes 196616 | tf_op jit(solution)/shard_map/ppermute | solution.py:33
  69.0 5.7 %collective-permute-start.21 = (f32[48,1024]{1,0:T(8,128)S(1)}, f32[48,1024]{1,0:T(8,128)S(1)}, u32[]{:S(2)}, u32[]{:S(2)}) collective-permute-start(f32[48,1024]{1,0:T(8,128)S(1)} %pad_maximum_fusion.refs_1_), channel_id=1, source_target_pairs={{0,4},{4,0},{8,12},{12,8},{16,20},{20,16},{24,28},{28,24},{1,5},{5... | collective-permute-start | bytes 589832 | tf_op jit(solution)/shard_map/ppermute | solution.py:33
  76.6 3.5 %collective-permute-start.24 = (f32[128,128]{1,0:T(8,128)S(1)}, f32[128,128]{1,0:T(8,128)S(1)}, u32[]{:S(2)}, u32[]{:S(2)}) collective-permute-start(f32[128,128]{1,0:T(8,128)S(1)} %get-tuple-element.113), channel_id=1, source_target_pairs={{0,1},{1,0},{2,3},{3,2},{4,5},{5,4},{6,7},{7,6},{8,9},{9,8},{10,11... | collective-permute-start | bytes 196616 | tf_op jit(solution)/shard_map/ppermute | solution.py:33
  76.6 3.7 %collective-permute-start.23 = (f32[128,128]{1,0:T(8,128)S(1)}, f32[128,128]{1,0:T(8,128)S(1)}, u32[]{:S(2)}, u32[]{:S(2)}) collective-permute-start(f32[128,128]{1,0:T(8,128)S(1)} %get-tuple-element.113), channel_id=1, source_target_pairs={{0,3},{1,2},{2,1},{3,0},{4,7},{5,6},{6,5},{7,4},{8,11},{9,10},{10,... | collective-permute-start | bytes 196616 | tf_op jit(solution)/shard_map/ppermute | solution.py:33
  77.2 5.2 %collective-permute-start.22 = (f32[128,128]{1,0:T(8,128)S(1)}, f32[128,128]{1,0:T(8,128)S(1)}, u32[]{:S(2)}, u32[]{:S(2)}) collective-permute-start(f32[128,128]{1,0:T(8,128)S(1)} %get-tuple-element.113), channel_id=1, source_target_pairs={{0,2},{1,3},{2,0},{3,1},{4,6},{5,7},{6,4},{7,5},{8,10},{9,11},{10,... | collective-permute-start | bytes 196616 | tf_op jit(solution)/shard_map/ppermute | solution.py:33

commit v14 on v12

--- a/solution.py
+++ b/solution.py
@@ -133,24 +133,18 @@
     )(rows, wide)
 
 
-def project_kernel(start, before, slices, own_ref, rows_ref, part_ref, *refs):
+def project_kernel(before, slices, own_ref, rows_ref, part_ref, *refs):
     old, refs = (refs[0], refs[1:]) if before else (None, refs)
     outs, total = (refs[:-1], refs[-1]) if slices else (refs, refs[0])
-    cols = rows_ref.shape[1]
-    for row in range(0, part_ref.shape[0], PIECE):
-        upper, rest = split(part_ref[row : row + PIECE].T)
-        stack = jnp.concatenate([upper, rest], 0)
-        width = upper.shape[0]
-        for t in range(cols // TILE):
-            tile = slice(t * TILE, (t + 1) * TILE)
-            d_upper, d_rest = split(rows_ref[start + row : start + row + PIECE, tile])
-            both = jnp.dot(stack, d_upper, preferred_element_type=f32)
-            value = both[:width] + both[width:] + jnp.dot(upper, d_rest, preferred_element_type=f32)
-            if row > 0:
-                value += total[:, tile]
-            elif before:
-                value += old[:, tile]
-            total[:, tile] = value
+    upper, rest = split(part_ref[...].T)
+    stack = jnp.concatenate([upper, rest], 0)
+    width = upper.shape[0]
+    for t in range(rows_ref.shape[1] // TILE):
+        tile = slice(t * TILE, (t + 1) * TILE)
+        d_upper, d_rest = split(rows_ref[:, tile])
+        both = jnp.dot(stack, d_upper, preferred_element_type=f32)
+        value = both[:width] + both[width:] + jnp.dot(upper, d_rest, preferred_element_type=f32)
+        total[:, tile] = value + old[:, tile] if before else value
     if slices:
         step = total.shape[0] // slices
         for place in range(slices):
@@ -159,7 +153,7 @@
             outs[2 * (place % 2) + group][row : row + step] = total[pl.ds(at, step)]
 
 
-def project(own, rows, part, before=None, slices=0, start=0):
+def project(own, rows, part, before=None, slices=0):
     cols = rows.shape[1]
     width = part.shape[1]
     args = [own, rows, part] + ([] if before is None else [before])
@@ -168,13 +162,13 @@
     else:
         out = [jax.ShapeDtypeStruct((width, cols), f32)]
     return pl.pallas_call(
-        functools.partial(project_kernel, start, before is not None, slices),
+        functools.partial(project_kernel, before is not None, slices),
         in_specs=[SMEM] + [VMEM] * (len(args) - 1),
         out_specs=[VMEM] * len(out),
         out_shape=out,
         scratch_shapes=[pltpu.VMEM((width, cols), f32)] if slices else [],
         compiler_params=params(),
-        cost_estimate=cost(6 * part.shape[0] / rows.shape[0]),
+        cost_estimate=cost(6),
         name="project",
     )(*args)
 
@@ -256,8 +250,8 @@
     step = total.shape[0] // SLICES
     for place in range(SLICES):
         at = pl.multiple_of((place ^ own_ref[1]) * step, step)
-        row = place // 2 * step
-        total[pl.ds(at, step)] = parts[place % 2][row : row + step]
+        group, row = (1, place // 2 * step - step) if place > 1 else (0, 0)
+        total[pl.ds(at, step)] = parts[2 * (place % 2) + group][row : row + step]
     upper, rest = split(inverse_ref[...])
     stack = jnp.concatenate([upper, rest], 0)
     width = upper.shape[0]
@@ -324,39 +318,41 @@
     gram = gram + far
     far = swap(gram, "row", bits[1])
     (acc,) = project(own, rows1, second, acc)
+    far, acc = fence((far, acc))
+    gram = gram + far
+    far = swap(gram, "col", 1)
     far, acc, third = fence((far, acc, third))
     gram = gram + far
     fourth = swap(third, "col", 1)
     (acc,) = project(own, rows2, third, acc)
     fourth, acc = fence((fourth, acc))
-    far = swap(gram, "col", 1)
     outer_keep, inner_keep, outer_send, inner_send = project(own, rows3, fourth, acc, SLICES)
-    far, outer_keep, inner_keep, outer_send, inner_send = fence(
-        (far, outer_keep, inner_keep, outer_send, inner_send)
+    gram, outer_keep, inner_keep, outer_send, inner_send = fence(
+        (gram, outer_keep, inner_keep, outer_send, inner_send)
     )
-    gram = gram + far
 
     step = outer_keep.shape[0] // 2
     outer_got = swap(outer_send, "row", 1)
     zero, six = outer_keep[:step] + outer_got[:step], outer_keep[step:] + outer_got[step:]
     zero, six = fence((zero, six))
     six = swap(six, "row", 6)
-    inner_got, far = fence((swap(inner_send, "row", 1), swap(gram, "col", 2)))
+    inner_got, far = fence((swap(inner_send, "row", 1), swap(gram, "row", bits[2])))
     gram = gram + far
     two, four = inner_keep[:step] + inner_got[:step], inner_keep[step:] + inner_got[step:]
     four, two = swap(four, "row", 4), swap(two, "row", 2)
-    for bit in bits[2:]:
+    for bit in bits[3:]:
         gram = gram + swap(gram, "row", bit)
-    six, four, two, state = fence((six, four, two, gram))
+    six, four, two, far = fence((six, four, two, swap(gram, "col", 2)))
+    state = gram + far
     zero = (zero + two) + (four + six)
     for bit in bits[3:]:
         zero = zero + swap(zero, "row", bit)
     zero, state = fence((zero, state))
-    got = [swap(zero, "row", q) for q in (2, 4, 6)]
+    got = [swap(zero, "row", q) for q in (2, 4, 6, 1)]
     *got, state = fence((*got, factor(0, 6, state)))
-    keep, state = fence((jnp.concatenate([zero, *got], 0), state))
-    got, inverse = fence((swap(keep, "row", 1), factor(6, 16, state)))
-    projected, small = finish(own, inverse, [keep, got])
+    others, state = fence((jnp.concatenate(got[:3], 0), state))
+    far, inverse = fence((swap(others, "row", 1), factor(6, 16, state)))
+    projected, small = finish(own, inverse, [zero, others, got[3], far])
 
     across = [swap(small, "col", bit) for bit in (2, 3, 1)]
     *across, basis = fence((*across, dot(sketched, inverse, 1, 1)))

time: 83.8 us -> 81.3 us (0.970)
  waiting for transfers between devices: 25 us -> 19.9 us
  starting transfers between devices: 29.2 us -> 31.5 us
    ppermute x24 -> x25, waiting for transfers between devices: 25 us -> 19.9 us  [swap(): lax.ppermute(value, axis, [(i, i ^ bit) for i in range(lax.axis_size(axis...]
    ppermute x24 -> x25, starting transfers between devices: 29.2 us -> 31.5 us  [swap(): lax.ppermute(value, axis, [(i, i ^ bit) for i in range(lax.axis_size(axis...]
  transfers between devices with their start and end apart: 24 -> 25, of which waited for: 13 -> 16; matrix products, arithmetic and copies ran while one was open for 3% -> 3% of each run, Pallas kernels for 23% -> 22%
where the time goes in v14:
time: 81.3 us; the launch traced here: 81.1 us
  starting transfers between devices  31.5 us (39%)
  Pallas kernels  25.4 us (31%)
  waiting for transfers between devices  19.9 us (24%)
  matrix products  2.4 us (3%)
  other arithmetic  1 us (1%)
  between operations  0.83 us (1%)
    ppermute x25, starting transfers between devices, swap(): lax.ppermute(value, axis, [(i, i ^ bit) for i in range(lax.axis_size(axis...  31.5 us
    ppermute x25, waiting for transfers between devices, swap(): lax.ppermute(value, axis, [(i, i ^ bit) for i in range(lax.axis_size(axis...  19.9 us
    pallas_call x2, Pallas kernels, sketch(): pl.pallas_call(functools.partial(sketch_kernel, places, ahead, first), in...  9.28 us
    pallas_call x4, Pallas kernels, project(): pl.pallas_call(functools.partial(project_kernel, before is not None, slic...  7.06 us
    pallas_call x2, Pallas kernels, factor(): pl.pallas_call(functools.partial(factor_kernel, first, end), in_specs=[VM...  5.95 us
    dot_general x2, matrix products, dot(): lax.dot_general(a, b, (((a_dim,), (b_dim,)), ((), ())), precision=precisi...  2.4 us
    pallas_call x1, Pallas kernels, finish(): pl.pallas_call(finish_kernel, in_specs=[SMEM] + [VMEM] * (1 + len(parts))...  1.86 us
  transfers between devices with their start and end apart: 25, of which 16 were waited for; matrix products, arithmetic and copies ran while one was open for 3% of the time, Pallas kernels for 22%

profile of v14, /device:TPU:0, one launch (start us, length us, event | category | flops | bytes accessed | tf_op | source)
XLA Modules:
  0.0 81.1 jit_solution(11763593734848465340)
XLA Ops:
  0.7 4.2 %partial_sketch.2 = (f32[1024,128]{1,0:T(8,128)S(1)}, f32[1024,1024]{1,0:T(8,128)S(1)}, f32[1024,1024]{1,0:T(8,128)S(1)}, bf16[1024,256]{1,0:T(8,128)(2,1)S(1)}) custom-call(s32[2]{0:T(128)S(1)} %pad_add_fusion.own_ref, f32[4096,1024]{1,0:T(8,128)} %data_ref.3, f32[1024,128]{1,0:T(8,128)} %omega_ref.1), custom_call_target="tpu_custom_call" | custom-call | flops 1 | bytes 10485 | tf_op jit(solution)/shard_map/partial_sketch/pallas_call | solution.py:107
  5.5 1.3 %partial_sketch_held.1 = f32[1024,128]{1,0:T(8,128)S(1)} custom-call(f32[1024,1024]{1,0:T(8,128)S(1)} %get-tuple-element.60.rows_ref, bf16[1024,256]{1,0:T(8,128)(2,1)S(1)} %get-tuple-element.63.wide_ref.omega_ref), custom_call_target="tpu_custom_call" | custom-call | flops 1 | bytes 10485 | tf_op jit(solution)/shard_map/partial_sketch_held/pallas_call | solution.py:125
  7.1 3.0 %collective-permute-start.3 = (f32[1024,128]{1,0:T(8,128)S(1)}, f32[1024,128]{1,0:T(8,128)S(1)}, u32[]{:S(2)}, u32[]{:S(2)}) collective-permute-start(f32[1024,128]{1,0:T(8,128)S(1)} %add.59), channel_id=1, source_target_pairs={{0,2},{1,3},{2,0},{3,1},{4,6},{5,7},{6,4},{7,5},{8,10},{9,11},{10,... | collective-permute-start | bytes 1572872 | tf_op jit(solution)/shard_map/ppermute | solution.py:33
  10.0 5.1 %partial_sketch.3 = (f32[1024,128]{1,0:T(8,128)S(1)}, f32[1024,128]{1,0:T(8,128)S(1)}, f32[1024,1024]{1,0:T(8,128)S(1)}, f32[1024,1024]{1,0:T(8,128)S(1)}) custom-call(s32[2]{0:T(128)S(1)} %pad_add_fusion.own_ref, f32[4096,1024]{1,0:T(8,128)} %data_ref.3, bf16[1024,256]{1,0:T(8,128)(2,1)S(1)} %get-tuple-element.63.wide_ref.omega_ref), custom_call_target="tpu_custom_call" | custom-call | flops 1 | bytes 10485 | tf_op jit(solution)/shard_map/partial_sketch/pallas_call | solution.py:107
  15.7 1.0 %collective-permute-done.2 = f32[512,128]{1,0:T(8,128)S(1)} collective-permute-done((f32[512,128]{1,0:T(8,128)S(1)}, f32[512,128]{1,0:T(8,128)S(1)}, u32[]{:S(2)}, u32[]{:S(2)}) %collective-permute-start.2) | collective-permute-done | bytes 262176 | tf_op jit(solution)/shard_map/ppermute | solution.py:33
  17.1 5.1 %collective-permute-done.3 = f32[1024,128]{1,0:T(8,128)S(1)} collective-permute-done((f32[1024,128]{1,0:T(8,128)S(1)}, f32[1024,128]{1,0:T(8,128)S(1)}, u32[]{:S(2)}, u32[]{:S(2)}) %collective-permute-start.3) | collective-permute-done | bytes 524320 | tf_op jit(solution)/shard_map/ppermute | solution.py:33
  22.4 1.8 %collective-permute-start.8 = (f32[1024,128]{1,0:T(8,128)S(1)}, f32[1024,128]{1,0:T(8,128)S(1)}, u32[]{:S(2)}, u32[]{:S(2)}) collective-permute-start(f32[1024,128]{1,0:T(8,128)S(1)} %fusion.part_ref), channel_id=1, source_target_pairs={{0,2},{1,3},{2,0},{3,1},{4,6},{5,7},{6,4},{7,5},{8,10},{9,11},{10,... | collective-permute-start | bytes 1572872 | tf_op jit(solution)/shard_map/ppermute | solution.py:33
  24.2 1.0 %fusion.2 = f32[128,128]{1,0:T(8,128)S(1)} fusion(f32[1024,128]{1,0:T(8,128)S(1)} %fusion.part_ref), kind=kOutput, calls=%fused_computation.11 | convolution fusion | flops 201326592 | bytes 589824 | tf_op jit(solution)/shard_map/dot_general | solution.py:37
  25.3 1.6 %collective-permute-start.4 = (f32[128,128]{1,0:T(8,128)S(1)}, f32[128,128]{1,0:T(8,128)S(1)}, u32[]{:S(2)}, u32[]{:S(2)}) collective-permute-start(f32[128,128]{1,0:T(8,128)S(1)} %fusion.2), channel_id=1, source_target_pairs={{0,4},{4,0},{8,12},{12,8},{16,20},{20,16},{24,28},{28,24},{1,5},{5... | collective-permute-start | bytes 196616 | tf_op jit(solution)/shard_map/ppermute | solution.py:33
  26.8 1.7 %project.4.refs_0_ = f32[128,1024]{1,0:T(8,128)S(1)} custom-call(s32[2]{0:T(128)S(1)} %pad_add_fusion.own_ref, f32[1024,1024]{1,0:T(8,128)S(1)} %get-tuple-element.70.rows_ref, f32[1024,128]{1,0:T(8,128)S(1)} %fusion.part_ref), custom_call_target="tpu_custom_call" | custom-call | flops 1 | bytes 6291456 | tf_op jit(solution)/shard_map/project/pallas_call | solution.py:164
  28.6 1.0 %collective-permute-done.4 = f32[128,128]{1,0:T(8,128)S(1)} collective-permute-done((f32[128,128]{1,0:T(8,128)S(1)}, f32[128,128]{1,0:T(8,128)S(1)}, u32[]{:S(2)}, u32[]{:S(2)}) %collective-permute-start.4) | collective-permute-done | bytes 65568 | tf_op jit(solution)/shard_map/ppermute | solution.py:33
  29.6 1.6 %collective-permute-start.6 = (f32[128,128]{1,0:T(8,128)S(1)}, f32[128,128]{1,0:T(8,128)S(1)}, u32[]{:S(2)}, u32[]{:S(2)}) collective-permute-start(f32[128,128]{1,0:T(8,128)S(1)} %add.62), channel_id=1, source_target_pairs={{0,8},{4,12},{8,0},{12,4},{16,24},{20,28},{24,16},{28,20},{1,9},{5... | collective-permute-start | bytes 196616 | tf_op jit(solution)/shard_map/ppermute | solution.py:33
  31.2 1.8 %project.5.refs_0_ = f32[128,1024]{1,0:T(8,128)S(1)} custom-call(s32[2]{0:T(128)S(1)} %pad_add_fusion.own_ref, f32[1024,1024]{1,0:T(8,128)S(1)} %get-tuple-element.72.rows_ref, f32[1024,128]{1,0:T(8,128)S(1)} %collective-permute-done.5.part_ref, f32[128,1024]{1,0:T(8,128)S(1)} %project.4.refs_0_), custom_call_target="tpu_custom_call" | custom-call | flops 1 | bytes 6291456 | tf_op jit(solution)/shard_map/project/pallas_call | solution.py:164
  34.0 2.7 %collective-permute-done.8.part_ref = f32[1024,128]{1,0:T(8,128)S(1)} collective-permute-done((f32[1024,128]{1,0:T(8,128)S(1)}, f32[1024,128]{1,0:T(8,128)S(1)}, u32[]{:S(2)}, u32[]{:S(2)}) %collective-permute-start.8) | collective-permute-done | bytes 524320 | tf_op jit(solution)/shard_map/ppermute | solution.py:33
  36.8 1.8 %project.6.refs_0_ = f32[128,1024]{1,0:T(8,128)S(1)} custom-call(s32[2]{0:T(128)S(1)} %pad_add_fusion.own_ref, f32[1024,1024]{1,0:T(8,128)S(1)} %get-tuple-element.60.rows_ref, f32[1024,128]{1,0:T(8,128)S(1)} %collective-permute-done.8.part_ref, f32[128,1024]{1,0:T(8,128)S(1)} %project.5.refs_0_), custom_call_target="tpu_custom_call" | custom-call | flops 1 | bytes 6291456 | tf_op jit(solution)/shard_map/project/pallas_call | solution.py:164
  38.7 1.8 %project.7 = (f32[32,1024]{1,0:T(8,128)S(1)}, f32[32,1024]{1,0:T(8,128)S(1)}, f32[32,1024]{1,0:T(8,128)S(1)}, f32[32,1024]{1,0:T(8,128)S(1)}) custom-call(s32[2]{0:T(128)S(1)} %pad_add_fusion.own_ref, f32[1024,1024]{1,0:T(8,128)S(1)} %get-tuple-element.78.rows_ref, f32[1024,128]{1,0:T(8,128)S(1)} %collective-permute-done.9.part_ref, ...), custom_call_target="tpu_custom_call" | custom-call | flops 1 | bytes 6291456 | tf_op jit(solution)/shard_map/project/pallas_call | solution.py:164
  40.5 1.8 %collective-permute-start.10 = (f32[32,1024]{1,0:T(8,128)S(1)}, f32[32,1024]{1,0:T(8,128)S(1)}, u32[]{:S(2)}, u32[]{:S(2)}) collective-permute-start(f32[32,1024]{1,0:T(8,128)S(1)} %get-tuple-element.88), channel_id=1, source_target_pairs={{0,4},{4,0},{8,12},{12,8},{16,20},{20,16},{24,28},{28,24},{1,5},{5... | collective-permute-start | bytes 393224 | tf_op jit(solution)/shard_map/ppermute | solution.py:33
  42.3 2.6 %collective-permute-start.13 = (f32[128,128]{1,0:T(8,128)S(1)}, f32[128,128]{1,0:T(8,128)S(1)}, u32[]{:S(2)}, u32[]{:S(2)}) collective-permute-start(f32[128,128]{1,0:T(8,128)S(1)} %add.64), channel_id=1, source_target_pairs={{0,16},{4,20},{8,24},{12,28},{16,0},{20,4},{24,8},{28,12},{1,17},{... | collective-permute-start | bytes 196616 | tf_op jit(solution)/shard_map/ppermute | solution.py:33
  46.4 4.4 %collective-permute-start.11 = (f32[16,1024]{1,0:T(8,128)S(1)}, f32[16,1024]{1,0:T(8,128)S(1)}, u32[]{:S(2)}, u32[]{:S(2)}) collective-permute-start(f32[16,1024]{1,0:T(8,128)S(1)} %get-tuple-element.90), channel_id=1, source_target_pairs={{0,24},{4,28},{8,16},{12,20},{16,8},{20,12},{24,0},{28,4},{1,25},{... | collective-permute-start | bytes 196616 | tf_op jit(solution)/shard_map/ppermute | solution.py:33
  51.8 1.9 %collective-permute-start.14 = (f32[16,1024]{1,0:T(8,128)S(1)}, f32[16,1024]{1,0:T(8,128)S(1)}, u32[]{:S(2)}, u32[]{:S(2)}) collective-permute-start(f32[16,1024]{1,0:T(8,128)S(1)} %get-tuple-element.120), channel_id=1, source_target_pairs={{0,16},{4,20},{8,24},{12,28},{16,0},{20,4},{24,8},{28,12},{1,17},{... | collective-permute-start | bytes 196616 | tf_op jit(solution)/shard_map/ppermute | solution.py:33
  53.7 1.5 %collective-permute-start.16 = (f32[128,128]{1,0:T(8,128)S(1)}, f32[128,128]{1,0:T(8,128)S(1)}, u32[]{:S(2)}, u32[]{:S(2)}) collective-permute-start(f32[128,128]{1,0:T(8,128)S(1)} %add.69), channel_id=1, source_target_pairs={{0,2},{1,3},{2,0},{3,1},{4,6},{5,7},{6,4},{7,5},{8,10},{9,11},{10,... | collective-permute-start | bytes 196616 | tf_op jit(solution)/shard_map/ppermute | solution.py:33
  55.3 2.4 %collective-permute-done.14 = f32[16,1024]{1,0:T(8,128)S(1)} collective-permute-done((f32[16,1024]{1,0:T(8,128)S(1)}, f32[16,1024]{1,0:T(8,128)S(1)}, u32[]{:S(2)}, u32[]{:S(2)}) %collective-permute-start.14) | collective-permute-done | bytes 65568 | tf_op jit(solution)/shard_map/ppermute | solution.py:33
  58.0 1.5 %collective-permute-start.20 = (f32[16,1024]{1,0:T(8,128)S(1)}, f32[16,1024]{1,0:T(8,128)S(1)}, u32[]{:S(2)}, u32[]{:S(2)}) collective-permute-start(f32[16,1024]{1,0:T(8,128)S(1)} %add_add_fusion.refs_0_), channel_id=1, source_target_pairs={{0,4},{4,0},{8,12},{12,8},{16,20},{20,16},{24,28},{28,24},{1,5},{5... | collective-permute-start | bytes 196616 | tf_op jit(solution)/shard_map/ppermute | solution.py:33
  59.5 1.7 %collective-permute-start.19 = (f32[16,1024]{1,0:T(8,128)S(1)}, f32[16,1024]{1,0:T(8,128)S(1)}, u32[]{:S(2)}, u32[]{:S(2)}) collective-permute-start(f32[16,1024]{1,0:T(8,128)S(1)} %add_add_fusion.refs_0_), channel_id=1, source_target_pairs={{0,24},{4,28},{8,16},{12,20},{16,8},{20,12},{24,0},{28,4},{1,25},{... | collective-permute-start | bytes 196616 | tf_op jit(solution)/shard_map/ppermute | solution.py:33
  61.4 2.5 %collective-permute-start.17 = (f32[16,1024]{1,0:T(8,128)S(1)}, f32[16,1024]{1,0:T(8,128)S(1)}, u32[]{:S(2)}, u32[]{:S(2)}) collective-permute-start(f32[16,1024]{1,0:T(8,128)S(1)} %add_add_fusion.refs_0_), channel_id=1, source_target_pairs={{0,8},{4,12},{8,0},{12,4},{16,24},{20,28},{24,16},{28,20},{1,9},{5... | collective-permute-start | bytes 196616 | tf_op jit(solution)/shard_map/ppermute | solution.py:33
  63.9 2.4 %factor.2.in_ref = f32[128,256]{1,0:T(8,128)S(1)} custom-call(f32[128,128]{1,0:T(8,128)S(1)} %add.73.in_ref), custom_call_target="tpu_custom_call" | custom-call | flops 1 | bytes 10485 | tf_op jit(solution)/shard_map/factor/pallas_call | solution.py:236
  67.6 3.6 %factor.3.inverse_ref = f32[128,128]{1,0:T(8,128)S(1)} custom-call(f32[128,256]{1,0:T(8,128)S(1)} %factor.2.in_ref), custom_call_target="tpu_custom_call" | custom-call | flops 1 | bytes 10485 | tf_op jit(solution)/shard_map/factor/pallas_call | solution.py:236
  71.2 1.5 %collective-permute-done.21.refs_3_ = f32[48,1024]{1,0:T(8,128)S(1)} collective-permute-done((f32[48,1024]{1,0:T(8,128)S(1)}, f32[48,1024]{1,0:T(8,128)S(1)}, u32[]{:S(2)}, u32[]{:S(2)}) %collective-permute-start.21) | collective-permute-done | bytes 196640 | tf_op jit(solution)/shard_map/ppermute | solution.py:33
  72.7 1.9 %finish.1 = (f32[128,1024]{1,0:T(8,128)}, f32[128,128]{1,0:T(8,128)S(1)}) custom-call(s32[2]{0:T(128)S(1)} %pad_add_fusion.own_ref, f32[128,128]{1,0:T(8,128)S(1)} %factor.3.inverse_ref, f32[16,1024]{1,0:T(8,128)S(1)} %add_add_fusion.refs_0_, f32[48,1024]{1,0:T(8,128)S(1)} %pad_maximum_fusion.refs_1_, f32[16,1024]{1,0:T(8,128)S(1)} %collective-permute-done.20.refs_2_, ...), custom_call_target="tpu_custom_call" | custom-call | flops 1 | bytes 8388608 | tf_op jit(solution)/shard_map/finish/pallas_call | solution.py:279
  74.6 1.6 %collective-permute-start.23 = (f32[128,128]{1,0:T(8,128)S(1)}, f32[128,128]{1,0:T(8,128)S(1)}, u32[]{:S(2)}, u32[]{:S(2)}) collective-permute-start(f32[128,128]{1,0:T(8,128)S(1)} %get-tuple-element.111), channel_id=1, source_target_pairs={{0,3},{1,2},{2,1},{3,0},{4,7},{5,6},{6,5},{7,4},{8,11},{9,10},{10,... | collective-permute-start | bytes 196616 | tf_op jit(solution)/shard_map/ppermute | solution.py:33
  76.7 1.4 %fusion.3 = f32[1024,128]{1,0:T(8,128)} fusion(f32[1024,128]{1,0:T(8,128)S(1)} %fusion.part_ref, f32[128,128]{1,0:T(8,128)S(1)} %factor.3.inverse_ref), kind=kOutput, calls=%fused_computation.12 | convolution fusion | flops 201326592 | bytes 1114112 | tf_op jit(solution)/shard_map/dot_general | solution.py:37
  78.7 1.8 %collective-permute-done.22 = f32[128,128]{1,0:T(8,128)S(1)} collective-permute-done((f32[128,128]{1,0:T(8,128)S(1)}, f32[128,128]{1,0:T(8,128)S(1)}, u32[]{:S(2)}, u32[]{:S(2)}) %collective-permute-start.22) | collective-permute-done | bytes 65568 | tf_op jit(solution)/shard_map/ppermute | solution.py:33
  (44 shorter events, 9.4 us)
Async XLA Ops:
  4.9 2.1 %collective-permute-start = (f32[1024,128]{1,0:T(8,128)S(1)}, f32[1024,128]{1,0:T(8,128)S(1)}, u32[]{:S(2)}, u32[]{:S(2)}) collective-permute-start(f32[1024,128]{1,0:T(8,128)S(1)} %get-tuple-element.62), channel_id=1, source_target_pairs={{0,1},{1,0},{2,3},{3,2},{4,5},{5,4},{6,7},{7,6},{8,9},{9,8},{10,11... | collective-permute-start | bytes 1572872 | tf_op jit(solution)/shard_map/ppermute | solution.py:33
  7.1 15.2 %collective-permute-start.3 = (f32[1024,128]{1,0:T(8,128)S(1)}, f32[1024,128]{1,0:T(8,128)S(1)}, u32[]{:S(2)}, u32[]{:S(2)}) collective-permute-start(f32[1024,128]{1,0:T(8,128)S(1)} %add.59), channel_id=1, source_target_pairs={{0,2},{1,3},{2,0},{3,1},{4,6},{5,7},{6,4},{7,5},{8,10},{9,11},{10,... | collective-permute-start | bytes 1572872 | tf_op jit(solution)/shard_map/ppermute | solution.py:33
  15.1 1.6 %collective-permute-start.2 = (f32[512,128]{1,0:T(8,128)S(1)}, f32[512,128]{1,0:T(8,128)S(1)}, u32[]{:S(2)}, u32[]{:S(2)}) collective-permute-start(f32[512,128]{1,0:T(8,128)S(1)} %get-tuple-element.117), channel_id=1, source_target_pairs={{0,1},{1,0},{2,3},{3,2},{4,5},{5,4},{6,7},{7,6},{8,9},{9,8},{10,11... | collective-permute-start | bytes 786440 | tf_op jit(solution)/shard_map/ppermute | solution.py:33
  15.2 1.9 %collective-permute-start.1 = (f32[512,128]{1,0:T(8,128)S(1)}, f32[512,128]{1,0:T(8,128)S(1)}, u32[]{:S(2)}, u32[]{:S(2)}) collective-permute-start(f32[512,128]{1,0:T(8,128)S(1)} %get-tuple-element.118), channel_id=1, source_target_pairs={{0,1},{1,0},{2,3},{3,2},{4,5},{5,4},{6,7},{7,6},{8,9},{9,8},{10,11... | collective-permute-start | bytes 786440 | tf_op jit(solution)/shard_map/ppermute | solution.py:33
  22.3 7.2 %collective-permute-start.5 = (f32[1024,128]{1,0:T(8,128)S(1)}, f32[1024,128]{1,0:T(8,128)S(1)}, u32[]{:S(2)}, u32[]{:S(2)}) collective-permute-start(f32[1024,128]{1,0:T(8,128)S(1)} %fusion.part_ref), channel_id=1, source_target_pairs={{0,1},{1,0},{2,3},{3,2},{4,5},{5,4},{6,7},{7,6},{8,9},{9,8},{10,11... | collective-permute-start | bytes 1572872 | tf_op jit(solution)/shard_map/ppermute | solution.py:33
  22.4 14.3 %collective-permute-start.8 = (f32[1024,128]{1,0:T(8,128)S(1)}, f32[1024,128]{1,0:T(8,128)S(1)}, u32[]{:S(2)}, u32[]{:S(2)}) collective-permute-start(f32[1024,128]{1,0:T(8,128)S(1)} %fusion.part_ref), channel_id=1, source_target_pairs={{0,2},{1,3},{2,0},{3,1},{4,6},{5,7},{6,4},{7,5},{8,10},{9,11},{10,... | collective-permute-start | bytes 1572872 | tf_op jit(solution)/shard_map/ppermute | solution.py:33
  25.3 4.3 %collective-permute-start.4 = (f32[128,128]{1,0:T(8,128)S(1)}, f32[128,128]{1,0:T(8,128)S(1)}, u32[]{:S(2)}, u32[]{:S(2)}) collective-permute-start(f32[128,128]{1,0:T(8,128)S(1)} %fusion.2), channel_id=1, source_target_pairs={{0,4},{4,0},{8,12},{12,8},{16,20},{20,16},{24,28},{28,24},{1,5},{5... | collective-permute-start | bytes 196616 | tf_op jit(solution)/shard_map/ppermute | solution.py:33
  29.6 4.3 %collective-permute-start.6 = (f32[128,128]{1,0:T(8,128)S(1)}, f32[128,128]{1,0:T(8,128)S(1)}, u32[]{:S(2)}, u32[]{:S(2)}) collective-permute-start(f32[128,128]{1,0:T(8,128)S(1)} %add.62), channel_id=1, source_target_pairs={{0,8},{4,12},{8,0},{12,4},{16,24},{20,28},{24,16},{28,20},{1,9},{5... | collective-permute-start | bytes 196616 | tf_op jit(solution)/shard_map/ppermute | solution.py:33
  33.9 2.8 %collective-permute-start.7 = (f32[128,128]{1,0:T(8,128)S(1)}, f32[128,128]{1,0:T(8,128)S(1)}, u32[]{:S(2)}, u32[]{:S(2)}) collective-permute-start(f32[128,128]{1,0:T(8,128)S(1)} %add.63), channel_id=1, source_target_pairs={{0,1},{1,0},{2,3},{3,2},{4,5},{5,4},{6,7},{7,6},{8,9},{9,8},{10,11... | collective-permute-start | bytes 196616 | tf_op jit(solution)/shard_map/ppermute | solution.py:33
  36.8 1.9 %collective-permute-start.9 = (f32[1024,128]{1,0:T(8,128)S(1)}, f32[1024,128]{1,0:T(8,128)S(1)}, u32[]{:S(2)}, u32[]{:S(2)}) collective-permute-start(f32[1024,128]{1,0:T(8,128)S(1)} %collective-permute-done.8.part_ref), channel_id=1, source_target_pairs={{0,1},{1,0},{2,3},{3,2},{4,5},{5,4},{6,7},{7,6},{8,9},{9,8},{10,11... | collective-permute-start | bytes 1572872 | tf_op jit(solution)/shard_map/ppermute | solution.py:33
  40.5 5.9 %collective-permute-start.10 = (f32[32,1024]{1,0:T(8,128)S(1)}, f32[32,1024]{1,0:T(8,128)S(1)}, u32[]{:S(2)}, u32[]{:S(2)}) collective-permute-start(f32[32,1024]{1,0:T(8,128)S(1)} %get-tuple-element.88), channel_id=1, source_target_pairs={{0,4},{4,0},{8,12},{12,8},{16,20},{20,16},{24,28},{28,24},{1,5},{5... | collective-permute-start | bytes 393224 | tf_op jit(solution)/shard_map/ppermute | solution.py:33
  42.3 8.5 %collective-permute-start.13 = (f32[128,128]{1,0:T(8,128)S(1)}, f32[128,128]{1,0:T(8,128)S(1)}, u32[]{:S(2)}, u32[]{:S(2)}) collective-permute-start(f32[128,128]{1,0:T(8,128)S(1)} %add.64), channel_id=1, source_target_pairs={{0,16},{4,20},{8,24},{12,28},{16,0},{20,4},{24,8},{28,12},{1,17},{... | collective-permute-start | bytes 196616 | tf_op jit(solution)/shard_map/ppermute | solution.py:33
  44.9 5.9 %collective-permute-start.12 = (f32[32,1024]{1,0:T(8,128)S(1)}, f32[32,1024]{1,0:T(8,128)S(1)}, u32[]{:S(2)}, u32[]{:S(2)}) collective-permute-start(f32[32,1024]{1,0:T(8,128)S(1)} %get-tuple-element.92), channel_id=1, source_target_pairs={{0,4},{4,0},{8,12},{12,8},{16,20},{20,16},{24,28},{28,24},{1,5},{5... | collective-permute-start | bytes 393224 | tf_op jit(solution)/shard_map/ppermute | solution.py:33
  46.4 8.8 %collective-permute-start.11 = (f32[16,1024]{1,0:T(8,128)S(1)}, f32[16,1024]{1,0:T(8,128)S(1)}, u32[]{:S(2)}, u32[]{:S(2)}) collective-permute-start(f32[16,1024]{1,0:T(8,128)S(1)} %get-tuple-element.90), channel_id=1, source_target_pairs={{0,24},{4,28},{8,16},{12,20},{16,8},{20,12},{24,0},{28,4},{1,25},{... | collective-permute-start | bytes 196616 | tf_op jit(solution)/shard_map/ppermute | solution.py:33
  50.8 4.5 %collective-permute-start.15 = (f32[16,1024]{1,0:T(8,128)S(1)}, f32[16,1024]{1,0:T(8,128)S(1)}, u32[]{:S(2)}, u32[]{:S(2)}) collective-permute-start(f32[16,1024]{1,0:T(8,128)S(1)} %get-tuple-element.119), channel_id=1, source_target_pairs={{0,8},{4,12},{8,0},{12,4},{16,24},{20,28},{24,16},{28,20},{1,9},{5... | collective-permute-start | bytes 196616 | tf_op jit(solution)/shard_map/ppermute | solution.py:33
  51.8 5.9 %collective-permute-start.14 = (f32[16,1024]{1,0:T(8,128)S(1)}, f32[16,1024]{1,0:T(8,128)S(1)}, u32[]{:S(2)}, u32[]{:S(2)}) collective-permute-start(f32[16,1024]{1,0:T(8,128)S(1)} %get-tuple-element.120), channel_id=1, source_target_pairs={{0,16},{4,20},{8,24},{12,28},{16,0},{20,4},{24,8},{28,12},{1,17},{... | collective-permute-start | bytes 196616 | tf_op jit(solution)/shard_map/ppermute | solution.py:33
  53.7 4.3 %collective-permute-start.16 = (f32[128,128]{1,0:T(8,128)S(1)}, f32[128,128]{1,0:T(8,128)S(1)}, u32[]{:S(2)}, u32[]{:S(2)}) collective-permute-start(f32[128,128]{1,0:T(8,128)S(1)} %add.69), channel_id=1, source_target_pairs={{0,2},{1,3},{2,0},{3,1},{4,6},{5,7},{6,4},{7,5},{8,10},{9,11},{10,... | collective-permute-start | bytes 196616 | tf_op jit(solution)/shard_map/ppermute | solution.py:33
  58.0 8.3 %collective-permute-start.20 = (f32[16,1024]{1,0:T(8,128)S(1)}, f32[16,1024]{1,0:T(8,128)S(1)}, u32[]{:S(2)}, u32[]{:S(2)}) collective-permute-start(f32[16,1024]{1,0:T(8,128)S(1)} %add_add_fusion.refs_0_), channel_id=1, source_target_pairs={{0,4},{4,0},{8,12},{12,8},{16,20},{20,16},{24,28},{28,24},{1,5},{5... | collective-permute-start | bytes 196616 | tf_op jit(solution)/shard_map/ppermute | solution.py:33
  59.5 6.8 %collective-permute-start.19 = (f32[16,1024]{1,0:T(8,128)S(1)}, f32[16,1024]{1,0:T(8,128)S(1)}, u32[]{:S(2)}, u32[]{:S(2)}) collective-permute-start(f32[16,1024]{1,0:T(8,128)S(1)} %add_add_fusion.refs_0_), channel_id=1, source_target_pairs={{0,24},{4,28},{8,16},{12,20},{16,8},{20,12},{24,0},{28,4},{1,25},{... | collective-permute-start | bytes 196616 | tf_op jit(solution)/shard_map/ppermute | solution.py:33
  61.2 5.8 %collective-permute-start.18 = (f32[16,1024]{1,0:T(8,128)S(1)}, f32[16,1024]{1,0:T(8,128)S(1)}, u32[]{:S(2)}, u32[]{:S(2)}) collective-permute-start(f32[16,1024]{1,0:T(8,128)S(1)} %add_add_fusion.refs_0_), channel_id=1, source_target_pairs={{0,16},{4,20},{8,24},{12,28},{16,0},{20,4},{24,8},{28,12},{1,17},{... | collective-permute-start | bytes 196616 | tf_op jit(solution)/shard_map/ppermute | solution.py:33
  61.4 5.6 %collective-permute-start.17 = (f32[16,1024]{1,0:T(8,128)S(1)}, f32[16,1024]{1,0:T(8,128)S(1)}, u32[]{:S(2)}, u32[]{:S(2)}) collective-permute-start(f32[16,1024]{1,0:T(8,128)S(1)} %add_add_fusion.refs_0_), channel_id=1, source_target_pairs={{0,8},{4,12},{8,0},{12,4},{16,24},{20,28},{24,16},{28,20},{1,9},{5... | collective-permute-start | bytes 196616 | tf_op jit(solution)/shard_map/ppermute | solution.py:33
  67.0 5.7 %collective-permute-start.21 = (f32[48,1024]{1,0:T(8,128)S(1)}, f32[48,1024]{1,0:T(8,128)S(1)}, u32[]{:S(2)}, u32[]{:S(2)}) collective-permute-start(f32[48,1024]{1,0:T(8,128)S(1)} %pad_maximum_fusion.refs_1_), channel_id=1, source_target_pairs={{0,4},{4,0},{8,12},{12,8},{16,20},{20,16},{24,28},{28,24},{1,5},{5... | collective-permute-start | bytes 589832 | tf_op jit(solution)/shard_map/ppermute | solution.py:33
  74.6 3.5 %collective-permute-start.24 = (f32[128,128]{1,0:T(8,128)S(1)}, f32[128,128]{1,0:T(8,128)S(1)}, u32[]{:S(2)}, u32[]{:S(2)}) collective-permute-start(f32[128,128]{1,0:T(8,128)S(1)} %get-tuple-element.111), channel_id=1, source_target_pairs={{0,1},{1,0},{2,3},{3,2},{4,5},{5,4},{6,7},{7,6},{8,9},{9,8},{10,11... | collective-permute-start | bytes 196616 | tf_op jit(solution)/shard_map/ppermute | solution.py:33
  74.6 4.1 %collective-permute-start.23 = (f32[128,128]{1,0:T(8,128)S(1)}, f32[128,128]{1,0:T(8,128)S(1)}, u32[]{:S(2)}, u32[]{:S(2)}) collective-permute-start(f32[128,128]{1,0:T(8,128)S(1)} %get-tuple-element.111), channel_id=1, source_target_pairs={{0,3},{1,2},{2,1},{3,0},{4,7},{5,6},{6,5},{7,4},{8,11},{9,10},{10,... | collective-permute-start | bytes 196616 | tf_op jit(solution)/shard_map/ppermute | solution.py:33
  76.2 4.3 %collective-permute-start.22 = (f32[128,128]{1,0:T(8,128)S(1)}, f32[128,128]{1,0:T(8,128)S(1)}, u32[]{:S(2)}, u32[]{:S(2)}) collective-permute-start(f32[128,128]{1,0:T(8,128)S(1)} %get-tuple-element.111), channel_id=1, source_target_pairs={{0,2},{1,3},{2,0},{3,1},{4,6},{5,7},{6,4},{7,5},{8,10},{9,11},{10,... | collective-permute-start | bytes 196616 | tf_op jit(solution)/shard_map/ppermute | solution.py:33

commit v15 on v14

--- a/solution.py
+++ b/solution.py
@@ -280,10 +280,7 @@
         finish_kernel,
         in_specs=[SMEM] + [VMEM] * (1 + len(parts)),
         out_specs=[VMEM] * 2,
-        out_shape=[
-            jax.ShapeDtypeStruct((width, cols), f32),
-            jax.ShapeDtypeStruct((width, width), f32),
-        ],
+        out_shape=[pltpu.VMEM((width, cols), f32), jax.ShapeDtypeStruct((width, width), f32)],
         scratch_shapes=[pltpu.VMEM((width, cols), f32)],
         compiler_params=params(),
         cost_estimate=cost(8),

time: 81.3 us -> 80.8 us (level)
  transfers between devices with their start and end apart: 25 -> 25, of which waited for: 16 -> 14; matrix products, arithmetic and copies ran while one was open for 3% -> 4% of each run, Pallas kernels for 22% -> 22%
where the time goes in v15:
time: 80.8 us; the launch traced here: 80.7 us
  starting transfers between devices  31.6 us (39%)
  Pallas kernels  24.9 us (31%)
  waiting for transfers between devices  19.2 us (24%)
  matrix products  2.4 us (3%)
  other arithmetic  1 us (1%)
  between operations  0.85 us (1%)
  local copies, waits for them, and re-layouts  0.83 us (1%)
    ppermute x25, starting transfers between devices, swap(): lax.ppermute(value, axis, [(i, i ^ bit) for i in range(lax.axis_size(axis...  31.6 us
    ppermute x25, waiting for transfers between devices, swap(): lax.ppermute(value, axis, [(i, i ^ bit) for i in range(lax.axis_size(axis...  19.2 us
    pallas_call x2, Pallas kernels, sketch(): pl.pallas_call(functools.partial(sketch_kernel, places, ahead, first), in...  9.28 us
    pallas_call x4, Pallas kernels, project(): pl.pallas_call(functools.partial(project_kernel, before is not None, slic...  7.06 us
    pallas_call x2, Pallas kernels, factor(): pl.pallas_call(functools.partial(factor_kernel, first, end), in_specs=[VM...  5.95 us
    dot_general x2, matrix products, dot(): lax.dot_general(a, b, (((a_dim,), (b_dim,)), ((), ())), precision=precisi...  2.4 us
  transfers between devices with their start and end apart: 25, of which 14 were waited for; matrix products, arithmetic and copies ran while one was open for 4% of the time, Pallas kernels for 22%

profile of v15, /device:TPU:0, one launch (start us, length us, event | category | flops | bytes accessed | tf_op | source)
XLA Modules:
  0.0 80.7 jit_solution(11250519945712365876)
XLA Ops:
  0.7 4.2 %partial_sketch.2 = (f32[1024,128]{1,0:T(8,128)S(1)}, f32[1024,1024]{1,0:T(8,128)S(1)}, f32[1024,1024]{1,0:T(8,128)S(1)}, bf16[1024,256]{1,0:T(8,128)(2,1)S(1)}) custom-call(s32[2]{0:T(128)S(1)} %pad_add_fusion.own_ref, f32[4096,1024]{1,0:T(8,128)} %data_ref.3, f32[1024,128]{1,0:T(8,128)} %omega_ref.1), custom_call_target="tpu_custom_call" | custom-call | flops 1 | bytes 10485 | tf_op jit(solution)/shard_map/partial_sketch/pallas_call | solution.py:107
  5.5 1.3 %partial_sketch_held.1 = f32[1024,128]{1,0:T(8,128)S(1)} custom-call(f32[1024,1024]{1,0:T(8,128)S(1)} %get-tuple-element.60.rows_ref, bf16[1024,256]{1,0:T(8,128)(2,1)S(1)} %get-tuple-element.63.wide_ref.omega_ref), custom_call_target="tpu_custom_call" | custom-call | flops 1 | bytes 10485 | tf_op jit(solution)/shard_map/partial_sketch_held/pallas_call | solution.py:125
  7.1 3.0 %collective-permute-start.3 = (f32[1024,128]{1,0:T(8,128)S(1)}, f32[1024,128]{1,0:T(8,128)S(1)}, u32[]{:S(2)}, u32[]{:S(2)}) collective-permute-start(f32[1024,128]{1,0:T(8,128)S(1)} %add.59), channel_id=1, source_target_pairs={{0,2},{1,3},{2,0},{3,1},{4,6},{5,7},{6,4},{7,5},{8,10},{9,11},{10,... | collective-permute-start | bytes 1572872 | tf_op jit(solution)/shard_map/ppermute | solution.py:33
  10.0 5.1 %partial_sketch.3 = (f32[1024,128]{1,0:T(8,128)S(1)}, f32[1024,128]{1,0:T(8,128)S(1)}, f32[1024,1024]{1,0:T(8,128)S(1)}, f32[1024,1024]{1,0:T(8,128)S(1)}) custom-call(s32[2]{0:T(128)S(1)} %pad_add_fusion.own_ref, f32[4096,1024]{1,0:T(8,128)} %data_ref.3, bf16[1024,256]{1,0:T(8,128)(2,1)S(1)} %get-tuple-element.63.wide_ref.omega_ref), custom_call_target="tpu_custom_call" | custom-call | flops 1 | bytes 10485 | tf_op jit(solution)/shard_map/partial_sketch/pallas_call | solution.py:107
  15.7 1.0 %collective-permute-done.2 = f32[512,128]{1,0:T(8,128)S(1)} collective-permute-done((f32[512,128]{1,0:T(8,128)S(1)}, f32[512,128]{1,0:T(8,128)S(1)}, u32[]{:S(2)}, u32[]{:S(2)}) %collective-permute-start.2) | collective-permute-done | bytes 262176 | tf_op jit(solution)/shard_map/ppermute | solution.py:33
  17.1 5.1 %collective-permute-done.3 = f32[1024,128]{1,0:T(8,128)S(1)} collective-permute-done((f32[1024,128]{1,0:T(8,128)S(1)}, f32[1024,128]{1,0:T(8,128)S(1)}, u32[]{:S(2)}, u32[]{:S(2)}) %collective-permute-start.3) | collective-permute-done | bytes 524320 | tf_op jit(solution)/shard_map/ppermute | solution.py:33
  22.4 1.8 %collective-permute-start.8 = (f32[1024,128]{1,0:T(8,128)S(1)}, f32[1024,128]{1,0:T(8,128)S(1)}, u32[]{:S(2)}, u32[]{:S(2)}) collective-permute-start(f32[1024,128]{1,0:T(8,128)S(1)} %fusion.part_ref), channel_id=1, source_target_pairs={{0,2},{1,3},{2,0},{3,1},{4,6},{5,7},{6,4},{7,5},{8,10},{9,11},{10,... | collective-permute-start | bytes 1572872 | tf_op jit(solution)/shard_map/ppermute | solution.py:33
  24.2 1.0 %fusion.2 = f32[128,128]{1,0:T(8,128)S(1)} fusion(f32[1024,128]{1,0:T(8,128)S(1)} %fusion.part_ref), kind=kOutput, calls=%fused_computation.11 | convolution fusion | flops 201326592 | bytes 589824 | tf_op jit(solution)/shard_map/dot_general | solution.py:37
  25.3 1.6 %collective-permute-start.4 = (f32[128,128]{1,0:T(8,128)S(1)}, f32[128,128]{1,0:T(8,128)S(1)}, u32[]{:S(2)}, u32[]{:S(2)}) collective-permute-start(f32[128,128]{1,0:T(8,128)S(1)} %fusion.2), channel_id=1, source_target_pairs={{0,4},{4,0},{8,12},{12,8},{16,20},{20,16},{24,28},{28,24},{1,5},{5... | collective-permute-start | bytes 196616 | tf_op jit(solution)/shard_map/ppermute | solution.py:33
  26.8 1.7 %project.4.refs_0_ = f32[128,1024]{1,0:T(8,128)S(1)} custom-call(s32[2]{0:T(128)S(1)} %pad_add_fusion.own_ref, f32[1024,1024]{1,0:T(8,128)S(1)} %get-tuple-element.70.rows_ref, f32[1024,128]{1,0:T(8,128)S(1)} %fusion.part_ref), custom_call_target="tpu_custom_call" | custom-call | flops 1 | bytes 6291456 | tf_op jit(solution)/shard_map/project/pallas_call | solution.py:164
  28.6 1.0 %collective-permute-done.4 = f32[128,128]{1,0:T(8,128)S(1)} collective-permute-done((f32[128,128]{1,0:T(8,128)S(1)}, f32[128,128]{1,0:T(8,128)S(1)}, u32[]{:S(2)}, u32[]{:S(2)}) %collective-permute-start.4) | collective-permute-done | bytes 65568 | tf_op jit(solution)/shard_map/ppermute | solution.py:33
  29.6 1.6 %collective-permute-start.6 = (f32[128,128]{1,0:T(8,128)S(1)}, f32[128,128]{1,0:T(8,128)S(1)}, u32[]{:S(2)}, u32[]{:S(2)}) collective-permute-start(f32[128,128]{1,0:T(8,128)S(1)} %add.62), channel_id=1, source_target_pairs={{0,8},{4,12},{8,0},{12,4},{16,24},{20,28},{24,16},{28,20},{1,9},{5... | collective-permute-start | bytes 196616 | tf_op jit(solution)/shard_map/ppermute | solution.py:33
  31.3 1.8 %project.5.refs_0_ = f32[128,1024]{1,0:T(8,128)S(1)} custom-call(s32[2]{0:T(128)S(1)} %pad_add_fusion.own_ref, f32[1024,1024]{1,0:T(8,128)S(1)} %get-tuple-element.72.rows_ref, f32[1024,128]{1,0:T(8,128)S(1)} %collective-permute-done.5.part_ref, f32[128,1024]{1,0:T(8,128)S(1)} %project.4.refs_0_), custom_call_target="tpu_custom_call" | custom-call | flops 1 | bytes 6291456 | tf_op jit(solution)/shard_map/project/pallas_call | solution.py:164
  34.0 2.7 %collective-permute-done.8.part_ref = f32[1024,128]{1,0:T(8,128)S(1)} collective-permute-done((f32[1024,128]{1,0:T(8,128)S(1)}, f32[1024,128]{1,0:T(8,128)S(1)}, u32[]{:S(2)}, u32[]{:S(2)}) %collective-permute-start.8) | collective-permute-done | bytes 524320 | tf_op jit(solution)/shard_map/ppermute | solution.py:33
  36.8 1.8 %project.6.refs_0_ = f32[128,1024]{1,0:T(8,128)S(1)} custom-call(s32[2]{0:T(128)S(1)} %pad_add_fusion.own_ref, f32[1024,1024]{1,0:T(8,128)S(1)} %get-tuple-element.60.rows_ref, f32[1024,128]{1,0:T(8,128)S(1)} %collective-permute-done.8.part_ref, f32[128,1024]{1,0:T(8,128)S(1)} %project.5.refs_0_), custom_call_target="tpu_custom_call" | custom-call | flops 1 | bytes 6291456 | tf_op jit(solution)/shard_map/project/pallas_call | solution.py:164
  38.7 1.8 %project.7 = (f32[32,1024]{1,0:T(8,128)S(1)}, f32[32,1024]{1,0:T(8,128)S(1)}, f32[32,1024]{1,0:T(8,128)S(1)}, f32[32,1024]{1,0:T(8,128)S(1)}) custom-call(s32[2]{0:T(128)S(1)} %pad_add_fusion.own_ref, f32[1024,1024]{1,0:T(8,128)S(1)} %get-tuple-element.78.rows_ref, f32[1024,128]{1,0:T(8,128)S(1)} %collective-permute-done.9.part_ref, ...), custom_call_target="tpu_custom_call" | custom-call | flops 1 | bytes 6291456 | tf_op jit(solution)/shard_map/project/pallas_call | solution.py:164
  40.5 1.8 %collective-permute-start.10 = (f32[32,1024]{1,0:T(8,128)S(1)}, f32[32,1024]{1,0:T(8,128)S(1)}, u32[]{:S(2)}, u32[]{:S(2)}) collective-permute-start(f32[32,1024]{1,0:T(8,128)S(1)} %get-tuple-element.88), channel_id=1, source_target_pairs={{0,4},{4,0},{8,12},{12,8},{16,20},{20,16},{24,28},{28,24},{1,5},{5... | collective-permute-start | bytes 393224 | tf_op jit(solution)/shard_map/ppermute | solution.py:33
  42.3 2.6 %collective-permute-start.13 = (f32[128,128]{1,0:T(8,128)S(1)}, f32[128,128]{1,0:T(8,128)S(1)}, u32[]{:S(2)}, u32[]{:S(2)}) collective-permute-start(f32[128,128]{1,0:T(8,128)S(1)} %add.64), channel_id=1, source_target_pairs={{0,16},{4,20},{8,24},{12,28},{16,0},{20,4},{24,8},{28,12},{1,17},{... | collective-permute-start | bytes 196616 | tf_op jit(solution)/shard_map/ppermute | solution.py:33
  46.4 4.4 %collective-permute-start.11 = (f32[16,1024]{1,0:T(8,128)S(1)}, f32[16,1024]{1,0:T(8,128)S(1)}, u32[]{:S(2)}, u32[]{:S(2)}) collective-permute-start(f32[16,1024]{1,0:T(8,128)S(1)} %get-tuple-element.90), channel_id=1, source_target_pairs={{0,24},{4,28},{8,16},{12,20},{16,8},{20,12},{24,0},{28,4},{1,25},{... | collective-permute-start | bytes 196616 | tf_op jit(solution)/shard_map/ppermute | solution.py:33
  51.8 1.9 %collective-permute-start.14 = (f32[16,1024]{1,0:T(8,128)S(1)}, f32[16,1024]{1,0:T(8,128)S(1)}, u32[]{:S(2)}, u32[]{:S(2)}) collective-permute-start(f32[16,1024]{1,0:T(8,128)S(1)} %get-tuple-element.120), channel_id=1, source_target_pairs={{0,16},{4,20},{8,24},{12,28},{16,0},{20,4},{24,8},{28,12},{1,17},{... | collective-permute-start | bytes 196616 | tf_op jit(solution)/shard_map/ppermute | solution.py:33
  53.6 1.5 %collective-permute-start.16 = (f32[128,128]{1,0:T(8,128)S(1)}, f32[128,128]{1,0:T(8,128)S(1)}, u32[]{:S(2)}, u32[]{:S(2)}) collective-permute-start(f32[128,128]{1,0:T(8,128)S(1)} %add.69), channel_id=1, source_target_pairs={{0,2},{1,3},{2,0},{3,1},{4,6},{5,7},{6,4},{7,5},{8,10},{9,11},{10,... | collective-permute-start | bytes 196616 | tf_op jit(solution)/shard_map/ppermute | solution.py:33
  55.2 1.8 %collective-permute-done.14 = f32[16,1024]{1,0:T(8,128)S(1)} collective-permute-done((f32[16,1024]{1,0:T(8,128)S(1)}, f32[16,1024]{1,0:T(8,128)S(1)}, u32[]{:S(2)}, u32[]{:S(2)}) %collective-permute-start.14) | collective-permute-done | bytes 65568 | tf_op jit(solution)/shard_map/ppermute | solution.py:33
  58.0 1.6 %collective-permute-start.20 = (f32[16,1024]{1,0:T(8,128)S(1)}, f32[16,1024]{1,0:T(8,128)S(1)}, u32[]{:S(2)}, u32[]{:S(2)}) collective-permute-start(f32[16,1024]{1,0:T(8,128)S(1)} %add_add_fusion.refs_0_), channel_id=1, source_target_pairs={{0,4},{4,0},{8,12},{12,8},{16,20},{20,16},{24,28},{28,24},{1,5},{5... | collective-permute-start | bytes 196616 | tf_op jit(solution)/shard_map/ppermute | solution.py:33
  59.5 1.7 %collective-permute-start.19 = (f32[16,1024]{1,0:T(8,128)S(1)}, f32[16,1024]{1,0:T(8,128)S(1)}, u32[]{:S(2)}, u32[]{:S(2)}) collective-permute-start(f32[16,1024]{1,0:T(8,128)S(1)} %add_add_fusion.refs_0_), channel_id=1, source_target_pairs={{0,24},{4,28},{8,16},{12,20},{16,8},{20,12},{24,0},{28,4},{1,25},{... | collective-permute-start | bytes 196616 | tf_op jit(solution)/shard_map/ppermute | solution.py:33
  61.4 2.5 %collective-permute-start.17 = (f32[16,1024]{1,0:T(8,128)S(1)}, f32[16,1024]{1,0:T(8,128)S(1)}, u32[]{:S(2)}, u32[]{:S(2)}) collective-permute-start(f32[16,1024]{1,0:T(8,128)S(1)} %add_add_fusion.refs_0_), channel_id=1, source_target_pairs={{0,8},{4,12},{8,0},{12,4},{16,24},{20,28},{24,16},{28,20},{1,9},{5... | collective-permute-start | bytes 196616 | tf_op jit(solution)/shard_map/ppermute | solution.py:33
  63.9 2.4 %factor.2.in_ref = f32[128,256]{1,0:T(8,128)S(1)} custom-call(f32[128,128]{1,0:T(8,128)S(1)} %add.73.in_ref), custom_call_target="tpu_custom_call" | custom-call | flops 1 | bytes 10485 | tf_op jit(solution)/shard_map/factor/pallas_call | solution.py:236
  67.6 3.6 %factor.3.inverse_ref = f32[128,128]{1,0:T(8,128)S(1)} custom-call(f32[128,256]{1,0:T(8,128)S(1)} %factor.2.in_ref), custom_call_target="tpu_custom_call" | custom-call | flops 1 | bytes 10485 | tf_op jit(solution)/shard_map/factor/pallas_call | solution.py:236
  71.2 1.6 %collective-permute-done.21.refs_3_ = f32[48,1024]{1,0:T(8,128)S(1)} collective-permute-done((f32[48,1024]{1,0:T(8,128)S(1)}, f32[48,1024]{1,0:T(8,128)S(1)}, u32[]{:S(2)}, u32[]{:S(2)}) %collective-permute-start.21) | collective-permute-done | bytes 196640 | tf_op jit(solution)/shard_map/ppermute | solution.py:33
  72.7 1.3 %finish.1 = (f32[128,1024]{1,0:T(8,128)S(1)}, f32[128,128]{1,0:T(8,128)S(1)}) custom-call(s32[2]{0:T(128)S(1)} %pad_add_fusion.own_ref, f32[128,128]{1,0:T(8,128)S(1)} %factor.3.inverse_ref, f32[16,1024]{1,0:T(8,128)S(1)} %add_add_fusion.refs_0_, f32[48,1024]{1,0:T(8,128)S(1)} %pad_maximum_fusion.refs_1_, f32[16,1024]{1,0:T(8,128)S(1)} %collective-permute-done.20.refs_2_, ...), custom_call_target="tpu_custom_call" | custom-call | flops 1 | bytes 8388608 | tf_op jit(solution)/shard_map/finish/pallas_call | solution.py:279
  74.1 1.6 %collective-permute-start.23 = (f32[128,128]{1,0:T(8,128)S(1)}, f32[128,128]{1,0:T(8,128)S(1)}, u32[]{:S(2)}, u32[]{:S(2)}) collective-permute-start(f32[128,128]{1,0:T(8,128)S(1)} %get-tuple-element.111), channel_id=1, source_target_pairs={{0,3},{1,2},{2,1},{3,0},{4,7},{5,6},{6,5},{7,4},{8,11},{9,10},{10,... | collective-permute-start | bytes 196616 | tf_op jit(solution)/shard_map/ppermute | solution.py:33
  76.3 1.4 %fusion.3 = f32[1024,128]{1,0:T(8,128)} fusion(f32[1024,128]{1,0:T(8,128)S(1)} %fusion.part_ref, f32[128,128]{1,0:T(8,128)S(1)} %factor.3.inverse_ref), kind=kOutput, calls=%fused_computation.12 | convolution fusion | flops 201326592 | bytes 1114112 | tf_op jit(solution)/shard_map/dot_general | solution.py:37
  78.5 1.6 %collective-permute-done.22 = f32[128,128]{1,0:T(8,128)S(1)} collective-permute-done((f32[128,128]{1,0:T(8,128)S(1)}, f32[128,128]{1,0:T(8,128)S(1)}, u32[]{:S(2)}, u32[]{:S(2)}) %collective-permute-start.22) | collective-permute-done | bytes 65568 | tf_op jit(solution)/shard_map/ppermute | solution.py:33
  (45 shorter events, 10.3 us)
Async XLA Ops:
  4.9 2.1 %collective-permute-start = (f32[1024,128]{1,0:T(8,128)S(1)}, f32[1024,128]{1,0:T(8,128)S(1)}, u32[]{:S(2)}, u32[]{:S(2)}) collective-permute-start(f32[1024,128]{1,0:T(8,128)S(1)} %get-tuple-element.62), channel_id=1, source_target_pairs={{0,1},{1,0},{2,3},{3,2},{4,5},{5,4},{6,7},{7,6},{8,9},{9,8},{10,11... | collective-permute-start | bytes 1572872 | tf_op jit(solution)/shard_map/ppermute | solution.py:33
  7.1 15.2 %collective-permute-start.3 = (f32[1024,128]{1,0:T(8,128)S(1)}, f32[1024,128]{1,0:T(8,128)S(1)}, u32[]{:S(2)}, u32[]{:S(2)}) collective-permute-start(f32[1024,128]{1,0:T(8,128)S(1)} %add.59), channel_id=1, source_target_pairs={{0,2},{1,3},{2,0},{3,1},{4,6},{5,7},{6,4},{7,5},{8,10},{9,11},{10,... | collective-permute-start | bytes 1572872 | tf_op jit(solution)/shard_map/ppermute | solution.py:33
  15.1 1.6 %collective-permute-start.2 = (f32[512,128]{1,0:T(8,128)S(1)}, f32[512,128]{1,0:T(8,128)S(1)}, u32[]{:S(2)}, u32[]{:S(2)}) collective-permute-start(f32[512,128]{1,0:T(8,128)S(1)} %get-tuple-element.117), channel_id=1, source_target_pairs={{0,1},{1,0},{2,3},{3,2},{4,5},{5,4},{6,7},{7,6},{8,9},{9,8},{10,11... | collective-permute-start | bytes 786440 | tf_op jit(solution)/shard_map/ppermute | solution.py:33
  15.2 1.9 %collective-permute-start.1 = (f32[512,128]{1,0:T(8,128)S(1)}, f32[512,128]{1,0:T(8,128)S(1)}, u32[]{:S(2)}, u32[]{:S(2)}) collective-permute-start(f32[512,128]{1,0:T(8,128)S(1)} %get-tuple-element.118), channel_id=1, source_target_pairs={{0,1},{1,0},{2,3},{3,2},{4,5},{5,4},{6,7},{7,6},{8,9},{9,8},{10,11... | collective-permute-start | bytes 786440 | tf_op jit(solution)/shard_map/ppermute | solution.py:33
  22.3 7.2 %collective-permute-start.5 = (f32[1024,128]{1,0:T(8,128)S(1)}, f32[1024,128]{1,0:T(8,128)S(1)}, u32[]{:S(2)}, u32[]{:S(2)}) collective-permute-start(f32[1024,128]{1,0:T(8,128)S(1)} %fusion.part_ref), channel_id=1, source_target_pairs={{0,1},{1,0},{2,3},{3,2},{4,5},{5,4},{6,7},{7,6},{8,9},{9,8},{10,11... | collective-permute-start | bytes 1572872 | tf_op jit(solution)/shard_map/ppermute | solution.py:33
  22.4 14.3 %collective-permute-start.8 = (f32[1024,128]{1,0:T(8,128)S(1)}, f32[1024,128]{1,0:T(8,128)S(1)}, u32[]{:S(2)}, u32[]{:S(2)}) collective-permute-start(f32[1024,128]{1,0:T(8,128)S(1)} %fusion.part_ref), channel_id=1, source_target_pairs={{0,2},{1,3},{2,0},{3,1},{4,6},{5,7},{6,4},{7,5},{8,10},{9,11},{10,... | collective-permute-start | bytes 1572872 | tf_op jit(solution)/shard_map/ppermute | solution.py:33
  25.3 4.3 %collective-permute-start.4 = (f32[128,128]{1,0:T(8,128)S(1)}, f32[128,128]{1,0:T(8,128)S(1)}, u32[]{:S(2)}, u32[]{:S(2)}) collective-permute-start(f32[128,128]{1,0:T(8,128)S(1)} %fusion.2), channel_id=1, source_target_pairs={{0,4},{4,0},{8,12},{12,8},{16,20},{20,16},{24,28},{28,24},{1,5},{5... | collective-permute-start | bytes 196616 | tf_op jit(solution)/shard_map/ppermute | solution.py:33
  29.6 4.3 %collective-permute-start.6 = (f32[128,128]{1,0:T(8,128)S(1)}, f32[128,128]{1,0:T(8,128)S(1)}, u32[]{:S(2)}, u32[]{:S(2)}) collective-permute-start(f32[128,128]{1,0:T(8,128)S(1)} %add.62), channel_id=1, source_target_pairs={{0,8},{4,12},{8,0},{12,4},{16,24},{20,28},{24,16},{28,20},{1,9},{5... | collective-permute-start | bytes 196616 | tf_op jit(solution)/shard_map/ppermute | solution.py:33
  34.0 2.8 %collective-permute-start.7 = (f32[128,128]{1,0:T(8,128)S(1)}, f32[128,128]{1,0:T(8,128)S(1)}, u32[]{:S(2)}, u32[]{:S(2)}) collective-permute-start(f32[128,128]{1,0:T(8,128)S(1)} %add.63), channel_id=1, source_target_pairs={{0,1},{1,0},{2,3},{3,2},{4,5},{5,4},{6,7},{7,6},{8,9},{9,8},{10,11... | collective-permute-start | bytes 196616 | tf_op jit(solution)/shard_map/ppermute | solution.py:33
  36.8 1.9 %collective-permute-start.9 = (f32[1024,128]{1,0:T(8,128)S(1)}, f32[1024,128]{1,0:T(8,128)S(1)}, u32[]{:S(2)}, u32[]{:S(2)}) collective-permute-start(f32[1024,128]{1,0:T(8,128)S(1)} %collective-permute-done.8.part_ref), channel_id=1, source_target_pairs={{0,1},{1,0},{2,3},{3,2},{4,5},{5,4},{6,7},{7,6},{8,9},{9,8},{10,11... | collective-permute-start | bytes 1572872 | tf_op jit(solution)/shard_map/ppermute | solution.py:33
  40.5 5.9 %collective-permute-start.10 = (f32[32,1024]{1,0:T(8,128)S(1)}, f32[32,1024]{1,0:T(8,128)S(1)}, u32[]{:S(2)}, u32[]{:S(2)}) collective-permute-start(f32[32,1024]{1,0:T(8,128)S(1)} %get-tuple-element.88), channel_id=1, source_target_pairs={{0,4},{4,0},{8,12},{12,8},{16,20},{20,16},{24,28},{28,24},{1,5},{5... | collective-permute-start | bytes 393224 | tf_op jit(solution)/shard_map/ppermute | solution.py:33
  42.3 8.5 %collective-permute-start.13 = (f32[128,128]{1,0:T(8,128)S(1)}, f32[128,128]{1,0:T(8,128)S(1)}, u32[]{:S(2)}, u32[]{:S(2)}) collective-permute-start(f32[128,128]{1,0:T(8,128)S(1)} %add.64), channel_id=1, source_target_pairs={{0,16},{4,20},{8,24},{12,28},{16,0},{20,4},{24,8},{28,12},{1,17},{... | collective-permute-start | bytes 196616 | tf_op jit(solution)/shard_map/ppermute | solution.py:33
  44.9 5.9 %collective-permute-start.12 = (f32[32,1024]{1,0:T(8,128)S(1)}, f32[32,1024]{1,0:T(8,128)S(1)}, u32[]{:S(2)}, u32[]{:S(2)}) collective-permute-start(f32[32,1024]{1,0:T(8,128)S(1)} %get-tuple-element.92), channel_id=1, source_target_pairs={{0,4},{4,0},{8,12},{12,8},{16,20},{20,16},{24,28},{28,24},{1,5},{5... | collective-permute-start | bytes 393224 | tf_op jit(solution)/shard_map/ppermute | solution.py:33
  46.4 8.8 %collective-permute-start.11 = (f32[16,1024]{1,0:T(8,128)S(1)}, f32[16,1024]{1,0:T(8,128)S(1)}, u32[]{:S(2)}, u32[]{:S(2)}) collective-permute-start(f32[16,1024]{1,0:T(8,128)S(1)} %get-tuple-element.90), channel_id=1, source_target_pairs={{0,24},{4,28},{8,16},{12,20},{16,8},{20,12},{24,0},{28,4},{1,25},{... | collective-permute-start | bytes 196616 | tf_op jit(solution)/shard_map/ppermute | solution.py:33
  50.9 4.3 %collective-permute-start.15 = (f32[16,1024]{1,0:T(8,128)S(1)}, f32[16,1024]{1,0:T(8,128)S(1)}, u32[]{:S(2)}, u32[]{:S(2)}) collective-permute-start(f32[16,1024]{1,0:T(8,128)S(1)} %get-tuple-element.119), channel_id=1, source_target_pairs={{0,8},{4,12},{8,0},{12,4},{16,24},{20,28},{24,16},{28,20},{1,9},{5... | collective-permute-start | bytes 196616 | tf_op jit(solution)/shard_map/ppermute | solution.py:33
  51.8 5.2 %collective-permute-start.14 = (f32[16,1024]{1,0:T(8,128)S(1)}, f32[16,1024]{1,0:T(8,128)S(1)}, u32[]{:S(2)}, u32[]{:S(2)}) collective-permute-start(f32[16,1024]{1,0:T(8,128)S(1)} %get-tuple-element.120), channel_id=1, source_target_pairs={{0,16},{4,20},{8,24},{12,28},{16,0},{20,4},{24,8},{28,12},{1,17},{... | collective-permute-start | bytes 196616 | tf_op jit(solution)/shard_map/ppermute | solution.py:33
  53.6 4.3 %collective-permute-start.16 = (f32[128,128]{1,0:T(8,128)S(1)}, f32[128,128]{1,0:T(8,128)S(1)}, u32[]{:S(2)}, u32[]{:S(2)}) collective-permute-start(f32[128,128]{1,0:T(8,128)S(1)} %add.69), channel_id=1, source_target_pairs={{0,2},{1,3},{2,0},{3,1},{4,6},{5,7},{6,4},{7,5},{8,10},{9,11},{10,... | collective-permute-start | bytes 196616 | tf_op jit(solution)/shard_map/ppermute | solution.py:33
  58.0 8.3 %collective-permute-start.20 = (f32[16,1024]{1,0:T(8,128)S(1)}, f32[16,1024]{1,0:T(8,128)S(1)}, u32[]{:S(2)}, u32[]{:S(2)}) collective-permute-start(f32[16,1024]{1,0:T(8,128)S(1)} %add_add_fusion.refs_0_), channel_id=1, source_target_pairs={{0,4},{4,0},{8,12},{12,8},{16,20},{20,16},{24,28},{28,24},{1,5},{5... | collective-permute-start | bytes 196616 | tf_op jit(solution)/shard_map/ppermute | solution.py:33
  59.5 6.8 %collective-permute-start.19 = (f32[16,1024]{1,0:T(8,128)S(1)}, f32[16,1024]{1,0:T(8,128)S(1)}, u32[]{:S(2)}, u32[]{:S(2)}) collective-permute-start(f32[16,1024]{1,0:T(8,128)S(1)} %add_add_fusion.refs_0_), channel_id=1, source_target_pairs={{0,24},{4,28},{8,16},{12,20},{16,8},{20,12},{24,0},{28,4},{1,25},{... | collective-permute-start | bytes 196616 | tf_op jit(solution)/shard_map/ppermute | solution.py:33
  61.2 5.8 %collective-permute-start.18 = (f32[16,1024]{1,0:T(8,128)S(1)}, f32[16,1024]{1,0:T(8,128)S(1)}, u32[]{:S(2)}, u32[]{:S(2)}) collective-permute-start(f32[16,1024]{1,0:T(8,128)S(1)} %add_add_fusion.refs_0_), channel_id=1, source_target_pairs={{0,16},{4,20},{8,24},{12,28},{16,0},{20,4},{24,8},{28,12},{1,17},{... | collective-permute-start | bytes 196616 | tf_op jit(solution)/shard_map/ppermute | solution.py:33
  61.4 5.6 %collective-permute-start.17 = (f32[16,1024]{1,0:T(8,128)S(1)}, f32[16,1024]{1,0:T(8,128)S(1)}, u32[]{:S(2)}, u32[]{:S(2)}) collective-permute-start(f32[16,1024]{1,0:T(8,128)S(1)} %add_add_fusion.refs_0_), channel_id=1, source_target_pairs={{0,8},{4,12},{8,0},{12,4},{16,24},{20,28},{24,16},{28,20},{1,9},{5... | collective-permute-start | bytes 196616 | tf_op jit(solution)/shard_map/ppermute | solution.py:33
  67.0 5.7 %collective-permute-start.21 = (f32[48,1024]{1,0:T(8,128)S(1)}, f32[48,1024]{1,0:T(8,128)S(1)}, u32[]{:S(2)}, u32[]{:S(2)}) collective-permute-start(f32[48,1024]{1,0:T(8,128)S(1)} %pad_maximum_fusion.refs_1_), channel_id=1, source_target_pairs={{0,4},{4,0},{8,12},{12,8},{16,20},{20,16},{24,28},{28,24},{1,5},{5... | collective-permute-start | bytes 589832 | tf_op jit(solution)/shard_map/ppermute | solution.py:33
  74.1 4.4 %collective-permute-start.24 = (f32[128,128]{1,0:T(8,128)S(1)}, f32[128,128]{1,0:T(8,128)S(1)}, u32[]{:S(2)}, u32[]{:S(2)}) collective-permute-start(f32[128,128]{1,0:T(8,128)S(1)} %get-tuple-element.111), channel_id=1, source_target_pairs={{0,1},{1,0},{2,3},{3,2},{4,5},{5,4},{6,7},{7,6},{8,9},{9,8},{10,11... | collective-permute-start | bytes 196616 | tf_op jit(solution)/shard_map/ppermute | solution.py:33
  74.1 4.3 %collective-permute-start.23 = (f32[128,128]{1,0:T(8,128)S(1)}, f32[128,128]{1,0:T(8,128)S(1)}, u32[]{:S(2)}, u32[]{:S(2)}) collective-permute-start(f32[128,128]{1,0:T(8,128)S(1)} %get-tuple-element.111), channel_id=1, source_target_pairs={{0,3},{1,2},{2,1},{3,0},{4,7},{5,6},{6,5},{7,4},{8,11},{9,10},{10,... | collective-permute-start | bytes 196616 | tf_op jit(solution)/shard_map/ppermute | solution.py:33
  75.8 4.3 %collective-permute-start.22 = (f32[128,128]{1,0:T(8,128)S(1)}, f32[128,128]{1,0:T(8,128)S(1)}, u32[]{:S(2)}, u32[]{:S(2)}) collective-permute-start(f32[128,128]{1,0:T(8,128)S(1)} %get-tuple-element.111), channel_id=1, source_target_pairs={{0,2},{1,3},{2,0},{3,1},{4,6},{5,7},{6,4},{7,5},{8,10},{9,11},{10,... | collective-permute-start | bytes 196616 | tf_op jit(solution)/shard_map/ppermute | solution.py:33
